TPU v7x, 32 devices: a whole 2x2x4 slice. The times are simulated.
32 devices in a mesh: gy: 4 (over x, core), gx: 2 (over y), rep: 4 (over z).
Axes of the slice: x: 2, y: 2, z: 4, core: 2. Of those that a mesh axis runs over, the one named last changes fastest.
Arguments:
- pages: bfloat16 [4, 128, 64, 384], P('rep', 'gy', 'gx'), may hold values from -6 to 6
- cotangent: bfloat16 [4, 128, 64, 384], P('rep', 'gy', 'gx'), may hold values from -6 to 6
- conv_kernel: float32 [7, 7, 384], replicated, may hold values from -0.875 to 0.875
- conv_bias: float32 [384], replicated, may hold values from -3 to 3
- norm_gain: float32 [384], replicated, may hold values from 0.1 to 1.9
- norm_bias: float32 [384], replicated, may hold values from -3 to 3
- w_in: bfloat16 [1536, 384], replicated, may hold values from -0.3125 to 0.3125
- b_in: float32 [1536], replicated, may hold values from -3 to 3
- w_out: bfloat16 [384, 1536], replicated, may hold values from -0.15625 to 0.15625
- b_out: float32 [384], replicated, may hold values from -3 to 3
- layer_scale: float32 [384], replicated, may hold values from 0.2 to 2
Outputs:
- result: bfloat16 [4, 128, 64, 384], P('rep', 'gy', 'gx')
- grad_pages: bfloat16 [4, 128, 64, 384], P('rep', 'gy', 'gx')
- grad_kernel: float32 [7, 7, 384], replicated
- grad_conv_bias: float32 [384], replicated
- grad_gain: float32 [384], replicated
- grad_norm_bias: float32 [384], replicated
- grad_w_in: float32 [1536, 384], replicated
- grad_b_in: float32 [1536], replicated
- grad_w_out: float32 [384, 1536], replicated
- grad_b_out: float32 [384], replicated
- grad_scale: float32 [384], replicated
All inputs are finite; a program needn't handle non-finite values.
Results may differ from a plain program's by a relative error of at most 0.0095.
Values may be sent and summed in bfloat16 or wider, within the bound.
No kernel may reach another device: no remote copies, remote signals or barrier semaphores. Data moves between devices by JAX's collectives and lax.ppermute only.
A program may use at most 128 MiB of HBM per device.

v0:
```python
import jax
import jax.numpy as jnp
from jax import lax
from jax.sharding import PartitionSpec as P

norm_epsilon = 1e-06
inv_root_two = 0.7071067811865476
inv_root_tau = 0.3989422804014327


def with_halo(block, sides, width):
    for axis, dim in sides:
        count = lax.axis_size(axis)
        forward = [(i, i + 1) for i in range(count - 1)]
        backward = [(target, source) for source, target in forward]
        low = lax.ppermute(
            lax.slice_in_dim(block, block.shape[dim] - width, None, axis=dim), axis, forward
        )
        high = lax.ppermute(lax.slice_in_dim(block, 0, width, axis=dim), axis, backward)
        block = jnp.concatenate([low, block, high], axis=dim)
    return block


def gelu_grad(values):
    cdf = 0.5 * (1.0 + lax.erf(values * inv_root_two))
    pdf = jnp.exp(-0.5 * values * values) * inv_root_tau
    return cdf + values * pdf


def shards(
    pages,
    cotangent,
    conv_kernel,
    conv_bias,
    norm_gain,
    norm_bias,
    w_in,
    b_in,
    w_out,
    b_out,
    layer_scale,
):
    tile_rows = pages.shape[1]
    tile_cols = pages.shape[2]
    channels = pages.shape[3]
    padded = with_halo(pages, (("gy", 1), ("gx", 2)), 3)
    accum = jnp.zeros(pages.shape, jnp.float32)
    for row_off in range(7):
        for col_off in range(7):
            accum = (
                accum
                + padded[:, row_off : row_off + tile_rows, col_off : col_off + tile_cols, :].astype(
                    jnp.float32
                )
                * conv_kernel[row_off, col_off]
            )
    depth_out = accum + conv_bias
    average = jnp.mean(depth_out, axis=-1, keepdims=True)
    centred = depth_out - average
    inv_std = lax.rsqrt(jnp.mean(centred * centred, axis=-1, keepdims=True) + norm_epsilon)
    normed = (centred * inv_std).reshape(-1, channels)
    inv_rows = inv_std.reshape(-1, 1)
    ln_out = (normed * norm_gain + norm_bias).astype(jnp.bfloat16)
    pre_act = (
        lax.dot_general(ln_out, w_in, (((1,), (1,)), ((), ())), preferred_element_type=jnp.float32)
        + b_in
    )
    hidden = jax.nn.gelu(pre_act, approximate=False).astype(jnp.bfloat16)
    branch = (
        lax.dot_general(hidden, w_out, (((1,), (1,)), ((), ())), preferred_element_type=jnp.float32)
        + b_out
    )
    page_rows = pages.reshape(-1, channels).astype(jnp.float32)
    result = (page_rows + layer_scale * branch).astype(jnp.bfloat16).reshape(pages.shape)
    cot_rows = cotangent.reshape(-1, channels).astype(jnp.float32)
    g_scale = jnp.sum(cot_rows * branch, axis=0)
    d_branch32 = layer_scale * cot_rows
    g_bout = jnp.sum(d_branch32, axis=0)
    d_branch = d_branch32.astype(jnp.bfloat16)
    g_wout = lax.dot_general(
        d_branch, hidden, (((0,), (0,)), ((), ())), preferred_element_type=jnp.float32
    )
    d_hidden = jnp.dot(d_branch, w_out, preferred_element_type=jnp.float32)
    d_pre32 = d_hidden * gelu_grad(pre_act)
    g_bin = jnp.sum(d_pre32, axis=0)
    d_pre = d_pre32.astype(jnp.bfloat16)
    g_win = lax.dot_general(
        d_pre, ln_out, (((0,), (0,)), ((), ())), preferred_element_type=jnp.float32
    )
    d_norm = jnp.dot(d_pre, w_in, preferred_element_type=jnp.float32)
    g_gain = jnp.sum(d_norm * normed, axis=0)
    g_nbias = jnp.sum(d_norm, axis=0)
    d_scaled = d_norm * norm_gain
    d_depth32 = inv_rows * (
        d_scaled
        - jnp.mean(d_scaled, axis=-1, keepdims=True)
        - normed * jnp.mean(d_scaled * normed, axis=-1, keepdims=True)
    )
    d_depth = d_depth32.astype(jnp.bfloat16).reshape(pages.shape)
    depth_f = d_depth.astype(jnp.float32)
    g_cbias = jnp.sum(depth_f, axis=(0, 1, 2))
    kernel_terms = []
    for row_off in range(7):
        for col_off in range(7):
            piece = padded[
                :, row_off : row_off + tile_rows, col_off : col_off + tile_cols, :
            ].astype(jnp.float32)
            kernel_terms.append(jnp.sum(depth_f * piece, axis=(0, 1, 2)))
    g_kernel = jnp.stack(kernel_terms).reshape(7, 7, channels)
    grad_pad = with_halo(d_depth, (("gy", 1), ("gx", 2)), 3)
    back = jnp.zeros(pages.shape, jnp.float32)
    for row_off in range(7):
        for col_off in range(7):
            back = (
                back
                + grad_pad[
                    :,
                    6 - row_off : 6 - row_off + tile_rows,
                    6 - col_off : 6 - col_off + tile_cols,
                    :,
                ].astype(jnp.float32)
                * conv_kernel[row_off, col_off]
            )
    grad_pages = (cotangent.astype(jnp.float32) + back).astype(jnp.bfloat16)
    summed = lax.psum(
        (g_win, g_wout, g_kernel, g_cbias, g_gain, g_nbias, g_bin, g_bout, g_scale),
        ("gy", "gx", "rep"),
    )
    sum_win, sum_wout = (summed[0], summed[1])
    small = summed[2:]
    pixels = (
        pages.shape[0]
        * tile_rows
        * tile_cols
        * lax.axis_size("gy")
        * lax.axis_size("gx")
        * lax.axis_size("rep")
    )
    factor = float(pixels) ** (-0.5)
    return (
        result,
        grad_pages,
        small[0] * factor,
        small[1] * factor,
        small[2] * factor,
        small[3] * factor,
        sum_win * factor,
        small[4] * factor,
        sum_wout * factor,
        small[5] * factor,
        small[6] * factor,
    )


def solution(mesh):
    placed = (
        P("rep", "gy", "gx", None),
        P("rep", "gy", "gx", None),
        P(),
        P(),
        P(),
        P(),
        P(),
        P(),
        P(),
        P(),
        P(),
    )
    return jax.shard_map(
        shards,
        mesh=mesh,
        in_specs=placed,
        out_specs=(
            P("rep", "gy", "gx", None),
            P("rep", "gy", "gx", None),
            P(),
            P(),
            P(),
            P(),
            P(),
            P(),
            P(),
            P(),
            P(),
        ),
        check_vma=False,
    )
```

profile of v0, /device:TPU:0, one launch (start us, length us, event | category | flops | bytes accessed | tf_op | source)
XLA Modules:
  0.0 310.9 jit_solution(3369739276873254366)
XLA Ops:
  7.2 0.0 copy-start
  7.2 0.0 copy-start.6
  7.2 0.0 all-reduce.4.cloned.1.call-start
  7.2 1.1 fusion.203
  8.3 2.4 collective-permute-start
  10.7 1.3 collective-permute-start.1
  12.0 1.2 slice_reduce_fusion.47
  13.2 1.4 fusion.138
  14.6 1.3 slice_reduce_fusion.48
  15.9 0.0 copy-start.13
  15.9 0.4 constant_dynamic-update-slice_fusion.3
  16.4 0.1 fusion.201
  16.5 4.3 %collective-permute-start.2 = (bf16[1,38,3,384]{3,2,1,0:T(4,128)(2,1)S(1)}, bf16[1,38,3,384]{3,2,1,0:T(4,128)(2,1)S(1)}, u32[]{:S(2)}, u32[]{:S(2)}) collective-permute-start(bf16[1,38,3,384]{3,2,1,0:T(4,128)(2,1)S(1)} %get-tuple-element.141), channel_id=1, source_target_pairs={{0,4},{1,5},{2,6},{3,7},{8,12},{9,13},{10,14},{11,15},{16,20},{17,... | collective-permute-start | bytes 262664 | tf_op jit(solution)/shard_map/ppermute | solution.py:16
  20.8 1.3 collective-permute-start.3
  22.1 1.0 slice_reduce_fusion.46
  23.0 0.1 collective-permute-done.2
  23.1 4.4 %collective-permute-done.3 = bf16[1,38,3,384]{3,2,1,0:T(4,128)(2,1)S(1)} collective-permute-done((bf16[1,38,3,384]{3,2,1,0:T(4,128)(2,1)S(1)}, bf16[1,38,3,384]{3,2,1,0:T(4,128)(2,1)S(1)}, u32[]{:S(2)}, u32[]{:S(2)}) %collective-permute-start.3) | collective-permute-done | bytes 87584 | tf_op jit(solution)/shard_map/ppermute | solution.py:19
  27.5 15.7 %fusion.199 = (f32[32,32]{1,0:T(8,128)S(1)}, f32[1,32,32,384]{3,2,1,0:T(8,128)S(1)}) fusion(f32[384]{0:T(512)S(1)} %copy-done.13, f32[384]{0:T(512)S(1)} %get-tuple-element.120, bf16[1,38,3,384]{3,2,1,0:T(4,128)(2,1)S(1)} %collective-permute-done.3, bf16[1,38,32,384]{3,2,1,0:T(8,128)(2,1)S(1)} %get-tuple-element.154, f32[384]{0:T(512)S(1)} %get-tuple-element.121, ...), kind=kLoop, calls=%fused_computation.445 | loop fusion | flops 107740160 | bytes 8267776 | tf_op jit(solution)/shard_map/reduce_sum | solution.py:58
  43.2 0.4 multiply_reduce_fusion
  43.6 0.0 copy-start.12
  43.6 0.0 copy-start.14
  43.7 0.4 subtract_multiply_fusion
  44.0 0.3 copy-done.12
  44.3 0.0 copy-done.14
  44.3 0.2 fusion.142
  44.5 0.5 copy-done.17
  45.0 15.1 %fusion.2 = (bf16[1024,1536]{1,0:T(8,128)(2,1)S(1)}, f32[1024,1536]{1,0:T(8,128)S(1)}) fusion(f32[1536]{0:T(1024)S(1)} %copy-done.17, bf16[1024,384]{1,0:T(8,128)(2,1)S(1)} %fusion.142, bf16[1536,384]{1,0:T(8,128)(2,1)S(1)} %copy-done), kind=kOutput, calls=%fused_computation.94 | convolution fusion | flops 1311768576 | bytes 11409408 | tf_op jit(solution)/shard_map/dot_general | solution.py:65
  60.2 2.9 fusion.140
  63.1 2.8 fusion.205
  66.0 3.9 %fusion.204 = (f32[1536]{0:T(1024)S(1)}, bf16[1024,1536]{1,0:T(8,128)(2,1)S(1)}) fusion(f32[1024,1536]{1,0:T(8,128)S(1)} %get-tuple-element.156, f32[1536]{0:T(1024)S(1)} %copy-done.17, bf16[1024,384]{1,0:T(8,128)(2,1)S(1)} %get-tuple-element.143, bf16[384,1536]{1,0:T(8,128)(2,1)S(1)} %copy-done.16), kind=kOutput, calls=%fused_computation.449 | convolution fusion | flops 1226832384 | bytes 11415552 | tf_op jit(solution)/shard_map/dot_general | solution.py:83
  69.9 3.3 %fusion.149 = f32[1536,384]{1,0:T(8,128)} fusion(bf16[1024,384]{1,0:T(8,128)(2,1)S(1)} %fusion.142, bf16[1024,1536]{1,0:T(8,128)(2,1)S(1)} %get-tuple-element.159), kind=kOutput, calls=%fused_computation.307 | convolution fusion | flops 1207959552 | bytes 6291456 | tf_op jit(solution)/shard_map/dot_general | solution.py:87
  73.1 3.0 fusion.147
  76.2 0.1 rsqrt.16
  76.2 2.4 convert_reduce_fusion
  78.7 0.4 fusion.105
  79.1 41.8 %all-reduce = (f32[384]{0:T(512)S(1)}, f32[384]{0:T(512)S(1)}, f32[384]{0:T(512)S(1)}, f32[1536]{0:T(1024)S(1)}, f32[384]{0:T(512)S(1)}, /*index=5*/f32[384]{0:T(512)S(1)}) all-reduce(f32[384]{0:T(512)S(1)} %get-tuple-element.131, f32[384]{0:T(512)S(1)} %get-tuple-element.11, ...), channel_id=1, replica_groups=mesh['gy'=4,'gx'=2,'rep'=4] {'gy','gx','rep'}, use_global_device_ids=true, to_apply=%region_55.0 | all-reduce | flops 3456 | bytes 27648 | tf_op jit(solution)/shard_map/psum | solution.py:125
  120.9 0.6 broadcast_multiply_fusion.4
  121.5 0.6 broadcast_multiply_fusion.10
  122.1 0.6 broadcast_multiply_fusion.11
  122.7 0.6 broadcast_multiply_fusion.7
  123.3 1.3 collective-permute-start.4
  124.6 0.0 copy-start.7
  124.6 1.4 collective-permute-start.5
  126.0 3.1 fusion.135
  129.1 2.7 fusion.131
  131.8 2.9 fusion.133
  134.7 3.1 fusion.136
  137.8 2.7 fusion.132
  140.5 0.6 broadcast_multiply_fusion.8
  141.1 0.1 pad_maximum_fusion.7
  141.2 1.3 collective-permute-start.6
  142.5 4.6 %collective-permute-start.7 = (bf16[1,38,3,384]{3,2,1,0:T(4,128)(2,1)S(1)}, bf16[1,38,3,384]{3,2,1,0:T(4,128)(2,1)S(1)}, u32[]{:S(2)}, u32[]{:S(2)}) collective-permute-start(bf16[1,38,3,384]{3,2,1,0:T(4,128)(2,1)S(1)} %get-tuple-element.140), channel_id=1, source_target_pairs={{0,4},{1,5},{2,6},{3,7},{8,12},{9,13},{10,14},{11,15},{16,20},{17,... | collective-permute-start | bytes 262664 | tf_op jit(solution)/shard_map/ppermute | solution.py:16
  147.1 0.6 broadcast_multiply_fusion.9
  148.2 0.2 stack.199
  148.4 0.7 reshape.266
  149.0 0.0 all-reduce.4.cloned.1.call-update
  149.0 0.4 collective-permute-done.7
  149.4 0.7 pad_maximum_fusion
  150.1 0.0 copy-done.9
  150.2 15.5 %fusion.137 = bf16[1,32,32,384]{3,2,1,0:T(8,128)(2,1)} fusion(bf16[1,32,32,384]{3,2,1,0:T(8,128)(2,1)S(1)} %copy-done.9, bf16[1,32,32,384]{3,2,1,0:T(8,128)(2,1)S(1)} %bitcast.97, bf16[1,3,32,384]{3,2,1,0:T(8,128)(2,1)S(1)} %collective-permute-done.4, bf16[1,3,32,384]{3,2,1,0:T(8,128)(2,1)S(1)} %collective-permute-done.5, ...), kind=kLoop, calls=%fused_computation.289 | loop fusion | flops 60948480 | bytes 35612160 | tf_op jit(solution)/shard_map/convert_element_type | solution.py:124
  165.7 132.7 %all-reduce.4.cloned.1.call-done = (f32[7,7,384]{2,1,0:T(8,128)}, f32[1536,384]{1,0:T(8,128)}, f32[384,1536]{1,0:T(8,128)}) async-done(((f32[7,7,384]{2,1,0:T(8,128)}, f32[1536,384]{1,0:T(8,128)}, f32[384,1536]{1,0:T(8,128)}), (f32[7,7,384]{2,1,0:T(8,128)}, f32[1536,384]{1,0:T(8,128)}, f32[384,1536]{1,0:T(8,128)})) %all-reduce.4.cloned.1.call-update) | async-done | bytes 4793872 | tf_op jit(solution)/shard_map/psum | solution.py:125
  298.4 3.4 %broadcast_multiply_fusion = f32[384,1536]{1,0:T(8,128)} fusion(f32[384,1536]{1,0:T(8,128)} %get-tuple-element.130), kind=kLoop, calls=%fused_computation.315 | loop fusion | flops 589824 | bytes 4718592 | tf_op jit(solution)/shard_map/mul | solution.py:149
  301.8 1.6 broadcast_multiply_fusion.1
  303.5 0.6 broadcast_multiply_fusion.2
  (88 shorter events, 0.3 us)
Async XLA Ops:
  7.2 37.3 %copy-start = (bf16[1536,384]{1,0:T(8,128)(2,1)S(1)}, bf16[1536,384]{1,0:T(8,128)(2,1)}, u32[]{:S(2)}) copy-start(bf16[1536,384]{1,0:T(8,128)(2,1)} %param.17) | copy-start | bytes 3538948
  7.2 8.7 %copy-start.6 = (bf16[1,32,32,384]{3,2,1,0:T(8,128)(2,1)S(1)}, bf16[1,32,32,384]{3,2,1,0:T(8,128)(2,1)}, u32[]{:S(2)}) copy-start(bf16[1,32,32,384]{3,2,1,0:T(8,128)(2,1)} %param.11) | copy-start | bytes 2359300
  7.2 291.2 %all-reduce.4.cloned.1.call-start = ((), (), s32[]{:S(2)}) async-start(), calls=%async_computation | async-start | bytes 9609216 | tf_op jit(solution)/shard_map/psum | solution.py:125
  8.3 7.5 %collective-permute-start = (bf16[1,3,32,384]{3,2,1,0:T(8,128)(2,1)S(1)}, bf16[1,3,32,384]{3,2,1,0:T(8,128)(2,1)S(1)}, u32[]{:S(2)}, u32[]{:S(2)}) collective-permute-start(bf16[1,3,32,384]{3,2,1,0:T(8,128)(2,1)S(1)} %get-tuple-element.150), channel_id=1, source_target_pairs={{0,8},{8,16},{16,24},{1,9},{9,17},{17,25},{2,10},{10,18},{18,26},{... | collective-permute-start | bytes 221192 | tf_op jit(solution)/shard_map/ppermute | solution.py:16
  10.7 5.6 %collective-permute-start.1 = (bf16[1,3,32,384]{3,2,1,0:T(8,128)(2,1)S(1)}, bf16[1,3,32,384]{3,2,1,0:T(8,128)(2,1)S(1)}, u32[]{:S(2)}, u32[]{:S(2)}) collective-permute-start(bf16[1,3,32,384]{3,2,1,0:T(8,128)(2,1)S(1)} %get-tuple-element.149), channel_id=1, source_target_pairs={{8,0},{16,8},{24,16},{9,1},{17,9},{25,17},{10,2},{18,10},{26,18},{... | collective-permute-start | bytes 221192 | tf_op jit(solution)/shard_map/ppermute | solution.py:19
  15.9 11.6 %copy-start.13 = (f32[384]{0:T(512)S(1)}, f32[384]{0:T(512)}, u32[]{:S(2)}) copy-start(f32[384]{0:T(512)} %param.14) | copy-start | bytes 4612
  16.3 26.9 %copy-start.3 = (bf16[1,35,32,384]{3,2,1,0:T(8,128)(2,1)}, bf16[1,35,32,384]{3,2,1,0:T(8,128)(2,1)S(1)}, u32[]{:S(2)}) copy-start(bf16[1,35,32,384]{3,2,1,0:T(8,128)(2,1)S(1)} %get-tuple-element.146) | copy-start | bytes 2580484
  16.4 26.8 %copy-start.1 = (bf16[1,35,32,384]{3,2,1,0:T(8,128)(2,1)}, bf16[1,35,32,384]{3,2,1,0:T(8,128)(2,1)S(1)}, u32[]{:S(2)}) copy-start(bf16[1,35,32,384]{3,2,1,0:T(8,128)(2,1)S(1)} %get-tuple-element.153) | copy-start | bytes 2580484
  16.5 6.6 %collective-permute-start.2 = (bf16[1,38,3,384]{3,2,1,0:T(4,128)(2,1)S(1)}, bf16[1,38,3,384]{3,2,1,0:T(4,128)(2,1)S(1)}, u32[]{:S(2)}, u32[]{:S(2)}) collective-permute-start(bf16[1,38,3,384]{3,2,1,0:T(4,128)(2,1)S(1)} %get-tuple-element.141), channel_id=1, source_target_pairs={{0,4},{1,5},{2,6},{3,7},{8,12},{9,13},{10,14},{11,15},{16,20},{17,... | collective-permute-start | bytes 262664 | tf_op jit(solution)/shard_map/ppermute | solution.py:16
  20.8 6.8 %collective-permute-start.3 = (bf16[1,38,3,384]{3,2,1,0:T(4,128)(2,1)S(1)}, bf16[1,38,3,384]{3,2,1,0:T(4,128)(2,1)S(1)}, u32[]{:S(2)}, u32[]{:S(2)}) collective-permute-start(bf16[1,38,3,384]{3,2,1,0:T(4,128)(2,1)S(1)} %get-tuple-element.142), channel_id=1, source_target_pairs={{4,0},{5,1},{6,2},{7,3},{12,8},{13,9},{14,10},{15,11},{20,16},{21,... | collective-permute-start | bytes 262664 | tf_op jit(solution)/shard_map/ppermute | solution.py:19
  43.6 0.7 copy-start.12
  43.6 0.7 copy-start.14
  44.3 28.8 %copy-start.5 = (f32[1,32,32,384]{3,2,1,0:T(8,128)}, f32[1,32,32,384]{3,2,1,0:T(8,128)S(1)}, u32[]{:S(2)}) copy-start(f32[1,32,32,384]{3,2,1,0:T(8,128)S(1)} %subtract_multiply_fusion) | copy-start | bytes 4718596
  44.3 0.7 copy-start.17
  45.0 15.1 %copy-start.8 = (bf16[1,32,32,384]{3,2,1,0:T(8,128)(2,1)S(1)}, bf16[1,32,32,384]{3,2,1,0:T(8,128)(2,1)}, u32[]{:S(2)}) copy-start(bf16[1,32,32,384]{3,2,1,0:T(8,128)(2,1)} %param.12) | copy-start | bytes 2359300
  45.0 15.1 %copy-start.15 = (f32[384]{0:T(512)S(1)}, f32[384]{0:T(512)}, u32[]{:S(2)}) copy-start(f32[384]{0:T(512)} %param.21) | copy-start | bytes 4612
  45.0 15.1 %copy-start.16 = (bf16[384,1536]{1,0:T(8,128)(2,1)S(1)}, bf16[384,1536]{1,0:T(8,128)(2,1)}, u32[]{:S(2)}) copy-start(bf16[384,1536]{1,0:T(8,128)(2,1)} %param.19) | copy-start | bytes 3538948
  45.0 15.2 %copy-start.18 = (f32[384]{0:T(512)S(1)}, f32[384]{0:T(512)}, u32[]{:S(2)}) copy-start(f32[384]{0:T(512)} %param.20) | copy-start | bytes 4612
  76.2 2.5 copy-start.4
  123.3 17.8 %collective-permute-start.4 = (bf16[1,3,32,384]{3,2,1,0:T(8,128)(2,1)S(1)}, bf16[1,3,32,384]{3,2,1,0:T(8,128)(2,1)S(1)}, u32[]{:S(2)}, u32[]{:S(2)}) collective-permute-start(bf16[1,3,32,384]{3,2,1,0:T(8,128)(2,1)S(1)} %get-tuple-element.145), channel_id=1, source_target_pairs={{0,8},{8,16},{16,24},{1,9},{9,17},{17,25},{2,10},{10,18},{18,26},{... | collective-permute-start | bytes 221192 | tf_op jit(solution)/shard_map/ppermute | solution.py:16
  124.6 7.2 %copy-start.2 = (bf16[1,35,32,384]{3,2,1,0:T(8,128)(2,1)S(1)}, bf16[1,35,32,384]{3,2,1,0:T(8,128)(2,1)}, u32[]{:S(2)}) copy-start(bf16[1,35,32,384]{3,2,1,0:T(8,128)(2,1)} %copy-done.1) | copy-start | bytes 2580484
  124.6 7.2 %copy-start.7 = (bf16[1,32,32,384]{3,2,1,0:T(8,128)(2,1)S(1)}, bf16[1,32,32,384]{3,2,1,0:T(8,128)(2,1)}, u32[]{:S(2)}) copy-start(bf16[1,32,32,384]{3,2,1,0:T(8,128)(2,1)} %param.11) | copy-start | bytes 2359300
  124.6 16.5 %collective-permute-start.5 = (bf16[1,3,32,384]{3,2,1,0:T(8,128)(2,1)S(1)}, bf16[1,3,32,384]{3,2,1,0:T(8,128)(2,1)S(1)}, u32[]{:S(2)}, u32[]{:S(2)}) collective-permute-start(bf16[1,3,32,384]{3,2,1,0:T(8,128)(2,1)S(1)} %get-tuple-element.144), channel_id=1, source_target_pairs={{8,0},{16,8},{24,16},{9,1},{17,9},{25,17},{10,2},{18,10},{26,18},{... | collective-permute-start | bytes 221192 | tf_op jit(solution)/shard_map/ppermute | solution.py:19
  141.2 7.8 %collective-permute-start.6 = (bf16[1,38,3,384]{3,2,1,0:T(4,128)(2,1)S(1)}, bf16[1,38,3,384]{3,2,1,0:T(4,128)(2,1)S(1)}, u32[]{:S(2)}, u32[]{:S(2)}) collective-permute-start(bf16[1,38,3,384]{3,2,1,0:T(4,128)(2,1)S(1)} %get-tuple-element.139), channel_id=1, source_target_pairs={{4,0},{5,1},{6,2},{7,3},{12,8},{13,9},{14,10},{15,11},{20,16},{21,... | collective-permute-start | bytes 262664 | tf_op jit(solution)/shard_map/ppermute | solution.py:19
  142.5 6.9 %collective-permute-start.7 = (bf16[1,38,3,384]{3,2,1,0:T(4,128)(2,1)S(1)}, bf16[1,38,3,384]{3,2,1,0:T(4,128)(2,1)S(1)}, u32[]{:S(2)}, u32[]{:S(2)}) collective-permute-start(bf16[1,38,3,384]{3,2,1,0:T(4,128)(2,1)S(1)} %get-tuple-element.140), channel_id=1, source_target_pairs={{0,4},{1,5},{2,6},{3,7},{8,12},{9,13},{10,14},{11,15},{16,20},{17,... | collective-permute-start | bytes 262664 | tf_op jit(solution)/shard_map/ppermute | solution.py:16
  149.0 1.1 copy-start.9
  298.4 3.4 %copy-start.10 = (f32[1536,384]{1,0:T(8,128)S(1)}, f32[1536,384]{1,0:T(8,128)}, u32[]{:S(2)}) copy-start(f32[1536,384]{1,0:T(8,128)} %get-tuple-element.129) | copy-start | bytes 7077892
  301.8 1.6 copy-start.11
Sparse Core Ops, SparseCore 0:
  149.1 149.2 all-reduce.3
where the time goes:
time: 312 us; the launch traced here: 311 us
  waiting for transfers between devices  138 us (44%)
  other arithmetic  60.8 us (19%)
  blocking collectives  41.8 us (13%)
  matrix products  31.1 us (10%)
  starting transfers between devices  17.8 us (6%)
  between operations  14.8 us (5%)
  local copies, waits for them, and re-layouts  7.09 us (2%)
    psum x1, waiting for transfers between devices, shards(): lax.psum((g_win, g_wout, g_kernel, g_cbias, g_gain, g_nbias, g_bin, g_bou...  133 us
    psum x1, blocking collectives, shards(): lax.psum((g_win, g_wout, g_kernel, g_cbias, g_gain, g_nbias, g_bin, g_bou...  41.8 us
    reduce_sum x1, other arithmetic, shards(): average = jnp.mean(depth_out, axis=-1, keepdims=True)  15.7 us
    convert_element_type x1, other arithmetic, shards(): grad_pages = (cotangent.astype(jnp.float32) + back).astype(jnp.bfloat16)  15.5 us
    dot_general x1, matrix products, shards(): lax.dot_general(ln_out, w_in, (((1,), (1,)), ((), ())), preferred_element...  15.1 us
    reduce_sum x6, other arithmetic, shards(): kernel_terms.append(jnp.sum(depth_f * piece, axis=(0, 1, 2)))  14.9 us
    ppermute x4, starting transfers between devices, with_halo(): lax.ppermute(lax.slice_in_dim(block, block.shape[dim] - width, None, axis...  12.5 us
  transfers between devices with their start and end apart: 9, of which 4 were waited for; matrix products, arithmetic and copies ran while one was open for 12% of the time, Pallas kernels for 0%

commit v1 on v0

v1 whole, which is shorter than its diff:
```python
import functools

import jax
import jax.numpy as jnp
from jax import lax
from jax.experimental import pallas as pl
from jax.experimental.pallas import tpu as pltpu
from jax.sharding import PartitionSpec as P

norm_epsilon = 1e-06
inv_root_two = 0.7071067811865476
inv_root_tau = 0.3989422804014327

LANES = 128
EDGE = 8
BAND = 16
AXES = ("gy", "gx", "rep")
f32 = jnp.float32
bf16 = jnp.bfloat16


def dot(a, b, dims):
    return lax.dot_general(a, b, (dims, ((), ())), preferred_element_type=f32)


NN = ((1,), (0,))
NT = ((1,), (1,))
TN = ((0,), (0,))


def pair_rounds(count):
    first = [(i, i + 1) for i in range(0, count - 1, 2)]
    second = [(i, i + 1) for i in range(1, count - 1, 2)]
    return [pairs + [(b, a) for a, b in pairs] for pairs in (first, second)]


def edges(block, axis, dim, width):
    size = block.shape[dim]
    even = lax.axis_index(axis) % 2 == 0
    low = lax.slice_in_dim(block, 0, width, axis=dim)
    high = lax.slice_in_dim(block, size - width, size, axis=dim)
    out = []
    for pairs, is_high in zip(pair_rounds(lax.axis_size(axis)), (even, ~even)):
        if pairs:
            out.append(lax.ppermute(jnp.where(is_high, high, low), axis, pairs))
        else:
            out.append(jnp.zeros_like(low))
    return out


def halo(tile):
    rows = edges(tile, "gy", 0, 3)
    even = lax.axis_index("gy") % 2 == 0
    top = jnp.where(even, rows[1], rows[0])
    bottom = jnp.where(even, rows[0], rows[1])
    even_x = lax.axis_index("gx") % 2 == 0
    size = tile.shape[1]
    column = [jnp.concatenate([part[:, :3], part[:, size - 3 :]], axis=1) for part in (top, tile, bottom)]
    column = jnp.concatenate(column, axis=0)
    out = []
    for pairs, is_high in zip(pair_rounds(lax.axis_size("gx")), (even_x, ~even_x)):
        if pairs:
            out.append(lax.ppermute(jnp.where(is_high, column[:, 3:], column[:, :3]), "gx", pairs))
        else:
            out.append(jnp.zeros_like(column[:, :3]))
    left = jnp.where(even_x, out[1], out[0])
    right = jnp.where(even_x, out[0], out[1])
    return top, bottom, left, right


def fill(pad, tile, top, bottom, left, right):
    rows, cols, channels = tile.shape
    for slab in range(channels // LANES):
        at = slice(slab * LANES, (slab + 1) * LANES)
        pad[slab, 0:3, EDGE : EDGE + cols, :] = top[:, :, at].astype(f32)
        pad[slab, 3 + rows :, EDGE : EDGE + cols, :] = bottom[:, :, at].astype(f32)
        pad[slab, :, EDGE - 3 : EDGE, :] = left[:, :, at].astype(f32)
        pad[slab, :, EDGE + cols : EDGE + cols + 3, :] = right[:, :, at].astype(f32)

        def body(row, _):
            pad[slab, row + 3, EDGE : EDGE + cols, :] = tile[row, :, at].astype(f32)
            return _

        lax.fori_loop(0, rows, body, 0, unroll=4)


def steps(rows, cols, channels, body):
    slabs, tiles, bands = channels // LANES, cols // 8, rows // BAND

    def step(i, _):
        slab = i // (tiles * bands)
        rest = i % (tiles * bands)
        body(slab, pl.multiple_of(rest // bands * 8, 8), rest % bands * BAND)
        return _

    lax.fori_loop(0, slabs * tiles * bands, step, 0)


def lanes(slab):
    return pl.ds(pl.multiple_of(slab * LANES, LANES), LANES)


def taps(pad, kernel, slab, col, row, flip):
    acc = [None] * BAND
    for b in range(7):
        scale = []
        for a in range(7):
            tap = (6 - a) * 7 + 6 - b if flip else a * 7 + b
            scale.append(jnp.broadcast_to(kernel[pl.ds(tap, 1), lanes(slab)], (8, LANES)))
        for r in range(BAND + 6):
            x = pad[slab, row + r, pl.ds(col + EDGE - 3 + b, 8), :]
            for a in range(7):
                i = r - a
                if 0 <= i < BAND:
                    acc[i] = x * scale[a] if acc[i] is None else acc[i] + x * scale[a]
    return acc


def conv_norm_kernel(
    tile, top, bottom, left, right, kernel, bias, gain, shift, normed_ref, inv_ref, ln_ref, pad, depth
):
    rows, cols, channels = tile.shape
    fill(pad, tile, top, bottom, left, right)

    def piece(slab, col, row):
        acc = taps(pad, kernel, slab, col, row, False)
        add = jnp.broadcast_to(bias[:, lanes(slab)], (8, LANES))
        for i in range(BAND):
            at = pl.ds(pl.multiple_of((row + i) * cols + col, 8), 8)
            depth[at, lanes(slab)] = acc[i] + add

    steps(rows, cols, channels, piece)
    block = 128

    def norm(i, _):
        at = pl.ds(pl.multiple_of(i * block, block), block)
        x = depth[at, :]
        centred = x - jnp.mean(x, axis=-1, keepdims=True)
        inv = lax.rsqrt(jnp.mean(centred * centred, axis=-1, keepdims=True) + norm_epsilon)
        normed = centred * inv
        normed_ref[at, :] = normed
        inv_ref[at, :] = jnp.broadcast_to(inv, (block, LANES))
        ln_ref[at, :] = (normed * gain[...] + shift[...]).astype(bf16)
        return _

    lax.fori_loop(0, rows * cols // block, norm, 0)


def gelu_pair(u):
    cdf = 0.5 * (1.0 + lax.erf(u * inv_root_two))
    pdf = jnp.exp(-0.5 * u * u) * inv_root_tau
    return u * cdf, cdf + u * pdf


def fold(x):
    return jnp.sum(x.reshape(-1, 8, x.shape[1]), axis=0)


def mlp_block(ln, d_branch, w_in, w_out, b_in, base, width, hid_ref, dpre_ref, gbin):
    sub = 256
    count = width // sub

    def products(s):
        at = pl.ds(base + s * sub, sub)
        return dot(ln, w_in[at, :], NT), dot(d_branch, w_out[:, at], NN)

    ahead = products(0)
    for s in range(count):
        pre, d_hidden = ahead
        if s + 1 < count:
            ahead = products(s + 1)
        act, slope = gelu_pair(pre + b_in[:, base + s * sub : base + (s + 1) * sub])
        d_pre = d_hidden * slope
        gbin[:, s * sub : (s + 1) * sub] += fold(d_pre)
        hid_ref[:, s * sub : (s + 1) * sub] = act.astype(bf16)
        dpre_ref[:, s * sub : (s + 1) * sub] = d_pre.astype(bf16)
    at = pl.ds(base, width)
    hidden, d_pre = hid_ref[...], dpre_ref[...]
    branch = dot(hidden, w_out[:, at], NT)
    d_norm = dot(d_pre, w_in[at, :], NN)
    return hidden, d_pre, branch, d_norm


def pack_grads(pack, gwin, gwout, gbin_ref, gbin):
    width, channels = gwin.shape
    pack[0:width, :] = gwin[...].astype(bf16)
    for j in range(width // channels):
        pack[width + j * channels : width + (j + 1) * channels, :] = gwout[
            :, j * channels : (j + 1) * channels
        ].astype(bf16)
    gbin_ref[...] = jnp.sum(gbin[...], axis=0, keepdims=True)


MLP_BLOCK = 256


def mlp_first_kernel(
    base, width, ln_ref, cot, w_in, w_out, b_in, scale, branch_ref, dnorm_ref, pack, gbin_ref,
    hid_ref, dpre_ref, gwin, gwout, gbin,
):
    gwin[...] = jnp.zeros_like(gwin)
    gwout[...] = jnp.zeros_like(gwout)
    gbin[...] = jnp.zeros_like(gbin)

    def step(i, _):
        at = pl.ds(pl.multiple_of(i * MLP_BLOCK, MLP_BLOCK), MLP_BLOCK)
        ln = ln_ref[at, :]
        d_branch = (scale[...] * cot[at, :].astype(f32)).astype(bf16)
        hidden, d_pre, branch, d_norm = mlp_block(
            ln, d_branch, w_in, w_out, b_in, base, width, hid_ref, dpre_ref, gbin
        )
        branch_ref[at, :] = branch
        dnorm_ref[at, :] = d_norm
        gwin[...] += dot(d_pre, ln, TN)
        gwout[...] += dot(d_branch, hidden, TN)
        return _

    lax.fori_loop(0, ln_ref.shape[0] // MLP_BLOCK, step, 0)
    pack_grads(pack, gwin, gwout, gbin_ref, gbin)


def mlp_second_kernel(
    base, width, ln_ref, cot, w_in, w_out, b_in, scale, b_out, gain, page, normed_ref, inv_ref,
    branch_ref, dnorm_ref,
    result, d_depth_ref, pack, gbin_ref, sums_ref,
    hid_ref, dpre_ref, gwin, gwout, gbin, sums,
):
    gwin[...] = jnp.zeros_like(gwin)
    gwout[...] = jnp.zeros_like(gwout)
    gbin[...] = jnp.zeros_like(gbin)
    sums[...] = jnp.zeros_like(sums)

    def step(i, _):
        at = pl.ds(pl.multiple_of(i * MLP_BLOCK, MLP_BLOCK), MLP_BLOCK)
        ln = ln_ref[at, :]
        cot32 = cot[at, :].astype(f32)
        d_branch32 = scale[...] * cot32
        d_branch = d_branch32.astype(bf16)
        hidden, d_pre, branch, d_norm = mlp_block(
            ln, d_branch, w_in, w_out, b_in, base, width, hid_ref, dpre_ref, gbin
        )
        gwin[...] += dot(d_pre, ln, TN)
        gwout[...] += dot(d_branch, hidden, TN)
        branch = branch + branch_ref[at, :] + b_out[...]
        result[at, :] = (page[at, :].astype(f32) + scale[...] * branch).astype(bf16)
        d_norm = d_norm + dnorm_ref[at, :]
        normed = normed_ref[at, :]
        inv = inv_ref[at, 0:1]
        weighted = d_norm * normed
        s = d_norm * gain[...]
        mean_s = jnp.mean(s, axis=-1, keepdims=True)
        mean_sn = jnp.mean(s * normed, axis=-1, keepdims=True)
        d_depth = (inv * (s - mean_s - normed * mean_sn)).astype(bf16)
        d_depth_ref[at, :] = d_depth
        sums[0] += fold(cot32 * branch)
        sums[1] += fold(d_branch32)
        sums[2] += fold(weighted)
        sums[3] += fold(d_norm)
        sums[4] += fold(d_depth.astype(f32))
        return _

    lax.fori_loop(0, ln_ref.shape[0] // MLP_BLOCK, step, 0)
    pack_grads(pack, gwin, gwout, gbin_ref, gbin)
    for j in range(5):
        sums_ref[j : j + 1, :] = jnp.sum(sums[j], axis=0, keepdims=True)


def kernel_grad_kernel(tile, top, bottom, left, right, d_depth, out, pad, d32, acc_ref):
    rows, cols, channels = tile.shape
    fill(pad, tile, top, bottom, left, right)
    d32[...] = d_depth[...].astype(f32)
    acc_ref[...] = jnp.zeros_like(acc_ref)

    def piece(slab, col, row):
        grads = []
        for i in range(BAND):
            at = pl.ds(pl.multiple_of((row + i) * cols + col, 8), 8)
            grads.append(d32[at, lanes(slab)])
        for b in range(7):
            acc = [None] * 7
            for r in range(BAND + 6):
                x = pad[slab, row + r, pl.ds(col + EDGE - 3 + b, 8), :]
                for a in range(7):
                    i = r - a
                    if 0 <= i < BAND:
                        acc[a] = x * grads[i] if acc[a] is None else acc[a] + x * grads[i]
            for a in range(7):
                acc_ref[slab, a * 7 + b] += acc[a]

    steps(rows, cols, channels, piece)
    for slab in range(channels // LANES):
        out[:, slab * LANES : (slab + 1) * LANES] = jnp.sum(acc_ref[slab], axis=1)


def conv_grad_kernel(tile, top, bottom, left, right, kernel, cot, out, pad, total):
    rows, cols, channels = tile.shape
    fill(pad, tile, top, bottom, left, right)

    def piece(slab, col, row):
        acc = taps(pad, kernel, slab, col, row, True)
        for i in range(BAND):
            at = pl.ds(pl.multiple_of((row + i) * cols + col, 8), 8)
            total[at, lanes(slab)] = acc[i]

    steps(rows, cols, channels, piece)
    block = 128

    def finish(i, _):
        at = pl.ds(pl.multiple_of(i * block, block), block)
        out[at, :] = (cot[at, :].astype(f32) + total[at, :]).astype(bf16)
        return _

    lax.fori_loop(0, rows * cols // block, finish, 0)


def call(body, outs, scratch, args, flops, size=24 << 20):
    vmem = pl.BlockSpec(memory_space=pltpu.VMEM)
    return pl.pallas_call(
        body,
        out_shape=[jax.ShapeDtypeStruct(shape, dtype) for shape, dtype in outs],
        in_specs=[vmem] * len(args),
        out_specs=[vmem] * len(outs),
        scratch_shapes=[pltpu.VMEM(shape, dtype) for shape, dtype in scratch],
        compiler_params=pltpu.CompilerParams(vmem_limit_bytes=size),
        cost_estimate=pl.CostEstimate(flops=flops, bytes_accessed=1 << 20, transcendentals=0),
    )(*args)


def bits(count):
    return max(count.bit_length() - 1, 0)


def sum_plan():
    plan = [("gy", 0)]
    rest = [("gy", j) for j in range(1, bits(lax.axis_size("gy")))]
    wide = [("gx", j) for j in range(bits(lax.axis_size("gx")))]
    deep = [("rep", j) for j in range(bits(lax.axis_size("rep")))]
    first = rest + wide + deep
    second = wide + rest + deep
    return [(plan[0], plan[0])] + list(zip(first, second))


def exchange(x, choice):
    sizes = [lax.axis_size(axis) for axis in AXES]
    perm = []
    for i in range(sizes[0] * sizes[1] * sizes[2]):
        at = {"gy": i // (sizes[1] * sizes[2]), "gx": i // sizes[2] % sizes[1], "rep": i % sizes[2]}
        axis, bit = choice[at["gy"] % 2]
        at[axis] ^= 1 << bit
        perm.append((i, (at["gy"] * sizes[1] + at["gx"]) * sizes[2] + at["rep"]))
    return lax.ppermute(x, AXES, perm)


def own_bit(choice):
    core = lax.axis_index("gy") % 2
    values = [lax.axis_index(axis) // (1 << bit) % 2 for axis, bit in choice]
    return jnp.where(core == 0, values[0], values[1])


def sum_scatter(x):
    for choice in sum_plan():
        bit = own_bit(choice)
        halves = x.reshape(2, x.shape[0] // 2, x.shape[1])
        keep = lax.dynamic_index_in_dim(halves, bit, 0, keepdims=False)
        send = lax.dynamic_index_in_dim(halves, 1 - bit, 0, keepdims=False)
        x = (keep.astype(f32) + exchange(send, choice).astype(f32)).astype(bf16)
    return x


def gather_back(x):
    for choice in reversed(sum_plan()):
        bit = own_bit(choice)
        other = exchange(x, choice)
        x = jnp.where(bit == 0, jnp.concatenate([x, other]), jnp.concatenate([other, x]))
    return x


def gather_call(x):
    plan = sum_plan()
    sizes = [lax.axis_size(axis) for axis in AXES]
    got = lax.all_gather(x, AXES)
    dims, place = [], {}
    for axis, size in zip(AXES, sizes):
        for j in reversed(range(bits(size))):
            place[(axis, j)] = len(dims)
            dims.append(2)
    got = got.reshape(*dims, *x.shape)
    parts = []
    for core in range(2):
        half = lax.index_in_dim(got, core, place[("gy", 0)], keepdims=True)
        order = [place[choice[core]] for choice in plan]
        parts.append(half.transpose(*order, len(dims), len(dims) + 1))
    return jnp.concatenate(parts).reshape(-1, x.shape[1])


def shards(
    pages,
    cotangent,
    conv_kernel,
    conv_bias,
    norm_gain,
    norm_bias,
    w_in,
    b_in,
    w_out,
    b_out,
    layer_scale,
):
    _, rows, cols, channels = pages.shape
    hid = w_in.shape[0]
    width = hid // 2
    pixels = rows * cols
    tile = pages.reshape(rows, cols, channels)
    page = pages.reshape(pixels, channels)
    cot = cotangent.reshape(pixels, channels)
    kernel = conv_kernel.reshape(49, channels)
    row = lambda v: v.reshape(1, -1)
    gain, shift, scale = row(norm_gain), row(norm_bias), row(layer_scale)
    pad = ((channels // LANES, rows + 6, EDGE + cols + 8, LANES), f32)
    full = (pixels, channels)

    around = halo(tile)
    conv_flops = 2 * 49 * pixels * channels * 60
    normed, inv, ln_out = call(
        conv_norm_kernel,
        [(full, f32), ((pixels, LANES), f32), (full, bf16)],
        [pad, (full, f32)],
        (tile, *around, kernel, row(conv_bias), gain, shift),
        conv_flops,
    )
    grads = [
        ((MLP_BLOCK, width), bf16),
        ((MLP_BLOCK, width), bf16),
        ((width, channels), f32),
        ((channels, width), f32),
        ((8, width), f32),
    ]
    packed = ((2 * width, channels), bf16)
    mlp_flops = 6 * pixels * channels * hid * 2
    weights = (w_in, w_out, row(b_in), scale)
    branch, d_norm, pack_a, gbin_a = call(
        functools.partial(mlp_first_kernel, 0, width),
        [(full, f32), (full, f32), packed, ((1, width), f32)],
        grads,
        (ln_out, cot, *weights),
        mlp_flops,
    )
    piece_a = sum_scatter(pack_a)
    result, d_depth, pack_b, gbin_b, sums = call(
        functools.partial(mlp_second_kernel, width, width),
        [(full, bf16), (full, bf16), packed, ((1, width), f32), ((8, channels), f32)],
        grads + [((8, 8, channels), f32)],
        (ln_out, cot, *weights, row(b_out), gain, page, normed, inv, branch, d_norm),
        mlp_flops,
    )
    piece_b = sum_scatter(pack_b)
    d_tile = d_depth.reshape(tile.shape)
    d_around = halo(d_tile)
    (g_kernel,) = call(
        kernel_grad_kernel,
        [((49, channels), f32)],
        [pad, (full, f32), ((channels // LANES, 49, 8, LANES), f32)],
        (tile, *around, d_depth),
        conv_flops,
    )
    small = jnp.concatenate(
        [g_kernel, sums[:5], gbin_a.reshape(-1, channels), gbin_b.reshape(-1, channels)]
    )
    (grad_pages,) = call(
        conv_grad_kernel,
        [(full, bf16)],
        [pad, (full, f32)],
        (d_tile, *d_around, kernel, cot),
        conv_flops,
    )
    factor = float(pixels * lax.axis_size("gy") * lax.axis_size("gx") * lax.axis_size("rep")) ** (-0.5)
    small = lax.psum(small, AXES) * factor
    both = [gather_back(piece_a), gather_call(piece_b)]
    sum_win = jnp.concatenate([g[:width] for g in both]).astype(f32) * factor
    blocks = [g[width + j * channels : width + (j + 1) * channels] for g in both for j in range(width // channels)]
    sum_wout = jnp.concatenate(blocks, axis=1).astype(f32) * factor
    return (
        result.reshape(pages.shape),
        grad_pages.reshape(pages.shape),
        small[:49].reshape(7, 7, channels),
        small[53],
        small[51],
        small[52],
        sum_win,
        small[54:].reshape(-1),
        sum_wout,
        small[50],
        small[49],
    )


def solution(mesh):
    split = P("rep", "gy", "gx", None)
    return jax.shard_map(
        shards,
        mesh=mesh,
        in_specs=(split, split) + (P(),) * 9,
        out_specs=(split, split) + (P(),) * 9,
        check_vma=False,
    )
```

time: 312 us -> 276 us (0.88)
  other arithmetic: 60.8 us -> 13.3 us
  blocking collectives: 41.8 us -> 0 us
  Pallas kernels: 0 us -> 35.8 us
  matrix products: 31.1 us -> 0 us
  waiting for transfers between devices: 138 us -> 169 us
  starting transfers between devices: 17.8 us -> 32.6 us
    psum x1 -> x0, blocking collectives: 41.8 us -> none  [shards(): lax.psum((g_win, g_wout, g_kernel, g_cbias, g_gain, g_nbias, g_bin, g_bou...]
    pallas_call x0 -> x5, Pallas kernels: none -> 35.8 us  [call(): pl.pallas_call(body, out_shape=[jax.ShapeDtypeStruct(shape, dtype) for sh...]
    reduce_sum x10 -> x0, other arithmetic: 34.7 us -> none  [the longest x1 15.7 us: shards(): average = jnp.mean(depth_out, axis=-1, keepdims=True)]
    dot_general x6 -> x0, matrix products: 31.1 us -> none  [the longest x1 15.1 us: shards(): lax.dot_general(ln_out, w_in, (((1,), (1,)), ((), ())), preferred_element...]
    ppermute x8 -> x21, waiting for transfers between devices: 4.91 us -> 32.7 us  [the longest x15 24.8 us: exchange(): return lax.ppermute(x, AXES, perm)]
    all_gather x0 -> x1, waiting for transfers between devices: none -> 20.1 us  [gather_call(): got = lax.all_gather(x, AXES)]
    psum x1, waiting for transfers between devices: 133 us -> 116 us  [shards(): small = lax.psum(small, AXES) * factor]
    ppermute x8 -> x21, starting transfers between devices: 17.8 us -> 32.5 us  [the longest x15 21.3 us: exchange(): return lax.ppermute(x, AXES, perm)]
  transfers between devices with their start and end apart: 9 -> 23, of which waited for: 4 -> 13; matrix products, arithmetic and copies ran while one was open for 12% -> 5% of each run, Pallas kernels for 0% -> 5%
where the time goes in v1:
time: 276 us; the launch traced here: 275 us
  waiting for transfers between devices  169 us (61%)
  Pallas kernels  35.8 us (13%)
  starting transfers between devices  32.6 us (12%)
  between operations  14.8 us (5%)
  other arithmetic  13.3 us (5%)
  local copies, waits for them, and re-layouts  10 us (4%)
    psum x1, waiting for transfers between devices, shards(): small = lax.psum(small, AXES) * factor  116 us
    pallas_call x5, Pallas kernels, call(): pl.pallas_call(body, out_shape=[jax.ShapeDtypeStruct(shape, dtype) for sh...  35.8 us
    ppermute x15, waiting for transfers between devices, exchange(): return lax.ppermute(x, AXES, perm)  24.8 us
    ppermute x15, starting transfers between devices, exchange(): return lax.ppermute(x, AXES, perm)  21.3 us
    all_gather x1, waiting for transfers between devices, gather_call(): got = lax.all_gather(x, AXES)  20.1 us
    ppermute x4, starting transfers between devices, edges(): out.append(lax.ppermute(jnp.where(is_high, high, low), axis, pairs))  8.44 us
    ppermute x2, waiting for transfers between devices, halo(): lax.ppermute(jnp.where(is_high, column[:, 3:], column[:, :3]), 'gx', pairs)  7.95 us
  transfers between devices with their start and end apart: 23, of which 13 were waited for; matrix products, arithmetic and copies ran while one was open for 5% of the time, Pallas kernels for 5%

profile of v1, /device:TPU:0, one launch (start us, length us, event | category | flops | bytes accessed | tf_op | source)
XLA Modules:
  0.0 275.0 jit_solution(3231714855677349484)
XLA Ops:
  7.3 0.9 select_bitcast_fusion
  8.3 0.7 collective-permute-start
  8.9 4.4 %collective-permute-start.1 = (bf16[3,32,384]{2,1,0:T(8,128)(2,1)S(1)}, bf16[3,32,384]{2,1,0:T(8,128)(2,1)S(1)}, u32[]{:S(2)}, u32[]{:S(2)}) collective-permute-start(bf16[3,32,384]{2,1,0:T(8,128)(2,1)S(1)} %get-tuple-element.52), channel_id=1, source_target_pairs={{0,8},{16,24},{8,0},{24,16},{1,9},{17,25},{9,1},{25,17},{2,10},{18... | collective-permute-start | bytes 221192 | tf_op jit(solution)/shard_map/ppermute | solution.py:45
  13.3 1.2 fusion.13
  14.6 0.1 maximum_maximum_fusion
  14.7 0.1 slice_select_fusion.1
  14.8 1.6 collective-permute-start.2
  16.6 4.1 %collective-permute-done.2 = bf16[38,3,384]{2,1,0:T(4,128)(2,1)S(1)} collective-permute-done((bf16[38,3,384]{2,1,0:T(4,128)(2,1)S(1)}, bf16[38,3,384]{2,1,0:T(4,128)(2,1)S(1)}, u32[]{:S(2)}, u32[]{:S(2)}) %collective-permute-start.2) | collective-permute-done | bytes 87584 | tf_op jit(solution)/shard_map/ppermute | solution.py:63
  20.9 7.6 %shard_map.194 = (f32[1024,384]{1,0:T(8,128)S(1)}, f32[1024,128]{1,0:T(8,128)S(1)}, bf16[1024,384]{1,0:T(8,128)(2,1)S(1)}) custom-call(bf16[32,32,384]{2,1,0:T(8,128)(2,1)S(1)} %bitcast.86, bf16[3,32,384]{2,1,0:T(8,128)(2,1)S(1)} %get-tuple-element.57.top, bf16[3,32,384]{2,1,0:T(8,128)(2,1)S(1)} %get-tuple-element.56.bottom, ...), custom_call_target="tpu_custom_call" | custom-call | flops 2312110080 | bytes 1048576 | tf_op jit(solution)/shard_map/pallas_call | solution.py:318
  28.5 6.4 %shard_map.195 = (f32[1024,384]{1,0:T(8,128)S(1)}, f32[1024,384]{1,0:T(8,128)S(1)}, bf16[1536,384]{1,0:T(8,128)(2,1)S(1)}, f32[1,768]{1,0:T(1,128)S(1)}) custom-call(bf16[1024,384]{1,0:T(8,128)(2,1)S(1)} %get-tuple-element.23.ln_ref, bf16[1024,384]{1,0:T(8,128)(2,1)S(1)} %bitcast.92, bf16[1536,384]{1,0:T(8,128)(2,1)S(1)} %copy-done.3, ...), custom_call_target="tpu_custom_call" | custom-call | flops 7247757312 | bytes 1048576 | tf_op jit(solution)/shard_map/pallas_call | solution.py:318
  34.9 8.2 %shard_map.196 = (bf16[1024,384]{1,0:T(8,128)(2,1)}, bf16[1024,384]{1,0:T(8,128)(2,1)S(1)}, bf16[1536,384]{1,0:T(8,128)(2,1)S(1)}, f32[1,768]{1,0:T(1,128)S(1)}, f32[8,384]{1,0:T(8,128)S(1)}) custom-call(bf16[1024,384]{1,0:T(8,128)(2,1)S(1)} %get-tuple-element.23.ln_ref, bf16[1024,384]{1,0:T(8,128)(2,1)S(1)} %bitcast.93, bf16[1536,384]{1,0:T(8,128)(2,1)S(1)} %copy-done.3, ...), custom_call_target="tpu_custom_call" | custom-call | flops 7247757312 | bytes 1048576 | tf_op jit(solution)/shard_map/pallas_call | solution.py:318
  43.0 1.0 dynamic-slice_bitcast_fusion
  44.0 0.9 dynamic-slice_bitcast_fusion.1
  44.9 0.5 collective-permute-start.6
  45.4 6.8 %shard_map.198 = f32[49,384]{1,0:T(8,128)S(1)} custom-call(bf16[32,32,384]{2,1,0:T(8,128)(2,1)S(1)} %bitcast.88, bf16[3,32,384]{2,1,0:T(8,128)(2,1)S(1)} %get-tuple-element.57.top, bf16[3,32,384]{2,1,0:T(8,128)(2,1)S(1)} %get-tuple-element.56.bottom, bf16[38,3,384]{2,1,0:T(4,128)(2,1)S(1)} %get-tuple-element.61.left, ...), custom_call_target="tpu_custom_call" | custom-call | flops 2312110080 | bytes 1048576 | tf_op jit(solution)/shard_map/pallas_call | solution.py:318
  52.2 0.7 pad_maximum_fusion.1
  53.0 1.6 broadcast_select_fusion.4
  54.5 0.7 collective-permute-start.3
  55.2 2.8 %collective-permute-start.4 = (bf16[3,32,384]{2,1,0:T(8,128)(2,1)S(1)}, bf16[3,32,384]{2,1,0:T(8,128)(2,1)}, u32[]{:S(2)}, u32[]{:S(2)}) collective-permute-start(bf16[3,32,384]{2,1,0:T(8,128)(2,1)S(1)} %bitcast.116), channel_id=1, source_target_pairs={{0,8},{16,24},{8,0},{24,16},{1,9},{17,25},{9,1},{25,17},{2,10},{18... | collective-permute-start | bytes 221192 | tf_op jit(solution)/shard_map/ppermute | solution.py:45
  58.0 1.1 fusion.12
  59.1 115.7 %all-reduce.2.cloned.1.call-done = f32[58,384]{1,0:T(8,128)} async-done(((f32[58,384]{1,0:T(8,128)}), f32[58,384]{1,0:T(8,128)}) %all-reduce.2.cloned.1.call-update) | async-done | bytes 89104 | tf_op jit(solution)/shard_map/psum | solution.py:477
  174.7 0.9 broadcast_multiply_fusion
  175.7 0.6 reshape.157
  176.3 0.6 reshape.169
  176.9 1.2 fusion.1
  178.2 1.6 collective-permute-start.7
  179.8 1.2 fusion
  181.0 0.6 collective-permute-start.17
  181.6 3.4 %collective-permute-done.7 = bf16[384,384]{1,0:T(8,128)(2,1)S(1)} collective-permute-done((bf16[384,384]{1,0:T(8,128)(2,1)S(1)}, bf16[384,384]{1,0:T(8,128)(2,1)S(1)}, u32[]{:S(2)}, u32[]{:S(2)}) %collective-permute-start.7) | collective-permute-done | bytes 294944 | tf_op jit(solution)/shard_map/ppermute | solution.py:351
  185.1 1.6 collective-permute-start.8
  186.7 3.1 %collective-permute-done.17 = bf16[384,384]{1,0:T(8,128)(2,1)S(1)} collective-permute-done((bf16[384,384]{1,0:T(8,128)(2,1)S(1)}, bf16[384,384]{1,0:T(8,128)(2,1)S(1)}, u32[]{:S(2)}, u32[]{:S(2)}) %collective-permute-start.17) | collective-permute-done | bytes 294944 | tf_op jit(solution)/shard_map/ppermute | solution.py:351
  189.9 1.6 collective-permute-start.18
  191.5 4.8 %collective-permute-start.9 = (bf16[96,384]{1,0:T(8,128)(2,1)S(1)}, bf16[96,384]{1,0:T(8,128)(2,1)S(1)}, u32[]{:S(2)}, u32[]{:S(2)}) collective-permute-start(bf16[96,384]{1,0:T(8,128)(2,1)S(1)} %dynamic-slice_bitcast_fusion.7), channel_id=1, source_target_pairs={{0,1},{1,0},{2,3},{3,2},{4,5},{5,4},{6,7},{7,6},{8,9},{9,8},{10,11... | collective-permute-start | bytes 221192 | tf_op jit(solution)/shard_map/ppermute | solution.py:351
  196.4 3.6 %collective-permute-start.19 = (bf16[96,384]{1,0:T(8,128)(2,1)S(1)}, bf16[96,384]{1,0:T(8,128)(2,1)S(1)}, u32[]{:S(2)}, u32[]{:S(2)}) collective-permute-start(bf16[96,384]{1,0:T(8,128)(2,1)S(1)} %dynamic-slice_bitcast_fusion.6), channel_id=1, source_target_pairs={{0,1},{1,0},{2,3},{3,2},{4,5},{5,4},{6,7},{7,6},{8,9},{9,8},{10,11... | collective-permute-start | bytes 221192 | tf_op jit(solution)/shard_map/ppermute | solution.py:351
  200.0 1.2 collective-permute-start.10
  201.3 1.1 collective-permute-done.19
  202.4 2.1 collective-permute-start.20
  204.5 0.9 collective-permute-done.10
  205.4 0.8 collective-permute-start.11
  206.2 1.1 collective-permute-done.20
  207.3 0.6 fusion.8
  208.0 2.6 collective-permute-done.11
  210.6 0.3 collective-permute-start.12
  210.8 0.9 broadcast_select_fusion.6
  211.7 3.2 %collective-permute-done.12 = bf16[96,384]{1,0:T(8,128)(2,1)S(1)} collective-permute-done((bf16[96,384]{1,0:T(8,128)(2,1)S(1)}, bf16[96,384]{1,0:T(8,128)(2,1)S(1)}, u32[]{:S(2)}, u32[]{:S(2)}) %collective-permute-start.12) | collective-permute-done | bytes 73760 | tf_op jit(solution)/shard_map/ppermute | solution.py:351
  215.0 1.3 collective-permute-start.13
  216.4 4.1 %collective-permute-done.13 = bf16[192,384]{1,0:T(8,128)(2,1)S(1)} collective-permute-done((bf16[192,384]{1,0:T(8,128)(2,1)S(1)}, bf16[192,384]{1,0:T(8,128)(2,1)S(1)}, u32[]{:S(2)}, u32[]{:S(2)}) %collective-permute-start.13) | collective-permute-done | bytes 147488 | tf_op jit(solution)/shard_map/ppermute | solution.py:351
  220.6 1.3 collective-permute-start.14
  221.9 0.1 maximum_maximum_fusion.1
  222.1 5.3 %collective-permute-done.14 = bf16[384,384]{1,0:T(8,128)(2,1)S(1)} collective-permute-done((bf16[384,384]{1,0:T(8,128)(2,1)S(1)}, bf16[384,384]{1,0:T(8,128)(2,1)S(1)}, u32[]{:S(2)}, u32[]{:S(2)}) %collective-permute-start.14) | collective-permute-done | bytes 294944 | tf_op jit(solution)/shard_map/ppermute | solution.py:351
  227.4 0.2 maximum_select_fusion.1
  227.8 1.2 collective-permute-start.5
  229.0 0.6 slice_reduce_fusion
  229.6 3.9 %collective-permute-done.5 = bf16[38,3,384]{2,1,0:T(4,128)(2,1)S(1)} collective-permute-done((bf16[38,3,384]{2,1,0:T(4,128)(2,1)S(1)}, bf16[38,3,384]{2,1,0:T(4,128)(2,1)S(1)}, u32[]{:S(2)}, u32[]{:S(2)}) %collective-permute-start.5) | collective-permute-done | bytes 87584 | tf_op jit(solution)/shard_map/ppermute | solution.py:63
  233.5 6.9 %shard_map.197 = bf16[1024,384]{1,0:T(8,128)(2,1)} custom-call(bf16[32,32,384]{2,1,0:T(8,128)(2,1)S(1)} %bitcast.90, bf16[3,32,384]{2,1,0:T(8,128)(2,1)S(1)} %get-tuple-element.55.top, bf16[3,32,384]{2,1,0:T(8,128)(2,1)S(1)} %get-tuple-element.54.bottom, bf16[38,3,384]{2,1,0:T(4,128)(2,1)S(1)} %get-tuple-element.59.left, ...), custom_call_target="tpu_custom_call" | custom-call | flops 2312110080 | bytes 1048576 | tf_op jit(solution)/shard_map/pallas_call | solution.py:318
  240.4 0.4 maximum_select_fusion
  241.0 0.9 copy-done.7
  241.9 20.1 %all-gather.3.cloned.1.call-done = bf16[1536,384]{1,0:T(8,128)(2,1)} async-done(((bf16[48,384]{1,0:T(8,128)(2,1)}), bf16[1536,384]{1,0:T(8,128)(2,1)}) %all-gather.3.cloned.1.call-update) | async-done | bytes 1179664 | tf_op jit(solution)/shard_map/all_gather | solution.py:381
  262.0 1.4 slice_bitcast_fusion
  263.5 0.1 pad_maximum_fusion
  263.7 0.1 copy.27
  263.9 1.0 slice-done
  264.9 1.6 convert_multiply_fusion.1
  266.5 1.7 convert_multiply_fusion
  (88 shorter events, 1.6 us)
Async XLA Ops:
  7.2 9.2 %copy-start.8 = (f32[7,7,384]{2,1,0:T(8,128)S(1)}, f32[7,7,384]{2,1,0:T(8,128)}, u32[]{:S(2)}) copy-start(f32[7,7,384]{2,1,0:T(8,128)} %param.13) | copy-start | bytes 225796
  7.2 9.2 %copy-start.10 = (f32[384]{0:T(512)S(1)}, f32[384]{0:T(512)}, u32[]{:S(2)}) copy-start(f32[384]{0:T(512)} %param.15) | copy-start | bytes 4612
  7.2 9.2 %copy-start.11 = (f32[384]{0:T(512)S(1)}, f32[384]{0:T(512)}, u32[]{:S(2)}) copy-start(f32[384]{0:T(512)} %param.14) | copy-start | bytes 4612
  7.2 9.2 %copy-start.12 = (f32[384]{0:T(512)S(1)}, f32[384]{0:T(512)}, u32[]{:S(2)}) copy-start(f32[384]{0:T(512)} %param.16) | copy-start | bytes 4612
  7.2 9.3 %copy-start.9 = (f32[1536]{0:T(1024)S(1)}, f32[1536]{0:T(1024)}, u32[]{:S(2)}) copy-start(f32[1536]{0:T(1024)} %param.18) | copy-start | bytes 18436
  7.2 9.3 %copy-start.13 = (f32[384]{0:T(512)S(1)}, f32[384]{0:T(512)}, u32[]{:S(2)}) copy-start(f32[384]{0:T(512)} %param.21) | copy-start | bytes 4612
  7.2 9.3 %copy-start.14 = (f32[384]{0:T(512)S(1)}, f32[384]{0:T(512)}, u32[]{:S(2)}) copy-start(f32[384]{0:T(512)} %param.20) | copy-start | bytes 4612
  7.2 167.5 %all-reduce.2.cloned.1.call-start = ((), (), s32[]{:S(2)}) async-start(), calls=%async_computation | async-start | bytes 196608 | tf_op jit(solution)/shard_map/psum | solution.py:477
  8.3 6.2 %collective-permute-start = (bf16[3,32,384]{2,1,0:T(8,128)(2,1)S(1)}, bf16[3,32,384]{2,1,0:T(8,128)(2,1)S(1)}, u32[]{:S(2)}, u32[]{:S(2)}) collective-permute-start(bf16[3,32,384]{2,1,0:T(8,128)(2,1)S(1)} %get-tuple-element.53), channel_id=1, source_target_pairs={{8,16},{16,8},{9,17},{17,9},{10,18},{18,10},{11,19},{19,11},{12,20... | collective-permute-start | bytes 221192 | tf_op jit(solution)/shard_map/ppermute | solution.py:45
  8.9 5.6 %collective-permute-start.1 = (bf16[3,32,384]{2,1,0:T(8,128)(2,1)S(1)}, bf16[3,32,384]{2,1,0:T(8,128)(2,1)S(1)}, u32[]{:S(2)}, u32[]{:S(2)}) collective-permute-start(bf16[3,32,384]{2,1,0:T(8,128)(2,1)S(1)} %get-tuple-element.52), channel_id=1, source_target_pairs={{0,8},{16,24},{8,0},{24,16},{1,9},{17,25},{9,1},{25,17},{2,10},{18... | collective-permute-start | bytes 221192 | tf_op jit(solution)/shard_map/ppermute | solution.py:45
  13.3 7.5 %copy-start = (bf16[1,32,32,384]{3,2,1,0:T(8,128)(2,1)S(1)}, bf16[1,32,32,384]{3,2,1,0:T(8,128)(2,1)}, u32[]{:S(2)}) copy-start(bf16[1,32,32,384]{3,2,1,0:T(8,128)(2,1)} %param.11) | copy-start | bytes 2359300
  14.8 5.9 %collective-permute-start.2 = (bf16[38,3,384]{2,1,0:T(4,128)(2,1)S(1)}, bf16[38,3,384]{2,1,0:T(4,128)(2,1)S(1)}, u32[]{:S(2)}, u32[]{:S(2)}) collective-permute-start(bf16[38,3,384]{2,1,0:T(4,128)(2,1)S(1)} %slice_select_fusion.1), channel_id=1, source_target_pairs={{0,4},{4,0},{1,5},{5,1},{2,6},{6,2},{3,7},{7,3},{8,12},{12,8},{9,1... | collective-permute-start | bytes 262664 | tf_op jit(solution)/shard_map/ppermute | solution.py:63
  20.8 7.6 %copy-start.3 = (bf16[1536,384]{1,0:T(8,128)(2,1)S(1)}, bf16[1536,384]{1,0:T(8,128)(2,1)}, u32[]{:S(2)}) copy-start(bf16[1536,384]{1,0:T(8,128)(2,1)} %w_in.3) | copy-start | bytes 3538948
  20.8 7.6 %copy-start.4 = (bf16[384,1536]{1,0:T(8,128)(2,1)S(1)}, bf16[384,1536]{1,0:T(8,128)(2,1)}, u32[]{:S(2)}) copy-start(bf16[384,1536]{1,0:T(8,128)(2,1)} %w_out.3) | copy-start | bytes 3538948
  20.8 7.6 %copy-start.5 = (bf16[1,32,32,384]{3,2,1,0:T(8,128)(2,1)S(1)}, bf16[1,32,32,384]{3,2,1,0:T(8,128)(2,1)}, u32[]{:S(2)}) copy-start(bf16[1,32,32,384]{3,2,1,0:T(8,128)(2,1)} %param.12) | copy-start | bytes 2359300
  43.0 2.3 copy-start.1
  44.0 135.8 %collective-permute-start.16 = (bf16[768,384]{1,0:T(8,128)(2,1)}, bf16[768,384]{1,0:T(8,128)(2,1)}, u32[]{:S(2)}, u32[]{:S(2)}) collective-permute-start(bf16[768,384]{1,0:T(8,128)(2,1)} %dynamic-slice_bitcast_fusion), channel_id=1, source_target_pairs={{0,8},{1,9},{2,10},{3,11},{4,12},{5,13},{6,14},{7,15},{8,0},{9,1},... | collective-permute-start | bytes 1769480 | tf_op jit(solution)/shard_map/ppermute | solution.py:351
  44.9 132.1 %collective-permute-start.6 = (bf16[768,384]{1,0:T(8,128)(2,1)}, bf16[768,384]{1,0:T(8,128)(2,1)}, u32[]{:S(2)}, u32[]{:S(2)}) collective-permute-start(bf16[768,384]{1,0:T(8,128)(2,1)} %dynamic-slice_bitcast_fusion.1), channel_id=1, source_target_pairs={{0,8},{1,9},{2,10},{3,11},{4,12},{5,13},{6,14},{7,15},{8,0},{9,1},... | collective-permute-start | bytes 1769480 | tf_op jit(solution)/shard_map/ppermute | solution.py:351
  52.9 209.1 %all-gather.3.cloned.1.call-start = ((), (), s32[]{:S(2)}) async-start(), calls=%async_computation.1 | async-start | bytes 1216512 | tf_op jit(solution)/shard_map/all_gather | solution.py:381
  54.5 156.3 %collective-permute-start.3 = (bf16[3,32,384]{2,1,0:T(8,128)(2,1)}, bf16[3,32,384]{2,1,0:T(8,128)(2,1)S(1)}, u32[]{:S(2)}, u32[]{:S(2)}) collective-permute-start(bf16[3,32,384]{2,1,0:T(8,128)(2,1)} %bitcast.7), channel_id=1, source_target_pairs={{8,16},{16,8},{9,17},{17,9},{10,18},{18,10},{11,19},{19,11},{12,20... | collective-permute-start | bytes 221192 | tf_op jit(solution)/shard_map/ppermute | solution.py:45
  55.2 155.6 %collective-permute-start.4 = (bf16[3,32,384]{2,1,0:T(8,128)(2,1)S(1)}, bf16[3,32,384]{2,1,0:T(8,128)(2,1)}, u32[]{:S(2)}, u32[]{:S(2)}) collective-permute-start(bf16[3,32,384]{2,1,0:T(8,128)(2,1)S(1)} %bitcast.116), channel_id=1, source_target_pairs={{0,8},{16,24},{8,0},{24,16},{1,9},{17,25},{9,1},{25,17},{2,10},{18... | collective-permute-start | bytes 221192 | tf_op jit(solution)/shard_map/ppermute | solution.py:45
  178.2 6.8 %collective-permute-start.7 = (bf16[384,384]{1,0:T(8,128)(2,1)S(1)}, bf16[384,384]{1,0:T(8,128)(2,1)S(1)}, u32[]{:S(2)}, u32[]{:S(2)}) collective-permute-start(bf16[384,384]{1,0:T(8,128)(2,1)S(1)} %dynamic-slice_bitcast_fusion.3), channel_id=1, source_target_pairs={{0,16},{1,17},{2,18},{3,19},{4,20},{5,21},{6,22},{7,23},{8,12},{9,... | collective-permute-start | bytes 884744 | tf_op jit(solution)/shard_map/ppermute | solution.py:351
  181.0 8.8 %collective-permute-start.17 = (bf16[384,384]{1,0:T(8,128)(2,1)S(1)}, bf16[384,384]{1,0:T(8,128)(2,1)S(1)}, u32[]{:S(2)}, u32[]{:S(2)}) collective-permute-start(bf16[384,384]{1,0:T(8,128)(2,1)S(1)} %dynamic-slice_bitcast_fusion.2), channel_id=1, source_target_pairs={{0,16},{1,17},{2,18},{3,19},{4,20},{5,21},{6,22},{7,23},{8,12},{9,... | collective-permute-start | bytes 884744 | tf_op jit(solution)/shard_map/ppermute | solution.py:351
  185.1 6.4 %collective-permute-start.8 = (bf16[192,384]{1,0:T(8,128)(2,1)S(1)}, bf16[192,384]{1,0:T(8,128)(2,1)S(1)}, u32[]{:S(2)}, u32[]{:S(2)}) collective-permute-start(bf16[192,384]{1,0:T(8,128)(2,1)S(1)} %dynamic-slice_bitcast_fusion.5), channel_id=1, source_target_pairs={{0,4},{1,5},{2,6},{3,7},{4,0},{5,1},{6,2},{7,3},{8,24},{9,25},{10,... | collective-permute-start | bytes 442376 | tf_op jit(solution)/shard_map/ppermute | solution.py:351
  189.9 6.5 %collective-permute-start.18 = (bf16[192,384]{1,0:T(8,128)(2,1)S(1)}, bf16[192,384]{1,0:T(8,128)(2,1)S(1)}, u32[]{:S(2)}, u32[]{:S(2)}) collective-permute-start(bf16[192,384]{1,0:T(8,128)(2,1)S(1)} %dynamic-slice_bitcast_fusion.4), channel_id=1, source_target_pairs={{0,4},{1,5},{2,6},{3,7},{4,0},{5,1},{6,2},{7,3},{8,24},{9,25},{10,... | collective-permute-start | bytes 442376 | tf_op jit(solution)/shard_map/ppermute | solution.py:351
  191.5 8.5 %collective-permute-start.9 = (bf16[96,384]{1,0:T(8,128)(2,1)S(1)}, bf16[96,384]{1,0:T(8,128)(2,1)S(1)}, u32[]{:S(2)}, u32[]{:S(2)}) collective-permute-start(bf16[96,384]{1,0:T(8,128)(2,1)S(1)} %dynamic-slice_bitcast_fusion.7), channel_id=1, source_target_pairs={{0,1},{1,0},{2,3},{3,2},{4,5},{5,4},{6,7},{7,6},{8,9},{9,8},{10,11... | collective-permute-start | bytes 221192 | tf_op jit(solution)/shard_map/ppermute | solution.py:351
  196.4 5.9 %collective-permute-start.19 = (bf16[96,384]{1,0:T(8,128)(2,1)S(1)}, bf16[96,384]{1,0:T(8,128)(2,1)S(1)}, u32[]{:S(2)}, u32[]{:S(2)}) collective-permute-start(bf16[96,384]{1,0:T(8,128)(2,1)S(1)} %dynamic-slice_bitcast_fusion.6), channel_id=1, source_target_pairs={{0,1},{1,0},{2,3},{3,2},{4,5},{5,4},{6,7},{7,6},{8,9},{9,8},{10,11... | collective-permute-start | bytes 221192 | tf_op jit(solution)/shard_map/ppermute | solution.py:351
  200.0 5.3 %collective-permute-start.10 = (bf16[48,384]{1,0:T(8,128)(2,1)S(1)}, bf16[48,384]{1,0:T(8,128)(2,1)S(1)}, u32[]{:S(2)}, u32[]{:S(2)}) collective-permute-start(bf16[48,384]{1,0:T(8,128)(2,1)S(1)} %dynamic-slice_bitcast_fusion.9), channel_id=1, source_target_pairs={{0,2},{1,3},{2,0},{3,1},{4,6},{5,7},{6,4},{7,5},{8,10},{9,11},{10,... | collective-permute-start | bytes 110600 | tf_op jit(solution)/shard_map/ppermute | solution.py:351
  202.4 4.9 %collective-permute-start.20 = (bf16[48,384]{1,0:T(8,128)(2,1)S(1)}, bf16[48,384]{1,0:T(8,128)(2,1)S(1)}, u32[]{:S(2)}, u32[]{:S(2)}) collective-permute-start(bf16[48,384]{1,0:T(8,128)(2,1)S(1)} %dynamic-slice_bitcast_fusion.8), channel_id=1, source_target_pairs={{0,2},{1,3},{2,0},{3,1},{4,6},{5,7},{6,4},{7,5},{8,10},{9,11},{10,... | collective-permute-start | bytes 110600 | tf_op jit(solution)/shard_map/ppermute | solution.py:351
  205.4 5.2 %collective-permute-start.11 = (bf16[48,384]{1,0:T(8,128)(2,1)S(1)}, bf16[48,384]{1,0:T(8,128)(2,1)S(1)}, u32[]{:S(2)}, u32[]{:S(2)}) collective-permute-start(bf16[48,384]{1,0:T(8,128)(2,1)S(1)} %fusion.9), channel_id=1, source_target_pairs={{0,2},{1,3},{2,0},{3,1},{4,6},{5,7},{6,4},{7,5},{8,10},{9,11},{10,... | collective-permute-start | bytes 110600 | tf_op jit(solution)/shard_map/ppermute | solution.py:351
  210.6 4.4 %collective-permute-start.12 = (bf16[96,384]{1,0:T(8,128)(2,1)S(1)}, bf16[96,384]{1,0:T(8,128)(2,1)S(1)}, u32[]{:S(2)}, u32[]{:S(2)}) collective-permute-start(bf16[96,384]{1,0:T(8,128)(2,1)S(1)} %maximum_select_fusion.4), channel_id=1, source_target_pairs={{0,1},{1,0},{2,3},{3,2},{4,5},{5,4},{6,7},{7,6},{8,9},{9,8},{10,11... | collective-permute-start | bytes 221192 | tf_op jit(solution)/shard_map/ppermute | solution.py:351
  215.0 5.5 %collective-permute-start.13 = (bf16[192,384]{1,0:T(8,128)(2,1)S(1)}, bf16[192,384]{1,0:T(8,128)(2,1)S(1)}, u32[]{:S(2)}, u32[]{:S(2)}) collective-permute-start(bf16[192,384]{1,0:T(8,128)(2,1)S(1)} %maximum_select_fusion.3), channel_id=1, source_target_pairs={{0,4},{1,5},{2,6},{3,7},{4,0},{5,1},{6,2},{7,3},{8,24},{9,25},{10,... | collective-permute-start | bytes 442376 | tf_op jit(solution)/shard_map/ppermute | solution.py:351
  220.6 6.8 %collective-permute-start.14 = (bf16[384,384]{1,0:T(8,128)(2,1)S(1)}, bf16[384,384]{1,0:T(8,128)(2,1)S(1)}, u32[]{:S(2)}, u32[]{:S(2)}) collective-permute-start(bf16[384,384]{1,0:T(8,128)(2,1)S(1)} %maximum_select_fusion.2), channel_id=1, source_target_pairs={{0,16},{1,17},{2,18},{3,19},{4,20},{5,21},{6,22},{7,23},{8,12},{9,... | collective-permute-start | bytes 884744 | tf_op jit(solution)/shard_map/ppermute | solution.py:351
  221.9 11.6 %copy-start.2 = (bf16[1024,384]{1,0:T(8,128)(2,1)S(1)}, bf16[1024,384]{1,0:T(8,128)(2,1)}, u32[]{:S(2)}) copy-start(bf16[1024,384]{1,0:T(8,128)(2,1)} %copy-done.1) | copy-start | bytes 2359300
  221.9 11.6 %copy-start.6 = (bf16[1,32,32,384]{3,2,1,0:T(8,128)(2,1)S(1)}, bf16[1,32,32,384]{3,2,1,0:T(8,128)(2,1)}, u32[]{:S(2)}) copy-start(bf16[1,32,32,384]{3,2,1,0:T(8,128)(2,1)} %param.12) | copy-start | bytes 2359300
  227.6 12.9 %collective-permute-start.15 = (bf16[768,384]{1,0:T(8,128)(2,1)S(1)}, bf16[768,384]{1,0:T(8,128)(2,1)S(1)}, u32[]{:S(2)}, u32[]{:S(2)}) collective-permute-start(bf16[768,384]{1,0:T(8,128)(2,1)S(1)} %maximum_select_fusion.1), channel_id=1, source_target_pairs={{0,8},{1,9},{2,10},{3,11},{4,12},{5,13},{6,14},{7,15},{8,0},{9,1},... | collective-permute-start | bytes 1769480 | tf_op jit(solution)/shard_map/ppermute | solution.py:351
  227.8 5.7 %collective-permute-start.5 = (bf16[38,3,384]{2,1,0:T(4,128)(2,1)S(1)}, bf16[38,3,384]{2,1,0:T(4,128)(2,1)S(1)}, u32[]{:S(2)}, u32[]{:S(2)}) collective-permute-start(bf16[38,3,384]{2,1,0:T(4,128)(2,1)S(1)} %slice_select_fusion), channel_id=1, source_target_pairs={{0,4},{4,0},{1,5},{5,1},{2,6},{6,2},{3,7},{7,3},{8,12},{12,8},{9,1... | collective-permute-start | bytes 262664 | tf_op jit(solution)/shard_map/ppermute | solution.py:63
  240.9 1.0 copy-start.7
  263.8 1.1 slice-start
Sparse Core Ops, SparseCore 0:
  53.0 121.6 all-reduce.1
  208.1 53.9 all-gather.2

commit v2 on v1

--- a/solution.py
+++ b/solution.py
@@ -1,4 +1,5 @@
 import functools
+import math
 
 import jax
 import jax.numpy as jnp
@@ -181,13 +182,17 @@
     return hidden, d_pre, branch, d_norm
 
 
-def pack_grads(pack, gwin, gwout, gbin_ref, gbin):
+def pack_grads(core, keep, send, gwin, gwout, gbin_ref, gbin):
     width, channels = gwin.shape
-    pack[0:width, :] = gwin[...].astype(bf16)
-    for j in range(width // channels):
-        pack[width + j * channels : width + (j + 1) * channels, :] = gwout[
-            :, j * channels : (j + 1) * channels
-        ].astype(bf16)
+
+    def store(first, second):
+        first[...] = gwin[...].astype(bf16)
+        for j in range(width // channels):
+            at = slice(j * channels, (j + 1) * channels)
+            second[at, :] = gwout[:, at].astype(bf16)
+
+    pl.when(core[0] == 0)(lambda: store(keep, send))
+    pl.when(core[0] != 0)(lambda: store(send, keep))
     gbin_ref[...] = jnp.sum(gbin[...], axis=0, keepdims=True)
 
 
@@ -195,7 +200,7 @@
 
 
 def mlp_first_kernel(
-    base, width, ln_ref, cot, w_in, w_out, b_in, scale, branch_ref, dnorm_ref, pack, gbin_ref,
+    base, width, core, ln_ref, cot, w_in, w_out, b_in, scale, branch_ref, dnorm_ref, keep, send, gbin_ref,
     hid_ref, dpre_ref, gwin, gwout, gbin,
 ):
     gwin[...] = jnp.zeros_like(gwin)
@@ -216,13 +221,13 @@
         return _
 
     lax.fori_loop(0, ln_ref.shape[0] // MLP_BLOCK, step, 0)
-    pack_grads(pack, gwin, gwout, gbin_ref, gbin)
+    pack_grads(core, keep, send, gwin, gwout, gbin_ref, gbin)
 
 
 def mlp_second_kernel(
-    base, width, ln_ref, cot, w_in, w_out, b_in, scale, b_out, gain, page, normed_ref, inv_ref,
+    base, width, core, ln_ref, cot, w_in, w_out, b_in, scale, b_out, gain, page, normed_ref, inv_ref,
     branch_ref, dnorm_ref,
-    result, d_depth_ref, pack, gbin_ref, sums_ref,
+    result, d_depth_ref, keep, send, gbin_ref, sums_ref,
     hid_ref, dpre_ref, gwin, gwout, gbin, sums,
 ):
     gwin[...] = jnp.zeros_like(gwin)
@@ -260,7 +265,7 @@
         return _
 
     lax.fori_loop(0, ln_ref.shape[0] // MLP_BLOCK, step, 0)
-    pack_grads(pack, gwin, gwout, gbin_ref, gbin)
+    pack_grads(core, keep, send, gwin, gwout, gbin_ref, gbin)
     for j in range(5):
         sums_ref[j : j + 1, :] = jnp.sum(sums[j], axis=0, keepdims=True)
 
@@ -313,12 +318,13 @@
     lax.fori_loop(0, rows * cols // block, finish, 0)
 
 
-def call(body, outs, scratch, args, flops, size=24 << 20):
+def call(body, outs, scratch, args, flops, scalars=0, size=24 << 20):
     vmem = pl.BlockSpec(memory_space=pltpu.VMEM)
+    smem = pl.BlockSpec(memory_space=pltpu.SMEM)
     return pl.pallas_call(
         body,
         out_shape=[jax.ShapeDtypeStruct(shape, dtype) for shape, dtype in outs],
-        in_specs=[vmem] * len(args),
+        in_specs=[smem] * scalars + [vmem] * (len(args) - scalars),
         out_specs=[vmem] * len(outs),
         scratch_shapes=[pltpu.VMEM(shape, dtype) for shape, dtype in scratch],
         compiler_params=pltpu.CompilerParams(vmem_limit_bytes=size),
@@ -357,8 +363,10 @@
     return jnp.where(core == 0, values[0], values[1])
 
 
-def sum_scatter(x):
-    for choice in sum_plan():
+def sum_scatter(keep, send):
+    plan = sum_plan()
+    x = (keep.astype(f32) + exchange(send, plan[0]).astype(f32)).astype(bf16)
+    for choice in plan[1:]:
         bit = own_bit(choice)
         halves = x.reshape(2, x.shape[0] // 2, x.shape[1])
         keep = lax.dynamic_index_in_dim(halves, bit, 0, keepdims=False)
@@ -375,22 +383,18 @@
     return x
 
 
-def gather_call(x):
-    plan = sum_plan()
-    sizes = [lax.axis_size(axis) for axis in AXES]
-    got = lax.all_gather(x, AXES)
-    dims, place = [], {}
-    for axis, size in zip(AXES, sizes):
-        for j in reversed(range(bits(size))):
-            place[(axis, j)] = len(dims)
-            dims.append(2)
-    got = got.reshape(*dims, *x.shape)
-    parts = []
-    for core in range(2):
-        half = lax.index_in_dim(got, core, place[("gy", 0)], keepdims=True)
-        order = [place[choice[core]] for choice in plan]
-        parts.append(half.transpose(*order, len(dims), len(dims) + 1))
-    return jnp.concatenate(parts).reshape(-1, x.shape[1])
+def sum_small(x):
+    rows, channels = x.shape
+    groups = (("gy", "gx"), ("rep",))
+    counts = [math.prod(lax.axis_size(axis) for axis in group) for group in groups]
+    whole = -(-rows // math.prod(counts)) * math.prod(counts)
+    x = jnp.pad(x, ((0, whole - rows), (0, 0)))
+    for group, count in zip(groups, counts):
+        got = lax.all_to_all(x, group, 0, 0, tiled=True)
+        x = jnp.sum(got.reshape(count, -1, channels), axis=0)
+    for group, count in reversed(list(zip(groups, counts))):
+        x = lax.all_to_all(jnp.tile(x, (count, 1)), group, 0, 0, tiled=True)
+    return x[:rows]
 
 
 def shards(
@@ -435,25 +439,28 @@
         ((channels, width), f32),
         ((8, width), f32),
     ]
-    packed = ((2 * width, channels), bf16)
+    packed = ((width, channels), bf16)
+    core = (lax.axis_index("gy") % 2).astype(jnp.int32).reshape(1)
     mlp_flops = 6 * pixels * channels * hid * 2
     weights = (w_in, w_out, row(b_in), scale)
-    branch, d_norm, pack_a, gbin_a = call(
+    branch, d_norm, keep_a, send_a, gbin_a = call(
         functools.partial(mlp_first_kernel, 0, width),
-        [(full, f32), (full, f32), packed, ((1, width), f32)],
+        [(full, f32), (full, f32), packed, packed, ((1, width), f32)],
         grads,
-        (ln_out, cot, *weights),
+        (core, ln_out, cot, *weights),
         mlp_flops,
-    )
-    piece_a = sum_scatter(pack_a)
-    result, d_depth, pack_b, gbin_b, sums = call(
+        1,
+    )
+    piece_a = sum_scatter(keep_a, send_a)
+    result, d_depth, keep_b, send_b, gbin_b, sums = call(
         functools.partial(mlp_second_kernel, width, width),
-        [(full, bf16), (full, bf16), packed, ((1, width), f32), ((8, channels), f32)],
+        [(full, bf16), (full, bf16), packed, packed, ((1, width), f32), ((8, channels), f32)],
         grads + [((8, 8, channels), f32)],
-        (ln_out, cot, *weights, row(b_out), gain, page, normed, inv, branch, d_norm),
+        (core, ln_out, cot, *weights, row(b_out), gain, page, normed, inv, branch, d_norm),
         mlp_flops,
-    )
-    piece_b = sum_scatter(pack_b)
+        1,
+    )
+    piece_b = sum_scatter(keep_b, send_b)
     d_tile = d_depth.reshape(tile.shape)
     d_around = halo(d_tile)
     (g_kernel,) = call(
@@ -474,8 +481,8 @@
         conv_flops,
     )
     factor = float(pixels * lax.axis_size("gy") * lax.axis_size("gx") * lax.axis_size("rep")) ** (-0.5)
-    small = lax.psum(small, AXES) * factor
-    both = [gather_back(piece_a), gather_call(piece_b)]
+    small = sum_small(small) * factor
+    both = [gather_back(piece_a), gather_back(piece_b)]
     sum_win = jnp.concatenate([g[:width] for g in both]).astype(f32) * factor
     blocks = [g[width + j * channels : width + (j + 1) * channels] for g in both for j in range(width // channels)]
     sum_wout = jnp.concatenate(blocks, axis=1).astype(f32) * factor

time: 276 us -> 142 us (0.51)
  waiting for transfers between devices: 169 us -> 28 us
  starting transfers between devices: 32.6 us -> 56.6 us
  between operations: 14.8 us -> 1.42 us
  other arithmetic: 13.3 us -> 10.1 us
    psum x1 -> x0, waiting for transfers between devices: 116 us -> none  [shards(): small = lax.psum(small, AXES) * factor]
    all_gather x1 -> x0, waiting for transfers between devices: 20.1 us -> none  [gather_call(): got = lax.all_gather(x, AXES)]
    all_to_all x0 -> x4, starting transfers between devices: none -> 17.7 us  [the longest x2 10.9 us: sum_small(): got = lax.all_to_all(x, group, 0, 0, tiled=True)]
    all_to_all x0 -> x4, waiting for transfers between devices: none -> 9.15 us  [the longest x2 9.14 us: sum_small(): got = lax.all_to_all(x, group, 0, 0, tiled=True)]
    ppermute x15 -> x20, waiting for transfers between devices: 24.8 us -> 16.2 us  [exchange(): return lax.ppermute(x, AXES, perm)]
    ppermute x15 -> x20, starting transfers between devices: 21.3 us -> 29.6 us  [exchange(): return lax.ppermute(x, AXES, perm)]
    ppermute x2, waiting for transfers between devices: 7.95 us -> 2.59 us  [halo(): lax.ppermute(jnp.where(is_high, column[:, 3:], column[:, :3]), 'gx', pairs)]
    convert_element_type x10 -> x8, other arithmetic: 3.38 us -> 0.34 us  [sum_scatter(): x = (keep.astype(f32) + exchange(send, choice).astype(f32)).astype(bf16)]
  transfers between devices with their start and end apart: 23 -> 30, of which waited for: 13 -> 10; matrix products, arithmetic and copies ran while one was open for 5% -> 7% of each run, Pallas kernels for 5% -> 5%
where the time goes in v2:
time: 142 us; the launch traced here: 141 us
  starting transfers between devices  56.6 us (40%)
  Pallas kernels  36.3 us (26%)
  waiting for transfers between devices  28 us (20%)
  other arithmetic  10.1 us (7%)
  local copies, waits for them, and re-layouts  8.96 us (6%)
  between operations  1.42 us (1%)
    pallas_call x5, Pallas kernels, call(): pl.pallas_call(body, out_shape=[jax.ShapeDtypeStruct(shape, dtype) for sh...  36.3 us
    ppermute x20, starting transfers between devices, exchange(): return lax.ppermute(x, AXES, perm)  29.6 us
    ppermute x20, waiting for transfers between devices, exchange(): return lax.ppermute(x, AXES, perm)  16.2 us
    all_to_all x2, starting transfers between devices, sum_small(): got = lax.all_to_all(x, group, 0, 0, tiled=True)  10.9 us
    all_to_all x2, waiting for transfers between devices, sum_small(): got = lax.all_to_all(x, group, 0, 0, tiled=True)  9.14 us
    all_to_all x2, starting transfers between devices, sum_small(): x = lax.all_to_all(jnp.tile(x, (count, 1)), group, 0, 0, tiled=True)  6.79 us
    ppermute x4, starting transfers between devices, edges(): out.append(lax.ppermute(jnp.where(is_high, high, low), axis, pairs))  5.52 us
    ppermute x2, starting transfers between devices, halo(): lax.ppermute(jnp.where(is_high, column[:, 3:], column[:, :3]), 'gx', pairs)  3.8 us
  transfers between devices with their start and end apart: 30, of which 10 were waited for; matrix products, arithmetic and copies ran while one was open for 7% of the time, Pallas kernels for 5%

profile of v2, /device:TPU:0, one launch (start us, length us, event | category | flops | bytes accessed | tf_op | source)
XLA Modules:
  0.0 141.3 jit_solution(12592026002136567905)
XLA Ops:
  0.7 1.0 select_bitcast_fusion
  1.7 0.5 collective-permute-start.1
  2.3 0.7 collective-permute-start
  2.9 1.1 fusion.12
  4.4 2.7 %collective-permute-start.2 = (bf16[38,3,384]{2,1,0:T(4,128)(2,1)S(1)}, bf16[38,3,384]{2,1,0:T(4,128)(2,1)S(1)}, u32[]{:S(2)}, u32[]{:S(2)}) collective-permute-start(bf16[38,3,384]{2,1,0:T(4,128)(2,1)S(1)} %slice_select_fusion.1), channel_id=1, source_target_pairs={{0,4},{4,0},{1,5},{5,1},{2,6},{6,2},{3,7},{7,3},{8,12},{12,8},{9,1... | collective-permute-start | bytes 262664 | tf_op jit(solution)/shard_map/ppermute | solution.py:64
  7.3 2.6 %collective-permute-done.2 = bf16[38,3,384]{2,1,0:T(4,128)(2,1)S(1)} collective-permute-done((bf16[38,3,384]{2,1,0:T(4,128)(2,1)S(1)}, bf16[38,3,384]{2,1,0:T(4,128)(2,1)S(1)}, u32[]{:S(2)}, u32[]{:S(2)}) %collective-permute-start.2) | collective-permute-done | bytes 87584 | tf_op jit(solution)/shard_map/ppermute | solution.py:64
  10.0 7.6 %shard_map.194 = (f32[1024,384]{1,0:T(8,128)S(1)}, f32[1024,128]{1,0:T(8,128)S(1)}, bf16[1024,384]{1,0:T(8,128)(2,1)S(1)}) custom-call(bf16[32,32,384]{2,1,0:T(8,128)(2,1)S(1)} %bitcast.66, bf16[3,32,384]{2,1,0:T(8,128)(2,1)S(1)} %get-tuple-element.59.top, bf16[3,32,384]{2,1,0:T(8,128)(2,1)S(1)} %get-tuple-element.58.bottom, ...), custom_call_target="tpu_custom_call" | custom-call | flops 2312110080 | bytes 1048576 | tf_op jit(solution)/shard_map/pallas_call | solution.py:324
  17.6 6.4 %shard_map.195 = (f32[1024,384]{1,0:T(8,128)S(1)}, f32[1024,384]{1,0:T(8,128)S(1)}, bf16[768,384]{1,0:T(8,128)(2,1)S(1)}, bf16[768,384]{1,0:T(8,128)(2,1)S(1)}, f32[1,768]{1,0:T(1,128)S(1)}) custom-call(s32[1]{0:T(128)} %bitcast.core, bf16[1024,384]{1,0:T(8,128)(2,1)S(1)} %get-tuple-element.25.ln_ref, bf16[1024,384]{1,0:T(8,128)(2,1)S(1)} %bitcast.72, ...), custom_call_target="tpu_custom_call" | custom-call | flops 7247757312 | bytes 1048576 | tf_op jit(solution)/shard_map/pallas_call | solution.py:324
  24.1 0.8 copy-done.5
  24.9 8.7 %shard_map.196 = (bf16[1024,384]{1,0:T(8,128)(2,1)}, bf16[1024,384]{1,0:T(8,128)(2,1)S(1)}, bf16[768,384]{1,0:T(8,128)(2,1)S(1)}, bf16[768,384]{1,0:T(8,128)(2,1...) custom-call(s32[1]{0:T(128)} %bitcast.core, bf16[1024,384]{1,0:T(8,128)(2,1)S(1)} %get-tuple-element.25.ln_ref, ...), custom_call_target="tpu_custom_call" | custom-call | flops 7247757312 | bytes 1048576 | tf_op jit(solution)/shard_map/pallas_call | solution.py:324
  33.5 6.8 %shard_map.198 = f32[49,384]{1,0:T(8,128)S(1)} custom-call(bf16[32,32,384]{2,1,0:T(8,128)(2,1)S(1)} %bitcast.68, bf16[3,32,384]{2,1,0:T(8,128)(2,1)S(1)} %get-tuple-element.59.top, bf16[3,32,384]{2,1,0:T(8,128)(2,1)S(1)} %get-tuple-element.58.bottom, bf16[38,3,384]{2,1,0:T(4,128)(2,1)S(1)} %get-tuple-element.63.left, ...), custom_call_target="tpu_custom_call" | custom-call | flops 2312110080 | bytes 1048576 | tf_op jit(solution)/shard_map/pallas_call | solution.py:324
  40.3 3.7 %collective-permute-start.4 = (bf16[3,32,384]{2,1,0:T(8,128)(2,1)S(1)}, bf16[3,32,384]{2,1,0:T(8,128)(2,1)S(1)}, u32[]{:S(2)}, u32[]{:S(2)}) collective-permute-start(bf16[3,32,384]{2,1,0:T(8,128)(2,1)S(1)} %bitcast.93), channel_id=1, source_target_pairs={{0,8},{16,24},{8,0},{24,16},{1,9},{17,25},{9,1},{25,17},{2,10},{18... | collective-permute-start | bytes 221192 | tf_op jit(solution)/shard_map/ppermute | solution.py:46
  44.0 0.7 collective-permute-start.3
  44.9 0.7 fusion.6
  45.5 6.0 %all-to-all-start = ((f32[8,8,384]{2,1,0:T(8,128)}), f32[8,8,384]{2,1,0:T(8,128)S(1)}, u32[]{:S(2)}, u32[]{:S(2)}) async-start(f32[8,8,384]{2,1,0:T(8,128)} %fusion.6), calls=%async_computation | async-start | bytes 196608 | tf_op jit(solution)/shard_map/all_to_all | solution.py:393
  51.5 1.0 collective-permute-start.16
  52.6 3.7 %all-to-all-done = f32[8,8,384]{2,1,0:T(8,128)S(1)} async-done(((f32[8,8,384]{2,1,0:T(8,128)}), f32[8,8,384]{2,1,0:T(8,128)S(1)}, u32[]{:S(2)}, u32[]{:S(2)}) %all-to-all-start) | async-done | bytes 98336 | tf_op jit(solution)/shard_map/all_to_all | solution.py:393
  56.3 0.6 all_to_all.24
  56.9 4.9 %all-to-all-start.1 = ((f32[4,2,384]{2,1,0:T(2,128)}), f32[4,2,384]{2,1,0:T(2,128)S(1)}, u32[]{:S(2)}, u32[]{:S(2)}) async-start(f32[4,2,384]{2,1,0:T(2,128)} %all_to_all.24), calls=%async_computation.1 | async-start | bytes 24576 | tf_op jit(solution)/shard_map/all_to_all | solution.py:393
  61.9 5.5 %all-to-all-done.1 = f32[4,2,384]{2,1,0:T(2,128)S(1)} async-done(((f32[4,2,384]{2,1,0:T(2,128)}), f32[4,2,384]{2,1,0:T(2,128)S(1)}, u32[]{:S(2)}, u32[]{:S(2)}) %all-to-all-start.1) | async-done | bytes 12320 | tf_op jit(solution)/shard_map/all_to_all | solution.py:393
  67.4 0.6 tile.6
  68.0 3.3 %all-to-all-start.2 = ((f32[4,2,384]{2,1,0:T(2,128)}), f32[4,2,384]{2,1,0:T(2,128)S(1)}, u32[]{:S(2)}, u32[]{:S(2)}) async-start(f32[4,2,384]{2,1,0:T(2,128)} %tile.6), calls=%async_computation.2 | async-start | bytes 24576 | tf_op jit(solution)/shard_map/all_to_all | solution.py:396
  71.3 0.8 copy-done.8
  72.1 1.2 add_convert_fusion
  73.4 0.8 collective-permute-start.17
  74.2 1.2 add_convert_fusion.1
  75.5 1.3 collective-permute-start.7
  76.8 3.3 %collective-permute-done.17 = bf16[384,384]{1,0:T(8,128)(2,1)S(1)} collective-permute-done((bf16[384,384]{1,0:T(8,128)(2,1)S(1)}, bf16[384,384]{1,0:T(8,128)(2,1)S(1)}, u32[]{:S(2)}, u32[]{:S(2)}) %collective-permute-start.17) | collective-permute-done | bytes 294944 | tf_op jit(solution)/shard_map/ppermute | solution.py:357
  80.3 1.0 collective-permute-start.18
  81.3 4.5 %collective-permute-done.7 = bf16[384,384]{1,0:T(8,128)(2,1)S(1)} collective-permute-done((bf16[384,384]{1,0:T(8,128)(2,1)S(1)}, bf16[384,384]{1,0:T(8,128)(2,1)S(1)}, u32[]{:S(2)}, u32[]{:S(2)}) %collective-permute-start.7) | collective-permute-done | bytes 294944 | tf_op jit(solution)/shard_map/ppermute | solution.py:357
  85.9 1.3 collective-permute-start.8
  87.3 2.3 %collective-permute-start.19 = (bf16[96,384]{1,0:T(8,128)(2,1)S(1)}, bf16[96,384]{1,0:T(8,128)(2,1)S(1)}, u32[]{:S(2)}, u32[]{:S(2)}) collective-permute-start(bf16[96,384]{1,0:T(8,128)(2,1)S(1)} %dynamic-slice_bitcast_fusion.4), channel_id=1, source_target_pairs={{0,1},{1,0},{2,3},{3,2},{4,5},{5,4},{6,7},{7,6},{8,9},{9,8},{10,11... | collective-permute-start | bytes 221192 | tf_op jit(solution)/shard_map/ppermute | solution.py:357
  89.6 1.5 %collective-permute-done.8 = bf16[192,384]{1,0:T(8,128)(2,1)S(1)} collective-permute-done((bf16[192,384]{1,0:T(8,128)(2,1)S(1)}, bf16[192,384]{1,0:T(8,128)(2,1)S(1)}, u32[]{:S(2)}, u32[]{:S(2)}) %collective-permute-start.8) | collective-permute-done | bytes 147488 | tf_op jit(solution)/shard_map/ppermute | solution.py:357
  91.2 2.3 %collective-permute-start.9 = (bf16[96,384]{1,0:T(8,128)(2,1)S(1)}, bf16[96,384]{1,0:T(8,128)(2,1)S(1)}, u32[]{:S(2)}, u32[]{:S(2)}) collective-permute-start(bf16[96,384]{1,0:T(8,128)(2,1)S(1)} %dynamic-slice_bitcast_fusion.5), channel_id=1, source_target_pairs={{0,1},{1,0},{2,3},{3,2},{4,5},{5,4},{6,7},{7,6},{8,9},{9,8},{10,11... | collective-permute-start | bytes 221192 | tf_op jit(solution)/shard_map/ppermute | solution.py:357
  93.6 2.4 %collective-permute-start.20 = (bf16[48,384]{1,0:T(8,128)(2,1)S(1)}, bf16[48,384]{1,0:T(8,128)(2,1)S(1)}, u32[]{:S(2)}, u32[]{:S(2)}) collective-permute-start(bf16[48,384]{1,0:T(8,128)(2,1)S(1)} %dynamic-slice_bitcast_fusion.6), channel_id=1, source_target_pairs={{0,2},{1,3},{2,0},{3,1},{4,6},{5,7},{6,4},{7,5},{8,10},{9,11},{10,... | collective-permute-start | bytes 110600 | tf_op jit(solution)/shard_map/ppermute | solution.py:357
  96.1 2.8 %collective-permute-start.10 = (bf16[48,384]{1,0:T(8,128)(2,1)S(1)}, bf16[48,384]{1,0:T(8,128)(2,1)S(1)}, u32[]{:S(2)}, u32[]{:S(2)}) collective-permute-start(bf16[48,384]{1,0:T(8,128)(2,1)S(1)} %dynamic-slice_bitcast_fusion.7), channel_id=1, source_target_pairs={{0,2},{1,3},{2,0},{3,1},{4,6},{5,7},{6,4},{7,5},{8,10},{9,11},{10,... | collective-permute-start | bytes 110600 | tf_op jit(solution)/shard_map/ppermute | solution.py:357
  98.9 0.9 collective-permute-done.20
  99.8 1.1 collective-permute-start.21
  101.0 2.9 %collective-permute-start.11 = (bf16[48,384]{1,0:T(8,128)(2,1)S(1)}, bf16[48,384]{1,0:T(8,128)(2,1)S(1)}, u32[]{:S(2)}, u32[]{:S(2)}) collective-permute-start(bf16[48,384]{1,0:T(8,128)(2,1)S(1)} %fusion.8), channel_id=1, source_target_pairs={{0,2},{1,3},{2,0},{3,1},{4,6},{5,7},{6,4},{7,5},{8,10},{9,11},{10,... | collective-permute-start | bytes 110600 | tf_op jit(solution)/shard_map/ppermute | solution.py:357
  104.0 1.2 collective-permute-done.21
  105.2 0.7 collective-permute-start.22
  106.0 2.3 %collective-permute-start.12 = (bf16[96,384]{1,0:T(8,128)(2,1)S(1)}, bf16[96,384]{1,0:T(8,128)(2,1)S(1)}, u32[]{:S(2)}, u32[]{:S(2)}) collective-permute-start(bf16[96,384]{1,0:T(8,128)(2,1)S(1)} %maximum_select_fusion.8), channel_id=1, source_target_pairs={{0,1},{1,0},{2,3},{3,2},{4,5},{5,4},{6,7},{7,6},{8,9},{9,8},{10,11... | collective-permute-start | bytes 221192 | tf_op jit(solution)/shard_map/ppermute | solution.py:357
  108.3 1.3 collective-permute-done.22
  109.6 1.1 collective-permute-start.23
  110.8 1.1 collective-permute-start.5
  111.9 0.7 tile.8
  112.6 3.5 %all-to-all-start.3 = ((f32[8,8,384]{2,1,0:T(8,128)}), f32[8,8,384]{2,1,0:T(8,128)S(1)}, u32[]{:S(2)}, u32[]{:S(2)}) async-start(f32[8,8,384]{2,1,0:T(8,128)} %tile.8), calls=%async_computation.3 | async-start | bytes 196608 | tf_op jit(solution)/shard_map/all_to_all | solution.py:396
  116.2 1.8 %collective-permute-start.13 = (bf16[192,384]{1,0:T(8,128)(2,1)S(1)}, bf16[192,384]{1,0:T(8,128)(2,1)S(1)}, u32[]{:S(2)}, u32[]{:S(2)}) collective-permute-start(bf16[192,384]{1,0:T(8,128)(2,1)S(1)} %maximum_select_fusion.6), channel_id=1, source_target_pairs={{0,4},{1,5},{2,6},{3,7},{4,0},{5,1},{6,2},{7,3},{8,24},{9,25},{10,... | collective-permute-start | bytes 442376 | tf_op jit(solution)/shard_map/ppermute | solution.py:357
  118.0 1.6 %collective-permute-start.24 = (bf16[384,384]{1,0:T(8,128)(2,1)S(1)}, bf16[384,384]{1,0:T(8,128)(2,1)S(1)}, u32[]{:S(2)}, u32[]{:S(2)}) collective-permute-start(bf16[384,384]{1,0:T(8,128)(2,1)S(1)} %maximum_select_fusion.5), channel_id=1, source_target_pairs={{0,16},{1,17},{2,18},{3,19},{4,20},{5,21},{6,22},{7,23},{8,12},{9,... | collective-permute-start | bytes 884744 | tf_op jit(solution)/shard_map/ppermute | solution.py:357
  119.7 3.4 %collective-permute-done.13 = bf16[192,384]{1,0:T(8,128)(2,1)S(1)} collective-permute-done((bf16[192,384]{1,0:T(8,128)(2,1)S(1)}, bf16[192,384]{1,0:T(8,128)(2,1)S(1)}, u32[]{:S(2)}, u32[]{:S(2)}) %collective-permute-start.13) | collective-permute-done | bytes 147488 | tf_op jit(solution)/shard_map/ppermute | solution.py:357
  123.2 1.9 %collective-permute-start.14 = (bf16[384,384]{1,0:T(8,128)(2,1)S(1)}, bf16[384,384]{1,0:T(8,128)(2,1)S(1)}, u32[]{:S(2)}, u32[]{:S(2)}) collective-permute-start(bf16[384,384]{1,0:T(8,128)(2,1)S(1)} %maximum_select_fusion.4), channel_id=1, source_target_pairs={{0,16},{1,17},{2,18},{3,19},{4,20},{5,21},{6,22},{7,23},{8,12},{9,... | collective-permute-start | bytes 884744 | tf_op jit(solution)/shard_map/ppermute | solution.py:357
  125.2 0.2 maximum_select_fusion.3
  125.5 6.9 %shard_map.197 = bf16[1024,384]{1,0:T(8,128)(2,1)} custom-call(bf16[32,32,384]{2,1,0:T(8,128)(2,1)S(1)} %bitcast.70, bf16[3,32,384]{2,1,0:T(8,128)(2,1)S(1)} %get-tuple-element.57.top, bf16[3,32,384]{2,1,0:T(8,128)(2,1)S(1)} %get-tuple-element.56.bottom, bf16[38,3,384]{2,1,0:T(4,128)(2,1)S(1)} %get-tuple-element.61.left, ...), custom_call_target="tpu_custom_call" | custom-call | flops 2312110080 | bytes 1048576 | tf_op jit(solution)/shard_map/pallas_call | solution.py:324
  132.4 0.6 reshape.167
  133.1 0.6 reshape.176
  133.7 0.2 maximum_select_fusion.2
  133.9 0.5 collective-permute-start.15
  134.4 0.6 slice_reduce_fusion
  135.0 0.4 maximum_select_fusion.1
  135.6 0.9 copy-done.7
  136.5 0.4 maximum_select_fusion
  137.1 0.9 slice-done
  138.0 1.6 %convert_multiply_fusion.1 = f32[1536,384]{1,0:T(8,128)} fusion(bf16[768,384]{1,0:T(8,128)(2,1)S(1)} %slice-done, bf16[768,384]{1,0:T(8,128)(2,1)S(1)} %slice.165), kind=kLoop, calls=%fused_computation.1 | loop fusion | flops 2949120 | bytes 3538944 | tf_op jit(solution)/shard_map/mul | solution.py:486
  139.6 1.7 %convert_multiply_fusion = f32[384,1536]{1,0:T(8,128)} fusion(bf16[384,384]{1,0:T(8,128)(2,1)S(1)} %get-tuple-element.47, bf16[384,384]{1,0:T(8,128)(2,1)S(1)} %get-tuple-element.46, bf16[384,384]{1,0:T(8,128)(2,1)S(1)} %get-tuple-element.45, bf16[384,384]{1,0:T(8,128)(2,1)S(1)} %get-tuple-element.44), kind=kLoop, calls=%fused_computation | loop fusion | flops 5308416 | bytes 3538944 | tf_op jit(solution)/shard_map/mul | solution.py:488
  (107 shorter events, 2.3 us)
Async XLA Ops:
  0.6 6.4 %copy-start.9 = (f32[7,7,384]{2,1,0:T(8,128)S(1)}, f32[7,7,384]{2,1,0:T(8,128)}, u32[]{:S(2)}) copy-start(f32[7,7,384]{2,1,0:T(8,128)} %param.13) | copy-start | bytes 225796
  0.7 6.5 %copy-start.11 = (f32[384]{0:T(512)S(1)}, f32[384]{0:T(512)}, u32[]{:S(2)}) copy-start(f32[384]{0:T(512)} %param.14) | copy-start | bytes 4612
  0.7 6.5 %copy-start.12 = (f32[384]{0:T(512)S(1)}, f32[384]{0:T(512)}, u32[]{:S(2)}) copy-start(f32[384]{0:T(512)} %param.15) | copy-start | bytes 4612
  0.7 6.5 %copy-start.13 = (f32[384]{0:T(512)S(1)}, f32[384]{0:T(512)}, u32[]{:S(2)}) copy-start(f32[384]{0:T(512)} %param.16) | copy-start | bytes 4612
  0.7 6.5 %copy-start.10 = (f32[1536]{0:T(1024)S(1)}, f32[1536]{0:T(1024)}, u32[]{:S(2)}) copy-start(f32[1536]{0:T(1024)} %param.18) | copy-start | bytes 18436
  0.7 6.5 %copy-start.14 = (f32[384]{0:T(512)S(1)}, f32[384]{0:T(512)}, u32[]{:S(2)}) copy-start(f32[384]{0:T(512)} %param.21) | copy-start | bytes 4612
  0.7 6.5 %copy-start.15 = (f32[384]{0:T(512)S(1)}, f32[384]{0:T(512)}, u32[]{:S(2)}) copy-start(f32[384]{0:T(512)} %param.20) | copy-start | bytes 4612
  1.7 8.3 %copy-start = (bf16[1,32,32,384]{3,2,1,0:T(8,128)(2,1)S(1)}, bf16[1,32,32,384]{3,2,1,0:T(8,128)(2,1)}, u32[]{:S(2)}) copy-start(bf16[1,32,32,384]{3,2,1,0:T(8,128)(2,1)} %param.11) | copy-start | bytes 2359300
  1.7 2.3 %collective-permute-start.1 = (bf16[3,32,384]{2,1,0:T(8,128)(2,1)S(1)}, bf16[3,32,384]{2,1,0:T(8,128)(2,1)S(1)}, u32[]{:S(2)}, u32[]{:S(2)}) collective-permute-start(bf16[3,32,384]{2,1,0:T(8,128)(2,1)S(1)} %get-tuple-element.54), channel_id=1, source_target_pairs={{0,8},{16,24},{8,0},{24,16},{1,9},{17,25},{9,1},{25,17},{2,10},{18... | collective-permute-start | bytes 221192 | tf_op jit(solution)/shard_map/ppermute | solution.py:46
  2.3 1.8 %collective-permute-start = (bf16[3,32,384]{2,1,0:T(8,128)(2,1)S(1)}, bf16[3,32,384]{2,1,0:T(8,128)(2,1)S(1)}, u32[]{:S(2)}, u32[]{:S(2)}) collective-permute-start(bf16[3,32,384]{2,1,0:T(8,128)(2,1)S(1)} %get-tuple-element.55), channel_id=1, source_target_pairs={{8,16},{16,8},{9,17},{17,9},{10,18},{18,10},{11,19},{19,11},{12,20... | collective-permute-start | bytes 221192 | tf_op jit(solution)/shard_map/ppermute | solution.py:46
  4.4 5.5 %collective-permute-start.2 = (bf16[38,3,384]{2,1,0:T(4,128)(2,1)S(1)}, bf16[38,3,384]{2,1,0:T(4,128)(2,1)S(1)}, u32[]{:S(2)}, u32[]{:S(2)}) collective-permute-start(bf16[38,3,384]{2,1,0:T(4,128)(2,1)S(1)} %slice_select_fusion.1), channel_id=1, source_target_pairs={{0,4},{4,0},{1,5},{5,1},{2,6},{6,2},{3,7},{7,3},{8,12},{12,8},{9,1... | collective-permute-start | bytes 262664 | tf_op jit(solution)/shard_map/ppermute | solution.py:64
  10.0 7.6 %copy-start.1 = (bf16[1536,384]{1,0:T(8,128)(2,1)S(1)}, bf16[1536,384]{1,0:T(8,128)(2,1)}, u32[]{:S(2)}) copy-start(bf16[1536,384]{1,0:T(8,128)(2,1)} %w_in.3) | copy-start | bytes 3538948
  10.0 7.6 %copy-start.2 = (bf16[384,1536]{1,0:T(8,128)(2,1)S(1)}, bf16[384,1536]{1,0:T(8,128)(2,1)}, u32[]{:S(2)}) copy-start(bf16[384,1536]{1,0:T(8,128)(2,1)} %w_out.3) | copy-start | bytes 3538948
  10.0 7.6 %copy-start.3 = (bf16[1,32,32,384]{3,2,1,0:T(8,128)(2,1)S(1)}, bf16[1,32,32,384]{3,2,1,0:T(8,128)(2,1)}, u32[]{:S(2)}) copy-start(bf16[1,32,32,384]{3,2,1,0:T(8,128)(2,1)} %param.12) | copy-start | bytes 2359300
  24.0 0.8 copy-start.5
  33.5 6.8 %copy-start.6 = (bf16[768,384]{1,0:T(8,128)(2,1)}, bf16[768,384]{1,0:T(8,128)(2,1)S(1)}, u32[]{:S(2)}) copy-start(bf16[768,384]{1,0:T(8,128)(2,1)S(1)} %get-tuple-element.38) | copy-start | bytes 1769476
  40.3 12.2 %collective-permute-start.4 = (bf16[3,32,384]{2,1,0:T(8,128)(2,1)S(1)}, bf16[3,32,384]{2,1,0:T(8,128)(2,1)S(1)}, u32[]{:S(2)}, u32[]{:S(2)}) collective-permute-start(bf16[3,32,384]{2,1,0:T(8,128)(2,1)S(1)} %bitcast.93), channel_id=1, source_target_pairs={{0,8},{16,24},{8,0},{24,16},{1,9},{17,25},{9,1},{25,17},{2,10},{18... | collective-permute-start | bytes 221192 | tf_op jit(solution)/shard_map/ppermute | solution.py:46
  44.0 8.5 %collective-permute-start.3 = (bf16[3,32,384]{2,1,0:T(8,128)(2,1)S(1)}, bf16[3,32,384]{2,1,0:T(8,128)(2,1)S(1)}, u32[]{:S(2)}, u32[]{:S(2)}) collective-permute-start(bf16[3,32,384]{2,1,0:T(8,128)(2,1)S(1)} %bitcast.92), channel_id=1, source_target_pairs={{8,16},{16,8},{9,17},{17,9},{10,18},{18,10},{11,19},{19,11},{12,20... | collective-permute-start | bytes 221192 | tf_op jit(solution)/shard_map/ppermute | solution.py:46
  45.5 10.8 %all-to-all-start = ((f32[8,8,384]{2,1,0:T(8,128)}), f32[8,8,384]{2,1,0:T(8,128)S(1)}, u32[]{:S(2)}, u32[]{:S(2)}) async-start(f32[8,8,384]{2,1,0:T(8,128)} %fusion.6), calls=%async_computation | async-start | bytes 196608 | tf_op jit(solution)/shard_map/all_to_all | solution.py:393
  51.5 19.8 %collective-permute-start.16 = (bf16[768,384]{1,0:T(8,128)(2,1)}, bf16[768,384]{1,0:T(8,128)(2,1)S(1)}, u32[]{:S(2)}, u32[]{:S(2)}) collective-permute-start(bf16[768,384]{1,0:T(8,128)(2,1)} %copy-done.6), channel_id=1, source_target_pairs={{0,8},{1,9},{2,10},{3,11},{4,12},{5,13},{6,14},{7,15},{8,0},{9,1},... | collective-permute-start | bytes 1769480 | tf_op jit(solution)/shard_map/ppermute | solution.py:357
  52.5 21.7 %collective-permute-start.6 = (bf16[768,384]{1,0:T(8,128)(2,1)}, bf16[768,384]{1,0:T(8,128)(2,1)}, u32[]{:S(2)}, u32[]{:S(2)}) collective-permute-start(bf16[768,384]{1,0:T(8,128)(2,1)} %copy-done.5), channel_id=1, source_target_pairs={{0,8},{1,9},{2,10},{3,11},{4,12},{5,13},{6,14},{7,15},{8,0},{9,1},... | collective-permute-start | bytes 1769480 | tf_op jit(solution)/shard_map/ppermute | solution.py:357
  56.9 10.5 %all-to-all-start.1 = ((f32[4,2,384]{2,1,0:T(2,128)}), f32[4,2,384]{2,1,0:T(2,128)S(1)}, u32[]{:S(2)}, u32[]{:S(2)}) async-start(f32[4,2,384]{2,1,0:T(2,128)} %all_to_all.24), calls=%async_computation.1 | async-start | bytes 24576 | tf_op jit(solution)/shard_map/all_to_all | solution.py:393
  68.0 43.9 %all-to-all-start.2 = ((f32[4,2,384]{2,1,0:T(2,128)}), f32[4,2,384]{2,1,0:T(2,128)S(1)}, u32[]{:S(2)}, u32[]{:S(2)}) async-start(f32[4,2,384]{2,1,0:T(2,128)} %tile.6), calls=%async_computation.2 | async-start | bytes 24576 | tf_op jit(solution)/shard_map/all_to_all | solution.py:396
  71.3 0.8 copy-start.8
  73.4 6.8 %collective-permute-start.17 = (bf16[384,384]{1,0:T(8,128)(2,1)S(1)}, bf16[384,384]{1,0:T(8,128)(2,1)S(1)}, u32[]{:S(2)}, u32[]{:S(2)}) collective-permute-start(bf16[384,384]{1,0:T(8,128)(2,1)S(1)} %dynamic-slice_bitcast_fusion), channel_id=1, source_target_pairs={{0,16},{1,17},{2,18},{3,19},{4,20},{5,21},{6,22},{7,23},{8,12},{9,... | collective-permute-start | bytes 884744 | tf_op jit(solution)/shard_map/ppermute | solution.py:357
  75.5 10.3 %collective-permute-start.7 = (bf16[384,384]{1,0:T(8,128)(2,1)S(1)}, bf16[384,384]{1,0:T(8,128)(2,1)S(1)}, u32[]{:S(2)}, u32[]{:S(2)}) collective-permute-start(bf16[384,384]{1,0:T(8,128)(2,1)S(1)} %dynamic-slice_bitcast_fusion.1), channel_id=1, source_target_pairs={{0,16},{1,17},{2,18},{3,19},{4,20},{5,21},{6,22},{7,23},{8,12},{9,... | collective-permute-start | bytes 884744 | tf_op jit(solution)/shard_map/ppermute | solution.py:357
  80.3 6.9 %collective-permute-start.18 = (bf16[192,384]{1,0:T(8,128)(2,1)S(1)}, bf16[192,384]{1,0:T(8,128)(2,1)S(1)}, u32[]{:S(2)}, u32[]{:S(2)}) collective-permute-start(bf16[192,384]{1,0:T(8,128)(2,1)S(1)} %dynamic-slice_bitcast_fusion.2), channel_id=1, source_target_pairs={{0,4},{1,5},{2,6},{3,7},{4,0},{5,1},{6,2},{7,3},{8,24},{9,25},{10,... | collective-permute-start | bytes 442376 | tf_op jit(solution)/shard_map/ppermute | solution.py:357
  85.9 5.2 %collective-permute-start.8 = (bf16[192,384]{1,0:T(8,128)(2,1)S(1)}, bf16[192,384]{1,0:T(8,128)(2,1)S(1)}, u32[]{:S(2)}, u32[]{:S(2)}) collective-permute-start(bf16[192,384]{1,0:T(8,128)(2,1)S(1)} %dynamic-slice_bitcast_fusion.3), channel_id=1, source_target_pairs={{0,4},{1,5},{2,6},{3,7},{4,0},{5,1},{6,2},{7,3},{8,24},{9,25},{10,... | collective-permute-start | bytes 442376 | tf_op jit(solution)/shard_map/ppermute | solution.py:357
  87.3 6.2 %collective-permute-start.19 = (bf16[96,384]{1,0:T(8,128)(2,1)S(1)}, bf16[96,384]{1,0:T(8,128)(2,1)S(1)}, u32[]{:S(2)}, u32[]{:S(2)}) collective-permute-start(bf16[96,384]{1,0:T(8,128)(2,1)S(1)} %dynamic-slice_bitcast_fusion.4), channel_id=1, source_target_pairs={{0,1},{1,0},{2,3},{3,2},{4,5},{5,4},{6,7},{7,6},{8,9},{9,8},{10,11... | collective-permute-start | bytes 221192 | tf_op jit(solution)/shard_map/ppermute | solution.py:357
  91.2 4.8 %collective-permute-start.9 = (bf16[96,384]{1,0:T(8,128)(2,1)S(1)}, bf16[96,384]{1,0:T(8,128)(2,1)S(1)}, u32[]{:S(2)}, u32[]{:S(2)}) collective-permute-start(bf16[96,384]{1,0:T(8,128)(2,1)S(1)} %dynamic-slice_bitcast_fusion.5), channel_id=1, source_target_pairs={{0,1},{1,0},{2,3},{3,2},{4,5},{5,4},{6,7},{7,6},{8,9},{9,8},{10,11... | collective-permute-start | bytes 221192 | tf_op jit(solution)/shard_map/ppermute | solution.py:357
  93.6 6.2 %collective-permute-start.20 = (bf16[48,384]{1,0:T(8,128)(2,1)S(1)}, bf16[48,384]{1,0:T(8,128)(2,1)S(1)}, u32[]{:S(2)}, u32[]{:S(2)}) collective-permute-start(bf16[48,384]{1,0:T(8,128)(2,1)S(1)} %dynamic-slice_bitcast_fusion.6), channel_id=1, source_target_pairs={{0,2},{1,3},{2,0},{3,1},{4,6},{5,7},{6,4},{7,5},{8,10},{9,11},{10,... | collective-permute-start | bytes 110600 | tf_op jit(solution)/shard_map/ppermute | solution.py:357
  96.1 4.9 %collective-permute-start.10 = (bf16[48,384]{1,0:T(8,128)(2,1)S(1)}, bf16[48,384]{1,0:T(8,128)(2,1)S(1)}, u32[]{:S(2)}, u32[]{:S(2)}) collective-permute-start(bf16[48,384]{1,0:T(8,128)(2,1)S(1)} %dynamic-slice_bitcast_fusion.7), channel_id=1, source_target_pairs={{0,2},{1,3},{2,0},{3,1},{4,6},{5,7},{6,4},{7,5},{8,10},{9,11},{10,... | collective-permute-start | bytes 110600 | tf_op jit(solution)/shard_map/ppermute | solution.py:357
  99.8 5.3 %collective-permute-start.21 = (bf16[48,384]{1,0:T(8,128)(2,1)S(1)}, bf16[48,384]{1,0:T(8,128)(2,1)S(1)}, u32[]{:S(2)}, u32[]{:S(2)}) collective-permute-start(bf16[48,384]{1,0:T(8,128)(2,1)S(1)} %fusion.7), channel_id=1, source_target_pairs={{0,2},{1,3},{2,0},{3,1},{4,6},{5,7},{6,4},{7,5},{8,10},{9,11},{10,... | collective-permute-start | bytes 110600 | tf_op jit(solution)/shard_map/ppermute | solution.py:357
  101.0 4.9 %collective-permute-start.11 = (bf16[48,384]{1,0:T(8,128)(2,1)S(1)}, bf16[48,384]{1,0:T(8,128)(2,1)S(1)}, u32[]{:S(2)}, u32[]{:S(2)}) collective-permute-start(bf16[48,384]{1,0:T(8,128)(2,1)S(1)} %fusion.8), channel_id=1, source_target_pairs={{0,2},{1,3},{2,0},{3,1},{4,6},{5,7},{6,4},{7,5},{8,10},{9,11},{10,... | collective-permute-start | bytes 110600 | tf_op jit(solution)/shard_map/ppermute | solution.py:357
  105.2 4.4 %collective-permute-start.22 = (bf16[96,384]{1,0:T(8,128)(2,1)S(1)}, bf16[96,384]{1,0:T(8,128)(2,1)S(1)}, u32[]{:S(2)}, u32[]{:S(2)}) collective-permute-start(bf16[96,384]{1,0:T(8,128)(2,1)S(1)} %maximum_select_fusion.9), channel_id=1, source_target_pairs={{0,1},{1,0},{2,3},{3,2},{4,5},{5,4},{6,7},{7,6},{8,9},{9,8},{10,11... | collective-permute-start | bytes 221192 | tf_op jit(solution)/shard_map/ppermute | solution.py:357
  106.0 10.1 %collective-permute-start.12 = (bf16[96,384]{1,0:T(8,128)(2,1)S(1)}, bf16[96,384]{1,0:T(8,128)(2,1)S(1)}, u32[]{:S(2)}, u32[]{:S(2)}) collective-permute-start(bf16[96,384]{1,0:T(8,128)(2,1)S(1)} %maximum_select_fusion.8), channel_id=1, source_target_pairs={{0,1},{1,0},{2,3},{3,2},{4,5},{5,4},{6,7},{7,6},{8,9},{9,8},{10,11... | collective-permute-start | bytes 221192 | tf_op jit(solution)/shard_map/ppermute | solution.py:357
  109.6 8.3 %collective-permute-start.23 = (bf16[192,384]{1,0:T(8,128)(2,1)S(1)}, bf16[192,384]{1,0:T(8,128)(2,1)S(1)}, u32[]{:S(2)}, u32[]{:S(2)}) collective-permute-start(bf16[192,384]{1,0:T(8,128)(2,1)S(1)} %maximum_select_fusion.7), channel_id=1, source_target_pairs={{0,4},{1,5},{2,6},{3,7},{4,0},{5,1},{6,2},{7,3},{8,24},{9,25},{10,... | collective-permute-start | bytes 442376 | tf_op jit(solution)/shard_map/ppermute | solution.py:357
  110.8 8.8 %collective-permute-start.5 = (bf16[38,3,384]{2,1,0:T(4,128)(2,1)S(1)}, bf16[38,3,384]{2,1,0:T(4,128)(2,1)S(1)}, u32[]{:S(2)}, u32[]{:S(2)}) collective-permute-start(bf16[38,3,384]{2,1,0:T(4,128)(2,1)S(1)} %slice_select_fusion), channel_id=1, source_target_pairs={{0,4},{4,0},{1,5},{5,1},{2,6},{6,2},{3,7},{7,3},{8,12},{12,8},{9,1... | collective-permute-start | bytes 262664 | tf_op jit(solution)/shard_map/ppermute | solution.py:64
  112.6 19.8 %all-to-all-start.3 = ((f32[8,8,384]{2,1,0:T(8,128)}), f32[8,8,384]{2,1,0:T(8,128)S(1)}, u32[]{:S(2)}, u32[]{:S(2)}) async-start(f32[8,8,384]{2,1,0:T(8,128)} %tile.8), calls=%async_computation.3 | async-start | bytes 196608 | tf_op jit(solution)/shard_map/all_to_all | solution.py:396
  116.2 7.0 %collective-permute-start.13 = (bf16[192,384]{1,0:T(8,128)(2,1)S(1)}, bf16[192,384]{1,0:T(8,128)(2,1)S(1)}, u32[]{:S(2)}, u32[]{:S(2)}) collective-permute-start(bf16[192,384]{1,0:T(8,128)(2,1)S(1)} %maximum_select_fusion.6), channel_id=1, source_target_pairs={{0,4},{1,5},{2,6},{3,7},{4,0},{5,1},{6,2},{7,3},{8,24},{9,25},{10,... | collective-permute-start | bytes 442376 | tf_op jit(solution)/shard_map/ppermute | solution.py:357
  118.0 7.4 %copy-start.4 = (bf16[1,32,32,384]{3,2,1,0:T(8,128)(2,1)S(1)}, bf16[1,32,32,384]{3,2,1,0:T(8,128)(2,1)}, u32[]{:S(2)}) copy-start(bf16[1,32,32,384]{3,2,1,0:T(8,128)(2,1)} %param.12) | copy-start | bytes 2359300
  118.0 7.1 %collective-permute-start.24 = (bf16[384,384]{1,0:T(8,128)(2,1)S(1)}, bf16[384,384]{1,0:T(8,128)(2,1)S(1)}, u32[]{:S(2)}, u32[]{:S(2)}) collective-permute-start(bf16[384,384]{1,0:T(8,128)(2,1)S(1)} %maximum_select_fusion.5), channel_id=1, source_target_pairs={{0,16},{1,17},{2,18},{3,19},{4,20},{5,21},{6,22},{7,23},{8,12},{9,... | collective-permute-start | bytes 884744 | tf_op jit(solution)/shard_map/ppermute | solution.py:357
  123.2 10.4 %collective-permute-start.14 = (bf16[384,384]{1,0:T(8,128)(2,1)S(1)}, bf16[384,384]{1,0:T(8,128)(2,1)S(1)}, u32[]{:S(2)}, u32[]{:S(2)}) collective-permute-start(bf16[384,384]{1,0:T(8,128)(2,1)S(1)} %maximum_select_fusion.4), channel_id=1, source_target_pairs={{0,16},{1,17},{2,18},{3,19},{4,20},{5,21},{6,22},{7,23},{8,12},{9,... | collective-permute-start | bytes 884744 | tf_op jit(solution)/shard_map/ppermute | solution.py:357
  125.4 9.7 %collective-permute-start.25 = (bf16[768,384]{1,0:T(8,128)(2,1)S(1)}, bf16[768,384]{1,0:T(8,128)(2,1)S(1)}, u32[]{:S(2)}, u32[]{:S(2)}) collective-permute-start(bf16[768,384]{1,0:T(8,128)(2,1)S(1)} %maximum_select_fusion.3), channel_id=1, source_target_pairs={{0,8},{1,9},{2,10},{3,11},{4,12},{5,13},{6,14},{7,15},{8,0},{9,1},... | collective-permute-start | bytes 1769480 | tf_op jit(solution)/shard_map/ppermute | solution.py:357
  133.9 2.6 %collective-permute-start.15 = (bf16[768,384]{1,0:T(8,128)(2,1)S(1)}, bf16[768,384]{1,0:T(8,128)(2,1)S(1)}, u32[]{:S(2)}, u32[]{:S(2)}) collective-permute-start(bf16[768,384]{1,0:T(8,128)(2,1)S(1)} %maximum_select_fusion.2), channel_id=1, source_target_pairs={{0,8},{1,9},{2,10},{3,11},{4,12},{5,13},{6,14},{7,15},{8,0},{9,1},... | collective-permute-start | bytes 1769480 | tf_op jit(solution)/shard_map/ppermute | solution.py:357
  135.5 1.0 copy-start.7
  136.9 1.1 slice-start

commit v3 on v2

--- a/solution.py
+++ b/solution.py
@@ -186,10 +186,12 @@
     width, channels = gwin.shape
 
     def store(first, second):
-        first[...] = gwin[...].astype(bf16)
-        for j in range(width // channels):
-            at = slice(j * channels, (j + 1) * channels)
-            second[at, :] = gwout[:, at].astype(bf16)
+        for j in range(channels // LANES):
+            first[j * width : (j + 1) * width, :] = gwin[:, j * LANES : (j + 1) * LANES].astype(bf16)
+        for j in range(width // LANES):
+            second[j * channels : (j + 1) * channels, :] = gwout[
+                :, j * LANES : (j + 1) * LANES
+            ].astype(bf16)
 
     pl.when(core[0] == 0)(lambda: store(keep, send))
     pl.when(core[0] != 0)(lambda: store(send, keep))
@@ -270,7 +272,12 @@
         sums_ref[j : j + 1, :] = jnp.sum(sums[j], axis=0, keepdims=True)
 
 
-def kernel_grad_kernel(tile, top, bottom, left, right, d_depth, out, pad, d32, acc_ref):
+SMALL = 64
+
+
+def kernel_grad_kernel(
+    core, tile, top, bottom, left, right, d_depth, sums, gbin_a, gbin_b, keep, send, pad, d32, acc_ref
+):
     rows, cols, channels = tile.shape
     fill(pad, tile, top, bottom, left, right)
     d32[...] = d_depth[...].astype(f32)
@@ -293,8 +300,26 @@
                 acc_ref[slab, a * 7 + b] += acc[a]
 
     steps(rows, cols, channels, piece)
-    for slab in range(channels // LANES):
-        out[:, slab * LANES : (slab + 1) * LANES] = jnp.sum(acc_ref[slab], axis=1)
+
+    def store(first, second):
+        second[...] = jnp.zeros_like(second)
+        slabs = channels // LANES
+        for slab in range(slabs):
+            at = slice(slab * LANES, (slab + 1) * LANES)
+            part = [jnp.sum(acc_ref[slab], axis=1), sums[:5, at]]
+            for j in range((gbin_a.shape[1] + gbin_b.shape[1]) // channels):
+                lane = (j * slabs + slab) * LANES
+                source = gbin_a if lane < gbin_a.shape[1] else gbin_b
+                lane = lane if lane < gbin_a.shape[1] else lane - gbin_a.shape[1]
+                part.append(source[:, lane : lane + LANES])
+            part = jnp.concatenate(part)
+            part = jnp.concatenate([part, jnp.zeros((SMALL - part.shape[0], LANES), f32)])
+            first[slab * SMALL : (slab + 1) * SMALL, :] = part.astype(bf16)
+        rest = first.shape[0] - slabs * SMALL
+        first[slabs * SMALL :, :] = jnp.zeros((rest, LANES), bf16)
+
+    pl.when(core[0] == 0)(lambda: store(keep, send))
+    pl.when(core[0] != 0)(lambda: store(send, keep))
 
 
 def conv_grad_kernel(tile, top, bottom, left, right, kernel, cot, out, pad, total):
@@ -318,83 +343,203 @@
     lax.fori_loop(0, rows * cols // block, finish, 0)
 
 
-def call(body, outs, scratch, args, flops, scalars=0, size=24 << 20):
+def call(body, outs, scratch, args, flops, scalars=0, after=(), size=24 << 20):
+    held = len(args)
+
+    def kernel(*refs):
+        body(*refs[:held], *refs[held + len(after) :])
+
     vmem = pl.BlockSpec(memory_space=pltpu.VMEM)
     smem = pl.BlockSpec(memory_space=pltpu.SMEM)
     return pl.pallas_call(
-        body,
+        kernel,
         out_shape=[jax.ShapeDtypeStruct(shape, dtype) for shape, dtype in outs],
-        in_specs=[smem] * scalars + [vmem] * (len(args) - scalars),
+        in_specs=[smem] * scalars
+        + [vmem] * (held - scalars)
+        + [pl.BlockSpec(memory_space=pl.ANY)] * len(after),
         out_specs=[vmem] * len(outs),
         scratch_shapes=[pltpu.VMEM(shape, dtype) for shape, dtype in scratch],
         compiler_params=pltpu.CompilerParams(vmem_limit_bytes=size),
-        cost_estimate=pl.CostEstimate(flops=flops, bytes_accessed=1 << 20, transcendentals=0),
-    )(*args)
-
-
-def bits(count):
-    return max(count.bit_length() - 1, 0)
-
-
-def sum_plan():
-    plan = [("gy", 0)]
-    rest = [("gy", j) for j in range(1, bits(lax.axis_size("gy")))]
-    wide = [("gx", j) for j in range(bits(lax.axis_size("gx")))]
-    deep = [("rep", j) for j in range(bits(lax.axis_size("rep")))]
-    first = rest + wide + deep
-    second = wide + rest + deep
-    return [(plan[0], plan[0])] + list(zip(first, second))
-
-
-def exchange(x, choice):
+        cost_estimate=pl.CostEstimate(flops=flops, bytes_accessed=flops >> 10, transcendentals=0),
+    )(*args, *after)
+
+
+def bits(axis):
+    return [(axis, j) for j in range(max(lax.axis_size(axis).bit_length() - 1, 0))]
+
+
+def rounds():
+    rest = bits("gy")[2:] + bits("gx")[1:] + bits("rep")
+    return [[("gy", 1), ("gx", 0)]] + [rest[i : i + 2] for i in range(0, len(rest), 2)]
+
+
+def exchange(x, flips):
     sizes = [lax.axis_size(axis) for axis in AXES]
     perm = []
-    for i in range(sizes[0] * sizes[1] * sizes[2]):
+    for i in range(math.prod(sizes)):
         at = {"gy": i // (sizes[1] * sizes[2]), "gx": i // sizes[2] % sizes[1], "rep": i % sizes[2]}
-        axis, bit = choice[at["gy"] % 2]
-        at[axis] ^= 1 << bit
+        for axis, bit in flips:
+            at[axis] ^= 1 << bit
         perm.append((i, (at["gy"] * sizes[1] + at["gx"]) * sizes[2] + at["rep"]))
     return lax.ppermute(x, AXES, perm)
 
 
-def own_bit(choice):
-    core = lax.axis_index("gy") % 2
-    values = [lax.axis_index(axis) // (1 << bit) % 2 for axis, bit in choice]
-    return jnp.where(core == 0, values[0], values[1])
-
-
-def sum_scatter(keep, send):
-    plan = sum_plan()
-    x = (keep.astype(f32) + exchange(send, plan[0]).astype(f32)).astype(bf16)
-    for choice in plan[1:]:
-        bit = own_bit(choice)
-        halves = x.reshape(2, x.shape[0] // 2, x.shape[1])
-        keep = lax.dynamic_index_in_dim(halves, bit, 0, keepdims=False)
-        send = lax.dynamic_index_in_dim(halves, 1 - bit, 0, keepdims=False)
-        x = (keep.astype(f32) + exchange(send, choice).astype(f32)).astype(bf16)
-    return x
-
-
-def gather_back(x):
-    for choice in reversed(sum_plan()):
-        bit = own_bit(choice)
-        other = exchange(x, choice)
-        x = jnp.where(bit == 0, jnp.concatenate([x, other]), jnp.concatenate([other, x]))
-    return x
-
-
-def sum_small(x):
-    rows, channels = x.shape
-    groups = (("gy", "gx"), ("rep",))
-    counts = [math.prod(lax.axis_size(axis) for axis in group) for group in groups]
-    whole = -(-rows // math.prod(counts)) * math.prod(counts)
-    x = jnp.pad(x, ((0, whole - rows), (0, 0)))
-    for group, count in zip(groups, counts):
-        got = lax.all_to_all(x, group, 0, 0, tiled=True)
-        x = jnp.sum(got.reshape(count, -1, channels), axis=0)
-    for group, count in reversed(list(zip(groups, counts))):
-        x = lax.all_to_all(jnp.tile(x, (count, 1)), group, 0, 0, tiled=True)
-    return x[:rows]
+def others(group):
+    return [[g for j, g in enumerate(group) if delta >> j & 1] for delta in range(1, 1 << len(group))]
+
+
+def place(group):
+    value = 0
+    for j, (axis, bit) in enumerate(group):
+        value = value + (lax.axis_index(axis) // (1 << bit) % 2 << j)
+    return jnp.asarray(value, jnp.int32).reshape(1)
+
+
+def hold(arrays):
+    return lax.optimization_barrier(arrays)
+
+
+def chunks(rows, body):
+    size = max(n for n in (128, 64, 32, 16) if rows % n == 0)
+
+    def step(i, _):
+        body(pl.multiple_of(i * size, size), size)
+        return _
+
+    lax.fori_loop(0, rows // size, step, 0, unroll=2 if rows // size > 1 else 1)
+
+
+def first_sum_kernel(has_small, mine, *refs):
+    wide, outs = refs[:2], refs[4 if has_small else 2 :]
+    rows = wide[0].shape[0] // len(outs)
+    for delta, out in enumerate(outs):
+        to = mine[0] ^ delta
+
+        def add(at, size):
+            part = pl.ds(pl.multiple_of(to * rows + at, 16), size)
+            out[pl.ds(at, size), :] = (wide[0][part, :].astype(f32) + wide[1][part, :].astype(f32)).astype(bf16)
+
+        chunks(rows, add)
+        end = rows
+        if has_small:
+            small = refs[2:4]
+            size = small[0].shape[0] // len(outs)
+            part = pl.ds(pl.multiple_of(to * size, 16), size)
+            out[end : end + size, :] = (small[0][part, :].astype(f32) + small[1][part, :].astype(f32)).astype(bf16)
+            end += size
+        if end < out.shape[0]:
+            out[end:, :] = jnp.zeros((out.shape[0] - end, LANES), bf16)
+
+
+def next_sum_kernel(count, mine, *refs):
+    ins, outs = refs[:count], refs[count:]
+    rows = outs[0].shape[0]
+    for delta, out in enumerate(outs):
+        start = (mine[0] ^ delta) * rows if len(outs) > 1 else 0
+
+        def add(at, size):
+            part = pl.ds(pl.multiple_of(start + at, 16), size)
+            out[pl.ds(at, size), :] = sum(r[part, :].astype(f32) for r in ins).astype(bf16)
+
+        chunks(rows, add)
+
+
+def join_kernel(count, mine, *refs):
+    out = refs[count]
+    rows = refs[0].shape[0]
+    for delta, ref in enumerate(refs[:count]):
+        out[pl.ds(pl.multiple_of((mine[0] ^ delta) * rows, 16), rows), :] = ref[...]
+
+
+def part_rows(weights, small):
+    step = 16 * math.prod(1 << len(group) for group in rounds()[1:])
+    return -(-(weights + small) // step) * step
+
+
+SUM_FLOPS = 1 << 20
+
+
+def scatter_start(keep, other, small=(), after=()):
+    plan = rounds()
+    count = 1 << len(plan[0])
+    rows = part_rows(keep.shape[0] // count, small[0].shape[0] // count if small else 0)
+    return call(
+        functools.partial(first_sum_kernel, bool(small)),
+        [((rows, LANES), bf16)] * count,
+        [],
+        (place(plan[0]), keep, other, *small),
+        SUM_FLOPS,
+        1,
+        after,
+    )
+
+
+def transfers():
+    plan = rounds()
+    return [(group, True) for group in plan] + [(group, False) for group in reversed(plan)]
+
+
+def send_parts(parts, step):
+    group, scatters = transfers()[step]
+    if not scatters:
+        parts = [parts[0]] * (1 << len(group))
+    return [parts[0]] + [exchange(x, flips) for x, flips in zip(parts[1:], others(group))]
+
+
+def combine(got, step):
+    steps = transfers()
+    group, scatters = steps[step]
+    rows = got[0].shape[0]
+    if not scatters:
+        shapes = [((len(got) * rows, LANES), bf16)]
+        body, mine = join_kernel, place(group)
+    else:
+        following = steps[step + 1][0] if steps[step + 1][1] else []
+        count = 1 << len(following)
+        shapes = [((rows // count, LANES), bf16)] * count
+        body, mine = next_sum_kernel, place(following)
+    return call(functools.partial(body, len(got)), shapes, [], (mine, *got), SUM_FLOPS, 1)
+
+
+def finish_kernel(
+    factor, widths, core, own_a, other_a, own_b, other_b,
+    win, wout, gk, scale, b_out, gain, shift, bias, b_in,
+):
+    channels = wout.shape[0]
+
+    def store(firsts, seconds):
+        base = 0
+        for width, first, second in zip(widths, firsts, seconds):
+            part = first.shape[0] // 4
+            block = width * channels // LANES // 4
+
+            def rows(ref, at):
+                start = at // block * part + at % block
+                return ref[start : start + LANES, :].astype(f32) * factor
+
+            for j in range(channels // LANES):
+                for i in range(0, width, LANES):
+                    win[base + i : base + i + LANES, j * LANES : (j + 1) * LANES] = rows(first, j * width + i)
+            for j in range(width // LANES):
+                for i in range(0, channels, LANES):
+                    wout[i : i + LANES, base + j * LANES : base + (j + 1) * LANES] = rows(
+                        second, j * channels + i
+                    )
+            base += width
+        slabs = channels // LANES
+        for slab in range(slabs):
+            at = slice(slab * LANES, (slab + 1) * LANES)
+            start = slab * part + block
+            values = firsts[1][start : start + SMALL, :].astype(f32) * factor
+            gk[:, at] = values[:49]
+            for j, ref in enumerate((scale, b_out, gain, shift, bias)):
+                ref[:, at] = values[49 + j : 50 + j]
+            for j in range(b_in.shape[1] // channels):
+                lane = (j * slabs + slab) * LANES
+                b_in[:, lane : lane + LANES] = values[54 + j : 55 + j]
+
+    pl.when(core[0] == 0)(lambda: store((own_a, own_b), (other_a, other_b)))
+    pl.when(core[0] != 0)(lambda: store((other_a, other_b), (own_a, own_b)))
 
 
 def shards(
@@ -412,7 +557,6 @@
 ):
     _, rows, cols, channels = pages.shape
     hid = w_in.shape[0]
-    width = hid // 2
     pixels = rows * cols
     tile = pages.reshape(rows, cols, channels)
     page = pages.reshape(pixels, channels)
@@ -432,72 +576,98 @@
         (tile, *around, kernel, row(conv_bias), gain, shift),
         conv_flops,
     )
-    grads = [
+    grads = lambda width: [
         ((MLP_BLOCK, width), bf16),
         ((MLP_BLOCK, width), bf16),
         ((width, channels), f32),
         ((channels, width), f32),
         ((8, width), f32),
     ]
-    packed = ((width, channels), bf16)
-    core = (lax.axis_index("gy") % 2).astype(jnp.int32).reshape(1)
-    mlp_flops = 6 * pixels * channels * hid * 2
+    packed = lambda width: [((width * channels // LANES, LANES), bf16)] * 2 + [((1, width), f32)]
+    core_flip = [("gy", 0)]
+    core = place(core_flip)
+    mlp_flops = 12 * pixels * channels * hid
     weights = (w_in, w_out, row(b_in), scale)
+    first, second = hid * 2 // 3, hid // 3
     branch, d_norm, keep_a, send_a, gbin_a = call(
-        functools.partial(mlp_first_kernel, 0, width),
-        [(full, f32), (full, f32), packed, packed, ((1, width), f32)],
-        grads,
+        functools.partial(mlp_first_kernel, 0, first),
+        [(full, f32), (full, f32)] + packed(first),
+        grads(first),
         (core, ln_out, cot, *weights),
         mlp_flops,
         1,
     )
-    piece_a = sum_scatter(keep_a, send_a)
+    other_a = exchange(send_a, core_flip)
     result, d_depth, keep_b, send_b, gbin_b, sums = call(
-        functools.partial(mlp_second_kernel, width, width),
-        [(full, bf16), (full, bf16), packed, packed, ((1, width), f32), ((8, channels), f32)],
-        grads + [((8, 8, channels), f32)],
+        functools.partial(mlp_second_kernel, first, second),
+        [(full, bf16), (full, bf16)] + packed(second) + [((8, channels), f32)],
+        grads(second) + [((8, 8, channels), f32)],
         (core, ln_out, cot, *weights, row(b_out), gain, page, normed, inv, branch, d_norm),
         mlp_flops,
         1,
     )
-    piece_b = sum_scatter(keep_b, send_b)
     d_tile = d_depth.reshape(tile.shape)
-    d_around = halo(d_tile)
-    (g_kernel,) = call(
+    parts_a = scatter_start(keep_a, other_a, after=(d_depth,))
+    d_edge, parts_a, keep_b, send_b = hold((d_tile, parts_a, keep_b, send_b))
+    got_a = send_parts(parts_a, 0)
+    other_b = exchange(send_b, core_flip)
+    d_around = halo(d_edge)
+    small_rows = ((4 * SMALL, LANES), bf16)
+    keep_s, send_s = call(
         kernel_grad_kernel,
-        [((49, channels), f32)],
+        [small_rows, small_rows],
         [pad, (full, f32), ((channels // LANES, 49, 8, LANES), f32)],
-        (tile, *around, d_depth),
+        (core, tile, *around, d_depth, sums, gbin_a, gbin_b),
         conv_flops,
-    )
-    small = jnp.concatenate(
-        [g_kernel, sums[:5], gbin_a.reshape(-1, channels), gbin_b.reshape(-1, channels)]
-    )
+        1,
+        (parts_a[1],),
+    )
+    got_a, keep_s, send_s, other_b = hold((got_a, keep_s, send_s, other_b))
+    other_s = exchange(send_s, core_flip)
+    parts_a = combine(got_a, 0)
+    parts_b = scatter_start(keep_b, other_b, (keep_s, other_s))
+    got_a, got_b = send_parts(parts_a, 1), send_parts(parts_b, 0)
     (grad_pages,) = call(
         conv_grad_kernel,
         [(full, bf16)],
         [pad, (full, f32)],
         (d_tile, *d_around, kernel, cot),
         conv_flops,
-    )
+        0,
+        (parts_a[1], parts_b[1]),
+    )
+    got_a, got_b, grad_pages = hold((got_a, got_b, grad_pages))
+    last = len(transfers()) - 1
+    for step in range(1, last):
+        parts_a, parts_b = combine(got_a, step), combine(got_b, step - 1)
+        got_a, got_b = hold((send_parts(parts_a, step + 1), send_parts(parts_b, step)))
+    (half_a,), parts_b = combine(got_a, last), combine(got_b, last - 1)
+    got_a, got_b = hold(([half_a, exchange(half_a, core_flip)], send_parts(parts_b, last)))
+    (half_b,) = combine(got_b, last)
+    got_b = [half_b, exchange(half_b, core_flip)]
     factor = float(pixels * lax.axis_size("gy") * lax.axis_size("gx") * lax.axis_size("rep")) ** (-0.5)
-    small = sum_small(small) * factor
-    both = [gather_back(piece_a), gather_back(piece_b)]
-    sum_win = jnp.concatenate([g[:width] for g in both]).astype(f32) * factor
-    blocks = [g[width + j * channels : width + (j + 1) * channels] for g in both for j in range(width // channels)]
-    sum_wout = jnp.concatenate(blocks, axis=1).astype(f32) * factor
+    line = ((1, channels), f32)
+    win, wout, gk, g_scale, g_bout, g_gain, g_shift, g_bias, g_bin = call(
+        functools.partial(finish_kernel, factor, (first, second)),
+        [((hid, channels), f32), ((channels, hid), f32), ((49, channels), f32)] + [line] * 5 + [((1, hid), f32)],
+        [],
+        (core, *got_a, *got_b),
+        SUM_FLOPS,
+        1,
+    )
+    flat = lambda v: v.reshape(-1)
     return (
         result.reshape(pages.shape),
         grad_pages.reshape(pages.shape),
-        small[:49].reshape(7, 7, channels),
-        small[53],
-        small[51],
-        small[52],
-        sum_win,
-        small[54:].reshape(-1),
-        sum_wout,
-        small[50],
-        small[49],
+        gk.reshape(7, 7, channels),
+        flat(g_bias),
+        flat(g_gain),
+        flat(g_shift),
+        win,
+        flat(g_bin),
+        wout,
+        flat(g_bout),
+        flat(g_scale),
     )
 
 

time: 142 us -> 127 us (0.89)
  starting transfers between devices: 56.6 us -> 41.7 us
  local copies, waits for them, and re-layouts: 8.96 us -> 14.4 us
  waiting for transfers between devices: 28 us -> 22.8 us
  other arithmetic: 10.1 us -> 5.35 us
  Pallas kernels: 36.3 us -> 40.8 us
    all_to_all x4 -> x0, starting transfers between devices: 17.7 us -> none  [the longest x2 10.9 us: sum_small(): got = lax.all_to_all(x, group, 0, 0, tiled=True)]
    unnamed x32 -> x44, local copies, waits for them, and re-layouts: 2.62 us -> 12.5 us
    all_to_all x4 -> x0, waiting for transfers between devices: 9.15 us -> none  [the longest x2 9.14 us: sum_small(): got = lax.all_to_all(x, group, 0, 0, tiled=True)]
    ppermute x20 -> x29, starting transfers between devices: 29.6 us -> 35.6 us  [exchange(): return lax.ppermute(x, AXES, perm)]
    pallas_call x5 -> x16, Pallas kernels: 36.3 us -> 40.8 us  [call(): pl.pallas_call(kernel, out_shape=[jax.ShapeDtypeStruct(shape, dtype) for...]
    ppermute x20 -> x29, waiting for transfers between devices: 16.2 us -> 20.1 us  [exchange(): return lax.ppermute(x, AXES, perm)]
    ppermute x4, starting transfers between devices: 5.52 us -> 1.91 us  [edges(): out.append(lax.ppermute(jnp.where(is_high, high, low), axis, pairs))]
    pallas_call x2 -> x6, other arithmetic: 0.03 us -> 3.59 us  [call(): pl.pallas_call(kernel, out_shape=[jax.ShapeDtypeStruct(shape, dtype) for...]
  transfers between devices with their start and end apart: 30 -> 35, of which waited for: 10 -> 9; matrix products, arithmetic and copies ran while one was open for 7% -> 1% of each run, Pallas kernels for 5% -> 17%
where the time goes in v3:
time: 127 us; the launch traced here: 126 us
  starting transfers between devices  41.7 us (33%)
  Pallas kernels  40.8 us (32%)
  waiting for transfers between devices  22.8 us (18%)
  local copies, waits for them, and re-layouts  14.4 us (11%)
  other arithmetic  5.35 us (4%)
    pallas_call x16, Pallas kernels, call(): pl.pallas_call(kernel, out_shape=[jax.ShapeDtypeStruct(shape, dtype) for...  40.8 us
    ppermute x29, starting transfers between devices, exchange(): return lax.ppermute(x, AXES, perm)  35.6 us
    ppermute x29, waiting for transfers between devices, exchange(): return lax.ppermute(x, AXES, perm)  20.1 us
    unnamed x44, local copies, waits for them, and re-layouts  12.5 us
    ppermute x2, starting transfers between devices, halo(): lax.ppermute(jnp.where(is_high, column[:, 3:], column[:, :3]), 'gx', pairs)  4.19 us
    pallas_call x6, other arithmetic, call(): pl.pallas_call(kernel, out_shape=[jax.ShapeDtypeStruct(shape, dtype) for...  3.59 us
    ppermute x2, waiting for transfers between devices, halo(): lax.ppermute(jnp.where(is_high, column[:, 3:], column[:, :3]), 'gx', pairs)  2.68 us
  transfers between devices with their start and end apart: 35, of which 9 were waited for; matrix products, arithmetic and copies ran while one was open for 1% of the time, Pallas kernels for 17%

profile of v3, /device:TPU:0, one launch (start us, length us, event | category | flops | bytes accessed | tf_op | source)
XLA Modules:
  0.0 126.3 jit_solution(4257187380427357099)
XLA Ops:
  0.7 1.1 select_bitcast_fusion
  1.8 0.5 collective-permute-start.1
  2.3 0.7 collective-permute-start
  3.0 1.1 fusion.1
  4.4 2.6 %collective-permute-start.2 = (bf16[38,3,384]{2,1,0:T(4,128)(2,1)S(1)}, bf16[38,3,384]{2,1,0:T(4,128)(2,1)S(1)}, u32[]{:S(2)}, u32[]{:S(2)}) collective-permute-start(bf16[38,3,384]{2,1,0:T(4,128)(2,1)S(1)} %slice_select_fusion.1), channel_id=1, source_target_pairs={{0,4},{4,0},{1,5},{5,1},{2,6},{6,2},{3,7},{7,3},{8,12},{12,8},{9,1... | collective-permute-start | bytes 262664 | tf_op jit(solution)/shard_map/ppermute | solution.py:64
  7.1 2.7 %collective-permute-done.2 = bf16[38,3,384]{2,1,0:T(4,128)(2,1)S(1)} collective-permute-done((bf16[38,3,384]{2,1,0:T(4,128)(2,1)S(1)}, bf16[38,3,384]{2,1,0:T(4,128)(2,1)S(1)}, u32[]{:S(2)}, u32[]{:S(2)}) %collective-permute-start.2) | collective-permute-done | bytes 87584 | tf_op jit(solution)/shard_map/ppermute | solution.py:64
  10.0 7.6 %shard_map.194 = (f32[1024,384]{1,0:T(8,128)S(1)}, f32[1024,128]{1,0:T(8,128)S(1)}, bf16[1024,384]{1,0:T(8,128)(2,1)S(1)}) custom-call(bf16[32,32,384]{2,1,0:T(8,128)(2,1)S(1)} %bitcast.17, bf16[3,32,384]{2,1,0:T(8,128)(2,1)S(1)} %get-tuple-element.194.refs_1_.refs_2_, bf16[3,32,384]{2,1,0:T(8,128)(2,1)S(1)} %get-tuple-element.193.refs_2_.refs_3_, ...), custom_call_target="tpu_custom_call" | custom-call | flops 2312110080 | bytes 2257920 | tf_op jit(solution)/shard_map/pallas_call | solution.py:354
  17.5 1.1 copy-done.7
  18.7 9.1 %shard_map.195 = (f32[1024,384]{1,0:T(8,128)S(1)}, f32[1024,384]{1,0:T(8,128)S(1)}, bf16[3072,128]{1,0:T(8,128)(2,1)S(1)}, bf16[3072,128]{1,0:T(8,128)(2,1)}, f32[1,1024]{1,0:T(1,128)S(1)}) custom-call(s32[1]{0:T(128)} %bitcast.refs_0_, bf16[1024,384]{1,0:T(8,128)(2,1)S(1)} %get-tuple-element.97.refs_1_, bf16[1024,384]{1,0:T(8,128)(2,1)S(1)} %bitcast.20, ...), custom_call_target="tpu_custom_call" | custom-call | flops 7247757312 | bytes 7077888 | tf_op jit(solution)/shard_map/pallas_call | solution.py:354
  27.8 1.1 copy-done.11
  29.0 1.2 copy-done.13
  30.2 3.8 %collective-permute-start.3 = (bf16[3072,128]{1,0:T(8,128)(2,1)}, bf16[3072,128]{1,0:T(8,128)(2,1)S(1)}, u32[]{:S(2)}, u32[]{:S(2)}) collective-permute-start(bf16[3072,128]{1,0:T(8,128)(2,1)} %get-tuple-element.105), channel_id=1, source_target_pairs={{0,8},{1,9},{2,10},{3,11},{4,12},{5,13},{6,14},{7,15},{8,0},{9,1},... | collective-permute-start | bytes 2359304 | tf_op jit(solution)/shard_map/ppermute | solution.py:384
  33.9 1.3 %copy-done.2 = bf16[1536,384]{1,0:T(8,128)(2,1)S(1)} copy-done((bf16[1536,384]{1,0:T(8,128)(2,1)S(1)}, bf16[1536,384]{1,0:T(8,128)(2,1)}, u32[]{:S(2)}) %copy-start.2) | copy-done | bytes 1179672
  35.2 1.3 %copy-done.4 = bf16[384,1536]{1,0:T(8,128)(2,1)S(1)} copy-done((bf16[384,1536]{1,0:T(8,128)(2,1)S(1)}, bf16[384,1536]{1,0:T(8,128)(2,1)}, u32[]{:S(2)}) %copy-start.4) | copy-done | bytes 1179672
  36.5 1.1 copy-done.6
  37.6 1.4 %copy-done.8 = f32[1024,384]{1,0:T(8,128)S(1)} copy-done((f32[1024,384]{1,0:T(8,128)S(1)}, f32[1024,384]{1,0:T(8,128)}, u32[]{:S(2)}) %copy-start.8) | copy-done | bytes 1572888
  39.0 1.1 copy-done.10
  40.1 1.4 %copy-done.12 = f32[1024,384]{1,0:T(8,128)S(1)} copy-done((f32[1024,384]{1,0:T(8,128)S(1)}, f32[1024,384]{1,0:T(8,128)}, u32[]{:S(2)}) %copy-start.12) | copy-done | bytes 1572888
  41.6 1.4 %copy-done.14 = f32[1024,384]{1,0:T(8,128)S(1)} copy-done((f32[1024,384]{1,0:T(8,128)S(1)}, f32[1024,384]{1,0:T(8,128)}, u32[]{:S(2)}) %copy-start.14) | copy-done | bytes 1572888
  43.0 6.9 %shard_map.196 = (bf16[1024,384]{1,0:T(8,128)(2,1)}, bf16[1024,384]{1,0:T(8,128)(2,1)S(1)}, bf16[1536,128]{1,0:T(8,128)(2,1)S(1)}, bf16[1536,128]{1,0:T(8,128)(2...) custom-call(s32[1]{0:T(128)} %bitcast.refs_0_, bf16[1024,384]{1,0:T(8,128)(2,1)S(1)} %copy-done.10, ...), custom_call_target="tpu_custom_call" | custom-call | flops 7247757312 | bytes 7077888 | tf_op jit(solution)/shard_map/pallas_call | solution.py:354
  49.8 0.3 shard_map.197
  50.2 0.7 collective-permute-start.15
  51.0 1.8 %collective-permute-start.5 = (bf16[768,128]{1,0:T(8,128)(2,1)S(1)}, bf16[768,128]{1,0:T(8,128)(2,1)S(1)}, u32[]{:S(2)}, u32[]{:S(2)}) collective-permute-start(bf16[768,128]{1,0:T(8,128)(2,1)S(1)} %get-tuple-element.114), channel_id=1, source_target_pairs={{0,4},{1,5},{2,6},{3,7},{4,0},{5,1},{6,2},{7,3},{8,12},{9,13},{10,... | collective-permute-start | bytes 589832 | tf_op jit(solution)/shard_map/ppermute | solution.py:384
  52.8 3.5 %collective-permute-start.6 = (bf16[768,128]{1,0:T(8,128)(2,1)S(1)}, bf16[768,128]{1,0:T(8,128)(2,1)S(1)}, u32[]{:S(2)}, u32[]{:S(2)}) collective-permute-start(bf16[768,128]{1,0:T(8,128)(2,1)S(1)} %get-tuple-element.115), channel_id=1, source_target_pairs={{0,20},{1,21},{2,22},{3,23},{4,16},{5,17},{6,18},{7,19},{8,28},{9,... | collective-permute-start | bytes 589832 | tf_op jit(solution)/shard_map/ppermute | solution.py:384
  56.4 1.2 collective-permute-start.7
  57.9 1.6 %collective-permute-start.17 = (bf16[38,3,384]{2,1,0:T(4,128)(2,1)S(1)}, bf16[38,3,384]{2,1,0:T(4,128)(2,1)S(1)}, u32[]{:S(2)}, u32[]{:S(2)}) collective-permute-start(bf16[38,3,384]{2,1,0:T(4,128)(2,1)S(1)} %slice_select_fusion), channel_id=1, source_target_pairs={{0,4},{4,0},{1,5},{5,1},{2,6},{6,2},{3,7},{7,3},{8,12},{12,8},{9,1... | collective-permute-start | bytes 262664 | tf_op jit(solution)/shard_map/ppermute | solution.py:64
  59.5 6.8 %shard_map.198 = (bf16[256,128]{1,0:T(8,128)(2,1)S(1)}, bf16[256,128]{1,0:T(8,128)(2,1)S(1)}) custom-call(s32[1]{0:T(128)} %bitcast.refs_0_, bf16[32,32,384]{2,1,0:T(8,128)(2,1)S(1)} %bitcast.19, bf16[3,32,384]{2,1,0:T(8,128)(2,1)S(1)} %get-tuple-element.194.refs_1_.refs_2_, bf16[3,32,384]{2,1,0:T(8,128)(2,1)S(1)} %get-tuple-element.193.refs_2_.refs_3_, ...), custom_call_target="tpu_custom_call" | custom-call | flops 2312110080 | bytes 2257920 | tf_op jit(solution)/shard_map/pallas_call | solution.py:354
  66.5 2.7 %collective-permute-start.9 = (bf16[192,128]{1,0:T(8,128)(2,1)S(1)}, bf16[192,128]{1,0:T(8,128)(2,1)S(1)}, u32[]{:S(2)}, u32[]{:S(2)}) collective-permute-start(bf16[192,128]{1,0:T(8,128)(2,1)S(1)} %get-tuple-element.128), channel_id=1, source_target_pairs={{0,2},{1,3},{2,0},{3,1},{4,6},{5,7},{6,4},{7,5},{8,10},{9,11},{10,... | collective-permute-start | bytes 147464 | tf_op jit(solution)/shard_map/ppermute | solution.py:384
  69.2 1.4 %collective-permute-start.10 = (bf16[192,128]{1,0:T(8,128)(2,1)S(1)}, bf16[192,128]{1,0:T(8,128)(2,1)S(1)}, u32[]{:S(2)}, u32[]{:S(2)}) collective-permute-start(bf16[192,128]{1,0:T(8,128)(2,1)S(1)} %get-tuple-element.129), channel_id=1, source_target_pairs={{0,3},{1,2},{2,1},{3,0},{4,7},{5,6},{6,5},{7,4},{8,11},{9,10},{10,... | collective-permute-start | bytes 147464 | tf_op jit(solution)/shard_map/ppermute | solution.py:384
  70.6 0.3 collective-permute-start.8
  71.1 0.6 collective-permute-start.13
  71.6 2.1 %collective-permute-start.14 = (bf16[448,128]{1,0:T(8,128)(2,1)S(1)}, bf16[448,128]{1,0:T(8,128)(2,1)S(1)}, u32[]{:S(2)}, u32[]{:S(2)}) collective-permute-start(bf16[448,128]{1,0:T(8,128)(2,1)S(1)} %get-tuple-element.137), channel_id=1, source_target_pairs={{0,20},{1,21},{2,22},{3,23},{4,16},{5,17},{6,18},{7,19},{8,28},{9,... | collective-permute-start | bytes 344072 | tf_op jit(solution)/shard_map/ppermute | solution.py:384
  73.8 0.8 collective-permute-start.12
  74.6 6.9 %shard_map.201 = bf16[1024,384]{1,0:T(8,128)(2,1)} custom-call(bf16[32,32,384]{2,1,0:T(8,128)(2,1)S(1)} %bitcast.15, bf16[3,32,384]{2,1,0:T(8,128)(2,1)S(1)} %get-tuple-element.192.refs_1_, bf16[3,32,384]{2,1,0:T(8,128)(2,1)S(1)} %get-tuple-element.191.refs_2_, bf16[38,3,384]{2,1,0:T(4,128)(2,1)S(1)} %get-tuple-element.196.refs_3_, ...), custom_call_target="tpu_custom_call" | custom-call | flops 2312110080 | bytes 2257920 | tf_op jit(solution)/shard_map/pallas_call | solution.py:354
  81.6 0.2 shard_map.203
  81.7 1.8 %collective-permute-start.21 = (bf16[112,128]{1,0:T(8,128)(2,1)S(1)}, bf16[112,128]{1,0:T(8,128)(2,1)S(1)}, u32[]{:S(2)}, u32[]{:S(2)}) collective-permute-start(bf16[112,128]{1,0:T(8,128)(2,1)S(1)} %get-tuple-element.149), channel_id=1, source_target_pairs={{0,1},{1,0},{2,3},{3,2},{4,5},{5,4},{6,7},{7,6},{8,9},{9,8},{10,11... | collective-permute-start | bytes 86024 | tf_op jit(solution)/shard_map/ppermute | solution.py:384
  83.5 2.5 %collective-permute-start.20 = (bf16[192,128]{1,0:T(8,128)(2,1)S(1)}, bf16[192,128]{1,0:T(8,128)(2,1)S(1)}, u32[]{:S(2)}, u32[]{:S(2)}) collective-permute-start(bf16[192,128]{1,0:T(8,128)(2,1)S(1)} %shard_map.202.refs_1_), channel_id=1, source_target_pairs={{0,3},{1,2},{2,1},{3,0},{4,7},{5,6},{6,5},{7,4},{8,11},{9,10},{10,... | collective-permute-start | bytes 147464 | tf_op jit(solution)/shard_map/ppermute | solution.py:384
  86.1 0.1 collective-permute-start.19
  86.2 1.8 %collective-permute-start.18 = (bf16[192,128]{1,0:T(8,128)(2,1)S(1)}, bf16[192,128]{1,0:T(8,128)(2,1)S(1)}, u32[]{:S(2)}, u32[]{:S(2)}) collective-permute-start(bf16[192,128]{1,0:T(8,128)(2,1)S(1)} %shard_map.202.refs_1_), channel_id=1, source_target_pairs={{0,1},{1,0},{2,3},{3,2},{4,5},{5,4},{6,7},{7,6},{8,9},{9,8},{10,11... | collective-permute-start | bytes 147464 | tf_op jit(solution)/shard_map/ppermute | solution.py:384
  88.0 1.6 %collective-permute-start.22 = (bf16[112,128]{1,0:T(8,128)(2,1)S(1)}, bf16[112,128]{1,0:T(8,128)(2,1)S(1)}, u32[]{:S(2)}, u32[]{:S(2)}) collective-permute-start(bf16[112,128]{1,0:T(8,128)(2,1)S(1)} %get-tuple-element.150), channel_id=1, source_target_pairs={{0,2},{1,3},{2,0},{3,1},{4,6},{5,7},{6,4},{7,5},{8,10},{9,11},{10,... | collective-permute-start | bytes 86024 | tf_op jit(solution)/shard_map/ppermute | solution.py:384
  89.6 1.0 collective-permute-start.23
  90.6 2.5 %collective-permute-done.22.refs_3_ = bf16[112,128]{1,0:T(8,128)(2,1)S(1)} collective-permute-done((bf16[112,128]{1,0:T(8,128)(2,1)S(1)}, bf16[112,128]{1,0:T(8,128)(2,1)S(1)}, u32[]{:S(2)}, u32[]{:S(2)}) %collective-permute-start.22) | collective-permute-done | bytes 28704 | tf_op jit(solution)/shard_map/ppermute | solution.py:384
  93.1 2.2 %collective-permute-done.23.refs_4_ = bf16[112,128]{1,0:T(8,128)(2,1)S(1)} collective-permute-done((bf16[112,128]{1,0:T(8,128)(2,1)S(1)}, bf16[112,128]{1,0:T(8,128)(2,1)S(1)}, u32[]{:S(2)}, u32[]{:S(2)}) %collective-permute-start.23) | collective-permute-done | bytes 28704 | tf_op jit(solution)/shard_map/ppermute | solution.py:384
  95.4 1.0 collective-permute-start.26
  96.3 1.4 %collective-permute-start.25 = (bf16[768,128]{1,0:T(8,128)(2,1)S(1)}, bf16[768,128]{1,0:T(8,128)(2,1)S(1)}, u32[]{:S(2)}, u32[]{:S(2)}) collective-permute-start(bf16[768,128]{1,0:T(8,128)(2,1)S(1)} %shard_map.204.refs_1_), channel_id=1, source_target_pairs={{0,4},{1,5},{2,6},{3,7},{4,0},{5,1},{6,2},{7,3},{8,12},{9,13},{10,... | collective-permute-start | bytes 589832 | tf_op jit(solution)/shard_map/ppermute | solution.py:384
  97.7 1.2 collective-permute-start.24
  98.9 1.0 collective-permute-start.29
  100.1 4.6 %collective-permute-done.29.refs_4_ = bf16[112,128]{1,0:T(8,128)(2,1)S(1)} collective-permute-done((bf16[112,128]{1,0:T(8,128)(2,1)S(1)}, bf16[112,128]{1,0:T(8,128)(2,1)S(1)}, u32[]{:S(2)}, u32[]{:S(2)}) %collective-permute-start.29) | collective-permute-done | bytes 28704 | tf_op jit(solution)/shard_map/ppermute | solution.py:384
  104.7 0.6 collective-permute-done.28.refs_3_
  105.3 3.3 %collective-permute-done.27.refs_2_ = bf16[112,128]{1,0:T(8,128)(2,1)S(1)} collective-permute-done((bf16[112,128]{1,0:T(8,128)(2,1)S(1)}, bf16[112,128]{1,0:T(8,128)(2,1)S(1)}, u32[]{:S(2)}, u32[]{:S(2)}) %collective-permute-start.27) | collective-permute-done | bytes 28704 | tf_op jit(solution)/shard_map/ppermute | solution.py:384
  108.8 0.9 collective-permute-start.33
  109.7 1.4 %collective-permute-start.32 = (bf16[448,128]{1,0:T(8,128)(2,1)S(1)}, bf16[448,128]{1,0:T(8,128)(2,1)S(1)}, u32[]{:S(2)}, u32[]{:S(2)}) collective-permute-start(bf16[448,128]{1,0:T(8,128)(2,1)S(1)} %shard_map.207.refs_1_), channel_id=1, source_target_pairs={{0,4},{1,5},{2,6},{3,7},{4,0},{5,1},{6,2},{7,3},{8,12},{9,13},{10,... | collective-permute-start | bytes 344072 | tf_op jit(solution)/shard_map/ppermute | solution.py:384
  111.1 1.2 collective-permute-start.31
  112.3 3.4 %collective-permute-done.33.refs_4_ = bf16[448,128]{1,0:T(8,128)(2,1)S(1)} collective-permute-done((bf16[448,128]{1,0:T(8,128)(2,1)S(1)}, bf16[448,128]{1,0:T(8,128)(2,1)S(1)}, u32[]{:S(2)}, u32[]{:S(2)}) %collective-permute-start.33) | collective-permute-done | bytes 114720 | tf_op jit(solution)/shard_map/ppermute | solution.py:384
  115.7 1.7 %collective-permute-done.32.refs_3_ = bf16[448,128]{1,0:T(8,128)(2,1)S(1)} collective-permute-done((bf16[448,128]{1,0:T(8,128)(2,1)S(1)}, bf16[448,128]{1,0:T(8,128)(2,1)S(1)}, u32[]{:S(2)}, u32[]{:S(2)}) %collective-permute-start.32) | collective-permute-done | bytes 114720 | tf_op jit(solution)/shard_map/ppermute | solution.py:384
  117.5 1.8 %collective-permute-done.34.refs_4_ = bf16[1792,128]{1,0:T(8,128)(2,1)S(1)} collective-permute-done((bf16[1792,128]{1,0:T(8,128)(2,1)S(1)}, bf16[1792,128]{1,0:T(8,128)(2,1)S(1)}, u32[]{:S(2)}, u32[]{:S(2)}) %collective-permute-start.34) | collective-permute-done | bytes 458784 | tf_op jit(solution)/shard_map/ppermute | solution.py:384
  119.3 2.7 %shard_map.209 = (f32[1536,384]{1,0:T(8,128)}, f32[384,1536]{1,0:T(8,128)}, f32[49,384]{1,0:T(8,128)S(1)}, f32[1,384]{1,0:T(1,128)S(1)}, f32[1,384]{1,0:T(1,128)...) custom-call(s32[1]{0:T(128)} %bitcast.refs_0_, ...), custom_call_target="tpu_custom_call" | custom-call | flops 1048576 | bytes 1024 | tf_op jit(solution)/shard_map/pallas_call | solution.py:354
  122.0 0.6 reshape.119
  122.7 0.6 reduce
  123.3 0.6 reduce.1
  123.9 0.6 reduce.2
  124.5 0.6 reduce.4
  125.1 0.6 reduce.5
  125.7 0.6 reduce.3
  (95 shorter events, 1.8 us)
Async XLA Ops:
  0.6 9.3 %copy-start = (bf16[1,32,32,384]{3,2,1,0:T(8,128)(2,1)S(1)}, bf16[1,32,32,384]{3,2,1,0:T(8,128)(2,1)}, u32[]{:S(2)}) copy-start(bf16[1,32,32,384]{3,2,1,0:T(8,128)(2,1)} %param.11) | copy-start | bytes 2359300
  0.7 6.4 %copy-start.17 = (f32[384]{0:T(512)S(1)}, f32[384]{0:T(512)}, u32[]{:S(2)}) copy-start(f32[384]{0:T(512)} %param.15) | copy-start | bytes 4612
  0.7 6.4 %copy-start.18 = (f32[384]{0:T(512)S(1)}, f32[384]{0:T(512)}, u32[]{:S(2)}) copy-start(f32[384]{0:T(512)} %param.21) | copy-start | bytes 4612
  0.7 6.4 %copy-start.19 = (f32[384]{0:T(512)S(1)}, f32[384]{0:T(512)}, u32[]{:S(2)}) copy-start(f32[384]{0:T(512)} %param.14) | copy-start | bytes 4612
  0.7 6.4 %copy-start.20 = (f32[384]{0:T(512)S(1)}, f32[384]{0:T(512)}, u32[]{:S(2)}) copy-start(f32[384]{0:T(512)} %param.16) | copy-start | bytes 4612
  0.7 6.4 %copy-start.16 = (f32[1536]{0:T(1024)S(1)}, f32[1536]{0:T(1024)}, u32[]{:S(2)}) copy-start(f32[1536]{0:T(1024)} %param.18) | copy-start | bytes 18436
  0.7 6.4 %copy-start.15 = (f32[7,7,384]{2,1,0:T(8,128)S(1)}, f32[7,7,384]{2,1,0:T(8,128)}, u32[]{:S(2)}) copy-start(f32[7,7,384]{2,1,0:T(8,128)} %param.13) | copy-start | bytes 225796
  1.8 2.3 %collective-permute-start.1 = (bf16[3,32,384]{2,1,0:T(8,128)(2,1)S(1)}, bf16[3,32,384]{2,1,0:T(8,128)(2,1)S(1)}, u32[]{:S(2)}, u32[]{:S(2)}) collective-permute-start(bf16[3,32,384]{2,1,0:T(8,128)(2,1)S(1)} %get-tuple-element.189), channel_id=1, source_target_pairs={{0,8},{16,24},{8,0},{24,16},{1,9},{17,25},{9,1},{25,17},{2,10},{18... | collective-permute-start | bytes 221192 | tf_op jit(solution)/shard_map/ppermute | solution.py:46
  2.3 1.8 %collective-permute-start = (bf16[3,32,384]{2,1,0:T(8,128)(2,1)S(1)}, bf16[3,32,384]{2,1,0:T(8,128)(2,1)S(1)}, u32[]{:S(2)}, u32[]{:S(2)}) collective-permute-start(bf16[3,32,384]{2,1,0:T(8,128)(2,1)S(1)} %get-tuple-element.190), channel_id=1, source_target_pairs={{8,16},{16,8},{9,17},{17,9},{10,18},{18,10},{11,19},{19,11},{12,20... | collective-permute-start | bytes 221192 | tf_op jit(solution)/shard_map/ppermute | solution.py:46
  4.4 5.4 %collective-permute-start.2 = (bf16[38,3,384]{2,1,0:T(4,128)(2,1)S(1)}, bf16[38,3,384]{2,1,0:T(4,128)(2,1)S(1)}, u32[]{:S(2)}, u32[]{:S(2)}) collective-permute-start(bf16[38,3,384]{2,1,0:T(4,128)(2,1)S(1)} %slice_select_fusion.1), channel_id=1, source_target_pairs={{0,4},{4,0},{1,5},{5,1},{2,6},{6,2},{3,7},{7,3},{8,12},{12,8},{9,1... | collective-permute-start | bytes 262664 | tf_op jit(solution)/shard_map/ppermute | solution.py:64
  9.9 8.8 %copy-start.1 = (bf16[1536,384]{1,0:T(8,128)(2,1)S(1)}, bf16[1536,384]{1,0:T(8,128)(2,1)}, u32[]{:S(2)}) copy-start(bf16[1536,384]{1,0:T(8,128)(2,1)} %refs_3_.3) | copy-start | bytes 3538948
  9.9 8.8 %copy-start.3 = (bf16[384,1536]{1,0:T(8,128)(2,1)S(1)}, bf16[384,1536]{1,0:T(8,128)(2,1)}, u32[]{:S(2)}) copy-start(bf16[384,1536]{1,0:T(8,128)(2,1)} %refs_4_.3) | copy-start | bytes 3538948
  9.9 8.7 %copy-start.5 = (bf16[1,32,32,384]{3,2,1,0:T(8,128)(2,1)S(1)}, bf16[1,32,32,384]{3,2,1,0:T(8,128)(2,1)}, u32[]{:S(2)}) copy-start(bf16[1,32,32,384]{3,2,1,0:T(8,128)(2,1)} %param.12) | copy-start | bytes 2359300
  17.5 1.1 copy-start.7
  18.7 9.2 %copy-start.9 = (bf16[1024,384]{1,0:T(8,128)(2,1)}, bf16[1024,384]{1,0:T(8,128)(2,1)S(1)}, u32[]{:S(2)}) copy-start(bf16[1024,384]{1,0:T(8,128)(2,1)S(1)} %get-tuple-element.97.refs_1_) | copy-start | bytes 2359300
  18.7 15.2 %copy-start.21 = (f32[384]{0:T(512)S(1)}, f32[384]{0:T(512)}, u32[]{:S(2)}) copy-start(f32[384]{0:T(512)} %param.20) | copy-start | bytes 4612
  27.8 1.1 copy-start.11
  29.0 1.2 copy-start.13
  30.2 19.7 %collective-permute-start.3 = (bf16[3072,128]{1,0:T(8,128)(2,1)}, bf16[3072,128]{1,0:T(8,128)(2,1)S(1)}, u32[]{:S(2)}, u32[]{:S(2)}) collective-permute-start(bf16[3072,128]{1,0:T(8,128)(2,1)} %get-tuple-element.105), channel_id=1, source_target_pairs={{0,8},{1,9},{2,10},{3,11},{4,12},{5,13},{6,14},{7,15},{8,0},{9,1},... | collective-permute-start | bytes 2359304 | tf_op jit(solution)/shard_map/ppermute | solution.py:384
  33.9 1.3 %copy-start.2 = (bf16[1536,384]{1,0:T(8,128)(2,1)S(1)}, bf16[1536,384]{1,0:T(8,128)(2,1)}, u32[]{:S(2)}) copy-start(bf16[1536,384]{1,0:T(8,128)(2,1)} %refs_3_.3) | copy-start | bytes 3538948
  35.2 1.3 %copy-start.4 = (bf16[384,1536]{1,0:T(8,128)(2,1)S(1)}, bf16[384,1536]{1,0:T(8,128)(2,1)}, u32[]{:S(2)}) copy-start(bf16[384,1536]{1,0:T(8,128)(2,1)} %refs_4_.3) | copy-start | bytes 3538948
  36.5 1.1 copy-start.6
  37.6 1.4 %copy-start.8 = (f32[1024,384]{1,0:T(8,128)S(1)}, f32[1024,384]{1,0:T(8,128)}, u32[]{:S(2)}) copy-start(f32[1024,384]{1,0:T(8,128)} %copy-done.7) | copy-start | bytes 4718596
  39.0 1.1 copy-start.10
  40.1 1.4 %copy-start.12 = (f32[1024,384]{1,0:T(8,128)S(1)}, f32[1024,384]{1,0:T(8,128)}, u32[]{:S(2)}) copy-start(f32[1024,384]{1,0:T(8,128)} %copy-done.11) | copy-start | bytes 4718596
  41.6 1.4 %copy-start.14 = (f32[1024,384]{1,0:T(8,128)S(1)}, f32[1024,384]{1,0:T(8,128)}, u32[]{:S(2)}) copy-start(f32[1024,384]{1,0:T(8,128)} %copy-done.13) | copy-start | bytes 4718596
  50.1 6.3 %collective-permute-start.16 = (bf16[3,32,384]{2,1,0:T(8,128)(2,1)S(1)}, bf16[3,32,384]{2,1,0:T(8,128)(2,1)S(1)}, u32[]{:S(2)}, u32[]{:S(2)}) collective-permute-start(bf16[3,32,384]{2,1,0:T(8,128)(2,1)S(1)} %get-tuple-element.185), channel_id=1, source_target_pairs={{0,8},{16,24},{8,0},{24,16},{1,9},{17,25},{9,1},{25,17},{2,10},{18... | collective-permute-start | bytes 221192 | tf_op jit(solution)/shard_map/ppermute | solution.py:46
  50.2 7.4 %collective-permute-start.15 = (bf16[3,32,384]{2,1,0:T(8,128)(2,1)S(1)}, bf16[3,32,384]{2,1,0:T(8,128)(2,1)S(1)}, u32[]{:S(2)}, u32[]{:S(2)}) collective-permute-start(bf16[3,32,384]{2,1,0:T(8,128)(2,1)S(1)} %get-tuple-element.186), channel_id=1, source_target_pairs={{8,16},{16,8},{9,17},{17,9},{10,18},{18,10},{11,19},{19,11},{12,20... | collective-permute-start | bytes 221192 | tf_op jit(solution)/shard_map/ppermute | solution.py:46
  51.0 15.3 %collective-permute-start.5 = (bf16[768,128]{1,0:T(8,128)(2,1)S(1)}, bf16[768,128]{1,0:T(8,128)(2,1)S(1)}, u32[]{:S(2)}, u32[]{:S(2)}) collective-permute-start(bf16[768,128]{1,0:T(8,128)(2,1)S(1)} %get-tuple-element.114), channel_id=1, source_target_pairs={{0,4},{1,5},{2,6},{3,7},{4,0},{5,1},{6,2},{7,3},{8,12},{9,13},{10,... | collective-permute-start | bytes 589832 | tf_op jit(solution)/shard_map/ppermute | solution.py:384
  52.8 13.5 %collective-permute-start.6 = (bf16[768,128]{1,0:T(8,128)(2,1)S(1)}, bf16[768,128]{1,0:T(8,128)(2,1)S(1)}, u32[]{:S(2)}, u32[]{:S(2)}) collective-permute-start(bf16[768,128]{1,0:T(8,128)(2,1)S(1)} %get-tuple-element.115), channel_id=1, source_target_pairs={{0,20},{1,21},{2,22},{3,23},{4,16},{5,17},{6,18},{7,19},{8,28},{9,... | collective-permute-start | bytes 589832 | tf_op jit(solution)/shard_map/ppermute | solution.py:384
  56.3 10.0 %collective-permute-start.4 = (bf16[768,128]{1,0:T(8,128)(2,1)S(1)}, bf16[768,128]{1,0:T(8,128)(2,1)S(1)}, u32[]{:S(2)}, u32[]{:S(2)}) collective-permute-start(bf16[768,128]{1,0:T(8,128)(2,1)S(1)} %get-tuple-element.113.refs_10_), channel_id=1, source_target_pairs={{0,16},{1,17},{2,18},{3,19},{4,20},{5,21},{6,22},{7,23},{8,24},{9,... | collective-permute-start | bytes 589832 | tf_op jit(solution)/shard_map/ppermute | solution.py:384
  56.4 10.0 %collective-permute-start.7 = (bf16[1536,128]{1,0:T(8,128)(2,1)S(1)}, bf16[1536,128]{1,0:T(8,128)(2,1)S(1)}, u32[]{:S(2)}, u32[]{:S(2)}) collective-permute-start(bf16[1536,128]{1,0:T(8,128)(2,1)S(1)} %get-tuple-element.121), channel_id=1, source_target_pairs={{0,8},{1,9},{2,10},{3,11},{4,12},{5,13},{6,14},{7,15},{8,0},{9,1},... | collective-permute-start | bytes 1179656 | tf_op jit(solution)/shard_map/ppermute | solution.py:384
  57.9 11.2 %collective-permute-start.17 = (bf16[38,3,384]{2,1,0:T(4,128)(2,1)S(1)}, bf16[38,3,384]{2,1,0:T(4,128)(2,1)S(1)}, u32[]{:S(2)}, u32[]{:S(2)}) collective-permute-start(bf16[38,3,384]{2,1,0:T(4,128)(2,1)S(1)} %slice_select_fusion), channel_id=1, source_target_pairs={{0,4},{4,0},{1,5},{5,1},{2,6},{6,2},{3,7},{7,3},{8,12},{12,8},{9,1... | collective-permute-start | bytes 262664 | tf_op jit(solution)/shard_map/ppermute | solution.py:64
  66.5 7.3 %collective-permute-start.9 = (bf16[192,128]{1,0:T(8,128)(2,1)S(1)}, bf16[192,128]{1,0:T(8,128)(2,1)S(1)}, u32[]{:S(2)}, u32[]{:S(2)}) collective-permute-start(bf16[192,128]{1,0:T(8,128)(2,1)S(1)} %get-tuple-element.128), channel_id=1, source_target_pairs={{0,2},{1,3},{2,0},{3,1},{4,6},{5,7},{6,4},{7,5},{8,10},{9,11},{10,... | collective-permute-start | bytes 147464 | tf_op jit(solution)/shard_map/ppermute | solution.py:384
  69.1 1.8 %collective-permute-start.11 = (bf16[256,128]{1,0:T(8,128)(2,1)S(1)}, bf16[256,128]{1,0:T(8,128)(2,1)S(1)}, u32[]{:S(2)}, u32[]{:S(2)}) collective-permute-start(bf16[256,128]{1,0:T(8,128)(2,1)S(1)} %get-tuple-element.133), channel_id=1, source_target_pairs={{0,8},{1,9},{2,10},{3,11},{4,12},{5,13},{6,14},{7,15},{8,0},{9,1},... | collective-permute-start | bytes 196616 | tf_op jit(solution)/shard_map/ppermute | solution.py:384
  69.2 12.3 %collective-permute-start.10 = (bf16[192,128]{1,0:T(8,128)(2,1)S(1)}, bf16[192,128]{1,0:T(8,128)(2,1)S(1)}, u32[]{:S(2)}, u32[]{:S(2)}) collective-permute-start(bf16[192,128]{1,0:T(8,128)(2,1)S(1)} %get-tuple-element.129), channel_id=1, source_target_pairs={{0,3},{1,2},{2,1},{3,0},{4,7},{5,6},{6,5},{7,4},{8,11},{9,10},{10,... | collective-permute-start | bytes 147464 | tf_op jit(solution)/shard_map/ppermute | solution.py:384
  70.6 10.9 %collective-permute-start.8 = (bf16[192,128]{1,0:T(8,128)(2,1)S(1)}, bf16[192,128]{1,0:T(8,128)(2,1)S(1)}, u32[]{:S(2)}, u32[]{:S(2)}) collective-permute-start(bf16[192,128]{1,0:T(8,128)(2,1)S(1)} %get-tuple-element.127.refs_7_), channel_id=1, source_target_pairs={{0,1},{1,0},{2,3},{3,2},{4,5},{5,4},{6,7},{7,6},{8,9},{9,8},{10,11... | collective-permute-start | bytes 147464 | tf_op jit(solution)/shard_map/ppermute | solution.py:384
  71.1 10.5 %collective-permute-start.13 = (bf16[448,128]{1,0:T(8,128)(2,1)S(1)}, bf16[448,128]{1,0:T(8,128)(2,1)S(1)}, u32[]{:S(2)}, u32[]{:S(2)}) collective-permute-start(bf16[448,128]{1,0:T(8,128)(2,1)S(1)} %get-tuple-element.136), channel_id=1, source_target_pairs={{0,4},{1,5},{2,6},{3,7},{4,0},{5,1},{6,2},{7,3},{8,12},{9,13},{10,... | collective-permute-start | bytes 344072 | tf_op jit(solution)/shard_map/ppermute | solution.py:384
  71.6 9.9 %collective-permute-start.14 = (bf16[448,128]{1,0:T(8,128)(2,1)S(1)}, bf16[448,128]{1,0:T(8,128)(2,1)S(1)}, u32[]{:S(2)}, u32[]{:S(2)}) collective-permute-start(bf16[448,128]{1,0:T(8,128)(2,1)S(1)} %get-tuple-element.137), channel_id=1, source_target_pairs={{0,20},{1,21},{2,22},{3,23},{4,16},{5,17},{6,18},{7,19},{8,28},{9,... | collective-permute-start | bytes 344072 | tf_op jit(solution)/shard_map/ppermute | solution.py:384
  73.8 7.8 %collective-permute-start.12 = (bf16[448,128]{1,0:T(8,128)(2,1)S(1)}, bf16[448,128]{1,0:T(8,128)(2,1)S(1)}, u32[]{:S(2)}, u32[]{:S(2)}) collective-permute-start(bf16[448,128]{1,0:T(8,128)(2,1)S(1)} %get-tuple-element.135.refs_8_), channel_id=1, source_target_pairs={{0,16},{1,17},{2,18},{3,19},{4,20},{5,21},{6,22},{7,23},{8,24},{9,... | collective-permute-start | bytes 344072 | tf_op jit(solution)/shard_map/ppermute | solution.py:384
  81.7 7.9 %collective-permute-start.21 = (bf16[112,128]{1,0:T(8,128)(2,1)S(1)}, bf16[112,128]{1,0:T(8,128)(2,1)S(1)}, u32[]{:S(2)}, u32[]{:S(2)}) collective-permute-start(bf16[112,128]{1,0:T(8,128)(2,1)S(1)} %get-tuple-element.149), channel_id=1, source_target_pairs={{0,1},{1,0},{2,3},{3,2},{4,5},{5,4},{6,7},{7,6},{8,9},{9,8},{10,11... | collective-permute-start | bytes 86024 | tf_op jit(solution)/shard_map/ppermute | solution.py:384
  83.5 11.8 %collective-permute-start.20 = (bf16[192,128]{1,0:T(8,128)(2,1)S(1)}, bf16[192,128]{1,0:T(8,128)(2,1)S(1)}, u32[]{:S(2)}, u32[]{:S(2)}) collective-permute-start(bf16[192,128]{1,0:T(8,128)(2,1)S(1)} %shard_map.202.refs_1_), channel_id=1, source_target_pairs={{0,3},{1,2},{2,1},{3,0},{4,7},{5,6},{6,5},{7,4},{8,11},{9,10},{10,... | collective-permute-start | bytes 147464 | tf_op jit(solution)/shard_map/ppermute | solution.py:384
  86.1 9.2 %collective-permute-start.19 = (bf16[192,128]{1,0:T(8,128)(2,1)S(1)}, bf16[192,128]{1,0:T(8,128)(2,1)S(1)}, u32[]{:S(2)}, u32[]{:S(2)}) collective-permute-start(bf16[192,128]{1,0:T(8,128)(2,1)S(1)} %shard_map.202.refs_1_), channel_id=1, source_target_pairs={{0,2},{1,3},{2,0},{3,1},{4,6},{5,7},{6,4},{7,5},{8,10},{9,11},{10,... | collective-permute-start | bytes 147464 | tf_op jit(solution)/shard_map/ppermute | solution.py:384
  86.2 9.1 %collective-permute-start.18 = (bf16[192,128]{1,0:T(8,128)(2,1)S(1)}, bf16[192,128]{1,0:T(8,128)(2,1)S(1)}, u32[]{:S(2)}, u32[]{:S(2)}) collective-permute-start(bf16[192,128]{1,0:T(8,128)(2,1)S(1)} %shard_map.202.refs_1_), channel_id=1, source_target_pairs={{0,1},{1,0},{2,3},{3,2},{4,5},{5,4},{6,7},{7,6},{8,9},{9,8},{10,11... | collective-permute-start | bytes 147464 | tf_op jit(solution)/shard_map/ppermute | solution.py:384
  88.0 5.1 %collective-permute-start.22 = (bf16[112,128]{1,0:T(8,128)(2,1)S(1)}, bf16[112,128]{1,0:T(8,128)(2,1)S(1)}, u32[]{:S(2)}, u32[]{:S(2)}) collective-permute-start(bf16[112,128]{1,0:T(8,128)(2,1)S(1)} %get-tuple-element.150), channel_id=1, source_target_pairs={{0,2},{1,3},{2,0},{3,1},{4,6},{5,7},{6,4},{7,5},{8,10},{9,11},{10,... | collective-permute-start | bytes 86024 | tf_op jit(solution)/shard_map/ppermute | solution.py:384
  89.6 5.7 %collective-permute-start.23 = (bf16[112,128]{1,0:T(8,128)(2,1)S(1)}, bf16[112,128]{1,0:T(8,128)(2,1)S(1)}, u32[]{:S(2)}, u32[]{:S(2)}) collective-permute-start(bf16[112,128]{1,0:T(8,128)(2,1)S(1)} %get-tuple-element.151), channel_id=1, source_target_pairs={{0,3},{1,2},{2,1},{3,0},{4,7},{5,6},{6,5},{7,4},{8,11},{9,10},{10,... | collective-permute-start | bytes 86024 | tf_op jit(solution)/shard_map/ppermute | solution.py:384
  95.4 13.2 %collective-permute-start.26 = (bf16[768,128]{1,0:T(8,128)(2,1)S(1)}, bf16[768,128]{1,0:T(8,128)(2,1)S(1)}, u32[]{:S(2)}, u32[]{:S(2)}) collective-permute-start(bf16[768,128]{1,0:T(8,128)(2,1)S(1)} %shard_map.204.refs_1_), channel_id=1, source_target_pairs={{0,20},{1,21},{2,22},{3,23},{4,16},{5,17},{6,18},{7,19},{8,28},{9,... | collective-permute-start | bytes 589832 | tf_op jit(solution)/shard_map/ppermute | solution.py:384
  96.3 12.3 %collective-permute-start.25 = (bf16[768,128]{1,0:T(8,128)(2,1)S(1)}, bf16[768,128]{1,0:T(8,128)(2,1)S(1)}, u32[]{:S(2)}, u32[]{:S(2)}) collective-permute-start(bf16[768,128]{1,0:T(8,128)(2,1)S(1)} %shard_map.204.refs_1_), channel_id=1, source_target_pairs={{0,4},{1,5},{2,6},{3,7},{4,0},{5,1},{6,2},{7,3},{8,12},{9,13},{10,... | collective-permute-start | bytes 589832 | tf_op jit(solution)/shard_map/ppermute | solution.py:384
  97.7 10.9 %collective-permute-start.24 = (bf16[768,128]{1,0:T(8,128)(2,1)S(1)}, bf16[768,128]{1,0:T(8,128)(2,1)S(1)}, u32[]{:S(2)}, u32[]{:S(2)}) collective-permute-start(bf16[768,128]{1,0:T(8,128)(2,1)S(1)} %shard_map.204.refs_1_), channel_id=1, source_target_pairs={{0,16},{1,17},{2,18},{3,19},{4,20},{5,21},{6,22},{7,23},{8,24},{9,... | collective-permute-start | bytes 589832 | tf_op jit(solution)/shard_map/ppermute | solution.py:384
  98.9 5.8 %collective-permute-start.29 = (bf16[112,128]{1,0:T(8,128)(2,1)S(1)}, bf16[112,128]{1,0:T(8,128)(2,1)S(1)}, u32[]{:S(2)}, u32[]{:S(2)}) collective-permute-start(bf16[112,128]{1,0:T(8,128)(2,1)S(1)} %shard_map.205.refs_1_), channel_id=1, source_target_pairs={{0,3},{1,2},{2,1},{3,0},{4,7},{5,6},{6,5},{7,4},{8,11},{9,10},{10,... | collective-permute-start | bytes 86024 | tf_op jit(solution)/shard_map/ppermute | solution.py:384
  100.0 5.3 %collective-permute-start.28 = (bf16[112,128]{1,0:T(8,128)(2,1)S(1)}, bf16[112,128]{1,0:T(8,128)(2,1)S(1)}, u32[]{:S(2)}, u32[]{:S(2)}) collective-permute-start(bf16[112,128]{1,0:T(8,128)(2,1)S(1)} %shard_map.205.refs_1_), channel_id=1, source_target_pairs={{0,2},{1,3},{2,0},{3,1},{4,6},{5,7},{6,4},{7,5},{8,10},{9,11},{10,... | collective-permute-start | bytes 86024 | tf_op jit(solution)/shard_map/ppermute | solution.py:384
  104.7 3.9 %collective-permute-start.27 = (bf16[112,128]{1,0:T(8,128)(2,1)S(1)}, bf16[112,128]{1,0:T(8,128)(2,1)S(1)}, u32[]{:S(2)}, u32[]{:S(2)}) collective-permute-start(bf16[112,128]{1,0:T(8,128)(2,1)S(1)} %shard_map.205.refs_1_), channel_id=1, source_target_pairs={{0,1},{1,0},{2,3},{3,2},{4,5},{5,4},{6,7},{7,6},{8,9},{9,8},{10,11... | collective-permute-start | bytes 86024 | tf_op jit(solution)/shard_map/ppermute | solution.py:384
  108.6 8.8 %collective-permute-start.30 = (bf16[3072,128]{1,0:T(8,128)(2,1)S(1)}, bf16[3072,128]{1,0:T(8,128)(2,1)S(1)}, u32[]{:S(2)}, u32[]{:S(2)}) collective-permute-start(bf16[3072,128]{1,0:T(8,128)(2,1)S(1)} %shard_map.206.refs_1_), channel_id=1, source_target_pairs={{0,8},{1,9},{2,10},{3,11},{4,12},{5,13},{6,14},{7,15},{8,0},{9,1},... | collective-permute-start | bytes 2359304 | tf_op jit(solution)/shard_map/ppermute | solution.py:384
  108.8 7.0 %collective-permute-start.33 = (bf16[448,128]{1,0:T(8,128)(2,1)S(1)}, bf16[448,128]{1,0:T(8,128)(2,1)S(1)}, u32[]{:S(2)}, u32[]{:S(2)}) collective-permute-start(bf16[448,128]{1,0:T(8,128)(2,1)S(1)} %shard_map.207.refs_1_), channel_id=1, source_target_pairs={{0,20},{1,21},{2,22},{3,23},{4,16},{5,17},{6,18},{7,19},{8,28},{9,... | collective-permute-start | bytes 344072 | tf_op jit(solution)/shard_map/ppermute | solution.py:384
  109.7 7.7 %collective-permute-start.32 = (bf16[448,128]{1,0:T(8,128)(2,1)S(1)}, bf16[448,128]{1,0:T(8,128)(2,1)S(1)}, u32[]{:S(2)}, u32[]{:S(2)}) collective-permute-start(bf16[448,128]{1,0:T(8,128)(2,1)S(1)} %shard_map.207.refs_1_), channel_id=1, source_target_pairs={{0,4},{1,5},{2,6},{3,7},{4,0},{5,1},{6,2},{7,3},{8,12},{9,13},{10,... | collective-permute-start | bytes 344072 | tf_op jit(solution)/shard_map/ppermute | solution.py:384
  111.1 6.3 %collective-permute-start.31 = (bf16[448,128]{1,0:T(8,128)(2,1)S(1)}, bf16[448,128]{1,0:T(8,128)(2,1)S(1)}, u32[]{:S(2)}, u32[]{:S(2)}) collective-permute-start(bf16[448,128]{1,0:T(8,128)(2,1)S(1)} %shard_map.207.refs_1_), channel_id=1, source_target_pairs={{0,16},{1,17},{2,18},{3,19},{4,20},{5,21},{6,22},{7,23},{8,24},{9,... | collective-permute-start | bytes 344072 | tf_op jit(solution)/shard_map/ppermute | solution.py:384
  117.5 1.9 %collective-permute-start.34 = (bf16[1792,128]{1,0:T(8,128)(2,1)S(1)}, bf16[1792,128]{1,0:T(8,128)(2,1)S(1)}, u32[]{:S(2)}, u32[]{:S(2)}) collective-permute-start(bf16[1792,128]{1,0:T(8,128)(2,1)S(1)} %shard_map.208.refs_3_), channel_id=1, source_target_pairs={{0,8},{1,9},{2,10},{3,11},{4,12},{5,13},{6,14},{7,15},{8,0},{9,1},... | collective-permute-start | bytes 1376264 | tf_op jit(solution)/shard_map/ppermute | solution.py:384

commit v4 on v3

--- a/solution.py
+++ b/solution.py
@@ -35,37 +35,23 @@
     return [pairs + [(b, a) for a, b in pairs] for pairs in (first, second)]
 
 
-def edges(block, axis, dim, width):
-    size = block.shape[dim]
-    even = lax.axis_index(axis) % 2 == 0
-    low = lax.slice_in_dim(block, 0, width, axis=dim)
-    high = lax.slice_in_dim(block, size - width, size, axis=dim)
-    out = []
-    for pairs, is_high in zip(pair_rounds(lax.axis_size(axis)), (even, ~even)):
-        if pairs:
-            out.append(lax.ppermute(jnp.where(is_high, high, low), axis, pairs))
-        else:
-            out.append(jnp.zeros_like(low))
-    return out
-
-
-def halo(tile):
-    rows = edges(tile, "gy", 0, 3)
-    even = lax.axis_index("gy") % 2 == 0
-    top = jnp.where(even, rows[1], rows[0])
-    bottom = jnp.where(even, rows[0], rows[1])
-    even_x = lax.axis_index("gx") % 2 == 0
-    size = tile.shape[1]
-    column = [jnp.concatenate([part[:, :3], part[:, size - 3 :]], axis=1) for part in (top, tile, bottom)]
-    column = jnp.concatenate(column, axis=0)
-    out = []
-    for pairs, is_high in zip(pair_rounds(lax.axis_size("gx")), (even_x, ~even_x)):
-        if pairs:
-            out.append(lax.ppermute(jnp.where(is_high, column[:, 3:], column[:, :3]), "gx", pairs))
-        else:
-            out.append(jnp.zeros_like(column[:, :3]))
-    left = jnp.where(even_x, out[1], out[0])
-    right = jnp.where(even_x, out[0], out[1])
+def halo(tile, even_y, even_x):
+    rows, cols, _ = tile.shape
+
+    def swap_edges(low, high, axis, even):
+        got = []
+        for pairs, is_high in zip(pair_rounds(lax.axis_size(axis)), (even, ~even)):
+            if pairs:
+                got.append(lax.ppermute(jnp.where(is_high, high, low), axis, pairs))
+            else:
+                got.append(jnp.zeros_like(low))
+        return jnp.where(even, got[1], got[0]), jnp.where(even, got[0], got[1])
+
+    top, bottom = swap_edges(tile[:3], tile[rows - 3 :], "gy", even_y)
+    column = [
+        jnp.concatenate([part[:, at : at + 3] for part in (top, tile, bottom)], axis=0) for at in (0, cols - 3)
+    ]
+    left, right = swap_edges(*column, "gx", even_x)
     return top, bottom, left, right
 
 
@@ -364,13 +350,10 @@
     )(*args, *after)
 
 
-def bits(axis):
-    return [(axis, j) for j in range(max(lax.axis_size(axis).bit_length() - 1, 0))]
-
-
-def rounds():
-    rest = bits("gy")[2:] + bits("gx")[1:] + bits("rep")
-    return [[("gy", 1), ("gx", 0)]] + [rest[i : i + 2] for i in range(0, len(rest), 2)]
+def groups():
+    sizes = [lax.axis_size(axis) for axis in AXES]
+    near = sizes[1] * sizes[2]
+    return [[i for i in range(math.prod(sizes)) if i // near % 2 == core] for core in range(2)]
 
 
 def exchange(x, flips):
@@ -384,15 +367,8 @@
     return lax.ppermute(x, AXES, perm)
 
 
-def others(group):
-    return [[g for j, g in enumerate(group) if delta >> j & 1] for delta in range(1, 1 << len(group))]
-
-
-def place(group):
-    value = 0
-    for j, (axis, bit) in enumerate(group):
-        value = value + (lax.axis_index(axis) // (1 << bit) % 2 << j)
-    return jnp.asarray(value, jnp.int32).reshape(1)
+def swap(x):
+    return lax.all_to_all(x, AXES, 0, 0, axis_index_groups=groups(), tiled=True)
 
 
 def hold(arrays):
@@ -409,96 +385,51 @@
     lax.fori_loop(0, rows // size, step, 0, unroll=2 if rows // size > 1 else 1)
 
 
-def first_sum_kernel(has_small, mine, *refs):
-    wide, outs = refs[:2], refs[4 if has_small else 2 :]
-    rows = wide[0].shape[0] // len(outs)
-    for delta, out in enumerate(outs):
-        to = mine[0] ^ delta
+def first_sum_kernel(*refs):
+    out = refs[-1]
+    start = 0
+    for one, two in zip(refs[:-1:2], refs[1:-1:2]):
 
         def add(at, size):
-            part = pl.ds(pl.multiple_of(to * rows + at, 16), size)
-            out[pl.ds(at, size), :] = (wide[0][part, :].astype(f32) + wide[1][part, :].astype(f32)).astype(bf16)
-
-        chunks(rows, add)
-        end = rows
-        if has_small:
-            small = refs[2:4]
-            size = small[0].shape[0] // len(outs)
-            part = pl.ds(pl.multiple_of(to * size, 16), size)
-            out[end : end + size, :] = (small[0][part, :].astype(f32) + small[1][part, :].astype(f32)).astype(bf16)
-            end += size
-        if end < out.shape[0]:
-            out[end:, :] = jnp.zeros((out.shape[0] - end, LANES), bf16)
-
-
-def next_sum_kernel(count, mine, *refs):
-    ins, outs = refs[:count], refs[count:]
-    rows = outs[0].shape[0]
-    for delta, out in enumerate(outs):
-        start = (mine[0] ^ delta) * rows if len(outs) > 1 else 0
-
-        def add(at, size):
-            part = pl.ds(pl.multiple_of(start + at, 16), size)
-            out[pl.ds(at, size), :] = sum(r[part, :].astype(f32) for r in ins).astype(bf16)
-
-        chunks(rows, add)
-
-
-def join_kernel(count, mine, *refs):
-    out = refs[count]
-    rows = refs[0].shape[0]
-    for delta, ref in enumerate(refs[:count]):
-        out[pl.ds(pl.multiple_of((mine[0] ^ delta) * rows, 16), rows), :] = ref[...]
-
-
-def part_rows(weights, small):
-    step = 16 * math.prod(1 << len(group) for group in rounds()[1:])
-    return -(-(weights + small) // step) * step
+            part = pl.ds(at, size)
+            to = pl.ds(pl.multiple_of(start + at, 16), size)
+            out[to, :] = (one[part, :].astype(f32) + two[part, :].astype(f32)).astype(bf16)
+
+        chunks(one.shape[0], add)
+        start += one.shape[0]
+    if start < out.shape[0]:
+        out[start:, :] = jnp.zeros((out.shape[0] - start, LANES), bf16)
+
+
+def sum_kernel(got, out):
+    count, rows, _ = got.shape
+
+    def add(at, size):
+        total = got[0, pl.ds(at, size), :].astype(f32)
+        for j in range(1, count):
+            total = total + got[j, pl.ds(at, size), :].astype(f32)
+        total = total.astype(bf16)
+        for j in range(count):
+            out[j, pl.ds(at, size), :] = total
+
+    chunks(rows, add)
 
 
 SUM_FLOPS = 1 << 20
 
 
-def scatter_start(keep, other, small=(), after=()):
-    plan = rounds()
-    count = 1 << len(plan[0])
-    rows = part_rows(keep.shape[0] // count, small[0].shape[0] // count if small else 0)
-    return call(
-        functools.partial(first_sum_kernel, bool(small)),
-        [((rows, LANES), bf16)] * count,
-        [],
-        (place(plan[0]), keep, other, *small),
-        SUM_FLOPS,
-        1,
-        after,
-    )
-
-
-def transfers():
-    plan = rounds()
-    return [(group, True) for group in plan] + [(group, False) for group in reversed(plan)]
-
-
-def send_parts(parts, step):
-    group, scatters = transfers()[step]
-    if not scatters:
-        parts = [parts[0]] * (1 << len(group))
-    return [parts[0]] + [exchange(x, flips) for x, flips in zip(parts[1:], others(group))]
-
-
-def combine(got, step):
-    steps = transfers()
-    group, scatters = steps[step]
-    rows = got[0].shape[0]
-    if not scatters:
-        shapes = [((len(got) * rows, LANES), bf16)]
-        body, mine = join_kernel, place(group)
-    else:
-        following = steps[step + 1][0] if steps[step + 1][1] else []
-        count = 1 << len(following)
-        shapes = [((rows // count, LANES), bf16)] * count
-        body, mine = next_sum_kernel, place(following)
-    return call(functools.partial(body, len(got)), shapes, [], (mine, *got), SUM_FLOPS, 1)
+def add_halves(*halves):
+    count = len(groups()[0])
+    rows = sum(x.shape[0] for x in halves[::2])
+    rows = -(-rows // (16 * count)) * 16 * count
+    (x,) = call(first_sum_kernel, [((rows, LANES), bf16)], [], halves, SUM_FLOPS)
+    return x
+
+
+def add_parts(x, after=()):
+    parts = x.reshape(len(groups()[0]), -1, LANES)
+    (y,) = call(sum_kernel, [(parts.shape, bf16)], [], (parts,), SUM_FLOPS, 0, after)
+    return y.reshape(x.shape)
 
 
 def finish_kernel(
@@ -510,33 +441,27 @@
     def store(firsts, seconds):
         base = 0
         for width, first, second in zip(widths, firsts, seconds):
-            part = first.shape[0] // 4
-            block = width * channels // LANES // 4
-
-            def rows(ref, at):
-                start = at // block * part + at % block
-                return ref[start : start + LANES, :].astype(f32) * factor
-
             for j in range(channels // LANES):
-                for i in range(0, width, LANES):
-                    win[base + i : base + i + LANES, j * LANES : (j + 1) * LANES] = rows(first, j * width + i)
+                win[base : base + width, j * LANES : (j + 1) * LANES] = (
+                    first[j * width : (j + 1) * width, :].astype(f32) * factor
+                )
             for j in range(width // LANES):
-                for i in range(0, channels, LANES):
-                    wout[i : i + LANES, base + j * LANES : base + (j + 1) * LANES] = rows(
-                        second, j * channels + i
-                    )
+                wout[:, base + j * LANES : base + (j + 1) * LANES] = (
+                    second[j * channels : (j + 1) * channels, :].astype(f32) * factor
+                )
             base += width
         slabs = channels // LANES
         for slab in range(slabs):
             at = slice(slab * LANES, (slab + 1) * LANES)
-            start = slab * part + block
+            start = widths[1] * channels // LANES + slab * SMALL
             values = firsts[1][start : start + SMALL, :].astype(f32) * factor
-            gk[:, at] = values[:49]
+            for j in range(7):
+                gk[j, :, at] = values[7 * j : 7 * j + 7]
             for j, ref in enumerate((scale, b_out, gain, shift, bias)):
-                ref[:, at] = values[49 + j : 50 + j]
-            for j in range(b_in.shape[1] // channels):
+                ref[at] = values[49 + j]
+            for j in range(b_in.shape[0] // channels):
                 lane = (j * slabs + slab) * LANES
-                b_in[:, lane : lane + LANES] = values[54 + j : 55 + j]
+                b_in[lane : lane + LANES] = values[54 + j]
 
     pl.when(core[0] == 0)(lambda: store((own_a, own_b), (other_a, other_b)))
     pl.when(core[0] != 0)(lambda: store((other_a, other_b), (own_a, own_b)))
@@ -567,7 +492,11 @@
     pad = ((channels // LANES, rows + 6, EDGE + cols + 8, LANES), f32)
     full = (pixels, channels)
 
-    around = halo(tile)
+    even_y = lax.axis_index("gy") % 2 == 0
+    even_x = lax.axis_index("gx") % 2 == 0
+    core = (lax.axis_index("gy") % 2).astype(jnp.int32).reshape(1)
+    even_y, even_x, core, tile = hold((even_y, even_x, core, tile))
+    around = halo(tile, even_y, even_x)
     conv_flops = 2 * 49 * pixels * channels * 60
     normed, inv, ln_out = call(
         conv_norm_kernel,
@@ -585,7 +514,6 @@
     ]
     packed = lambda width: [((width * channels // LANES, LANES), bf16)] * 2 + [((1, width), f32)]
     core_flip = [("gy", 0)]
-    core = place(core_flip)
     mlp_flops = 12 * pixels * channels * hid
     weights = (w_in, w_out, row(b_in), scale)
     first, second = hid * 2 // 3, hid // 3
@@ -607,26 +535,25 @@
         1,
     )
     d_tile = d_depth.reshape(tile.shape)
-    parts_a = scatter_start(keep_a, other_a, after=(d_depth,))
-    d_edge, parts_a, keep_b, send_b = hold((d_tile, parts_a, keep_b, send_b))
-    got_a = send_parts(parts_a, 0)
+    other_a, d_tile, keep_b, send_b = hold((other_a, d_tile, keep_b, send_b))
+    parts_a = add_halves(keep_a, other_a)
+    got_a = swap(parts_a)
     other_b = exchange(send_b, core_flip)
-    d_around = halo(d_edge)
+    d_around = halo(d_tile, even_y, even_x)
     small_rows = ((4 * SMALL, LANES), bf16)
     keep_s, send_s = call(
         kernel_grad_kernel,
         [small_rows, small_rows],
         [pad, (full, f32), ((channels // LANES, 49, 8, LANES), f32)],
-        (core, tile, *around, d_depth, sums, gbin_a, gbin_b),
+        (core, tile, *around, d_tile.reshape(full), sums, gbin_a, gbin_b),
         conv_flops,
         1,
-        (parts_a[1],),
-    )
-    got_a, keep_s, send_s, other_b = hold((got_a, keep_s, send_s, other_b))
+        (parts_a,),
+    )
+    keep_s, send_s, other_b = hold((keep_s, send_s, other_b))
     other_s = exchange(send_s, core_flip)
-    parts_a = combine(got_a, 0)
-    parts_b = scatter_start(keep_b, other_b, (keep_s, other_s))
-    got_a, got_b = send_parts(parts_a, 1), send_parts(parts_b, 0)
+    parts_b = add_halves(keep_b, other_b, keep_s, other_s)
+    got_b = swap(parts_b)
     (grad_pages,) = call(
         conv_grad_kernel,
         [(full, bf16)],
@@ -634,40 +561,36 @@
         (d_tile, *d_around, kernel, cot),
         conv_flops,
         0,
-        (parts_a[1], parts_b[1]),
-    )
-    got_a, got_b, grad_pages = hold((got_a, got_b, grad_pages))
-    last = len(transfers()) - 1
-    for step in range(1, last):
-        parts_a, parts_b = combine(got_a, step), combine(got_b, step - 1)
-        got_a, got_b = hold((send_parts(parts_a, step + 1), send_parts(parts_b, step)))
-    (half_a,), parts_b = combine(got_a, last), combine(got_b, last - 1)
-    got_a, got_b = hold(([half_a, exchange(half_a, core_flip)], send_parts(parts_b, last)))
-    (half_b,) = combine(got_b, last)
+        (parts_b,),
+    )
+    got_a, grad_pages = hold((got_a, grad_pages))
+    sum_a = add_parts(got_a)
+    half_a = swap(sum_a)
+    half_b = swap(add_parts(got_b, (sum_a,)))
+    got_a = [half_a, exchange(half_a, core_flip)]
     got_b = [half_b, exchange(half_b, core_flip)]
     factor = float(pixels * lax.axis_size("gy") * lax.axis_size("gx") * lax.axis_size("rep")) ** (-0.5)
-    line = ((1, channels), f32)
+    line = ((channels,), f32)
     win, wout, gk, g_scale, g_bout, g_gain, g_shift, g_bias, g_bin = call(
         functools.partial(finish_kernel, factor, (first, second)),
-        [((hid, channels), f32), ((channels, hid), f32), ((49, channels), f32)] + [line] * 5 + [((1, hid), f32)],
+        [((hid, channels), f32), ((channels, hid), f32), ((7, 7, channels), f32)] + [line] * 5 + [((hid,), f32)],
         [],
         (core, *got_a, *got_b),
         SUM_FLOPS,
         1,
     )
-    flat = lambda v: v.reshape(-1)
     return (
         result.reshape(pages.shape),
         grad_pages.reshape(pages.shape),
-        gk.reshape(7, 7, channels),
-        flat(g_bias),
-        flat(g_gain),
-        flat(g_shift),
+        gk,
+        g_bias,
+        g_gain,
+        g_shift,
         win,
-        flat(g_bin),
+        g_bin,
         wout,
-        flat(g_bout),
-        flat(g_scale),
+        g_bout,
+        g_scale,
     )
 
 

time: 127 us -> 138 us (1.087)
  waiting for transfers between devices: 22.8 us -> 51.5 us
  local copies, waits for them, and re-layouts: 14.4 us -> 5.84 us
  starting transfers between devices: 41.7 us -> 34.9 us
  other arithmetic: 5.35 us -> 1.57 us
  Pallas kernels: 40.8 us -> 42.8 us
    all_to_all x0 -> x4, waiting for transfers between devices: none -> 42.9 us  [swap(): return lax.all_to_all(x, AXES, 0, 0, axis_index_groups=groups(), tiled=True)]
    ppermute x29 -> x5, starting transfers between devices: 35.6 us -> 7.76 us  [exchange(): return lax.ppermute(x, AXES, perm)]
    all_to_all x0 -> x4, starting transfers between devices: none -> 20.5 us  [swap(): return lax.all_to_all(x, AXES, 0, 0, axis_index_groups=groups(), tiled=True)]
    ppermute x29 -> x5, waiting for transfers between devices: 20.1 us -> 3.04 us  [exchange(): return lax.ppermute(x, AXES, perm)]
    unnamed x44 -> x16, local copies, waits for them, and re-layouts: 12.5 us -> 1.17 us
    pallas_call x6 -> x0, other arithmetic: 3.59 us -> none  [call(): pl.pallas_call(kernel, out_shape=[jax.ShapeDtypeStruct(shape, dtype) for...]
    reshape x6, local copies, waits for them, and re-layouts: 0.02 us -> 3.43 us  [shards(): row = lambda v: v.reshape(1, -1)]
    ppermute x6, waiting for transfers between devices: 2.7 us -> 5.56 us  [swap_edges(): got.append(lax.ppermute(jnp.where(is_high, high, low), axis, pairs))]
  transfers between devices with their start and end apart: 35 -> 15, of which waited for: 9 -> 6; matrix products, arithmetic and copies ran while one was open for 1% -> 4% of each run, Pallas kernels for 17% -> 17%
where the time goes in v4:
time: 138 us
  waiting for transfers between devices  51.5 us (37%)
  Pallas kernels  42.8 us (31%)
  starting transfers between devices  34.9 us (25%)
  local copies, waits for them, and re-layouts  5.84 us (4%)
  other arithmetic  1.57 us (1%)
    all_to_all x4, waiting for transfers between devices, swap(): return lax.all_to_all(x, AXES, 0, 0, axis_index_groups=groups(), tiled=True)  42.9 us
    pallas_call x10, Pallas kernels, call(): pl.pallas_call(kernel, out_shape=[jax.ShapeDtypeStruct(shape, dtype) for...  42.8 us
    all_to_all x4, starting transfers between devices, swap(): return lax.all_to_all(x, AXES, 0, 0, axis_index_groups=groups(), tiled=True)  20.5 us
    ppermute x5, starting transfers between devices, exchange(): return lax.ppermute(x, AXES, perm)  7.76 us
    ppermute x6, starting transfers between devices, swap_edges(): got.append(lax.ppermute(jnp.where(is_high, high, low), axis, pairs))  6.57 us
    ppermute x6, waiting for transfers between devices, swap_edges(): got.append(lax.ppermute(jnp.where(is_high, high, low), axis, pairs))  5.56 us
    reshape x6, local copies, waits for them, and re-layouts, shards(): row = lambda v: v.reshape(1, -1)  3.43 us
    ppermute x5, waiting for transfers between devices, exchange(): return lax.ppermute(x, AXES, perm)  3.04 us
  transfers between devices with their start and end apart: 15, of which 6 were waited for; matrix products, arithmetic and copies ran while one was open for 4% of the time, Pallas kernels for 17%

profile of v4, /device:TPU:0, one launch (start us, length us, event | category | flops | bytes accessed | tf_op | source)
XLA Modules:
  0.0 137.6 jit_solution(6441269429303090498)
XLA Ops:
  0.6 0.0 copy-start
  0.7 0.0 copy-start.6
  0.7 1.0 broadcast_select_fusion.11
  1.7 0.5 collective-permute-start.1
  2.2 0.7 collective-permute-start
  2.9 1.1 fusion.1
  4.0 0.0 collective-permute-done.1
  4.0 0.0 collective-permute-done
  4.1 0.2 maximum_select_fusion
  4.2 2.6 %collective-permute-start.2 = (bf16[38,3,384]{2,1,0:T(4,128)(2,1)S(1)}, bf16[38,3,384]{2,1,0:T(4,128)(2,1)S(1)}, u32[]{:S(2)}, u32[]{:S(2)}) collective-permute-start(bf16[38,3,384]{2,1,0:T(4,128)(2,1)S(1)} %maximum_select_fusion), channel_id=1, source_target_pairs={{0,4},{4,0},{1,5},{5,1},{2,6},{6,2},{3,7},{7,3},{8,12},{12,8},{9,1... | collective-permute-start | bytes 262664 | tf_op jit(solution)/shard_map/ppermute | solution.py:45
  6.8 0.7 reshape.90.refs_7_.refs_8_
  7.5 0.7 reshape.94.refs_6_
  8.2 0.7 reshape.89.refs_6_
  8.9 0.7 reshape.91.refs_8_
  9.6 0.7 reshape.93.refs_5_
  10.3 0.0 copy-done.6
  10.3 0.0 collective-permute-done.2
  10.3 0.1 broadcast_select_fusion.2
  10.4 0.0 copy-done
  10.4 0.0 copy-start.1
  10.4 0.0 copy-start.2
  10.4 0.0 copy-start.3
  10.4 7.6 %shard_map.194 = (f32[1024,384]{1,0:T(8,128)S(1)}, f32[1024,128]{1,0:T(8,128)S(1)}, bf16[1024,384]{1,0:T(8,128)(2,1)S(1)}) custom-call(bf16[32,32,384]{2,1,0:T(8,128)(2,1)S(1)} %bitcast.21, bf16[3,32,384]{2,1,0:T(8,128)(2,1)S(1)} %get-tuple-element.98.refs_1_.refs_2_, bf16[3,32,384]{2,1,0:T(8,128)(2,1)S(1)} %get-tuple-element.97.refs_2_.refs_3_, ...), custom_call_target="tpu_custom_call" | custom-call | flops 2312110080 | bytes 2257920 | tf_op jit(solution)/shard_map/pallas_call | solution.py:340
  18.0 0.0 copy-done.1
  18.0 0.0 copy-done.2
  18.1 0.0 copy-start.7
  18.1 8.0 %shard_map.195 = (f32[1024,384]{1,0:T(8,128)S(1)}, f32[1024,384]{1,0:T(8,128)S(1)}, bf16[3072,128]{1,0:T(8,128)(2,1)S(1)}, bf16[3072,128]{1,0:T(8,128)(2,1)S(1)}, f32[1,1024]{1,0:T(1,128)S(1)}) custom-call(s32[1]{0:T(128)} %bitcast.refs_0_, bf16[1024,384]{1,0:T(8,128)(2,1)S(1)} %get-tuple-element.53.refs_1_, bf16[1024,384]{1,0:T(8,128)(2,1)S(1)} %bitcast.27, ...), custom_call_target="tpu_custom_call" | custom-call | flops 7247757312 | bytes 7077888 | tf_op jit(solution)/shard_map/pallas_call | solution.py:340
  26.1 4.4 %collective-permute-start.3 = (bf16[3072,128]{1,0:T(8,128)(2,1)S(1)}, bf16[3072,128]{1,0:T(8,128)(2,1)S(1)}, u32[]{:S(2)}, u32[]{:S(2)}) collective-permute-start(bf16[3072,128]{1,0:T(8,128)(2,1)S(1)} %get-tuple-element.60), channel_id=1, source_target_pairs={{0,8},{1,9},{2,10},{3,11},{4,12},{5,13},{6,14},{7,15},{8,0},{9,1},... | collective-permute-start | bytes 2359304 | tf_op jit(solution)/shard_map/ppermute | solution.py:367
  30.6 6.8 %shard_map.196 = (bf16[1024,384]{1,0:T(8,128)(2,1)}, bf16[1024,384]{1,0:T(8,128)(2,1)S(1)}, bf16[1536,128]{1,0:T(8,128)(2,1)S(1)}, bf16[1536,128]{1,0:T(8,128)(2...) custom-call(s32[1]{0:T(128)} %bitcast.refs_0_, bf16[1024,384]{1,0:T(8,128)(2,1)S(1)} %get-tuple-element.53.refs_1_, ...), custom_call_target="tpu_custom_call" | custom-call | flops 7247757312 | bytes 7077888 | tf_op jit(solution)/shard_map/pallas_call | solution.py:340
  37.4 0.0 collective-permute-done.3.refs_1_
  37.4 1.1 shard_map.197.refs_10_
  38.5 6.2 %all-to-all-start = ((bf16[16,192,128]{2,1,0:T(8,128)(2,1)}), bf16[16,192,128]{2,1,0:T(8,128)(2,1)S(1)}, u32[]{:S(2)}, u32[]{:S(2)}) async-start(bf16[16,192,128]{2,1,0:T(8,128)(2,1)} %bitcast.6), calls=%async_computation | async-start | bytes 1572864 | tf_op jit(solution)/shard_map/all_to_all | solution.py:371
  44.8 0.3 collective-permute-start.5
  45.0 0.7 collective-permute-start.4
  45.7 3.2 %collective-permute-start.7 = (bf16[1536,128]{1,0:T(8,128)(2,1)}, bf16[1536,128]{1,0:T(8,128)(2,1)S(1)}, u32[]{:S(2)}, u32[]{:S(2)}) collective-permute-start(bf16[1536,128]{1,0:T(8,128)(2,1)} %copy-done.5), channel_id=1, source_target_pairs={{0,8},{1,9},{2,10},{3,11},{4,12},{5,13},{6,14},{7,15},{8,0},{9,1},... | collective-permute-start | bytes 1179656 | tf_op jit(solution)/shard_map/ppermute | solution.py:367
  48.9 0.1 fusion
  49.0 6.8 %shard_map.198 = (bf16[256,128]{1,0:T(8,128)(2,1)S(1)}, bf16[256,128]{1,0:T(8,128)(2,1)S(1)}) custom-call(s32[1]{0:T(128)} %bitcast.refs_0_, bf16[32,32,384]{2,1,0:T(8,128)(2,1)S(1)} %bitcast.23, bf16[3,32,384]{2,1,0:T(8,128)(2,1)S(1)} %get-tuple-element.98.refs_1_.refs_2_, bf16[3,32,384]{2,1,0:T(8,128)(2,1)S(1)} %get-tuple-element.97.refs_2_.refs_3_, ...), custom_call_target="tpu_custom_call" | custom-call | flops 2312110080 | bytes 2257920 | tf_op jit(solution)/shard_map/pallas_call | solution.py:340
  55.8 0.0 collective-permute-done.5
  55.8 0.0 collective-permute-done.4
  55.8 0.0 collective-permute-done.7.refs_1_
  55.8 0.1 collective-permute-start.8
  55.9 1.2 collective-permute-done.8.refs_3_
  57.1 0.9 shard_map.199.refs_7_
  58.1 9.2 %all-to-all-done = bf16[16,192,128]{2,1,0:T(8,128)(2,1)S(1)} async-done(((bf16[16,192,128]{2,1,0:T(8,128)(2,1)}), bf16[16,192,128]{2,1,0:T(8,128)(2,1)S(1)}, u32[]{:S(2)}, u32[]{:S(2)}) %all-to-all-start) | async-done | bytes 786464 | tf_op jit(solution)/shard_map/all_to_all | solution.py:371
  67.2 3.6 %all-to-all-start.2 = ((bf16[16,112,128]{2,1,0:T(8,128)(2,1)}), bf16[16,112,128]{2,1,0:T(8,128)(2,1)S(1)}, u32[]{:S(2)}, u32[]{:S(2)}) async-start(bf16[16,112,128]{2,1,0:T(8,128)(2,1)} %bitcast.12), calls=%async_computation.2 | async-start | bytes 917504 | tf_op jit(solution)/shard_map/all_to_all | solution.py:371
  70.8 0.2 maximum_select_fusion.1
  71.0 1.9 %collective-permute-start.6 = (bf16[38,3,384]{2,1,0:T(4,128)(2,1)S(1)}, bf16[38,3,384]{2,1,0:T(4,128)(2,1)S(1)}, u32[]{:S(2)}, u32[]{:S(2)}) collective-permute-start(bf16[38,3,384]{2,1,0:T(4,128)(2,1)S(1)} %maximum_select_fusion.1), channel_id=1, source_target_pairs={{0,4},{4,0},{1,5},{5,1},{2,6},{6,2},{3,7},{7,3},{8,12},{12,8},{9,1... | collective-permute-start | bytes 262664 | tf_op jit(solution)/shard_map/ppermute | solution.py:45
  72.9 5.6 %collective-permute-done.6 = bf16[38,3,384]{2,1,0:T(4,128)(2,1)S(1)} collective-permute-done((bf16[38,3,384]{2,1,0:T(4,128)(2,1)S(1)}, bf16[38,3,384]{2,1,0:T(4,128)(2,1)S(1)}, u32[]{:S(2)}, u32[]{:S(2)}) %collective-permute-start.6) | collective-permute-done | bytes 87584 | tf_op jit(solution)/shard_map/ppermute | solution.py:45
  78.4 0.1 broadcast_select_fusion
  78.5 0.0 copy-start.4
  78.5 1.1 copy-done.4
  79.7 6.9 %shard_map.200 = bf16[1024,384]{1,0:T(8,128)(2,1)} custom-call(bf16[32,32,384]{2,1,0:T(8,128)(2,1)S(1)} %bitcast.26, bf16[3,32,384]{2,1,0:T(8,128)(2,1)S(1)} %get-tuple-element.96.refs_1_, bf16[3,32,384]{2,1,0:T(8,128)(2,1)S(1)} %get-tuple-element.95.refs_2_, bf16[38,3,384]{2,1,0:T(4,128)(2,1)S(1)} %get-tuple-element.100.refs_3_, ...), custom_call_target="tpu_custom_call" | custom-call | flops 2312110080 | bytes 2257920 | tf_op jit(solution)/shard_map/pallas_call | solution.py:340
  86.6 1.0 shard_map.201
  87.6 0.0 all-to-all-done.2.refs_0_
  87.6 7.2 %all-to-all-start.1 = ((bf16[16,192,128]{2,1,0:T(8,128)(2,1)}), bf16[16,192,128]{2,1,0:T(8,128)(2,1)S(1)}, u32[]{:S(2)}, u32[]{:S(2)}) async-start(bf16[16,192,128]{2,1,0:T(8,128)(2,1)} %shard_map.201), calls=%async_computation.1 | async-start | bytes 1572864 | tf_op jit(solution)/shard_map/all_to_all | solution.py:371
  94.8 0.9 shard_map.202
  95.6 19.9 %all-to-all-done.1 = bf16[16,192,128]{2,1,0:T(8,128)(2,1)S(1)} async-done(((bf16[16,192,128]{2,1,0:T(8,128)(2,1)}), bf16[16,192,128]{2,1,0:T(8,128)(2,1)S(1)}, u32[]{:S(2)}, u32[]{:S(2)}) %all-to-all-start.1) | async-done | bytes 786464 | tf_op jit(solution)/shard_map/all_to_all | solution.py:371
  115.5 3.6 %all-to-all-start.3 = ((bf16[16,112,128]{2,1,0:T(8,128)(2,1)}), bf16[16,112,128]{2,1,0:T(8,128)(2,1)S(1)}, u32[]{:S(2)}, u32[]{:S(2)}) async-start(bf16[16,112,128]{2,1,0:T(8,128)(2,1)} %shard_map.202), calls=%async_computation.3 | async-start | bytes 917504 | tf_op jit(solution)/shard_map/all_to_all | solution.py:371
  119.1 0.1 collective-permute-start.9
  119.1 13.9 %all-to-all-done.3 = bf16[16,112,128]{2,1,0:T(8,128)(2,1)S(1)} async-done(((bf16[16,112,128]{2,1,0:T(8,128)(2,1)}), bf16[16,112,128]{2,1,0:T(8,128)(2,1)S(1)}, u32[]{:S(2)}, u32[]{:S(2)}) %all-to-all-start.3) | async-done | bytes 458784 | tf_op jit(solution)/shard_map/all_to_all | solution.py:371
  133.0 0.0 collective-permute-start.10
  133.0 1.8 %collective-permute-done.10.refs_4_ = bf16[1792,128]{1,0:T(8,128)(2,1)S(1)} collective-permute-done((bf16[1792,128]{1,0:T(8,128)(2,1)S(1)}, bf16[1792,128]{1,0:T(8,128)(2,1)S(1)}, u32[]{:S(2)}, u32[]{:S(2)}) %collective-permute-start.10) | collective-permute-done | bytes 458784 | tf_op jit(solution)/shard_map/ppermute | solution.py:367
  134.8 0.0 collective-permute-done.9.refs_2_
  134.8 2.7 %shard_map.203 = (f32[1536,384]{1,0:T(8,128)}, f32[384,1536]{1,0:T(8,128)}, f32[7,7,384]{2,1,0:T(8,128)}, f32[384]{0:T(512)}, f32[384]{0:T(512)}, /*index=5*/f32...) custom-call(s32[1]{0:T(128)} %bitcast.refs_0_, bf16[3072,128]{1,0:T(8,128)(2,1)S(1)} %bitcast.16, ...), custom_call_target="tpu_custom_call" | custom-call | flops 1048576 | bytes 1024 | tf_op jit(solution)/shard_map/pallas_call | solution.py:340
  (12 shorter events, 0.1 us)
Async XLA Ops:
  0.6 9.8 %copy-start = (bf16[1,32,32,384]{3,2,1,0:T(8,128)(2,1)S(1)}, bf16[1,32,32,384]{3,2,1,0:T(8,128)(2,1)}, u32[]{:S(2)}) copy-start(bf16[1,32,32,384]{3,2,1,0:T(8,128)(2,1)} %param.11) | copy-start | bytes 2359300
  0.7 9.6 %copy-start.6 = (f32[7,7,384]{2,1,0:T(8,128)S(1)}, f32[7,7,384]{2,1,0:T(8,128)}, u32[]{:S(2)}) copy-start(f32[7,7,384]{2,1,0:T(8,128)} %param.13) | copy-start | bytes 225796
  1.7 2.3 %collective-permute-start.1 = (bf16[3,32,384]{2,1,0:T(8,128)(2,1)S(1)}, bf16[3,32,384]{2,1,0:T(8,128)(2,1)S(1)}, u32[]{:S(2)}, u32[]{:S(2)}) collective-permute-start(bf16[3,32,384]{2,1,0:T(8,128)(2,1)S(1)} %get-tuple-element.93), channel_id=1, source_target_pairs={{0,8},{16,24},{8,0},{24,16},{1,9},{17,25},{9,1},{25,17},{2,10},{18... | collective-permute-start | bytes 221192 | tf_op jit(solution)/shard_map/ppermute | solution.py:45
  2.2 1.8 %collective-permute-start = (bf16[3,32,384]{2,1,0:T(8,128)(2,1)S(1)}, bf16[3,32,384]{2,1,0:T(8,128)(2,1)S(1)}, u32[]{:S(2)}, u32[]{:S(2)}) collective-permute-start(bf16[3,32,384]{2,1,0:T(8,128)(2,1)S(1)} %get-tuple-element.94), channel_id=1, source_target_pairs={{8,16},{16,8},{9,17},{17,9},{10,18},{18,10},{11,19},{19,11},{12,20... | collective-permute-start | bytes 221192 | tf_op jit(solution)/shard_map/ppermute | solution.py:45
  4.2 6.1 %collective-permute-start.2 = (bf16[38,3,384]{2,1,0:T(4,128)(2,1)S(1)}, bf16[38,3,384]{2,1,0:T(4,128)(2,1)S(1)}, u32[]{:S(2)}, u32[]{:S(2)}) collective-permute-start(bf16[38,3,384]{2,1,0:T(4,128)(2,1)S(1)} %maximum_select_fusion), channel_id=1, source_target_pairs={{0,4},{4,0},{1,5},{5,1},{2,6},{6,2},{3,7},{7,3},{8,12},{12,8},{9,1... | collective-permute-start | bytes 262664 | tf_op jit(solution)/shard_map/ppermute | solution.py:45
  10.4 7.6 %copy-start.1 = (bf16[1536,384]{1,0:T(8,128)(2,1)S(1)}, bf16[1536,384]{1,0:T(8,128)(2,1)}, u32[]{:S(2)}) copy-start(bf16[1536,384]{1,0:T(8,128)(2,1)} %refs_3_.3) | copy-start | bytes 3538948
  10.4 7.6 %copy-start.2 = (bf16[384,1536]{1,0:T(8,128)(2,1)S(1)}, bf16[384,1536]{1,0:T(8,128)(2,1)}, u32[]{:S(2)}) copy-start(bf16[384,1536]{1,0:T(8,128)(2,1)} %refs_4_.3) | copy-start | bytes 3538948
  10.4 7.6 %copy-start.3 = (bf16[1,32,32,384]{3,2,1,0:T(8,128)(2,1)S(1)}, bf16[1,32,32,384]{3,2,1,0:T(8,128)(2,1)}, u32[]{:S(2)}) copy-start(bf16[1,32,32,384]{3,2,1,0:T(8,128)(2,1)} %param.12) | copy-start | bytes 2359300
  18.1 12.5 %copy-start.7 = (f32[384]{0:T(512)S(1)}, f32[384]{0:T(512)}, u32[]{:S(2)}) copy-start(f32[384]{0:T(512)} %param.20) | copy-start | bytes 4612
  26.1 11.2 %collective-permute-start.3 = (bf16[3072,128]{1,0:T(8,128)(2,1)S(1)}, bf16[3072,128]{1,0:T(8,128)(2,1)S(1)}, u32[]{:S(2)}, u32[]{:S(2)}) collective-permute-start(bf16[3072,128]{1,0:T(8,128)(2,1)S(1)} %get-tuple-element.60), channel_id=1, source_target_pairs={{0,8},{1,9},{2,10},{3,11},{4,12},{5,13},{6,14},{7,15},{8,0},{9,1},... | collective-permute-start | bytes 2359304 | tf_op jit(solution)/shard_map/ppermute | solution.py:367
  37.4 1.1 copy-start.5
  38.5 28.7 %all-to-all-start = ((bf16[16,192,128]{2,1,0:T(8,128)(2,1)}), bf16[16,192,128]{2,1,0:T(8,128)(2,1)S(1)}, u32[]{:S(2)}, u32[]{:S(2)}) async-start(bf16[16,192,128]{2,1,0:T(8,128)(2,1)} %bitcast.6), calls=%async_computation | async-start | bytes 1572864 | tf_op jit(solution)/shard_map/all_to_all | solution.py:371
  44.8 11.0 %collective-permute-start.5 = (bf16[3,32,384]{2,1,0:T(8,128)(2,1)S(1)}, bf16[3,32,384]{2,1,0:T(8,128)(2,1)S(1)}, u32[]{:S(2)}, u32[]{:S(2)}) collective-permute-start(bf16[3,32,384]{2,1,0:T(8,128)(2,1)S(1)} %get-tuple-element.89), channel_id=1, source_target_pairs={{0,8},{16,24},{8,0},{24,16},{1,9},{17,25},{9,1},{25,17},{2,10},{18... | collective-permute-start | bytes 221192 | tf_op jit(solution)/shard_map/ppermute | solution.py:45
  45.0 10.7 %collective-permute-start.4 = (bf16[3,32,384]{2,1,0:T(8,128)(2,1)S(1)}, bf16[3,32,384]{2,1,0:T(8,128)(2,1)S(1)}, u32[]{:S(2)}, u32[]{:S(2)}) collective-permute-start(bf16[3,32,384]{2,1,0:T(8,128)(2,1)S(1)} %get-tuple-element.90), channel_id=1, source_target_pairs={{8,16},{16,8},{9,17},{17,9},{10,18},{18,10},{11,19},{19,11},{12,20... | collective-permute-start | bytes 221192 | tf_op jit(solution)/shard_map/ppermute | solution.py:45
  45.7 10.1 %collective-permute-start.7 = (bf16[1536,128]{1,0:T(8,128)(2,1)}, bf16[1536,128]{1,0:T(8,128)(2,1)S(1)}, u32[]{:S(2)}, u32[]{:S(2)}) collective-permute-start(bf16[1536,128]{1,0:T(8,128)(2,1)} %copy-done.5), channel_id=1, source_target_pairs={{0,8},{1,9},{2,10},{3,11},{4,12},{5,13},{6,14},{7,15},{8,0},{9,1},... | collective-permute-start | bytes 1179656 | tf_op jit(solution)/shard_map/ppermute | solution.py:367
  55.8 1.3 collective-permute-start.8
  67.2 20.3 %all-to-all-start.2 = ((bf16[16,112,128]{2,1,0:T(8,128)(2,1)}), bf16[16,112,128]{2,1,0:T(8,128)(2,1)S(1)}, u32[]{:S(2)}, u32[]{:S(2)}) async-start(bf16[16,112,128]{2,1,0:T(8,128)(2,1)} %bitcast.12), calls=%async_computation.2 | async-start | bytes 917504 | tf_op jit(solution)/shard_map/all_to_all | solution.py:371
  71.0 7.4 %collective-permute-start.6 = (bf16[38,3,384]{2,1,0:T(4,128)(2,1)S(1)}, bf16[38,3,384]{2,1,0:T(4,128)(2,1)S(1)}, u32[]{:S(2)}, u32[]{:S(2)}) collective-permute-start(bf16[38,3,384]{2,1,0:T(4,128)(2,1)S(1)} %maximum_select_fusion.1), channel_id=1, source_target_pairs={{0,4},{4,0},{1,5},{5,1},{2,6},{6,2},{3,7},{7,3},{8,12},{12,8},{9,1... | collective-permute-start | bytes 262664 | tf_op jit(solution)/shard_map/ppermute | solution.py:45
  78.5 1.1 copy-start.4
  87.6 27.9 %all-to-all-start.1 = ((bf16[16,192,128]{2,1,0:T(8,128)(2,1)}), bf16[16,192,128]{2,1,0:T(8,128)(2,1)S(1)}, u32[]{:S(2)}, u32[]{:S(2)}) async-start(bf16[16,192,128]{2,1,0:T(8,128)(2,1)} %shard_map.201), calls=%async_computation.1 | async-start | bytes 1572864 | tf_op jit(solution)/shard_map/all_to_all | solution.py:371
  115.5 17.5 %all-to-all-start.3 = ((bf16[16,112,128]{2,1,0:T(8,128)(2,1)}), bf16[16,112,128]{2,1,0:T(8,128)(2,1)S(1)}, u32[]{:S(2)}, u32[]{:S(2)}) async-start(bf16[16,112,128]{2,1,0:T(8,128)(2,1)} %shard_map.202), calls=%async_computation.3 | async-start | bytes 917504 | tf_op jit(solution)/shard_map/all_to_all | solution.py:371
  119.1 15.8 %collective-permute-start.9 = (bf16[3072,128]{1,0:T(8,128)(2,1)S(1)}, bf16[3072,128]{1,0:T(8,128)(2,1)S(1)}, u32[]{:S(2)}, u32[]{:S(2)}) collective-permute-start(bf16[3072,128]{1,0:T(8,128)(2,1)S(1)} %bitcast.15), channel_id=1, source_target_pairs={{0,8},{1,9},{2,10},{3,11},{4,12},{5,13},{6,14},{7,15},{8,0},{9,1},... | collective-permute-start | bytes 2359304 | tf_op jit(solution)/shard_map/ppermute | solution.py:367
  133.0 1.8 %collective-permute-start.10 = (bf16[1792,128]{1,0:T(8,128)(2,1)S(1)}, bf16[1792,128]{1,0:T(8,128)(2,1)S(1)}, u32[]{:S(2)}, u32[]{:S(2)}) collective-permute-start(bf16[1792,128]{1,0:T(8,128)(2,1)S(1)} %bitcast.17), channel_id=1, source_target_pairs={{0,8},{1,9},{2,10},{3,11},{4,12},{5,13},{6,14},{7,15},{8,0},{9,1},... | collective-permute-start | bytes 1376264 | tf_op jit(solution)/shard_map/ppermute | solution.py:367

commit v5 on v4

--- a/solution.py
+++ b/solution.py
@@ -350,10 +350,16 @@
     )(*args, *after)
 
 
-def groups():
-    sizes = [lax.axis_size(axis) for axis in AXES]
-    near = sizes[1] * sizes[2]
-    return [[i for i in range(math.prod(sizes)) if i // near % 2 == core] for core in range(2)]
+def bits(axis):
+    return [(axis, j) for j in range(max(lax.axis_size(axis).bit_length() - 1, 0))]
+
+
+def plane():
+    return [("gy", 1), ("gx", 0)]
+
+
+def beyond():
+    return bits("gy")[2:] + bits("gx")[1:] + bits("rep")
 
 
 def exchange(x, flips):
@@ -367,8 +373,9 @@
     return lax.ppermute(x, AXES, perm)
 
 
-def swap(x):
-    return lax.all_to_all(x, AXES, 0, 0, axis_index_groups=groups(), tiled=True)
+def spread(parts):
+    flips = [[g for j, g in enumerate(plane()) if delta >> j & 1] for delta in range(1, 4)]
+    return [parts[0]] + [exchange(x, flip) for x, flip in zip(parts[1:], flips)]
 
 
 def hold(arrays):
@@ -385,51 +392,68 @@
     lax.fori_loop(0, rows // size, step, 0, unroll=2 if rows // size > 1 else 1)
 
 
-def first_sum_kernel(*refs):
+def first_sum_kernel(has_small, mine, *refs):
+    wide, outs = refs[:2], refs[4 if has_small else 2 :]
+    rows = wide[0].shape[0] // len(outs)
+    for delta, out in enumerate(outs):
+        to = mine[0] ^ delta
+
+        def add(at, size):
+            part = pl.ds(pl.multiple_of(to * rows + at, 16), size)
+            out[pl.ds(at, size), :] = (wide[0][part, :].astype(f32) + wide[1][part, :].astype(f32)).astype(bf16)
+
+        chunks(rows, add)
+        end = rows
+        if has_small:
+            small = refs[2:4]
+            size = small[0].shape[0] // len(outs)
+            part = pl.ds(pl.multiple_of(to * size, 16), size)
+            out[end : end + size, :] = (small[0][part, :].astype(f32) + small[1][part, :].astype(f32)).astype(bf16)
+            end += size
+        if end < out.shape[0]:
+            out[end:, :] = jnp.zeros((out.shape[0] - end, LANES), bf16)
+
+
+def sum_kernel(*refs):
+    ins, out = refs[:-1], refs[-1]
+
+    def add(at, size):
+        part = pl.ds(at, size)
+        out[part, :] = sum(r[part, :].astype(f32) for r in ins).astype(bf16)
+
+    chunks(out.shape[0], add)
+
+
+def join_kernel(mine, *refs):
     out = refs[-1]
-    start = 0
-    for one, two in zip(refs[:-1:2], refs[1:-1:2]):
-
-        def add(at, size):
-            part = pl.ds(at, size)
-            to = pl.ds(pl.multiple_of(start + at, 16), size)
-            out[to, :] = (one[part, :].astype(f32) + two[part, :].astype(f32)).astype(bf16)
-
-        chunks(one.shape[0], add)
-        start += one.shape[0]
-    if start < out.shape[0]:
-        out[start:, :] = jnp.zeros((out.shape[0] - start, LANES), bf16)
-
-
-def sum_kernel(got, out):
-    count, rows, _ = got.shape
-
-    def add(at, size):
-        total = got[0, pl.ds(at, size), :].astype(f32)
-        for j in range(1, count):
-            total = total + got[j, pl.ds(at, size), :].astype(f32)
-        total = total.astype(bf16)
-        for j in range(count):
-            out[j, pl.ds(at, size), :] = total
-
-    chunks(rows, add)
+    rows = refs[0].shape[0]
+    for delta, ref in enumerate(refs[:-1]):
+        out[pl.ds(pl.multiple_of((mine[0] ^ delta) * rows, 16), rows), :] = ref[...]
 
 
 SUM_FLOPS = 1 << 20
 
 
-def add_halves(*halves):
-    count = len(groups()[0])
-    rows = sum(x.shape[0] for x in halves[::2])
-    rows = -(-rows // (16 * count)) * 16 * count
-    (x,) = call(first_sum_kernel, [((rows, LANES), bf16)], [], halves, SUM_FLOPS)
+def add_halves(mine, keep, other, *small):
+    rows = (keep.shape[0] + (small[0].shape[0] if small else 0)) // 4
+    return call(
+        functools.partial(first_sum_kernel, bool(small)),
+        [((rows, LANES), bf16)] * 4,
+        [],
+        (mine, keep, other, *small),
+        SUM_FLOPS,
+        1,
+    )
+
+
+def add(*arrays):
+    (x,) = call(sum_kernel, [(arrays[0].shape, bf16)], [], arrays, SUM_FLOPS)
     return x
 
 
-def add_parts(x, after=()):
-    parts = x.reshape(len(groups()[0]), -1, LANES)
-    (y,) = call(sum_kernel, [(parts.shape, bf16)], [], (parts,), SUM_FLOPS, 0, after)
-    return y.reshape(x.shape)
+def join(mine, *parts):
+    (x,) = call(join_kernel, [((4 * parts[0].shape[0], LANES), bf16)], [], (mine, *parts), SUM_FLOPS, 1)
+    return x
 
 
 def finish_kernel(
@@ -441,19 +465,26 @@
     def store(firsts, seconds):
         base = 0
         for width, first, second in zip(widths, firsts, seconds):
+            part = first.shape[0] // 4
+            block = width * channels // LANES // 4
+
+            def rows(ref, at):
+                start = at // block * part + at % block
+                return ref[start : start + LANES, :].astype(f32) * factor
+
             for j in range(channels // LANES):
-                win[base : base + width, j * LANES : (j + 1) * LANES] = (
-                    first[j * width : (j + 1) * width, :].astype(f32) * factor
-                )
+                for i in range(0, width, LANES):
+                    win[base + i : base + i + LANES, j * LANES : (j + 1) * LANES] = rows(first, j * width + i)
             for j in range(width // LANES):
-                wout[:, base + j * LANES : base + (j + 1) * LANES] = (
-                    second[j * channels : (j + 1) * channels, :].astype(f32) * factor
-                )
+                for i in range(0, channels, LANES):
+                    wout[i : i + LANES, base + j * LANES : base + (j + 1) * LANES] = rows(
+                        second, j * channels + i
+                    )
             base += width
         slabs = channels // LANES
         for slab in range(slabs):
             at = slice(slab * LANES, (slab + 1) * LANES)
-            start = widths[1] * channels // LANES + slab * SMALL
+            start = slab * part + block
             values = firsts[1][start : start + SMALL, :].astype(f32) * factor
             for j in range(7):
                 gk[j, :, at] = values[7 * j : 7 * j + 7]
@@ -495,7 +526,8 @@
     even_y = lax.axis_index("gy") % 2 == 0
     even_x = lax.axis_index("gx") % 2 == 0
     core = (lax.axis_index("gy") % 2).astype(jnp.int32).reshape(1)
-    even_y, even_x, core, tile = hold((even_y, even_x, core, tile))
+    mine = (lax.axis_index("gy") // 2 % 2 + lax.axis_index("gx") % 2 * 2).astype(jnp.int32).reshape(1)
+    even_y, even_x, core, mine, tile = hold((even_y, even_x, core, mine, tile))
     around = halo(tile, even_y, even_x)
     conv_flops = 2 * 49 * pixels * channels * 60
     normed, inv, ln_out = call(
@@ -536,8 +568,8 @@
     )
     d_tile = d_depth.reshape(tile.shape)
     other_a, d_tile, keep_b, send_b = hold((other_a, d_tile, keep_b, send_b))
-    parts_a = add_halves(keep_a, other_a)
-    got_a = swap(parts_a)
+    parts_a = add_halves(mine, keep_a, other_a)
+    got_a = spread(parts_a)
     other_b = exchange(send_b, core_flip)
     d_around = halo(d_tile, even_y, even_x)
     small_rows = ((4 * SMALL, LANES), bf16)
@@ -548,12 +580,14 @@
         (core, tile, *around, d_tile.reshape(full), sums, gbin_a, gbin_b),
         conv_flops,
         1,
-        (parts_a,),
-    )
-    keep_s, send_s, other_b = hold((keep_s, send_s, other_b))
+        (parts_a[1],),
+    )
+    got_a, keep_s, send_s, other_b = hold((got_a, keep_s, send_s, other_b))
     other_s = exchange(send_s, core_flip)
-    parts_b = add_halves(keep_b, other_b, keep_s, other_s)
-    got_b = swap(parts_b)
+    part_a = add(*got_a)
+    parts_b = add_halves(mine, keep_b, other_b, keep_s, other_s)
+    flips = [[bit] for bit in beyond()]
+    got_a, got_b = exchange(part_a, flips[0]), spread(parts_b)
     (grad_pages,) = call(
         conv_grad_kernel,
         [(full, bf16)],
@@ -561,13 +595,17 @@
         (d_tile, *d_around, kernel, cot),
         conv_flops,
         0,
-        (parts_b,),
-    )
-    got_a, grad_pages = hold((got_a, grad_pages))
-    sum_a = add_parts(got_a)
-    half_a = swap(sum_a)
-    half_b = swap(add_parts(got_b, (sum_a,)))
-    got_a = [half_a, exchange(half_a, core_flip)]
+        (part_a, parts_b[1]),
+    )
+    got_a, got_b, grad_pages = hold((got_a, got_b, grad_pages))
+    part_a, part_b = add(part_a, got_a), add(*got_b)
+    for ahead, behind in zip(flips[1:], flips):
+        got_a, got_b = hold((exchange(part_a, ahead), exchange(part_b, behind)))
+        part_a, part_b = add(part_a, got_a), add(part_b, got_b)
+    got_a, got_b = hold((spread([part_a] * 4), exchange(part_b, flips[-1])))
+    half_a, part_b = join(mine, *got_a), add(part_b, got_b)
+    got_a, got_b = hold(([half_a, exchange(half_a, core_flip)], spread([part_b] * 4)))
+    half_b = join(mine, *got_b)
     got_b = [half_b, exchange(half_b, core_flip)]
     factor = float(pixels * lax.axis_size("gy") * lax.axis_size("gx") * lax.axis_size("rep")) ** (-0.5)
     line = ((channels,), f32)

time: 138 us -> 102 us (0.74)
  waiting for transfers between devices: 51.5 us -> 22.8 us
  Pallas kernels: 42.8 us -> 39.8 us
  starting transfers between devices: 34.9 us -> 32.2 us
    all_to_all x4 -> x0, waiting for transfers between devices: 42.9 us -> none  [swap(): return lax.all_to_all(x, AXES, 0, 0, axis_index_groups=groups(), tiled=True)]
    all_to_all x4 -> x0, starting transfers between devices: 20.5 us -> none  [swap(): return lax.all_to_all(x, AXES, 0, 0, axis_index_groups=groups(), tiled=True)]
    ppermute x5 -> x21, waiting for transfers between devices: 3.04 us -> 22.8 us  [exchange(): return lax.ppermute(x, AXES, perm)]
    ppermute x5 -> x21, starting transfers between devices: 7.76 us -> 26.2 us  [exchange(): return lax.ppermute(x, AXES, perm)]
    ppermute x6, waiting for transfers between devices: 5.56 us -> 0.02 us  [swap_edges(): got.append(lax.ppermute(jnp.where(is_high, high, low), axis, pairs))]
    pallas_call x10 -> x16, Pallas kernels: 42.8 us -> 39.8 us  [call(): pl.pallas_call(kernel, out_shape=[jax.ShapeDtypeStruct(shape, dtype) for...]
  transfers between devices with their start and end apart: 15 -> 27, of which waited for: 6 -> 7; matrix products, arithmetic and copies ran while one was open for 4% -> 5% of each run, Pallas kernels for 17% -> 21%
where the time goes in v5:
time: 102 us
  Pallas kernels  39.8 us (39%)
  starting transfers between devices  32.2 us (32%)
  waiting for transfers between devices  22.8 us (22%)
  local copies, waits for them, and re-layouts  4.71 us (5%)
  other arithmetic  1.56 us (2%)
  between operations  1.07 us (1%)
    pallas_call x16, Pallas kernels, call(): pl.pallas_call(kernel, out_shape=[jax.ShapeDtypeStruct(shape, dtype) for...  39.8 us
    ppermute x21, starting transfers between devices, exchange(): return lax.ppermute(x, AXES, perm)  26.2 us
    ppermute x21, waiting for transfers between devices, exchange(): return lax.ppermute(x, AXES, perm)  22.8 us
    ppermute x6, starting transfers between devices, swap_edges(): got.append(lax.ppermute(jnp.where(is_high, high, low), axis, pairs))  5.95 us
    reshape x6, local copies, waits for them, and re-layouts, shards(): row = lambda v: v.reshape(1, -1)  3.43 us
  transfers between devices with their start and end apart: 27, of which 7 were waited for; matrix products, arithmetic and copies ran while one was open for 5% of the time, Pallas kernels for 21%

profile of v5, /device:TPU:0, one launch (start us, length us, event | category | flops | bytes accessed | tf_op | source)
XLA Modules:
  0.0 102.1 jit_solution(7158615727482136152)
XLA Ops:
  0.6 0.0 copy-start
  0.7 1.0 broadcast_select_fusion.11
  1.7 0.5 collective-permute-start.1
  2.2 0.7 collective-permute-start
  2.9 1.1 %fusion.1 = (bf16[32,3,384]{2,1,0:T(4,128)(2,1)S(1)}, bf16[32,3,384]{2,1,0:T(4,128)(2,1)S(1)}) fusion(bf16[32,32,384]{2,1,0:T(8,128)(2,1)} %bitcast.10), kind=kLoop, calls=%fused_computation.15 | loop fusion | bytes 294912 | tf_op jit(solution)/shard_map/slice | solution.py:52
  4.1 0.2 maximum_select_fusion
  4.2 2.6 %collective-permute-start.2 = (bf16[38,3,384]{2,1,0:T(4,128)(2,1)S(1)}, bf16[38,3,384]{2,1,0:T(4,128)(2,1)S(1)}, u32[]{:S(2)}, u32[]{:S(2)}) collective-permute-start(bf16[38,3,384]{2,1,0:T(4,128)(2,1)S(1)} %maximum_select_fusion), channel_id=1, source_target_pairs={{0,4},{4,0},{1,5},{5,1},{2,6},{6,2},{3,7},{7,3},{8,12},{12,8},{9,1... | collective-permute-start | bytes 262664 | tf_op jit(solution)/shard_map/ppermute | solution.py:45
  6.9 0.7 reshape.75.refs_7_.refs_8_
  7.5 0.7 reshape.79.refs_6_
  8.2 0.7 reshape.74.refs_6_
  8.9 0.7 reshape.76.refs_8_
  9.6 0.7 reshape.78.refs_5_
  10.3 0.1 broadcast_select_fusion.2
  10.4 0.0 copy-start.1
  10.4 0.0 copy-start.2
  10.5 0.0 copy-start.3
  10.5 7.6 %shard_map.194 = (f32[1024,384]{1,0:T(8,128)S(1)}, f32[1024,128]{1,0:T(8,128)S(1)}, bf16[1024,384]{1,0:T(8,128)(2,1)S(1)}) custom-call(bf16[32,32,384]{2,1,0:T(8,128)(2,1)S(1)} %bitcast.11, bf16[3,32,384]{2,1,0:T(8,128)(2,1)S(1)} %get-tuple-element.158.refs_1_.refs_2_, bf16[3,32,384]{2,1,0:T(8,128)(2,1)S(1)} %get-tuple-element.157.refs_2_.refs_3_, ...), custom_call_target="tpu_custom_call" | custom-call | flops 2312110080 | bytes 2257920 | tf_op jit(solution)/shard_map/pallas_call | solution.py:340
  18.1 0.0 copy-start.5
  18.1 8.0 %shard_map.195 = (f32[1024,384]{1,0:T(8,128)S(1)}, f32[1024,384]{1,0:T(8,128)S(1)}, bf16[3072,128]{1,0:T(8,128)(2,1)S(1)}, bf16[3072,128]{1,0:T(8,128)(2,1)S(1)}, f32[1,1024]{1,0:T(1,128)S(1)}) custom-call(s32[1]{0:T(128)} %bitcast.refs_0_, bf16[1024,384]{1,0:T(8,128)(2,1)S(1)} %get-tuple-element.83.refs_1_, bf16[1024,384]{1,0:T(8,128)(2,1)S(1)} %bitcast.17, ...), custom_call_target="tpu_custom_call" | custom-call | flops 7247757312 | bytes 7077888 | tf_op jit(solution)/shard_map/pallas_call | solution.py:340
  26.1 4.4 %collective-permute-start.3 = (bf16[3072,128]{1,0:T(8,128)(2,1)S(1)}, bf16[3072,128]{1,0:T(8,128)(2,1)S(1)}, u32[]{:S(2)}, u32[]{:S(2)}) collective-permute-start(bf16[3072,128]{1,0:T(8,128)(2,1)S(1)} %get-tuple-element.91), channel_id=1, source_target_pairs={{0,8},{1,9},{2,10},{3,11},{4,12},{5,13},{6,14},{7,15},{8,0},{9,1},... | collective-permute-start | bytes 2359304 | tf_op jit(solution)/shard_map/ppermute | solution.py:373
  30.6 6.9 %shard_map.196 = (bf16[1024,384]{1,0:T(8,128)(2,1)}, bf16[1024,384]{1,0:T(8,128)(2,1)S(1)}, bf16[1536,128]{1,0:T(8,128)(2,1)S(1)}, bf16[1536,128]{1,0:T(8,128)(2...) custom-call(s32[1]{0:T(128)} %bitcast.refs_0_, bf16[1024,384]{1,0:T(8,128)(2,1)S(1)} %get-tuple-element.83.refs_1_, ...), custom_call_target="tpu_custom_call" | custom-call | flops 7247757312 | bytes 7077888 | tf_op jit(solution)/shard_map/pallas_call | solution.py:340
  37.4 0.0 collective-permute-done.3.refs_2_
  37.5 0.1 collective-permute-start.14
  37.6 0.7 collective-permute-start.13
  38.2 0.1 fusion
  38.3 0.3 shard_map.197
  38.6 0.5 collective-permute-start.5
  39.2 4.3 %collective-permute-start.6 = (bf16[768,128]{1,0:T(8,128)(2,1)S(1)}, bf16[768,128]{1,0:T(8,128)(2,1)S(1)}, u32[]{:S(2)}, u32[]{:S(2)}) collective-permute-start(bf16[768,128]{1,0:T(8,128)(2,1)S(1)} %get-tuple-element.99), channel_id=1, source_target_pairs={{0,20},{1,21},{2,22},{3,23},{4,16},{5,17},{6,18},{7,19},{8,28},{9,... | collective-permute-start | bytes 589832 | tf_op jit(solution)/shard_map/ppermute | solution.py:373
  43.5 0.7 collective-permute-start.7
  44.2 0.2 maximum_select_fusion.1
  44.4 1.4 %collective-permute-start.15 = (bf16[38,3,384]{2,1,0:T(4,128)(2,1)S(1)}, bf16[38,3,384]{2,1,0:T(4,128)(2,1)S(1)}, u32[]{:S(2)}, u32[]{:S(2)}) collective-permute-start(bf16[38,3,384]{2,1,0:T(4,128)(2,1)S(1)} %maximum_select_fusion.1), channel_id=1, source_target_pairs={{0,4},{4,0},{1,5},{5,1},{2,6},{6,2},{3,7},{7,3},{8,12},{12,8},{9,1... | collective-permute-start | bytes 262664 | tf_op jit(solution)/shard_map/ppermute | solution.py:45
  45.8 6.8 %shard_map.198 = (bf16[256,128]{1,0:T(8,128)(2,1)S(1)}, bf16[256,128]{1,0:T(8,128)(2,1)S(1)}) custom-call(s32[1]{0:T(128)} %bitcast.refs_0_, bf16[32,32,384]{2,1,0:T(8,128)(2,1)S(1)} %bitcast.13, bf16[3,32,384]{2,1,0:T(8,128)(2,1)S(1)} %get-tuple-element.158.refs_1_.refs_2_, bf16[3,32,384]{2,1,0:T(8,128)(2,1)S(1)} %get-tuple-element.157.refs_2_.refs_3_, ...), custom_call_target="tpu_custom_call" | custom-call | flops 2312110080 | bytes 2257920 | tf_op jit(solution)/shard_map/pallas_call | solution.py:340
  52.6 0.1 collective-permute-start.9
  52.7 0.1 broadcast_select_fusion
  52.8 0.1 shard_map.199.refs_7_.refs_0_
  53.0 1.6 %collective-permute-start.8 = (bf16[768,128]{1,0:T(8,128)(2,1)S(1)}, bf16[768,128]{1,0:T(8,128)(2,1)S(1)}, u32[]{:S(2)}, u32[]{:S(2)}) collective-permute-start(bf16[768,128]{1,0:T(8,128)(2,1)S(1)} %shard_map.199.refs_7_.refs_0_), channel_id=1, source_target_pairs={{0,1},{1,0},{2,3},{3,2},{4,5},{5,4},{6,7},{7,6},{8,9},{9,8},{10,11... | collective-permute-start | bytes 589832 | tf_op jit(solution)/shard_map/ppermute | solution.py:373
  54.6 0.1 shard_map.200
  54.7 1.2 %collective-permute-start.11 = (bf16[448,128]{1,0:T(8,128)(2,1)S(1)}, bf16[448,128]{1,0:T(8,128)(2,1)S(1)}, u32[]{:S(2)}, u32[]{:S(2)}) collective-permute-start(bf16[448,128]{1,0:T(8,128)(2,1)S(1)} %get-tuple-element.117), channel_id=1, source_target_pairs={{0,4},{1,5},{2,6},{3,7},{4,0},{5,1},{6,2},{7,3},{8,12},{9,13},{10,... | collective-permute-start | bytes 344072 | tf_op jit(solution)/shard_map/ppermute | solution.py:373
  55.9 1.9 %collective-permute-start.12 = (bf16[448,128]{1,0:T(8,128)(2,1)S(1)}, bf16[448,128]{1,0:T(8,128)(2,1)S(1)}, u32[]{:S(2)}, u32[]{:S(2)}) collective-permute-start(bf16[448,128]{1,0:T(8,128)(2,1)S(1)} %get-tuple-element.118), channel_id=1, source_target_pairs={{0,20},{1,21},{2,22},{3,23},{4,16},{5,17},{6,18},{7,19},{8,28},{9,... | collective-permute-start | bytes 344072 | tf_op jit(solution)/shard_map/ppermute | solution.py:373
  57.9 0.4 collective-permute-start.10
  58.3 6.9 %shard_map.201 = bf16[1024,384]{1,0:T(8,128)(2,1)} custom-call(bf16[32,32,384]{2,1,0:T(8,128)(2,1)S(1)} %bitcast.16, bf16[3,32,384]{2,1,0:T(8,128)(2,1)S(1)} %get-tuple-element.156.refs_1_, bf16[3,32,384]{2,1,0:T(8,128)(2,1)S(1)} %get-tuple-element.155.refs_2_, bf16[38,3,384]{2,1,0:T(4,128)(2,1)S(1)} %get-tuple-element.160.refs_3_, ...), custom_call_target="tpu_custom_call" | custom-call | flops 2312110080 | bytes 2257920 | tf_op jit(solution)/shard_map/pallas_call | solution.py:340
  65.2 0.1 shard_map.202.refs_0_
  65.3 2.6 %collective-permute-start.16 = (bf16[768,128]{1,0:T(8,128)(2,1)S(1)}, bf16[768,128]{1,0:T(8,128)(2,1)S(1)}, u32[]{:S(2)}, u32[]{:S(2)}) collective-permute-start(bf16[768,128]{1,0:T(8,128)(2,1)S(1)} %shard_map.202.refs_0_), channel_id=1, source_target_pairs={{0,2},{1,3},{2,0},{3,1},{4,6},{5,7},{6,4},{7,5},{8,10},{9,11},{10,... | collective-permute-start | bytes 589832 | tf_op jit(solution)/shard_map/ppermute | solution.py:373
  67.9 0.1 shard_map.203.refs_0_
  68.0 1.0 collective-permute-start.17
  69.0 5.1 %collective-permute-done.17.refs_1_ = bf16[448,128]{1,0:T(8,128)(2,1)S(1)} collective-permute-done((bf16[448,128]{1,0:T(8,128)(2,1)S(1)}, bf16[448,128]{1,0:T(8,128)(2,1)S(1)}, u32[]{:S(2)}, u32[]{:S(2)}) %collective-permute-start.17) | collective-permute-done | bytes 114720 | tf_op jit(solution)/shard_map/ppermute | solution.py:373
  74.1 2.5 %collective-permute-done.16.refs_1_ = bf16[768,128]{1,0:T(8,128)(2,1)S(1)} collective-permute-done((bf16[768,128]{1,0:T(8,128)(2,1)S(1)}, bf16[768,128]{1,0:T(8,128)(2,1)S(1)}, u32[]{:S(2)}, u32[]{:S(2)}) %collective-permute-start.16) | collective-permute-done | bytes 196640 | tf_op jit(solution)/shard_map/ppermute | solution.py:373
  76.6 0.1 shard_map.204.refs_1_
  76.7 1.6 %collective-permute-start.20 = (bf16[768,128]{1,0:T(8,128)(2,1)S(1)}, bf16[768,128]{1,0:T(8,128)(2,1)S(1)}, u32[]{:S(2)}, u32[]{:S(2)}) collective-permute-start(bf16[768,128]{1,0:T(8,128)(2,1)S(1)} %shard_map.204.refs_1_), channel_id=1, source_target_pairs={{0,20},{1,21},{2,22},{3,23},{4,16},{5,17},{6,18},{7,19},{8,28},{9,... | collective-permute-start | bytes 589832 | tf_op jit(solution)/shard_map/ppermute | solution.py:373
  78.2 1.2 %collective-permute-start.19 = (bf16[768,128]{1,0:T(8,128)(2,1)S(1)}, bf16[768,128]{1,0:T(8,128)(2,1)S(1)}, u32[]{:S(2)}, u32[]{:S(2)}) collective-permute-start(bf16[768,128]{1,0:T(8,128)(2,1)S(1)} %shard_map.204.refs_1_), channel_id=1, source_target_pairs={{0,4},{1,5},{2,6},{3,7},{4,0},{5,1},{6,2},{7,3},{8,12},{9,13},{10,... | collective-permute-start | bytes 589832 | tf_op jit(solution)/shard_map/ppermute | solution.py:373
  79.5 0.8 collective-permute-start.18
  80.3 0.1 collective-permute-start.21
  80.4 7.2 %collective-permute-done.21.refs_1_ = bf16[448,128]{1,0:T(8,128)(2,1)S(1)} collective-permute-done((bf16[448,128]{1,0:T(8,128)(2,1)S(1)}, bf16[448,128]{1,0:T(8,128)(2,1)S(1)}, u32[]{:S(2)}, u32[]{:S(2)}) %collective-permute-start.21) | collective-permute-done | bytes 114720 | tf_op jit(solution)/shard_map/ppermute | solution.py:373
  87.6 0.7 collective-permute-done.19.refs_3_
  88.3 0.1 shard_map.206.refs_1_
  88.4 0.1 collective-permute-start.22
  88.5 1.5 %collective-permute-start.25 = (bf16[448,128]{1,0:T(8,128)(2,1)S(1)}, bf16[448,128]{1,0:T(8,128)(2,1)S(1)}, u32[]{:S(2)}, u32[]{:S(2)}) collective-permute-start(bf16[448,128]{1,0:T(8,128)(2,1)S(1)} %shard_map.207.refs_1_), channel_id=1, source_target_pairs={{0,20},{1,21},{2,22},{3,23},{4,16},{5,17},{6,18},{7,19},{8,28},{9,... | collective-permute-start | bytes 344072 | tf_op jit(solution)/shard_map/ppermute | solution.py:373
  90.0 1.0 %collective-permute-start.24 = (bf16[448,128]{1,0:T(8,128)(2,1)S(1)}, bf16[448,128]{1,0:T(8,128)(2,1)S(1)}, u32[]{:S(2)}, u32[]{:S(2)}) collective-permute-start(bf16[448,128]{1,0:T(8,128)(2,1)S(1)} %shard_map.207.refs_1_), channel_id=1, source_target_pairs={{0,4},{1,5},{2,6},{3,7},{4,0},{5,1},{6,2},{7,3},{8,12},{9,13},{10,... | collective-permute-start | bytes 344072 | tf_op jit(solution)/shard_map/ppermute | solution.py:373
  91.0 1.0 %collective-permute-start.23 = (bf16[448,128]{1,0:T(8,128)(2,1)S(1)}, bf16[448,128]{1,0:T(8,128)(2,1)S(1)}, u32[]{:S(2)}, u32[]{:S(2)}) collective-permute-start(bf16[448,128]{1,0:T(8,128)(2,1)S(1)} %shard_map.207.refs_1_), channel_id=1, source_target_pairs={{0,16},{1,17},{2,18},{3,19},{4,20},{5,21},{6,22},{7,23},{8,24},{9,... | collective-permute-start | bytes 344072 | tf_op jit(solution)/shard_map/ppermute | solution.py:373
  92.0 3.4 %collective-permute-done.25.refs_4_ = bf16[448,128]{1,0:T(8,128)(2,1)S(1)} collective-permute-done((bf16[448,128]{1,0:T(8,128)(2,1)S(1)}, bf16[448,128]{1,0:T(8,128)(2,1)S(1)}, u32[]{:S(2)}, u32[]{:S(2)}) %collective-permute-start.25) | collective-permute-done | bytes 114720 | tf_op jit(solution)/shard_map/ppermute | solution.py:373
  95.4 2.0 %collective-permute-done.24.refs_3_ = bf16[448,128]{1,0:T(8,128)(2,1)S(1)} collective-permute-done((bf16[448,128]{1,0:T(8,128)(2,1)S(1)}, bf16[448,128]{1,0:T(8,128)(2,1)S(1)}, u32[]{:S(2)}, u32[]{:S(2)}) %collective-permute-start.24) | collective-permute-done | bytes 114720 | tf_op jit(solution)/shard_map/ppermute | solution.py:373
  97.5 0.1 collective-permute-start.26
  97.6 1.8 %collective-permute-done.26.refs_4_ = bf16[1792,128]{1,0:T(8,128)(2,1)S(1)} collective-permute-done((bf16[1792,128]{1,0:T(8,128)(2,1)S(1)}, bf16[1792,128]{1,0:T(8,128)(2,1)S(1)}, u32[]{:S(2)}, u32[]{:S(2)}) %collective-permute-start.26) | collective-permute-done | bytes 458784 | tf_op jit(solution)/shard_map/ppermute | solution.py:373
  99.4 2.7 %shard_map.209 = (f32[1536,384]{1,0:T(8,128)}, f32[384,1536]{1,0:T(8,128)}, f32[7,7,384]{2,1,0:T(8,128)}, f32[384]{0:T(512)}, f32[384]{0:T(512)}, /*index=5*/f32...) custom-call(s32[1]{0:T(128)} %bitcast.refs_0_, bf16[3072,128]{1,0:T(8,128)(2,1)S(1)} %shard_map.206.refs_1_, ...), custom_call_target="tpu_custom_call" | custom-call | flops 1048576 | bytes 1024 | tf_op jit(solution)/shard_map/pallas_call | solution.py:340
  (38 shorter events, 0.3 us)
Async XLA Ops:
  0.6 9.8 %copy-start = (bf16[1,32,32,384]{3,2,1,0:T(8,128)(2,1)S(1)}, bf16[1,32,32,384]{3,2,1,0:T(8,128)(2,1)}, u32[]{:S(2)}) copy-start(bf16[1,32,32,384]{3,2,1,0:T(8,128)(2,1)} %param.11) | copy-start | bytes 2359300
  0.7 9.6 %copy-start.4 = (f32[7,7,384]{2,1,0:T(8,128)S(1)}, f32[7,7,384]{2,1,0:T(8,128)}, u32[]{:S(2)}) copy-start(f32[7,7,384]{2,1,0:T(8,128)} %param.13) | copy-start | bytes 225796
  1.7 2.3 %collective-permute-start.1 = (bf16[3,32,384]{2,1,0:T(8,128)(2,1)S(1)}, bf16[3,32,384]{2,1,0:T(8,128)(2,1)S(1)}, u32[]{:S(2)}, u32[]{:S(2)}) collective-permute-start(bf16[3,32,384]{2,1,0:T(8,128)(2,1)S(1)} %get-tuple-element.153), channel_id=1, source_target_pairs={{0,8},{16,24},{8,0},{24,16},{1,9},{17,25},{9,1},{25,17},{2,10},{18... | collective-permute-start | bytes 221192 | tf_op jit(solution)/shard_map/ppermute | solution.py:45
  2.2 1.8 %collective-permute-start = (bf16[3,32,384]{2,1,0:T(8,128)(2,1)S(1)}, bf16[3,32,384]{2,1,0:T(8,128)(2,1)S(1)}, u32[]{:S(2)}, u32[]{:S(2)}) collective-permute-start(bf16[3,32,384]{2,1,0:T(8,128)(2,1)S(1)} %get-tuple-element.154), channel_id=1, source_target_pairs={{8,16},{16,8},{9,17},{17,9},{10,18},{18,10},{11,19},{19,11},{12,20... | collective-permute-start | bytes 221192 | tf_op jit(solution)/shard_map/ppermute | solution.py:45
  4.2 6.1 %collective-permute-start.2 = (bf16[38,3,384]{2,1,0:T(4,128)(2,1)S(1)}, bf16[38,3,384]{2,1,0:T(4,128)(2,1)S(1)}, u32[]{:S(2)}, u32[]{:S(2)}) collective-permute-start(bf16[38,3,384]{2,1,0:T(4,128)(2,1)S(1)} %maximum_select_fusion), channel_id=1, source_target_pairs={{0,4},{4,0},{1,5},{5,1},{2,6},{6,2},{3,7},{7,3},{8,12},{12,8},{9,1... | collective-permute-start | bytes 262664 | tf_op jit(solution)/shard_map/ppermute | solution.py:45
  10.4 7.6 %copy-start.1 = (bf16[1536,384]{1,0:T(8,128)(2,1)S(1)}, bf16[1536,384]{1,0:T(8,128)(2,1)}, u32[]{:S(2)}) copy-start(bf16[1536,384]{1,0:T(8,128)(2,1)} %refs_3_.3) | copy-start | bytes 3538948
  10.4 7.6 %copy-start.2 = (bf16[384,1536]{1,0:T(8,128)(2,1)S(1)}, bf16[384,1536]{1,0:T(8,128)(2,1)}, u32[]{:S(2)}) copy-start(bf16[384,1536]{1,0:T(8,128)(2,1)} %refs_4_.3) | copy-start | bytes 3538948
  10.5 7.6 %copy-start.3 = (bf16[1,32,32,384]{3,2,1,0:T(8,128)(2,1)S(1)}, bf16[1,32,32,384]{3,2,1,0:T(8,128)(2,1)}, u32[]{:S(2)}) copy-start(bf16[1,32,32,384]{3,2,1,0:T(8,128)(2,1)} %param.12) | copy-start | bytes 2359300
  18.1 12.5 %copy-start.5 = (f32[384]{0:T(512)S(1)}, f32[384]{0:T(512)}, u32[]{:S(2)}) copy-start(f32[384]{0:T(512)} %param.20) | copy-start | bytes 4612
  26.1 11.3 %collective-permute-start.3 = (bf16[3072,128]{1,0:T(8,128)(2,1)S(1)}, bf16[3072,128]{1,0:T(8,128)(2,1)S(1)}, u32[]{:S(2)}, u32[]{:S(2)}) collective-permute-start(bf16[3072,128]{1,0:T(8,128)(2,1)S(1)} %get-tuple-element.91), channel_id=1, source_target_pairs={{0,8},{1,9},{2,10},{3,11},{4,12},{5,13},{6,14},{7,15},{8,0},{9,1},... | collective-permute-start | bytes 2359304 | tf_op jit(solution)/shard_map/ppermute | solution.py:373
  37.5 6.0 %collective-permute-start.14 = (bf16[3,32,384]{2,1,0:T(8,128)(2,1)S(1)}, bf16[3,32,384]{2,1,0:T(8,128)(2,1)S(1)}, u32[]{:S(2)}, u32[]{:S(2)}) collective-permute-start(bf16[3,32,384]{2,1,0:T(8,128)(2,1)S(1)} %get-tuple-element.149), channel_id=1, source_target_pairs={{0,8},{16,24},{8,0},{24,16},{1,9},{17,25},{9,1},{25,17},{2,10},{18... | collective-permute-start | bytes 221192 | tf_op jit(solution)/shard_map/ppermute | solution.py:45
  37.6 6.6 %collective-permute-start.13 = (bf16[3,32,384]{2,1,0:T(8,128)(2,1)S(1)}, bf16[3,32,384]{2,1,0:T(8,128)(2,1)S(1)}, u32[]{:S(2)}, u32[]{:S(2)}) collective-permute-start(bf16[3,32,384]{2,1,0:T(8,128)(2,1)S(1)} %get-tuple-element.150), channel_id=1, source_target_pairs={{8,16},{16,8},{9,17},{17,9},{10,18},{18,10},{11,19},{19,11},{12,20... | collective-permute-start | bytes 221192 | tf_op jit(solution)/shard_map/ppermute | solution.py:45
  38.6 14.0 %collective-permute-start.5 = (bf16[768,128]{1,0:T(8,128)(2,1)S(1)}, bf16[768,128]{1,0:T(8,128)(2,1)S(1)}, u32[]{:S(2)}, u32[]{:S(2)}) collective-permute-start(bf16[768,128]{1,0:T(8,128)(2,1)S(1)} %get-tuple-element.98), channel_id=1, source_target_pairs={{0,4},{1,5},{2,6},{3,7},{4,0},{5,1},{6,2},{7,3},{8,12},{9,13},{10,... | collective-permute-start | bytes 589832 | tf_op jit(solution)/shard_map/ppermute | solution.py:373
  39.2 13.5 %collective-permute-start.6 = (bf16[768,128]{1,0:T(8,128)(2,1)S(1)}, bf16[768,128]{1,0:T(8,128)(2,1)S(1)}, u32[]{:S(2)}, u32[]{:S(2)}) collective-permute-start(bf16[768,128]{1,0:T(8,128)(2,1)S(1)} %get-tuple-element.99), channel_id=1, source_target_pairs={{0,20},{1,21},{2,22},{3,23},{4,16},{5,17},{6,18},{7,19},{8,28},{9,... | collective-permute-start | bytes 589832 | tf_op jit(solution)/shard_map/ppermute | solution.py:373
  43.5 9.1 %collective-permute-start.4 = (bf16[768,128]{1,0:T(8,128)(2,1)S(1)}, bf16[768,128]{1,0:T(8,128)(2,1)S(1)}, u32[]{:S(2)}, u32[]{:S(2)}) collective-permute-start(bf16[768,128]{1,0:T(8,128)(2,1)S(1)} %get-tuple-element.97.refs_10_), channel_id=1, source_target_pairs={{0,16},{1,17},{2,18},{3,19},{4,20},{5,21},{6,22},{7,23},{8,24},{9,... | collective-permute-start | bytes 589832 | tf_op jit(solution)/shard_map/ppermute | solution.py:373
  43.5 9.1 %collective-permute-start.7 = (bf16[1536,128]{1,0:T(8,128)(2,1)S(1)}, bf16[1536,128]{1,0:T(8,128)(2,1)S(1)}, u32[]{:S(2)}, u32[]{:S(2)}) collective-permute-start(bf16[1536,128]{1,0:T(8,128)(2,1)S(1)} %get-tuple-element.106), channel_id=1, source_target_pairs={{0,8},{1,9},{2,10},{3,11},{4,12},{5,13},{6,14},{7,15},{8,0},{9,1},... | collective-permute-start | bytes 1179656 | tf_op jit(solution)/shard_map/ppermute | solution.py:373
  44.4 8.3 %collective-permute-start.15 = (bf16[38,3,384]{2,1,0:T(4,128)(2,1)S(1)}, bf16[38,3,384]{2,1,0:T(4,128)(2,1)S(1)}, u32[]{:S(2)}, u32[]{:S(2)}) collective-permute-start(bf16[38,3,384]{2,1,0:T(4,128)(2,1)S(1)} %maximum_select_fusion.1), channel_id=1, source_target_pairs={{0,4},{4,0},{1,5},{5,1},{2,6},{6,2},{3,7},{7,3},{8,12},{12,8},{9,1... | collective-permute-start | bytes 262664 | tf_op jit(solution)/shard_map/ppermute | solution.py:45
  52.6 2.0 %collective-permute-start.9 = (bf16[256,128]{1,0:T(8,128)(2,1)S(1)}, bf16[256,128]{1,0:T(8,128)(2,1)S(1)}, u32[]{:S(2)}, u32[]{:S(2)}) collective-permute-start(bf16[256,128]{1,0:T(8,128)(2,1)S(1)} %get-tuple-element.114), channel_id=1, source_target_pairs={{0,8},{1,9},{2,10},{3,11},{4,12},{5,13},{6,14},{7,15},{8,0},{9,1},... | collective-permute-start | bytes 196616 | tf_op jit(solution)/shard_map/ppermute | solution.py:373
  53.0 12.2 %collective-permute-start.8 = (bf16[768,128]{1,0:T(8,128)(2,1)S(1)}, bf16[768,128]{1,0:T(8,128)(2,1)S(1)}, u32[]{:S(2)}, u32[]{:S(2)}) collective-permute-start(bf16[768,128]{1,0:T(8,128)(2,1)S(1)} %shard_map.199.refs_7_.refs_0_), channel_id=1, source_target_pairs={{0,1},{1,0},{2,3},{3,2},{4,5},{5,4},{6,7},{7,6},{8,9},{9,8},{10,11... | collective-permute-start | bytes 589832 | tf_op jit(solution)/shard_map/ppermute | solution.py:373
  54.7 10.5 %collective-permute-start.11 = (bf16[448,128]{1,0:T(8,128)(2,1)S(1)}, bf16[448,128]{1,0:T(8,128)(2,1)S(1)}, u32[]{:S(2)}, u32[]{:S(2)}) collective-permute-start(bf16[448,128]{1,0:T(8,128)(2,1)S(1)} %get-tuple-element.117), channel_id=1, source_target_pairs={{0,4},{1,5},{2,6},{3,7},{4,0},{5,1},{6,2},{7,3},{8,12},{9,13},{10,... | collective-permute-start | bytes 344072 | tf_op jit(solution)/shard_map/ppermute | solution.py:373
  55.9 9.2 %collective-permute-start.12 = (bf16[448,128]{1,0:T(8,128)(2,1)S(1)}, bf16[448,128]{1,0:T(8,128)(2,1)S(1)}, u32[]{:S(2)}, u32[]{:S(2)}) collective-permute-start(bf16[448,128]{1,0:T(8,128)(2,1)S(1)} %get-tuple-element.118), channel_id=1, source_target_pairs={{0,20},{1,21},{2,22},{3,23},{4,16},{5,17},{6,18},{7,19},{8,28},{9,... | collective-permute-start | bytes 344072 | tf_op jit(solution)/shard_map/ppermute | solution.py:373
  57.9 7.3 %collective-permute-start.10 = (bf16[448,128]{1,0:T(8,128)(2,1)S(1)}, bf16[448,128]{1,0:T(8,128)(2,1)S(1)}, u32[]{:S(2)}, u32[]{:S(2)}) collective-permute-start(bf16[448,128]{1,0:T(8,128)(2,1)S(1)} %get-tuple-element.116.refs_8_), channel_id=1, source_target_pairs={{0,16},{1,17},{2,18},{3,19},{4,20},{5,21},{6,22},{7,23},{8,24},{9,... | collective-permute-start | bytes 344072 | tf_op jit(solution)/shard_map/ppermute | solution.py:373
  65.3 11.3 %collective-permute-start.16 = (bf16[768,128]{1,0:T(8,128)(2,1)S(1)}, bf16[768,128]{1,0:T(8,128)(2,1)S(1)}, u32[]{:S(2)}, u32[]{:S(2)}) collective-permute-start(bf16[768,128]{1,0:T(8,128)(2,1)S(1)} %shard_map.202.refs_0_), channel_id=1, source_target_pairs={{0,2},{1,3},{2,0},{3,1},{4,6},{5,7},{6,4},{7,5},{8,10},{9,11},{10,... | collective-permute-start | bytes 589832 | tf_op jit(solution)/shard_map/ppermute | solution.py:373
  68.0 6.1 %collective-permute-start.17 = (bf16[448,128]{1,0:T(8,128)(2,1)S(1)}, bf16[448,128]{1,0:T(8,128)(2,1)S(1)}, u32[]{:S(2)}, u32[]{:S(2)}) collective-permute-start(bf16[448,128]{1,0:T(8,128)(2,1)S(1)} %shard_map.203.refs_0_), channel_id=1, source_target_pairs={{0,1},{1,0},{2,3},{3,2},{4,5},{5,4},{6,7},{7,6},{8,9},{9,8},{10,11... | collective-permute-start | bytes 344072 | tf_op jit(solution)/shard_map/ppermute | solution.py:373
  76.7 10.9 %collective-permute-start.20 = (bf16[768,128]{1,0:T(8,128)(2,1)S(1)}, bf16[768,128]{1,0:T(8,128)(2,1)S(1)}, u32[]{:S(2)}, u32[]{:S(2)}) collective-permute-start(bf16[768,128]{1,0:T(8,128)(2,1)S(1)} %shard_map.204.refs_1_), channel_id=1, source_target_pairs={{0,20},{1,21},{2,22},{3,23},{4,16},{5,17},{6,18},{7,19},{8,28},{9,... | collective-permute-start | bytes 589832 | tf_op jit(solution)/shard_map/ppermute | solution.py:373
  78.2 10.1 %collective-permute-start.19 = (bf16[768,128]{1,0:T(8,128)(2,1)S(1)}, bf16[768,128]{1,0:T(8,128)(2,1)S(1)}, u32[]{:S(2)}, u32[]{:S(2)}) collective-permute-start(bf16[768,128]{1,0:T(8,128)(2,1)S(1)} %shard_map.204.refs_1_), channel_id=1, source_target_pairs={{0,4},{1,5},{2,6},{3,7},{4,0},{5,1},{6,2},{7,3},{8,12},{9,13},{10,... | collective-permute-start | bytes 589832 | tf_op jit(solution)/shard_map/ppermute | solution.py:373
  79.5 8.8 %collective-permute-start.18 = (bf16[768,128]{1,0:T(8,128)(2,1)S(1)}, bf16[768,128]{1,0:T(8,128)(2,1)S(1)}, u32[]{:S(2)}, u32[]{:S(2)}) collective-permute-start(bf16[768,128]{1,0:T(8,128)(2,1)S(1)} %shard_map.204.refs_1_), channel_id=1, source_target_pairs={{0,16},{1,17},{2,18},{3,19},{4,20},{5,21},{6,22},{7,23},{8,24},{9,... | collective-permute-start | bytes 589832 | tf_op jit(solution)/shard_map/ppermute | solution.py:373
  80.3 7.3 %collective-permute-start.21 = (bf16[448,128]{1,0:T(8,128)(2,1)S(1)}, bf16[448,128]{1,0:T(8,128)(2,1)S(1)}, u32[]{:S(2)}, u32[]{:S(2)}) collective-permute-start(bf16[448,128]{1,0:T(8,128)(2,1)S(1)} %shard_map.205.refs_0_), channel_id=1, source_target_pairs={{0,2},{1,3},{2,0},{3,1},{4,6},{5,7},{6,4},{7,5},{8,10},{9,11},{10,... | collective-permute-start | bytes 344072 | tf_op jit(solution)/shard_map/ppermute | solution.py:373
  88.4 9.1 %collective-permute-start.22 = (bf16[3072,128]{1,0:T(8,128)(2,1)S(1)}, bf16[3072,128]{1,0:T(8,128)(2,1)S(1)}, u32[]{:S(2)}, u32[]{:S(2)}) collective-permute-start(bf16[3072,128]{1,0:T(8,128)(2,1)S(1)} %shard_map.206.refs_1_), channel_id=1, source_target_pairs={{0,8},{1,9},{2,10},{3,11},{4,12},{5,13},{6,14},{7,15},{8,0},{9,1},... | collective-permute-start | bytes 2359304 | tf_op jit(solution)/shard_map/ppermute | solution.py:373
  88.5 6.9 %collective-permute-start.25 = (bf16[448,128]{1,0:T(8,128)(2,1)S(1)}, bf16[448,128]{1,0:T(8,128)(2,1)S(1)}, u32[]{:S(2)}, u32[]{:S(2)}) collective-permute-start(bf16[448,128]{1,0:T(8,128)(2,1)S(1)} %shard_map.207.refs_1_), channel_id=1, source_target_pairs={{0,20},{1,21},{2,22},{3,23},{4,16},{5,17},{6,18},{7,19},{8,28},{9,... | collective-permute-start | bytes 344072 | tf_op jit(solution)/shard_map/ppermute | solution.py:373
  90.0 7.5 %collective-permute-start.24 = (bf16[448,128]{1,0:T(8,128)(2,1)S(1)}, bf16[448,128]{1,0:T(8,128)(2,1)S(1)}, u32[]{:S(2)}, u32[]{:S(2)}) collective-permute-start(bf16[448,128]{1,0:T(8,128)(2,1)S(1)} %shard_map.207.refs_1_), channel_id=1, source_target_pairs={{0,4},{1,5},{2,6},{3,7},{4,0},{5,1},{6,2},{7,3},{8,12},{9,13},{10,... | collective-permute-start | bytes 344072 | tf_op jit(solution)/shard_map/ppermute | solution.py:373
  91.0 6.4 %collective-permute-start.23 = (bf16[448,128]{1,0:T(8,128)(2,1)S(1)}, bf16[448,128]{1,0:T(8,128)(2,1)S(1)}, u32[]{:S(2)}, u32[]{:S(2)}) collective-permute-start(bf16[448,128]{1,0:T(8,128)(2,1)S(1)} %shard_map.207.refs_1_), channel_id=1, source_target_pairs={{0,16},{1,17},{2,18},{3,19},{4,20},{5,21},{6,22},{7,23},{8,24},{9,... | collective-permute-start | bytes 344072 | tf_op jit(solution)/shard_map/ppermute | solution.py:373
  97.5 1.9 %collective-permute-start.26 = (bf16[1792,128]{1,0:T(8,128)(2,1)S(1)}, bf16[1792,128]{1,0:T(8,128)(2,1)S(1)}, u32[]{:S(2)}, u32[]{:S(2)}) collective-permute-start(bf16[1792,128]{1,0:T(8,128)(2,1)S(1)} %shard_map.208.refs_3_), channel_id=1, source_target_pairs={{0,8},{1,9},{2,10},{3,11},{4,12},{5,13},{6,14},{7,15},{8,0},{9,1},... | collective-permute-start | bytes 1376264 | tf_op jit(solution)/shard_map/ppermute | solution.py:373

commit v6 on v5

--- a/solution.py
+++ b/solution.py
@@ -11,10 +11,11 @@
 norm_epsilon = 1e-06
 inv_root_two = 0.7071067811865476
 inv_root_tau = 0.3989422804014327
+log2_e = 1.4426950408889634
 
 LANES = 128
 EDGE = 8
-BAND = 16
+BAND = 32
 AXES = ("gy", "gx", "rep")
 f32 = jnp.float32
 bf16 = jnp.bfloat16
@@ -92,8 +93,8 @@
     for b in range(7):
         scale = []
         for a in range(7):
-            tap = (6 - a) * 7 + 6 - b if flip else a * 7 + b
-            scale.append(jnp.broadcast_to(kernel[pl.ds(tap, 1), lanes(slab)], (8, LANES)))
+            i, j = (6 - a, 6 - b) if flip else (a, b)
+            scale.append(jnp.broadcast_to(kernel[i, j : j + 1, lanes(slab)], (8, LANES)))
         for r in range(BAND + 6):
             x = pad[slab, row + r, pl.ds(col + EDGE - 3 + b, 8), :]
             for a in range(7):
@@ -103,6 +104,10 @@
     return acc
 
 
+def line(ref, at=slice(None)):
+    return ref[at].reshape(1, -1)
+
+
 def conv_norm_kernel(
     tile, top, bottom, left, right, kernel, bias, gain, shift, normed_ref, inv_ref, ln_ref, pad, depth
 ):
@@ -111,7 +116,7 @@
 
     def piece(slab, col, row):
         acc = taps(pad, kernel, slab, col, row, False)
-        add = jnp.broadcast_to(bias[:, lanes(slab)], (8, LANES))
+        add = jnp.broadcast_to(line(bias, lanes(slab)), (8, LANES))
         for i in range(BAND):
             at = pl.ds(pl.multiple_of((row + i) * cols + col, 8), 8)
             depth[at, lanes(slab)] = acc[i] + add
@@ -127,16 +132,21 @@
         normed = centred * inv
         normed_ref[at, :] = normed
         inv_ref[at, :] = jnp.broadcast_to(inv, (block, LANES))
-        ln_ref[at, :] = (normed * gain[...] + shift[...]).astype(bf16)
+        ln_ref[at, :] = (normed * line(gain) + line(shift)).astype(bf16)
         return _
 
     lax.fori_loop(0, rows * cols // block, norm, 0)
 
 
 def gelu_pair(u):
-    cdf = 0.5 * (1.0 + lax.erf(u * inv_root_two))
-    pdf = jnp.exp(-0.5 * u * u) * inv_root_tau
-    return u * cdf, cdf + u * pdf
+    bell = jnp.exp2(u * u * (-0.5 * log2_e))
+    t = 1.0 / (1.0 + jnp.abs(u) * (0.3275911 * inv_root_two))
+    poly = 0.5 * 1.061405429
+    for term in (-1.453152027, 1.421413741, -0.284496736, 0.254829592):
+        poly = poly * t + 0.5 * term
+    tail = poly * t * bell
+    cdf = jnp.where(u < 0.0, tail, 1.0 - tail)
+    return u * cdf, cdf + u * (bell * inv_root_tau)
 
 
 def fold(x):
@@ -156,7 +166,7 @@
         pre, d_hidden = ahead
         if s + 1 < count:
             ahead = products(s + 1)
-        act, slope = gelu_pair(pre + b_in[:, base + s * sub : base + (s + 1) * sub])
+        act, slope = gelu_pair(pre + line(b_in, pl.ds(base + s * sub, sub)))
         d_pre = d_hidden * slope
         gbin[:, s * sub : (s + 1) * sub] += fold(d_pre)
         hid_ref[:, s * sub : (s + 1) * sub] = act.astype(bf16)
@@ -198,7 +208,7 @@
     def step(i, _):
         at = pl.ds(pl.multiple_of(i * MLP_BLOCK, MLP_BLOCK), MLP_BLOCK)
         ln = ln_ref[at, :]
-        d_branch = (scale[...] * cot[at, :].astype(f32)).astype(bf16)
+        d_branch = (line(scale) * cot[at, :].astype(f32)).astype(bf16)
         hidden, d_pre, branch, d_norm = mlp_block(
             ln, d_branch, w_in, w_out, b_in, base, width, hid_ref, dpre_ref, gbin
         )
@@ -227,20 +237,20 @@
         at = pl.ds(pl.multiple_of(i * MLP_BLOCK, MLP_BLOCK), MLP_BLOCK)
         ln = ln_ref[at, :]
         cot32 = cot[at, :].astype(f32)
-        d_branch32 = scale[...] * cot32
+        d_branch32 = line(scale) * cot32
         d_branch = d_branch32.astype(bf16)
         hidden, d_pre, branch, d_norm = mlp_block(
             ln, d_branch, w_in, w_out, b_in, base, width, hid_ref, dpre_ref, gbin
         )
         gwin[...] += dot(d_pre, ln, TN)
         gwout[...] += dot(d_branch, hidden, TN)
-        branch = branch + branch_ref[at, :] + b_out[...]
-        result[at, :] = (page[at, :].astype(f32) + scale[...] * branch).astype(bf16)
+        branch = branch + branch_ref[at, :] + line(b_out)
+        result[at, :] = (page[at, :].astype(f32) + line(scale) * branch).astype(bf16)
         d_norm = d_norm + dnorm_ref[at, :]
         normed = normed_ref[at, :]
         inv = inv_ref[at, 0:1]
         weighted = d_norm * normed
-        s = d_norm * gain[...]
+        s = d_norm * line(gain)
         mean_s = jnp.mean(s, axis=-1, keepdims=True)
         mean_sn = jnp.mean(s * normed, axis=-1, keepdims=True)
         d_depth = (inv * (s - mean_s - normed * mean_sn)).astype(bf16)
@@ -460,32 +470,29 @@
     factor, widths, core, own_a, other_a, own_b, other_b,
     win, wout, gk, scale, b_out, gain, shift, bias, b_in,
 ):
-    channels = wout.shape[0]
-
-    def store(firsts, seconds):
-        base = 0
-        for width, first, second in zip(widths, firsts, seconds):
-            part = first.shape[0] // 4
-            block = width * channels // LANES // 4
-
-            def rows(ref, at):
-                start = at // block * part + at % block
-                return ref[start : start + LANES, :].astype(f32) * factor
-
-            for j in range(channels // LANES):
-                for i in range(0, width, LANES):
-                    win[base + i : base + i + LANES, j * LANES : (j + 1) * LANES] = rows(first, j * width + i)
-            for j in range(width // LANES):
-                for i in range(0, channels, LANES):
-                    wout[i : i + LANES, base + j * LANES : base + (j + 1) * LANES] = rows(
-                        second, j * channels + i
-                    )
-            base += width
-        slabs = channels // LANES
+    channels, unit = wout.shape
+    slabs = channels // LANES
+
+    def rows(ref, width, at):
+        part, block = ref.shape[0] // 4, width * slabs // 4
+        start = at // block * part + at % block
+        return ref[start : start + LANES, :].astype(f32) * factor
+
+    def store(first, second, width, offset):
+        for j in range(slabs):
+            for i in range(0, unit, LANES):
+                win[i : i + LANES, j * LANES : (j + 1) * LANES] = rows(first, width, j * width + offset + i)
+        for j in range(unit // LANES):
+            for i in range(0, channels, LANES):
+                wout[i : i + LANES, j * LANES : (j + 1) * LANES] = rows(
+                    second, width, (offset // LANES + j) * channels + i
+                )
+
+    def store_small(first):
         for slab in range(slabs):
             at = slice(slab * LANES, (slab + 1) * LANES)
-            start = slab * part + block
-            values = firsts[1][start : start + SMALL, :].astype(f32) * factor
+            start = slab * (first.shape[0] // 4) + widths[1] * slabs // 4
+            values = first[start : start + SMALL, :].astype(f32) * factor
             for j in range(7):
                 gk[j, :, at] = values[7 * j : 7 * j + 7]
             for j, ref in enumerate((scale, b_out, gain, shift, bias)):
@@ -494,8 +501,36 @@
                 lane = (j * slabs + slab) * LANES
                 b_in[lane : lane + LANES] = values[54 + j]
 
-    pl.when(core[0] == 0)(lambda: store((own_a, own_b), (other_a, other_b)))
-    pl.when(core[0] != 0)(lambda: store((other_a, other_b), (own_a, own_b)))
+    is_first = core[0] == 0
+    step = pl.program_id(0)
+    for i in range(sum(widths) // unit):
+        offset, halves = i * unit, (own_a, other_a)
+        width = widths[0]
+        if offset >= widths[0]:
+            offset, halves, width = offset - widths[0], (own_b, other_b), widths[1]
+        here = step == i
+        pl.when(here & is_first)(functools.partial(store, *halves, width, offset))
+        pl.when(here & ~is_first)(functools.partial(store, *halves[::-1], width, offset))
+    pl.when((step == 0) & is_first)(lambda: store_small(own_b))
+    pl.when((step == 0) & ~is_first)(lambda: store_small(other_b))
+
+
+def finish(factor, widths, channels, core, *halves):
+    hid, unit = sum(widths), widths[1]
+    vmem = pl.BlockSpec(memory_space=pltpu.VMEM)
+    outs = [(hid, channels), (channels, hid), (7, 7, channels)] + [(channels,)] * 5 + [(hid,)]
+    return pl.pallas_call(
+        functools.partial(finish_kernel, factor, widths),
+        grid=(hid // unit,),
+        out_shape=[jax.ShapeDtypeStruct(shape, f32) for shape in outs],
+        in_specs=[pl.BlockSpec(memory_space=pltpu.SMEM)] + [vmem] * len(halves),
+        out_specs=[
+            pl.BlockSpec((unit, channels), lambda i: (i, 0)),
+            pl.BlockSpec((channels, unit), lambda i: (0, i)),
+        ]
+        + [vmem] * 7,
+        compiler_params=pltpu.CompilerParams(vmem_limit_bytes=24 << 20),
+    )(core, *halves)
 
 
 def shards(
@@ -517,9 +552,6 @@
     tile = pages.reshape(rows, cols, channels)
     page = pages.reshape(pixels, channels)
     cot = cotangent.reshape(pixels, channels)
-    kernel = conv_kernel.reshape(49, channels)
-    row = lambda v: v.reshape(1, -1)
-    gain, shift, scale = row(norm_gain), row(norm_bias), row(layer_scale)
     pad = ((channels // LANES, rows + 6, EDGE + cols + 8, LANES), f32)
     full = (pixels, channels)
 
@@ -534,7 +566,7 @@
         conv_norm_kernel,
         [(full, f32), ((pixels, LANES), f32), (full, bf16)],
         [pad, (full, f32)],
-        (tile, *around, kernel, row(conv_bias), gain, shift),
+        (tile, *around, conv_kernel, conv_bias, norm_gain, norm_bias),
         conv_flops,
     )
     grads = lambda width: [
@@ -547,7 +579,7 @@
     packed = lambda width: [((width * channels // LANES, LANES), bf16)] * 2 + [((1, width), f32)]
     core_flip = [("gy", 0)]
     mlp_flops = 12 * pixels * channels * hid
-    weights = (w_in, w_out, row(b_in), scale)
+    weights = (w_in, w_out, b_in, layer_scale)
     first, second = hid * 2 // 3, hid // 3
     branch, d_norm, keep_a, send_a, gbin_a = call(
         functools.partial(mlp_first_kernel, 0, first),
@@ -562,7 +594,7 @@
         functools.partial(mlp_second_kernel, first, second),
         [(full, bf16), (full, bf16)] + packed(second) + [((8, channels), f32)],
         grads(second) + [((8, 8, channels), f32)],
-        (core, ln_out, cot, *weights, row(b_out), gain, page, normed, inv, branch, d_norm),
+        (core, ln_out, cot, *weights, b_out, norm_gain, page, normed, inv, branch, d_norm),
         mlp_flops,
         1,
     )
@@ -592,7 +624,7 @@
         conv_grad_kernel,
         [(full, bf16)],
         [pad, (full, f32)],
-        (d_tile, *d_around, kernel, cot),
+        (d_tile, *d_around, conv_kernel, cot),
         conv_flops,
         0,
         (part_a, parts_b[1]),
@@ -608,14 +640,8 @@
     half_b = join(mine, *got_b)
     got_b = [half_b, exchange(half_b, core_flip)]
     factor = float(pixels * lax.axis_size("gy") * lax.axis_size("gx") * lax.axis_size("rep")) ** (-0.5)
-    line = ((channels,), f32)
-    win, wout, gk, g_scale, g_bout, g_gain, g_shift, g_bias, g_bin = call(
-        functools.partial(finish_kernel, factor, (first, second)),
-        [((hid, channels), f32), ((channels, hid), f32), ((7, 7, channels), f32)] + [line] * 5 + [((hid,), f32)],
-        [],
-        (core, *got_a, *got_b),
-        SUM_FLOPS,
-        1,
+    win, wout, gk, g_scale, g_bout, g_gain, g_shift, g_bias, g_bin = finish(
+        factor, (first, second), channels, core, *got_a, *got_b
     )
     return (
         result.reshape(pages.shape),

time: 102 us -> 104 us (1.020)
  local copies, waits for them, and re-layouts: 4.71 us -> 1.29 us
  waiting for transfers between devices: 22.8 us -> 25.6 us
  Pallas kernels: 39.8 us -> 41.8 us
    reshape x7 -> x0, local copies, waits for them, and re-layouts: 3.45 us -> none  [the longest x6 3.43 us: shards(): row = lambda v: v.reshape(1, -1)]
    ppermute x6, waiting for transfers between devices: 0.02 us -> 2.81 us  [swap_edges(): got.append(lax.ppermute(jnp.where(is_high, high, low), axis, pairs))]
    pallas_call x0 -> x1, Pallas kernels: none -> 2.69 us  [finish(): pl.pallas_call(functools.partial(finish_kernel, factor, widths), grid=(hi...]
    pallas_call x16 -> x15, Pallas kernels: 39.8 us -> 39.1 us  [call(): pl.pallas_call(kernel, out_shape=[jax.ShapeDtypeStruct(shape, dtype) for...]
  transfers between devices with their start and end apart: 27 -> 27, of which waited for: 7 -> 8; matrix products, arithmetic and copies ran while one was open for 5% -> 1% of each run, Pallas kernels for 21% -> 21%
where the time goes in v6:
time: 104 us
  Pallas kernels  41.8 us (40%)
  starting transfers between devices  32.9 us (32%)
  waiting for transfers between devices  25.6 us (25%)
  other arithmetic  1.55 us (1%)
  local copies, waits for them, and re-layouts  1.29 us (1%)
  between operations  1.15 us (1%)
    pallas_call x15, Pallas kernels, call(): pl.pallas_call(kernel, out_shape=[jax.ShapeDtypeStruct(shape, dtype) for...  39.1 us
    ppermute x21, starting transfers between devices, exchange(): return lax.ppermute(x, AXES, perm)  26.7 us
    ppermute x21, waiting for transfers between devices, exchange(): return lax.ppermute(x, AXES, perm)  22.8 us
    ppermute x6, starting transfers between devices, swap_edges(): got.append(lax.ppermute(jnp.where(is_high, high, low), axis, pairs))  6.11 us
    ppermute x6, waiting for transfers between devices, swap_edges(): got.append(lax.ppermute(jnp.where(is_high, high, low), axis, pairs))  2.81 us
    pallas_call x1, Pallas kernels, finish(): pl.pallas_call(functools.partial(finish_kernel, factor, widths), grid=(hi...  2.69 us
  transfers between devices with their start and end apart: 27, of which 8 were waited for; matrix products, arithmetic and copies ran while one was open for 1% of the time, Pallas kernels for 21%

profile of v6, /device:TPU:0, one launch (start us, length us, event | category | flops | bytes accessed | tf_op | source)
XLA Modules:
  0.0 104.2 jit_solution(5677236693231316627)
XLA Ops:
  0.6 0.0 copy-start
  0.7 1.0 broadcast_select_fusion.11
  1.8 0.5 collective-permute-start.1
  2.3 0.7 collective-permute-start
  2.9 1.1 %fusion.1 = (bf16[32,3,384]{2,1,0:T(4,128)(2,1)S(1)}, bf16[32,3,384]{2,1,0:T(4,128)(2,1)S(1)}) fusion(bf16[32,32,384]{2,1,0:T(8,128)(2,1)} %bitcast.10), kind=kLoop, calls=%fused_computation.15 | loop fusion | bytes 294912 | tf_op jit(solution)/shard_map/slice | solution.py:53
  4.0 0.0 collective-permute-done.1
  4.1 0.2 maximum_select_fusion
  4.3 2.6 %collective-permute-start.2 = (bf16[38,3,384]{2,1,0:T(4,128)(2,1)S(1)}, bf16[38,3,384]{2,1,0:T(4,128)(2,1)S(1)}, u32[]{:S(2)}, u32[]{:S(2)}) collective-permute-start(bf16[38,3,384]{2,1,0:T(4,128)(2,1)S(1)} %maximum_select_fusion), channel_id=1, source_target_pairs={{0,4},{4,0},{1,5},{5,1},{2,6},{6,2},{3,7},{7,3},{8,12},{12,8},{9,1... | collective-permute-start | bytes 262664 | tf_op jit(solution)/shard_map/ppermute | solution.py:46
  6.9 2.8 %collective-permute-done.2 = bf16[38,3,384]{2,1,0:T(4,128)(2,1)S(1)} collective-permute-done((bf16[38,3,384]{2,1,0:T(4,128)(2,1)S(1)}, bf16[38,3,384]{2,1,0:T(4,128)(2,1)S(1)}, u32[]{:S(2)}, u32[]{:S(2)}) %collective-permute-start.2) | collective-permute-done | bytes 87584 | tf_op jit(solution)/shard_map/ppermute | solution.py:46
  9.7 0.1 broadcast_select_fusion.2
  9.8 0.0 copy-start.1
  9.8 0.0 copy-start.2
  9.8 0.0 copy-start.3
  9.9 0.0 copy-start.5
  9.9 0.0 copy-start.9
  9.9 7.3 %shard_map.194 = (f32[1024,384]{1,0:T(8,128)S(1)}, f32[1024,128]{1,0:T(8,128)S(1)}, bf16[1024,384]{1,0:T(8,128)(2,1)S(1)}) custom-call(bf16[32,32,384]{2,1,0:T(8,128)(2,1)S(1)} %bitcast.11, bf16[3,32,384]{2,1,0:T(8,128)(2,1)S(1)} %get-tuple-element.158.refs_1_.refs_2_, bf16[3,32,384]{2,1,0:T(8,128)(2,1)S(1)} %get-tuple-element.157.refs_2_.refs_3_, ...), custom_call_target="tpu_custom_call" | custom-call | flops 2312110080 | bytes 2257920 | tf_op jit(solution)/shard_map/pallas_call | solution.py:350
  17.3 0.0 copy-start.10
  17.3 9.7 %shard_map.195 = (f32[1024,384]{1,0:T(8,128)S(1)}, f32[1024,384]{1,0:T(8,128)S(1)}, bf16[3072,128]{1,0:T(8,128)(2,1)S(1)}, bf16[3072,128]{1,0:T(8,128)(2,1)S(1)}, f32[1,1024]{1,0:T(1,128)S(1)}) custom-call(s32[1]{0:T(128)} %bitcast.refs_0_.core, bf16[1024,384]{1,0:T(8,128)(2,1)S(1)} %get-tuple-element.83.refs_1_, bf16[1024,384]{1,0:T(8,128)(2,1)S(1)} %bitcast.17, ...), custom_call_target="tpu_custom_call" | custom-call | flops 7247757312 | bytes 7077888 | tf_op jit(solution)/shard_map/pallas_call | solution.py:350
  27.0 3.8 %collective-permute-start.3 = (bf16[3072,128]{1,0:T(8,128)(2,1)S(1)}, bf16[3072,128]{1,0:T(8,128)(2,1)S(1)}, u32[]{:S(2)}, u32[]{:S(2)}) collective-permute-start(bf16[3072,128]{1,0:T(8,128)(2,1)S(1)} %get-tuple-element.91), channel_id=1, source_target_pairs={{0,8},{1,9},{2,10},{3,11},{4,12},{5,13},{6,14},{7,15},{8,0},{9,1},... | collective-permute-start | bytes 2359304 | tf_op jit(solution)/shard_map/ppermute | solution.py:383
  30.8 7.6 %shard_map.196 = (bf16[1024,384]{1,0:T(8,128)(2,1)}, bf16[1024,384]{1,0:T(8,128)(2,1)S(1)}, bf16[1536,128]{1,0:T(8,128)(2,1)S(1)}, bf16[1536,128]{1,0:T(8,128)(2...) custom-call(s32[1]{0:T(128)} %bitcast.refs_0_.core, bf16[1024,384]{1,0:T(8,128)(2,1)S(1)} %get-tuple-element.83.refs_1_, ...), custom_call_target="tpu_custom_call" | custom-call | flops 7247757312 | bytes 7077888 | tf_op jit(solution)/shard_map/pallas_call | solution.py:350
  38.4 0.1 collective-permute-start.14
  38.5 0.7 collective-permute-start.13
  39.2 0.1 fusion
  39.3 0.3 shard_map.197
  39.6 1.8 %collective-permute-start.5 = (bf16[768,128]{1,0:T(8,128)(2,1)S(1)}, bf16[768,128]{1,0:T(8,128)(2,1)S(1)}, u32[]{:S(2)}, u32[]{:S(2)}) collective-permute-start(bf16[768,128]{1,0:T(8,128)(2,1)S(1)} %get-tuple-element.98), channel_id=1, source_target_pairs={{0,4},{1,5},{2,6},{3,7},{4,0},{5,1},{6,2},{7,3},{8,12},{9,13},{10,... | collective-permute-start | bytes 589832 | tf_op jit(solution)/shard_map/ppermute | solution.py:383
  41.4 3.5 %collective-permute-start.6 = (bf16[768,128]{1,0:T(8,128)(2,1)S(1)}, bf16[768,128]{1,0:T(8,128)(2,1)S(1)}, u32[]{:S(2)}, u32[]{:S(2)}) collective-permute-start(bf16[768,128]{1,0:T(8,128)(2,1)S(1)} %get-tuple-element.99), channel_id=1, source_target_pairs={{0,20},{1,21},{2,22},{3,23},{4,16},{5,17},{6,18},{7,19},{8,28},{9,... | collective-permute-start | bytes 589832 | tf_op jit(solution)/shard_map/ppermute | solution.py:383
  44.9 0.1 collective-permute-start.4
  45.0 0.0 collective-permute-done.14
  45.0 1.2 %collective-permute-start.7 = (bf16[1536,128]{1,0:T(8,128)(2,1)S(1)}, bf16[1536,128]{1,0:T(8,128)(2,1)S(1)}, u32[]{:S(2)}, u32[]{:S(2)}) collective-permute-start(bf16[1536,128]{1,0:T(8,128)(2,1)S(1)} %get-tuple-element.106), channel_id=1, source_target_pairs={{0,8},{1,9},{2,10},{3,11},{4,12},{5,13},{6,14},{7,15},{8,0},{9,1},... | collective-permute-start | bytes 1179656 | tf_op jit(solution)/shard_map/ppermute | solution.py:383
  46.3 0.2 maximum_select_fusion.1
  46.4 1.6 %collective-permute-start.15 = (bf16[38,3,384]{2,1,0:T(4,128)(2,1)S(1)}, bf16[38,3,384]{2,1,0:T(4,128)(2,1)S(1)}, u32[]{:S(2)}, u32[]{:S(2)}) collective-permute-start(bf16[38,3,384]{2,1,0:T(4,128)(2,1)S(1)} %maximum_select_fusion.1), channel_id=1, source_target_pairs={{0,4},{4,0},{1,5},{5,1},{2,6},{6,2},{3,7},{7,3},{8,12},{12,8},{9,1... | collective-permute-start | bytes 262664 | tf_op jit(solution)/shard_map/ppermute | solution.py:46
  48.0 6.9 %shard_map.198 = (bf16[256,128]{1,0:T(8,128)(2,1)S(1)}, bf16[256,128]{1,0:T(8,128)(2,1)S(1)}) custom-call(s32[1]{0:T(128)} %bitcast.refs_0_.core, bf16[32,32,384]{2,1,0:T(8,128)(2,1)S(1)} %bitcast.13, bf16[3,32,384]{2,1,0:T(8,128)(2,1)S(1)} %get-tuple-element.158.refs_1_.refs_2_, bf16[3,32,384]{2,1,0:T(8,128)(2,1)S(1)} %get-tuple-element.157.refs_2_.refs_3_, ...), custom_call_target="tpu_custom_call" | custom-call | flops 2312110080 | bytes 2257920 | tf_op jit(solution)/shard_map/pallas_call | solution.py:350
  55.0 0.1 collective-permute-start.9
  55.0 0.1 broadcast_select_fusion
  55.1 0.1 shard_map.199.refs_7_.refs_0_
  55.3 1.6 %collective-permute-start.8 = (bf16[768,128]{1,0:T(8,128)(2,1)S(1)}, bf16[768,128]{1,0:T(8,128)(2,1)S(1)}, u32[]{:S(2)}, u32[]{:S(2)}) collective-permute-start(bf16[768,128]{1,0:T(8,128)(2,1)S(1)} %shard_map.199.refs_7_.refs_0_), channel_id=1, source_target_pairs={{0,1},{1,0},{2,3},{3,2},{4,5},{5,4},{6,7},{7,6},{8,9},{9,8},{10,11... | collective-permute-start | bytes 589832 | tf_op jit(solution)/shard_map/ppermute | solution.py:383
  56.9 0.1 shard_map.200
  57.0 0.6 collective-permute-start.11
  57.6 2.1 %collective-permute-start.12 = (bf16[448,128]{1,0:T(8,128)(2,1)S(1)}, bf16[448,128]{1,0:T(8,128)(2,1)S(1)}, u32[]{:S(2)}, u32[]{:S(2)}) collective-permute-start(bf16[448,128]{1,0:T(8,128)(2,1)S(1)} %get-tuple-element.118), channel_id=1, source_target_pairs={{0,20},{1,21},{2,22},{3,23},{4,16},{5,17},{6,18},{7,19},{8,28},{9,... | collective-permute-start | bytes 344072 | tf_op jit(solution)/shard_map/ppermute | solution.py:383
  59.7 0.9 collective-permute-start.10
  60.6 6.7 %shard_map.201 = bf16[1024,384]{1,0:T(8,128)(2,1)} custom-call(bf16[32,32,384]{2,1,0:T(8,128)(2,1)S(1)} %bitcast.16, bf16[3,32,384]{2,1,0:T(8,128)(2,1)S(1)} %get-tuple-element.156.refs_1_, bf16[3,32,384]{2,1,0:T(8,128)(2,1)S(1)} %get-tuple-element.155.refs_2_, bf16[38,3,384]{2,1,0:T(4,128)(2,1)S(1)} %get-tuple-element.160.refs_3_, ...), custom_call_target="tpu_custom_call" | custom-call | flops 2312110080 | bytes 2257920 | tf_op jit(solution)/shard_map/pallas_call | solution.py:350
  67.3 0.1 shard_map.202.refs_0_
  67.4 2.6 %collective-permute-start.16 = (bf16[768,128]{1,0:T(8,128)(2,1)S(1)}, bf16[768,128]{1,0:T(8,128)(2,1)S(1)}, u32[]{:S(2)}, u32[]{:S(2)}) collective-permute-start(bf16[768,128]{1,0:T(8,128)(2,1)S(1)} %shard_map.202.refs_0_), channel_id=1, source_target_pairs={{0,2},{1,3},{2,0},{3,1},{4,6},{5,7},{6,4},{7,5},{8,10},{9,11},{10,... | collective-permute-start | bytes 589832 | tf_op jit(solution)/shard_map/ppermute | solution.py:383
  70.0 0.1 shard_map.203.refs_0_
  70.1 1.0 collective-permute-start.17
  71.1 5.1 %collective-permute-done.17.refs_1_ = bf16[448,128]{1,0:T(8,128)(2,1)S(1)} collective-permute-done((bf16[448,128]{1,0:T(8,128)(2,1)S(1)}, bf16[448,128]{1,0:T(8,128)(2,1)S(1)}, u32[]{:S(2)}, u32[]{:S(2)}) %collective-permute-start.17) | collective-permute-done | bytes 114720 | tf_op jit(solution)/shard_map/ppermute | solution.py:383
  76.2 2.5 %collective-permute-done.16.refs_1_ = bf16[768,128]{1,0:T(8,128)(2,1)S(1)} collective-permute-done((bf16[768,128]{1,0:T(8,128)(2,1)S(1)}, bf16[768,128]{1,0:T(8,128)(2,1)S(1)}, u32[]{:S(2)}, u32[]{:S(2)}) %collective-permute-start.16) | collective-permute-done | bytes 196640 | tf_op jit(solution)/shard_map/ppermute | solution.py:383
  78.8 0.1 shard_map.204.refs_1_
  78.8 1.3 %collective-permute-start.20 = (bf16[768,128]{1,0:T(8,128)(2,1)S(1)}, bf16[768,128]{1,0:T(8,128)(2,1)S(1)}, u32[]{:S(2)}, u32[]{:S(2)}) collective-permute-start(bf16[768,128]{1,0:T(8,128)(2,1)S(1)} %shard_map.204.refs_1_), channel_id=1, source_target_pairs={{0,20},{1,21},{2,22},{3,23},{4,16},{5,17},{6,18},{7,19},{8,28},{9,... | collective-permute-start | bytes 589832 | tf_op jit(solution)/shard_map/ppermute | solution.py:383
  80.1 1.4 %collective-permute-start.19 = (bf16[768,128]{1,0:T(8,128)(2,1)S(1)}, bf16[768,128]{1,0:T(8,128)(2,1)S(1)}, u32[]{:S(2)}, u32[]{:S(2)}) collective-permute-start(bf16[768,128]{1,0:T(8,128)(2,1)S(1)} %shard_map.204.refs_1_), channel_id=1, source_target_pairs={{0,4},{1,5},{2,6},{3,7},{4,0},{5,1},{6,2},{7,3},{8,12},{9,13},{10,... | collective-permute-start | bytes 589832 | tf_op jit(solution)/shard_map/ppermute | solution.py:383
  81.5 0.9 collective-permute-start.18
  82.4 0.1 collective-permute-start.21
  82.5 7.2 %collective-permute-done.21.refs_1_ = bf16[448,128]{1,0:T(8,128)(2,1)S(1)} collective-permute-done((bf16[448,128]{1,0:T(8,128)(2,1)S(1)}, bf16[448,128]{1,0:T(8,128)(2,1)S(1)}, u32[]{:S(2)}, u32[]{:S(2)}) %collective-permute-start.21) | collective-permute-done | bytes 114720 | tf_op jit(solution)/shard_map/ppermute | solution.py:383
  89.7 0.7 collective-permute-done.19.refs_3_
  90.4 0.1 shard_map.206.own_a
  90.5 0.1 collective-permute-start.22
  90.6 1.2 %collective-permute-start.25 = (bf16[448,128]{1,0:T(8,128)(2,1)S(1)}, bf16[448,128]{1,0:T(8,128)(2,1)S(1)}, u32[]{:S(2)}, u32[]{:S(2)}) collective-permute-start(bf16[448,128]{1,0:T(8,128)(2,1)S(1)} %shard_map.207.refs_1_), channel_id=1, source_target_pairs={{0,20},{1,21},{2,22},{3,23},{4,16},{5,17},{6,18},{7,19},{8,28},{9,... | collective-permute-start | bytes 344072 | tf_op jit(solution)/shard_map/ppermute | solution.py:383
  91.9 1.4 %collective-permute-start.24 = (bf16[448,128]{1,0:T(8,128)(2,1)S(1)}, bf16[448,128]{1,0:T(8,128)(2,1)S(1)}, u32[]{:S(2)}, u32[]{:S(2)}) collective-permute-start(bf16[448,128]{1,0:T(8,128)(2,1)S(1)} %shard_map.207.refs_1_), channel_id=1, source_target_pairs={{0,4},{1,5},{2,6},{3,7},{4,0},{5,1},{6,2},{7,3},{8,12},{9,13},{10,... | collective-permute-start | bytes 344072 | tf_op jit(solution)/shard_map/ppermute | solution.py:383
  93.3 0.9 collective-permute-start.23
  94.2 3.4 %collective-permute-done.25.refs_4_ = bf16[448,128]{1,0:T(8,128)(2,1)S(1)} collective-permute-done((bf16[448,128]{1,0:T(8,128)(2,1)S(1)}, bf16[448,128]{1,0:T(8,128)(2,1)S(1)}, u32[]{:S(2)}, u32[]{:S(2)}) %collective-permute-start.25) | collective-permute-done | bytes 114720 | tf_op jit(solution)/shard_map/ppermute | solution.py:383
  97.6 2.0 %collective-permute-done.24.refs_3_ = bf16[448,128]{1,0:T(8,128)(2,1)S(1)} collective-permute-done((bf16[448,128]{1,0:T(8,128)(2,1)S(1)}, bf16[448,128]{1,0:T(8,128)(2,1)S(1)}, u32[]{:S(2)}, u32[]{:S(2)}) %collective-permute-start.24) | collective-permute-done | bytes 114720 | tf_op jit(solution)/shard_map/ppermute | solution.py:383
  99.6 0.1 collective-permute-start.26
  99.7 1.8 %collective-permute-done.26.other_b = bf16[1792,128]{1,0:T(8,128)(2,1)S(1)} collective-permute-done((bf16[1792,128]{1,0:T(8,128)(2,1)S(1)}, bf16[1792,128]{1,0:T(8,128)(2,1)S(1)}, u32[]{:S(2)}, u32[]{:S(2)}) %collective-permute-start.26) | collective-permute-done | bytes 458784 | tf_op jit(solution)/shard_map/ppermute | solution.py:383
  101.5 2.7 %shard_map.209 = (f32[1536,384]{1,0:T(8,128)}, f32[384,1536]{1,0:T(8,128)}, f32[7,7,384]{2,1,0:T(8,128)}, f32[384]{0:T(512)}, f32[384]{0:T(512)}, /*index=5*/f32...) custom-call(s32[1]{0:T(128)} %bitcast.refs_0_.core, bf16[3072,128]{1,0:T(8,128)(2,1)S(1)} %shard_map.206.own_a, ...), custom_call_target="tpu_custom_call" | custom-call | tf_op jit(solution)/shard_map/pallas_call | solution.py:522
  (41 shorter events, 0.3 us)
Async XLA Ops:
  0.6 9.1 %copy-start = (bf16[1,32,32,384]{3,2,1,0:T(8,128)(2,1)S(1)}, bf16[1,32,32,384]{3,2,1,0:T(8,128)(2,1)}, u32[]{:S(2)}) copy-start(bf16[1,32,32,384]{3,2,1,0:T(8,128)(2,1)} %param.11) | copy-start | bytes 2359300
  0.7 9.1 %copy-start.8 = (f32[384]{0:T(512)S(1)}, f32[384]{0:T(512)}, u32[]{:S(2)}) copy-start(f32[384]{0:T(512)} %refs_8_.3) | copy-start | bytes 4612
  0.7 9.1 %copy-start.4 = (f32[7,7,384]{2,1,0:T(8,128)S(1)}, f32[7,7,384]{2,1,0:T(8,128)}, u32[]{:S(2)}) copy-start(f32[7,7,384]{2,1,0:T(8,128)} %refs_5_.7) | copy-start | bytes 225796
  0.7 9.1 %copy-start.7 = (f32[384]{0:T(512)S(1)}, f32[384]{0:T(512)}, u32[]{:S(2)}) copy-start(f32[384]{0:T(512)} %refs_8_.2) | copy-start | bytes 4612
  0.7 9.1 %copy-start.6 = (f32[384]{0:T(512)S(1)}, f32[384]{0:T(512)}, u32[]{:S(2)}) copy-start(f32[384]{0:T(512)} %refs_6_.3) | copy-start | bytes 4612
  1.8 2.3 %collective-permute-start.1 = (bf16[3,32,384]{2,1,0:T(8,128)(2,1)S(1)}, bf16[3,32,384]{2,1,0:T(8,128)(2,1)S(1)}, u32[]{:S(2)}, u32[]{:S(2)}) collective-permute-start(bf16[3,32,384]{2,1,0:T(8,128)(2,1)S(1)} %get-tuple-element.153), channel_id=1, source_target_pairs={{0,8},{16,24},{8,0},{24,16},{1,9},{17,25},{9,1},{25,17},{2,10},{18... | collective-permute-start | bytes 221192 | tf_op jit(solution)/shard_map/ppermute | solution.py:46
  2.3 1.8 %collective-permute-start = (bf16[3,32,384]{2,1,0:T(8,128)(2,1)S(1)}, bf16[3,32,384]{2,1,0:T(8,128)(2,1)S(1)}, u32[]{:S(2)}, u32[]{:S(2)}) collective-permute-start(bf16[3,32,384]{2,1,0:T(8,128)(2,1)S(1)} %get-tuple-element.154), channel_id=1, source_target_pairs={{8,16},{16,8},{9,17},{17,9},{10,18},{18,10},{11,19},{19,11},{12,20... | collective-permute-start | bytes 221192 | tf_op jit(solution)/shard_map/ppermute | solution.py:46
  4.3 5.4 %collective-permute-start.2 = (bf16[38,3,384]{2,1,0:T(4,128)(2,1)S(1)}, bf16[38,3,384]{2,1,0:T(4,128)(2,1)S(1)}, u32[]{:S(2)}, u32[]{:S(2)}) collective-permute-start(bf16[38,3,384]{2,1,0:T(4,128)(2,1)S(1)} %maximum_select_fusion), channel_id=1, source_target_pairs={{0,4},{4,0},{1,5},{5,1},{2,6},{6,2},{3,7},{7,3},{8,12},{12,8},{9,1... | collective-permute-start | bytes 262664 | tf_op jit(solution)/shard_map/ppermute | solution.py:46
  9.8 7.4 %copy-start.1 = (bf16[1536,384]{1,0:T(8,128)(2,1)S(1)}, bf16[1536,384]{1,0:T(8,128)(2,1)}, u32[]{:S(2)}) copy-start(bf16[1536,384]{1,0:T(8,128)(2,1)} %refs_3_.3) | copy-start | bytes 3538948
  9.8 7.4 %copy-start.2 = (bf16[384,1536]{1,0:T(8,128)(2,1)S(1)}, bf16[384,1536]{1,0:T(8,128)(2,1)}, u32[]{:S(2)}) copy-start(bf16[384,1536]{1,0:T(8,128)(2,1)} %refs_4_.3) | copy-start | bytes 3538948
  9.8 7.4 %copy-start.3 = (bf16[1,32,32,384]{3,2,1,0:T(8,128)(2,1)S(1)}, bf16[1,32,32,384]{3,2,1,0:T(8,128)(2,1)}, u32[]{:S(2)}) copy-start(bf16[1,32,32,384]{3,2,1,0:T(8,128)(2,1)} %param.12) | copy-start | bytes 2359300
  9.9 7.4 %copy-start.5 = (f32[1536]{0:T(1024)S(1)}, f32[1536]{0:T(1024)}, u32[]{:S(2)}) copy-start(f32[1536]{0:T(1024)} %refs_5_.6) | copy-start | bytes 18436
  9.9 7.4 %copy-start.9 = (f32[384]{0:T(512)S(1)}, f32[384]{0:T(512)}, u32[]{:S(2)}) copy-start(f32[384]{0:T(512)} %refs_6_.5) | copy-start | bytes 4612
  17.3 13.6 %copy-start.10 = (f32[384]{0:T(512)S(1)}, f32[384]{0:T(512)}, u32[]{:S(2)}) copy-start(f32[384]{0:T(512)} %refs_7_.3) | copy-start | bytes 4612
  27.0 11.4 %collective-permute-start.3 = (bf16[3072,128]{1,0:T(8,128)(2,1)S(1)}, bf16[3072,128]{1,0:T(8,128)(2,1)S(1)}, u32[]{:S(2)}, u32[]{:S(2)}) collective-permute-start(bf16[3072,128]{1,0:T(8,128)(2,1)S(1)} %get-tuple-element.91), channel_id=1, source_target_pairs={{0,8},{1,9},{2,10},{3,11},{4,12},{5,13},{6,14},{7,15},{8,0},{9,1},... | collective-permute-start | bytes 2359304 | tf_op jit(solution)/shard_map/ppermute | solution.py:383
  38.4 6.5 %collective-permute-start.14 = (bf16[3,32,384]{2,1,0:T(8,128)(2,1)S(1)}, bf16[3,32,384]{2,1,0:T(8,128)(2,1)S(1)}, u32[]{:S(2)}, u32[]{:S(2)}) collective-permute-start(bf16[3,32,384]{2,1,0:T(8,128)(2,1)S(1)} %get-tuple-element.149), channel_id=1, source_target_pairs={{0,8},{16,24},{8,0},{24,16},{1,9},{17,25},{9,1},{25,17},{2,10},{18... | collective-permute-start | bytes 221192 | tf_op jit(solution)/shard_map/ppermute | solution.py:46
  38.5 7.7 %collective-permute-start.13 = (bf16[3,32,384]{2,1,0:T(8,128)(2,1)S(1)}, bf16[3,32,384]{2,1,0:T(8,128)(2,1)S(1)}, u32[]{:S(2)}, u32[]{:S(2)}) collective-permute-start(bf16[3,32,384]{2,1,0:T(8,128)(2,1)S(1)} %get-tuple-element.150), channel_id=1, source_target_pairs={{8,16},{16,8},{9,17},{17,9},{10,18},{18,10},{11,19},{19,11},{12,20... | collective-permute-start | bytes 221192 | tf_op jit(solution)/shard_map/ppermute | solution.py:46
  39.6 15.4 %collective-permute-start.5 = (bf16[768,128]{1,0:T(8,128)(2,1)S(1)}, bf16[768,128]{1,0:T(8,128)(2,1)S(1)}, u32[]{:S(2)}, u32[]{:S(2)}) collective-permute-start(bf16[768,128]{1,0:T(8,128)(2,1)S(1)} %get-tuple-element.98), channel_id=1, source_target_pairs={{0,4},{1,5},{2,6},{3,7},{4,0},{5,1},{6,2},{7,3},{8,12},{9,13},{10,... | collective-permute-start | bytes 589832 | tf_op jit(solution)/shard_map/ppermute | solution.py:383
  41.4 13.6 %collective-permute-start.6 = (bf16[768,128]{1,0:T(8,128)(2,1)S(1)}, bf16[768,128]{1,0:T(8,128)(2,1)S(1)}, u32[]{:S(2)}, u32[]{:S(2)}) collective-permute-start(bf16[768,128]{1,0:T(8,128)(2,1)S(1)} %get-tuple-element.99), channel_id=1, source_target_pairs={{0,20},{1,21},{2,22},{3,23},{4,16},{5,17},{6,18},{7,19},{8,28},{9,... | collective-permute-start | bytes 589832 | tf_op jit(solution)/shard_map/ppermute | solution.py:383
  44.9 10.0 %collective-permute-start.4 = (bf16[768,128]{1,0:T(8,128)(2,1)S(1)}, bf16[768,128]{1,0:T(8,128)(2,1)S(1)}, u32[]{:S(2)}, u32[]{:S(2)}) collective-permute-start(bf16[768,128]{1,0:T(8,128)(2,1)S(1)} %get-tuple-element.97.refs_10_), channel_id=1, source_target_pairs={{0,16},{1,17},{2,18},{3,19},{4,20},{5,21},{6,22},{7,23},{8,24},{9,... | collective-permute-start | bytes 589832 | tf_op jit(solution)/shard_map/ppermute | solution.py:383
  45.0 10.0 %collective-permute-start.7 = (bf16[1536,128]{1,0:T(8,128)(2,1)S(1)}, bf16[1536,128]{1,0:T(8,128)(2,1)S(1)}, u32[]{:S(2)}, u32[]{:S(2)}) collective-permute-start(bf16[1536,128]{1,0:T(8,128)(2,1)S(1)} %get-tuple-element.106), channel_id=1, source_target_pairs={{0,8},{1,9},{2,10},{3,11},{4,12},{5,13},{6,14},{7,15},{8,0},{9,1},... | collective-permute-start | bytes 1179656 | tf_op jit(solution)/shard_map/ppermute | solution.py:383
  46.4 8.6 %collective-permute-start.15 = (bf16[38,3,384]{2,1,0:T(4,128)(2,1)S(1)}, bf16[38,3,384]{2,1,0:T(4,128)(2,1)S(1)}, u32[]{:S(2)}, u32[]{:S(2)}) collective-permute-start(bf16[38,3,384]{2,1,0:T(4,128)(2,1)S(1)} %maximum_select_fusion.1), channel_id=1, source_target_pairs={{0,4},{4,0},{1,5},{5,1},{2,6},{6,2},{3,7},{7,3},{8,12},{12,8},{9,1... | collective-permute-start | bytes 262664 | tf_op jit(solution)/shard_map/ppermute | solution.py:46
  55.0 2.0 %collective-permute-start.9 = (bf16[256,128]{1,0:T(8,128)(2,1)S(1)}, bf16[256,128]{1,0:T(8,128)(2,1)S(1)}, u32[]{:S(2)}, u32[]{:S(2)}) collective-permute-start(bf16[256,128]{1,0:T(8,128)(2,1)S(1)} %get-tuple-element.114), channel_id=1, source_target_pairs={{0,8},{1,9},{2,10},{3,11},{4,12},{5,13},{6,14},{7,15},{8,0},{9,1},... | collective-permute-start | bytes 196616 | tf_op jit(solution)/shard_map/ppermute | solution.py:383
  55.3 12.0 %collective-permute-start.8 = (bf16[768,128]{1,0:T(8,128)(2,1)S(1)}, bf16[768,128]{1,0:T(8,128)(2,1)S(1)}, u32[]{:S(2)}, u32[]{:S(2)}) collective-permute-start(bf16[768,128]{1,0:T(8,128)(2,1)S(1)} %shard_map.199.refs_7_.refs_0_), channel_id=1, source_target_pairs={{0,1},{1,0},{2,3},{3,2},{4,5},{5,4},{6,7},{7,6},{8,9},{9,8},{10,11... | collective-permute-start | bytes 589832 | tf_op jit(solution)/shard_map/ppermute | solution.py:383
  57.0 10.3 %collective-permute-start.11 = (bf16[448,128]{1,0:T(8,128)(2,1)S(1)}, bf16[448,128]{1,0:T(8,128)(2,1)S(1)}, u32[]{:S(2)}, u32[]{:S(2)}) collective-permute-start(bf16[448,128]{1,0:T(8,128)(2,1)S(1)} %get-tuple-element.117), channel_id=1, source_target_pairs={{0,4},{1,5},{2,6},{3,7},{4,0},{5,1},{6,2},{7,3},{8,12},{9,13},{10,... | collective-permute-start | bytes 344072 | tf_op jit(solution)/shard_map/ppermute | solution.py:383
  57.6 9.7 %collective-permute-start.12 = (bf16[448,128]{1,0:T(8,128)(2,1)S(1)}, bf16[448,128]{1,0:T(8,128)(2,1)S(1)}, u32[]{:S(2)}, u32[]{:S(2)}) collective-permute-start(bf16[448,128]{1,0:T(8,128)(2,1)S(1)} %get-tuple-element.118), channel_id=1, source_target_pairs={{0,20},{1,21},{2,22},{3,23},{4,16},{5,17},{6,18},{7,19},{8,28},{9,... | collective-permute-start | bytes 344072 | tf_op jit(solution)/shard_map/ppermute | solution.py:383
  59.7 7.6 %collective-permute-start.10 = (bf16[448,128]{1,0:T(8,128)(2,1)S(1)}, bf16[448,128]{1,0:T(8,128)(2,1)S(1)}, u32[]{:S(2)}, u32[]{:S(2)}) collective-permute-start(bf16[448,128]{1,0:T(8,128)(2,1)S(1)} %get-tuple-element.116.refs_8_), channel_id=1, source_target_pairs={{0,16},{1,17},{2,18},{3,19},{4,20},{5,21},{6,22},{7,23},{8,24},{9,... | collective-permute-start | bytes 344072 | tf_op jit(solution)/shard_map/ppermute | solution.py:383
  67.4 11.3 %collective-permute-start.16 = (bf16[768,128]{1,0:T(8,128)(2,1)S(1)}, bf16[768,128]{1,0:T(8,128)(2,1)S(1)}, u32[]{:S(2)}, u32[]{:S(2)}) collective-permute-start(bf16[768,128]{1,0:T(8,128)(2,1)S(1)} %shard_map.202.refs_0_), channel_id=1, source_target_pairs={{0,2},{1,3},{2,0},{3,1},{4,6},{5,7},{6,4},{7,5},{8,10},{9,11},{10,... | collective-permute-start | bytes 589832 | tf_op jit(solution)/shard_map/ppermute | solution.py:383
  70.1 6.1 %collective-permute-start.17 = (bf16[448,128]{1,0:T(8,128)(2,1)S(1)}, bf16[448,128]{1,0:T(8,128)(2,1)S(1)}, u32[]{:S(2)}, u32[]{:S(2)}) collective-permute-start(bf16[448,128]{1,0:T(8,128)(2,1)S(1)} %shard_map.203.refs_0_), channel_id=1, source_target_pairs={{0,1},{1,0},{2,3},{3,2},{4,5},{5,4},{6,7},{7,6},{8,9},{9,8},{10,11... | collective-permute-start | bytes 344072 | tf_op jit(solution)/shard_map/ppermute | solution.py:383
  78.8 10.9 %collective-permute-start.20 = (bf16[768,128]{1,0:T(8,128)(2,1)S(1)}, bf16[768,128]{1,0:T(8,128)(2,1)S(1)}, u32[]{:S(2)}, u32[]{:S(2)}) collective-permute-start(bf16[768,128]{1,0:T(8,128)(2,1)S(1)} %shard_map.204.refs_1_), channel_id=1, source_target_pairs={{0,20},{1,21},{2,22},{3,23},{4,16},{5,17},{6,18},{7,19},{8,28},{9,... | collective-permute-start | bytes 589832 | tf_op jit(solution)/shard_map/ppermute | solution.py:383
  80.1 10.3 %collective-permute-start.19 = (bf16[768,128]{1,0:T(8,128)(2,1)S(1)}, bf16[768,128]{1,0:T(8,128)(2,1)S(1)}, u32[]{:S(2)}, u32[]{:S(2)}) collective-permute-start(bf16[768,128]{1,0:T(8,128)(2,1)S(1)} %shard_map.204.refs_1_), channel_id=1, source_target_pairs={{0,4},{1,5},{2,6},{3,7},{4,0},{5,1},{6,2},{7,3},{8,12},{9,13},{10,... | collective-permute-start | bytes 589832 | tf_op jit(solution)/shard_map/ppermute | solution.py:383
  81.5 9.0 %collective-permute-start.18 = (bf16[768,128]{1,0:T(8,128)(2,1)S(1)}, bf16[768,128]{1,0:T(8,128)(2,1)S(1)}, u32[]{:S(2)}, u32[]{:S(2)}) collective-permute-start(bf16[768,128]{1,0:T(8,128)(2,1)S(1)} %shard_map.204.refs_1_), channel_id=1, source_target_pairs={{0,16},{1,17},{2,18},{3,19},{4,20},{5,21},{6,22},{7,23},{8,24},{9,... | collective-permute-start | bytes 589832 | tf_op jit(solution)/shard_map/ppermute | solution.py:383
  82.4 7.3 %collective-permute-start.21 = (bf16[448,128]{1,0:T(8,128)(2,1)S(1)}, bf16[448,128]{1,0:T(8,128)(2,1)S(1)}, u32[]{:S(2)}, u32[]{:S(2)}) collective-permute-start(bf16[448,128]{1,0:T(8,128)(2,1)S(1)} %shard_map.205.refs_0_), channel_id=1, source_target_pairs={{0,2},{1,3},{2,0},{3,1},{4,6},{5,7},{6,4},{7,5},{8,10},{9,11},{10,... | collective-permute-start | bytes 344072 | tf_op jit(solution)/shard_map/ppermute | solution.py:383
  90.5 9.1 %collective-permute-start.22 = (bf16[3072,128]{1,0:T(8,128)(2,1)S(1)}, bf16[3072,128]{1,0:T(8,128)(2,1)S(1)}, u32[]{:S(2)}, u32[]{:S(2)}) collective-permute-start(bf16[3072,128]{1,0:T(8,128)(2,1)S(1)} %shard_map.206.own_a), channel_id=1, source_target_pairs={{0,8},{1,9},{2,10},{3,11},{4,12},{5,13},{6,14},{7,15},{8,0},{9,1},... | collective-permute-start | bytes 2359304 | tf_op jit(solution)/shard_map/ppermute | solution.py:383
  90.6 6.9 %collective-permute-start.25 = (bf16[448,128]{1,0:T(8,128)(2,1)S(1)}, bf16[448,128]{1,0:T(8,128)(2,1)S(1)}, u32[]{:S(2)}, u32[]{:S(2)}) collective-permute-start(bf16[448,128]{1,0:T(8,128)(2,1)S(1)} %shard_map.207.refs_1_), channel_id=1, source_target_pairs={{0,20},{1,21},{2,22},{3,23},{4,16},{5,17},{6,18},{7,19},{8,28},{9,... | collective-permute-start | bytes 344072 | tf_op jit(solution)/shard_map/ppermute | solution.py:383
  91.9 7.7 %collective-permute-start.24 = (bf16[448,128]{1,0:T(8,128)(2,1)S(1)}, bf16[448,128]{1,0:T(8,128)(2,1)S(1)}, u32[]{:S(2)}, u32[]{:S(2)}) collective-permute-start(bf16[448,128]{1,0:T(8,128)(2,1)S(1)} %shard_map.207.refs_1_), channel_id=1, source_target_pairs={{0,4},{1,5},{2,6},{3,7},{4,0},{5,1},{6,2},{7,3},{8,12},{9,13},{10,... | collective-permute-start | bytes 344072 | tf_op jit(solution)/shard_map/ppermute | solution.py:383
  93.3 6.3 %collective-permute-start.23 = (bf16[448,128]{1,0:T(8,128)(2,1)S(1)}, bf16[448,128]{1,0:T(8,128)(2,1)S(1)}, u32[]{:S(2)}, u32[]{:S(2)}) collective-permute-start(bf16[448,128]{1,0:T(8,128)(2,1)S(1)} %shard_map.207.refs_1_), channel_id=1, source_target_pairs={{0,16},{1,17},{2,18},{3,19},{4,20},{5,21},{6,22},{7,23},{8,24},{9,... | collective-permute-start | bytes 344072 | tf_op jit(solution)/shard_map/ppermute | solution.py:383
  99.6 1.9 %collective-permute-start.26 = (bf16[1792,128]{1,0:T(8,128)(2,1)S(1)}, bf16[1792,128]{1,0:T(8,128)(2,1)S(1)}, u32[]{:S(2)}, u32[]{:S(2)}) collective-permute-start(bf16[1792,128]{1,0:T(8,128)(2,1)S(1)} %shard_map.208.own_b), channel_id=1, source_target_pairs={{0,8},{1,9},{2,10},{3,11},{4,12},{5,13},{6,14},{7,15},{8,0},{9,1},... | collective-permute-start | bytes 1376264 | tf_op jit(solution)/shard_map/ppermute | solution.py:383

commit v7 on v6

--- a/solution.py
+++ b/solution.py
@@ -11,7 +11,6 @@
 norm_epsilon = 1e-06
 inv_root_two = 0.7071067811865476
 inv_root_tau = 0.3989422804014327
-log2_e = 1.4426950408889634
 
 LANES = 128
 EDGE = 8
@@ -139,27 +138,24 @@
 
 
 def gelu_pair(u):
-    bell = jnp.exp2(u * u * (-0.5 * log2_e))
-    t = 1.0 / (1.0 + jnp.abs(u) * (0.3275911 * inv_root_two))
-    poly = 0.5 * 1.061405429
-    for term in (-1.453152027, 1.421413741, -0.284496736, 0.254829592):
-        poly = poly * t + 0.5 * term
-    tail = poly * t * bell
-    cdf = jnp.where(u < 0.0, tail, 1.0 - tail)
-    return u * cdf, cdf + u * (bell * inv_root_tau)
+    cdf = 0.5 * (1.0 + lax.erf(u * inv_root_two))
+    pdf = jnp.exp(-0.5 * u * u) * inv_root_tau
+    return u * cdf, cdf + u * pdf
 
 
 def fold(x):
     return jnp.sum(x.reshape(-1, 8, x.shape[1]), axis=0)
 
 
-def mlp_block(ln, d_branch, w_in, w_out, b_in, base, width, hid_ref, dpre_ref, gbin):
+def mlp(core, ln_ref, d_branch, w_in, w_out, b_in, base, width, hid_ref, dpre_ref, keep, send, gbin_ref):
     sub = 256
     count = width // sub
+    channels = ln_ref.shape[1]
+    ln = ln_ref[...]
 
     def products(s):
         at = pl.ds(base + s * sub, sub)
-        return dot(ln, w_in[at, :], NT), dot(d_branch, w_out[:, at], NN)
+        return dot(ln, w_in[at, :], NT), dot(d_branch[...], w_out[:, at], NN)
 
     ahead = products(0)
     for s in range(count):
@@ -168,85 +164,63 @@
             ahead = products(s + 1)
         act, slope = gelu_pair(pre + line(b_in, pl.ds(base + s * sub, sub)))
         d_pre = d_hidden * slope
-        gbin[:, s * sub : (s + 1) * sub] += fold(d_pre)
-        hid_ref[:, s * sub : (s + 1) * sub] = act.astype(bf16)
-        dpre_ref[:, s * sub : (s + 1) * sub] = d_pre.astype(bf16)
-    at = pl.ds(base, width)
-    hidden, d_pre = hid_ref[...], dpre_ref[...]
-    branch = dot(hidden, w_out[:, at], NT)
-    d_norm = dot(d_pre, w_in[at, :], NN)
-    return hidden, d_pre, branch, d_norm
-
-
-def pack_grads(core, keep, send, gwin, gwout, gbin_ref, gbin):
-    width, channels = gwin.shape
+        at = slice(s * sub, (s + 1) * sub)
+        gbin_ref[:, at] = jnp.sum(d_pre, axis=0, keepdims=True)
+        hid_ref[:, at] = act.astype(bf16)
+        dpre_ref[:, at] = d_pre.astype(bf16)
 
     def store(first, second):
-        for j in range(channels // LANES):
-            first[j * width : (j + 1) * width, :] = gwin[:, j * LANES : (j + 1) * LANES].astype(bf16)
-        for j in range(width // LANES):
-            second[j * channels : (j + 1) * channels, :] = gwout[
-                :, j * LANES : (j + 1) * LANES
-            ].astype(bf16)
+        for s in range(count):
+            at = slice(s * sub, (s + 1) * sub)
+            gwin = dot(dpre_ref[:, at], ln_ref[...], TN).astype(bf16)
+            for j in range(channels // LANES):
+                start = j * width + s * sub
+                first[start : start + sub, :] = gwin[:, j * LANES : (j + 1) * LANES]
+            gwout = dot(d_branch[...], hid_ref[:, at], TN).astype(bf16)
+            for j in range(sub // LANES):
+                start = (s * sub // LANES + j) * channels
+                second[start : start + channels, :] = gwout[:, j * LANES : (j + 1) * LANES]
 
     pl.when(core[0] == 0)(lambda: store(keep, send))
     pl.when(core[0] != 0)(lambda: store(send, keep))
-    gbin_ref[...] = jnp.sum(gbin[...], axis=0, keepdims=True)
-
-
-MLP_BLOCK = 256
+
+
+PIXELS = 256
 
 
 def mlp_first_kernel(
-    base, width, core, ln_ref, cot, w_in, w_out, b_in, scale, branch_ref, dnorm_ref, keep, send, gbin_ref,
-    hid_ref, dpre_ref, gwin, gwout, gbin,
+    base, width, core, ln_ref, cot, w_in, w_out, b_in, scale, branch_ref, dnorm_ref, d_branch_ref,
+    keep, send, gbin_ref, hid_ref, dpre_ref,
 ):
-    gwin[...] = jnp.zeros_like(gwin)
-    gwout[...] = jnp.zeros_like(gwout)
-    gbin[...] = jnp.zeros_like(gbin)
+    d_branch_ref[...] = (line(scale) * cot[...].astype(f32)).astype(bf16)
+    mlp(core, ln_ref, d_branch_ref, w_in, w_out, b_in, base, width, hid_ref, dpre_ref, keep, send, gbin_ref)
+    at = pl.ds(base, width)
 
     def step(i, _):
-        at = pl.ds(pl.multiple_of(i * MLP_BLOCK, MLP_BLOCK), MLP_BLOCK)
-        ln = ln_ref[at, :]
-        d_branch = (line(scale) * cot[at, :].astype(f32)).astype(bf16)
-        hidden, d_pre, branch, d_norm = mlp_block(
-            ln, d_branch, w_in, w_out, b_in, base, width, hid_ref, dpre_ref, gbin
-        )
-        branch_ref[at, :] = branch
-        dnorm_ref[at, :] = d_norm
-        gwin[...] += dot(d_pre, ln, TN)
-        gwout[...] += dot(d_branch, hidden, TN)
+        to = pl.ds(pl.multiple_of(i * PIXELS, PIXELS), PIXELS)
+        branch_ref[to, :] = dot(hid_ref[to, :], w_out[:, at], NT)
+        dnorm_ref[to, :] = dot(dpre_ref[to, :], w_in[at, :], NN)
         return _
 
-    lax.fori_loop(0, ln_ref.shape[0] // MLP_BLOCK, step, 0)
-    pack_grads(core, keep, send, gwin, gwout, gbin_ref, gbin)
+    lax.fori_loop(0, ln_ref.shape[0] // PIXELS, step, 0)
 
 
 def mlp_second_kernel(
     base, width, core, ln_ref, cot, w_in, w_out, b_in, scale, b_out, gain, page, normed_ref, inv_ref,
-    branch_ref, dnorm_ref,
+    branch_ref, dnorm_ref, d_branch_ref,
     result, d_depth_ref, keep, send, gbin_ref, sums_ref,
-    hid_ref, dpre_ref, gwin, gwout, gbin, sums,
+    hid_ref, dpre_ref, sums,
 ):
-    gwin[...] = jnp.zeros_like(gwin)
-    gwout[...] = jnp.zeros_like(gwout)
-    gbin[...] = jnp.zeros_like(gbin)
     sums[...] = jnp.zeros_like(sums)
+    mlp(core, ln_ref, d_branch_ref, w_in, w_out, b_in, base, width, hid_ref, dpre_ref, keep, send, gbin_ref)
+    units = pl.ds(base, width)
 
     def step(i, _):
-        at = pl.ds(pl.multiple_of(i * MLP_BLOCK, MLP_BLOCK), MLP_BLOCK)
-        ln = ln_ref[at, :]
+        at = pl.ds(pl.multiple_of(i * PIXELS, PIXELS), PIXELS)
         cot32 = cot[at, :].astype(f32)
-        d_branch32 = line(scale) * cot32
-        d_branch = d_branch32.astype(bf16)
-        hidden, d_pre, branch, d_norm = mlp_block(
-            ln, d_branch, w_in, w_out, b_in, base, width, hid_ref, dpre_ref, gbin
-        )
-        gwin[...] += dot(d_pre, ln, TN)
-        gwout[...] += dot(d_branch, hidden, TN)
-        branch = branch + branch_ref[at, :] + line(b_out)
+        branch = dot(hid_ref[at, :], w_out[:, units], NT) + branch_ref[at, :] + line(b_out)
         result[at, :] = (page[at, :].astype(f32) + line(scale) * branch).astype(bf16)
-        d_norm = d_norm + dnorm_ref[at, :]
+        d_norm = dot(dpre_ref[at, :], w_in[units, :], NN) + dnorm_ref[at, :]
         normed = normed_ref[at, :]
         inv = inv_ref[at, 0:1]
         weighted = d_norm * normed
@@ -256,14 +230,13 @@
         d_depth = (inv * (s - mean_s - normed * mean_sn)).astype(bf16)
         d_depth_ref[at, :] = d_depth
         sums[0] += fold(cot32 * branch)
-        sums[1] += fold(d_branch32)
+        sums[1] += fold(line(scale) * cot32)
         sums[2] += fold(weighted)
         sums[3] += fold(d_norm)
         sums[4] += fold(d_depth.astype(f32))
         return _
 
-    lax.fori_loop(0, ln_ref.shape[0] // MLP_BLOCK, step, 0)
-    pack_grads(core, keep, send, gwin, gwout, gbin_ref, gbin)
+    lax.fori_loop(0, ln_ref.shape[0] // PIXELS, step, 0)
     for j in range(5):
         sums_ref[j : j + 1, :] = jnp.sum(sums[j], axis=0, keepdims=True)
 
@@ -298,8 +271,7 @@
     steps(rows, cols, channels, piece)
 
     def store(first, second):
-        second[...] = jnp.zeros_like(second)
-        slabs = channels // LANES
+        slabs, half = channels // LANES, SMALL // 2
         for slab in range(slabs):
             at = slice(slab * LANES, (slab + 1) * LANES)
             part = [jnp.sum(acc_ref[slab], axis=1), sums[:5, at]]
@@ -310,9 +282,10 @@
                 part.append(source[:, lane : lane + LANES])
             part = jnp.concatenate(part)
             part = jnp.concatenate([part, jnp.zeros((SMALL - part.shape[0], LANES), f32)])
-            first[slab * SMALL : (slab + 1) * SMALL, :] = part.astype(bf16)
-        rest = first.shape[0] - slabs * SMALL
-        first[slabs * SMALL :, :] = jnp.zeros((rest, LANES), bf16)
+            first[slab * half : (slab + 1) * half, :] = part[:half].astype(bf16)
+            second[slab * half : (slab + 1) * half, :] = part[half:].astype(bf16)
+        for ref in (first, second):
+            ref[slabs * half :, :] = jnp.zeros((ref.shape[0] - slabs * half, LANES), bf16)
 
     pl.when(core[0] == 0)(lambda: store(keep, send))
     pl.when(core[0] != 0)(lambda: store(send, keep))
@@ -488,11 +461,11 @@
                     second, width, (offset // LANES + j) * channels + i
                 )
 
-    def store_small(first):
+    def store_small(*halves):
         for slab in range(slabs):
             at = slice(slab * LANES, (slab + 1) * LANES)
-            start = slab * (first.shape[0] // 4) + widths[1] * slabs // 4
-            values = first[start : start + SMALL, :].astype(f32) * factor
+            start = slab * (halves[0].shape[0] // 4) + widths[1] * slabs // 4
+            values = jnp.concatenate([ref[start : start + SMALL // 2, :].astype(f32) for ref in halves]) * factor
             for j in range(7):
                 gk[j, :, at] = values[7 * j : 7 * j + 7]
             for j, ref in enumerate((scale, b_out, gain, shift, bias)):
@@ -511,8 +484,8 @@
         here = step == i
         pl.when(here & is_first)(functools.partial(store, *halves, width, offset))
         pl.when(here & ~is_first)(functools.partial(store, *halves[::-1], width, offset))
-    pl.when((step == 0) & is_first)(lambda: store_small(own_b))
-    pl.when((step == 0) & ~is_first)(lambda: store_small(other_b))
+    pl.when((step == 0) & is_first)(lambda: store_small(own_b, other_b))
+    pl.when((step == 0) & ~is_first)(lambda: store_small(other_b, own_b))
 
 
 def finish(factor, widths, channels, core, *halves):
@@ -569,22 +542,16 @@
         (tile, *around, conv_kernel, conv_bias, norm_gain, norm_bias),
         conv_flops,
     )
-    grads = lambda width: [
-        ((MLP_BLOCK, width), bf16),
-        ((MLP_BLOCK, width), bf16),
-        ((width, channels), f32),
-        ((channels, width), f32),
-        ((8, width), f32),
-    ]
+    acts = lambda width: [((pixels, width), bf16)] * 2
     packed = lambda width: [((width * channels // LANES, LANES), bf16)] * 2 + [((1, width), f32)]
     core_flip = [("gy", 0)]
     mlp_flops = 12 * pixels * channels * hid
     weights = (w_in, w_out, b_in, layer_scale)
     first, second = hid * 2 // 3, hid // 3
-    branch, d_norm, keep_a, send_a, gbin_a = call(
+    branch, d_norm, d_branch, keep_a, send_a, gbin_a = call(
         functools.partial(mlp_first_kernel, 0, first),
-        [(full, f32), (full, f32)] + packed(first),
-        grads(first),
+        [(full, f32), (full, f32), (full, bf16)] + packed(first),
+        acts(first),
         (core, ln_out, cot, *weights),
         mlp_flops,
         1,
@@ -593,8 +560,8 @@
     result, d_depth, keep_b, send_b, gbin_b, sums = call(
         functools.partial(mlp_second_kernel, first, second),
         [(full, bf16), (full, bf16)] + packed(second) + [((8, channels), f32)],
-        grads(second) + [((8, 8, channels), f32)],
-        (core, ln_out, cot, *weights, b_out, norm_gain, page, normed, inv, branch, d_norm),
+        acts(second) + [((8, 8, channels), f32)],
+        (core, ln_out, cot, *weights, b_out, norm_gain, page, normed, inv, branch, d_norm, d_branch),
         mlp_flops,
         1,
     )
@@ -604,7 +571,7 @@
     got_a = spread(parts_a)
     other_b = exchange(send_b, core_flip)
     d_around = halo(d_tile, even_y, even_x)
-    small_rows = ((4 * SMALL, LANES), bf16)
+    small_rows = ((2 * SMALL, LANES), bf16)
     keep_s, send_s = call(
         kernel_grad_kernel,
         [small_rows, small_rows],
@@ -620,6 +587,8 @@
     parts_b = add_halves(mine, keep_b, other_b, keep_s, other_s)
     flips = [[bit] for bit in beyond()]
     got_a, got_b = exchange(part_a, flips[0]), spread(parts_b)
+    got_a, got_b = hold((got_a, got_b))
+    part_a, part_b = add(part_a, got_a), add(*got_b)
     (grad_pages,) = call(
         conv_grad_kernel,
         [(full, bf16)],
@@ -627,12 +596,10 @@
         (d_tile, *d_around, conv_kernel, cot),
         conv_flops,
         0,
-        (part_a, parts_b[1]),
-    )
-    got_a, got_b, grad_pages = hold((got_a, got_b, grad_pages))
-    part_a, part_b = add(part_a, got_a), add(*got_b)
+        (part_a, part_b),
+    )
     for ahead, behind in zip(flips[1:], flips):
-        got_a, got_b = hold((exchange(part_a, ahead), exchange(part_b, behind)))
+        got_a, got_b, grad_pages = hold((exchange(part_a, ahead), exchange(part_b, behind), grad_pages))
         part_a, part_b = add(part_a, got_a), add(part_b, got_b)
     got_a, got_b = hold((spread([part_a] * 4), exchange(part_b, flips[-1])))
     half_a, part_b = join(mine, *got_a), add(part_b, got_b)

time: 104 us -> 97.9 us (0.941)
  waiting for transfers between devices: 25.6 us -> 21.1 us
  Pallas kernels: 41.8 us -> 39.6 us
    ppermute x21, waiting for transfers between devices: 22.8 us -> 18.3 us  [exchange(): return lax.ppermute(x, AXES, perm)]
    pallas_call x15, Pallas kernels: 39.1 us -> 36.9 us  [call(): pl.pallas_call(kernel, out_shape=[jax.ShapeDtypeStruct(shape, dtype) for...]
  transfers between devices with their start and end apart: 27 -> 27, of which waited for: 8 -> 8; matrix products, arithmetic and copies ran while one was open for 1% -> 2% of each run, Pallas kernels for 21% -> 21%
where the time goes in v7:
time: 97.9 us; the launch traced here: 97.7 us
  Pallas kernels  39.6 us (40%)
  starting transfers between devices  32.9 us (34%)
  waiting for transfers between devices  21.1 us (22%)
  other arithmetic  1.55 us (2%)
  local copies, waits for them, and re-layouts  1.29 us (1%)
  between operations  1.29 us (1%)
    pallas_call x15, Pallas kernels, call(): pl.pallas_call(kernel, out_shape=[jax.ShapeDtypeStruct(shape, dtype) for...  36.9 us
    ppermute x21, starting transfers between devices, exchange(): return lax.ppermute(x, AXES, perm)  26.8 us
    ppermute x21, waiting for transfers between devices, exchange(): return lax.ppermute(x, AXES, perm)  18.3 us
    ppermute x6, starting transfers between devices, swap_edges(): got.append(lax.ppermute(jnp.where(is_high, high, low), axis, pairs))  6.11 us
    ppermute x6, waiting for transfers between devices, swap_edges(): got.append(lax.ppermute(jnp.where(is_high, high, low), axis, pairs))  2.81 us
    pallas_call x1, Pallas kernels, finish(): pl.pallas_call(functools.partial(finish_kernel, factor, widths), grid=(hi...  2.69 us
  transfers between devices with their start and end apart: 27, of which 8 were waited for; matrix products, arithmetic and copies ran while one was open for 2% of the time, Pallas kernels for 21%

profile of v7, /device:TPU:0, one launch (start us, length us, event | category | flops | bytes accessed | tf_op | source)
XLA Modules:
  0.0 97.7 jit_solution(9627207760354681460)
XLA Ops:
  0.6 0.0 copy-start
  0.7 1.0 %broadcast_select_fusion.11 = (bf16[3,32,384]{2,1,0:T(8,128)(2,1)S(1)}, bf16[3,32,384]{2,1,0:T(8,128)(2,1)S(1)}) fusion(pred[]{:T(512)S(6)} %eq.12, bf16[32,32,384]{2,1,0:T(8,128)(2,1)} %bitcast.9, pred[]{:T(512)S(6)} %not.4), kind=kLoop, calls=%fused_computation.13 | loop fusion | flops 73728 | bytes 294914 | tf_op jit(solution)/shard_map/jit(_where)/select_n | solution.py:45
  1.8 0.5 collective-permute-start.1
  2.3 0.7 collective-permute-start
  2.9 1.1 %fusion.1 = (bf16[32,3,384]{2,1,0:T(4,128)(2,1)S(1)}, bf16[32,3,384]{2,1,0:T(4,128)(2,1)S(1)}) fusion(bf16[32,32,384]{2,1,0:T(8,128)(2,1)} %bitcast.10), kind=kLoop, calls=%fused_computation.15 | loop fusion | bytes 294912 | tf_op jit(solution)/shard_map/slice | solution.py:52
  4.0 0.0 collective-permute-done
  4.1 0.2 maximum_select_fusion
  4.3 2.6 %collective-permute-start.2 = (bf16[38,3,384]{2,1,0:T(4,128)(2,1)S(1)}, bf16[38,3,384]{2,1,0:T(4,128)(2,1)S(1)}, u32[]{:S(2)}, u32[]{:S(2)}) collective-permute-start(bf16[38,3,384]{2,1,0:T(4,128)(2,1)S(1)} %maximum_select_fusion), channel_id=1, source_target_pairs={{0,4},{4,0},{1,5},{5,1},{2,6},{6,2},{3,7},{7,3},{8,12},{12,8},{9,1... | collective-permute-start | bytes 262664 | tf_op jit(solution)/shard_map/ppermute | solution.py:45
  6.9 2.8 %collective-permute-done.2 = bf16[38,3,384]{2,1,0:T(4,128)(2,1)S(1)} collective-permute-done((bf16[38,3,384]{2,1,0:T(4,128)(2,1)S(1)}, bf16[38,3,384]{2,1,0:T(4,128)(2,1)S(1)}, u32[]{:S(2)}, u32[]{:S(2)}) %collective-permute-start.2) | collective-permute-done | bytes 87584 | tf_op jit(solution)/shard_map/ppermute | solution.py:45
  9.7 0.1 broadcast_select_fusion.2
  9.8 0.0 copy-start.1
  9.8 0.0 copy-start.2
  9.8 0.0 copy-start.3
  9.9 0.0 copy-start.5
  9.9 0.0 copy-start.9
  9.9 7.3 %shard_map.194 = (f32[1024,384]{1,0:T(8,128)S(1)}, f32[1024,128]{1,0:T(8,128)S(1)}, bf16[1024,384]{1,0:T(8,128)(2,1)S(1)}) custom-call(bf16[32,32,384]{2,1,0:T(8,128)(2,1)S(1)} %bitcast.11, bf16[3,32,384]{2,1,0:T(8,128)(2,1)S(1)} %get-tuple-element.160.refs_1_.refs_2_, bf16[3,32,384]{2,1,0:T(8,128)(2,1)S(1)} %get-tuple-element.159.refs_2_.refs_3_, ...), custom_call_target="tpu_custom_call" | custom-call | flops 2312110080 | bytes 2257920 | tf_op jit(solution)/shard_map/pallas_call | solution.py:323
  17.3 0.0 copy-start.10
  17.3 8.5 %shard_map.195 = (f32[1024,384]{1,0:T(8,128)S(1)}, f32[1024,384]{1,0:T(8,128)S(1)}, bf16[1024,384]{1,0:T(8,128)(2,1)S(1)}, bf16[3072,128]{1,0:T(8,128)(2,1)S(1)}...) custom-call(s32[1]{0:T(128)} %bitcast.refs_0_.core, bf16[1024,384]{1,0:T(8,128)(2,1)S(1)} %get-tuple-element.84.refs_1_, ...), custom_call_target="tpu_custom_call" | custom-call | flops 7247757312 | bytes 7077888 | tf_op jit(solution)/shard_map/pallas_call | solution.py:323
  25.8 3.8 %collective-permute-start.3 = (bf16[3072,128]{1,0:T(8,128)(2,1)S(1)}, bf16[3072,128]{1,0:T(8,128)(2,1)S(1)}, u32[]{:S(2)}, u32[]{:S(2)}) collective-permute-start(bf16[3072,128]{1,0:T(8,128)(2,1)S(1)} %get-tuple-element.93), channel_id=1, source_target_pairs={{0,8},{1,9},{2,10},{3,11},{4,12},{5,13},{6,14},{7,15},{8,0},{9,1},... | collective-permute-start | bytes 2359304 | tf_op jit(solution)/shard_map/ppermute | solution.py:356
  29.6 6.6 %shard_map.196 = (bf16[1024,384]{1,0:T(8,128)(2,1)}, bf16[1024,384]{1,0:T(8,128)(2,1)S(1)}, bf16[1536,128]{1,0:T(8,128)(2,1)S(1)}, bf16[1536,128]{1,0:T(8,128)(2...) custom-call(s32[1]{0:T(128)} %bitcast.refs_0_.core, bf16[1024,384]{1,0:T(8,128)(2,1)S(1)} %get-tuple-element.84.refs_1_, ...), custom_call_target="tpu_custom_call" | custom-call | flops 7247757312 | bytes 7077888 | tf_op jit(solution)/shard_map/pallas_call | solution.py:323
  36.2 0.1 collective-permute-start.16
  36.3 0.7 collective-permute-start.15
  37.0 0.1 fusion
  37.1 0.3 shard_map.197
  37.4 1.8 %collective-permute-start.5 = (bf16[768,128]{1,0:T(8,128)(2,1)S(1)}, bf16[768,128]{1,0:T(8,128)(2,1)S(1)}, u32[]{:S(2)}, u32[]{:S(2)}) collective-permute-start(bf16[768,128]{1,0:T(8,128)(2,1)S(1)} %get-tuple-element.100), channel_id=1, source_target_pairs={{0,4},{1,5},{2,6},{3,7},{4,0},{5,1},{6,2},{7,3},{8,12},{9,13},{10,... | collective-permute-start | bytes 589832 | tf_op jit(solution)/shard_map/ppermute | solution.py:356
  39.2 3.5 %collective-permute-start.6 = (bf16[768,128]{1,0:T(8,128)(2,1)S(1)}, bf16[768,128]{1,0:T(8,128)(2,1)S(1)}, u32[]{:S(2)}, u32[]{:S(2)}) collective-permute-start(bf16[768,128]{1,0:T(8,128)(2,1)S(1)} %get-tuple-element.101), channel_id=1, source_target_pairs={{0,20},{1,21},{2,22},{3,23},{4,16},{5,17},{6,18},{7,19},{8,28},{9,... | collective-permute-start | bytes 589832 | tf_op jit(solution)/shard_map/ppermute | solution.py:356
  42.7 0.1 collective-permute-start.4
  42.8 1.2 %collective-permute-start.7 = (bf16[1536,128]{1,0:T(8,128)(2,1)S(1)}, bf16[1536,128]{1,0:T(8,128)(2,1)S(1)}, u32[]{:S(2)}, u32[]{:S(2)}) collective-permute-start(bf16[1536,128]{1,0:T(8,128)(2,1)S(1)} %get-tuple-element.108), channel_id=1, source_target_pairs={{0,8},{1,9},{2,10},{3,11},{4,12},{5,13},{6,14},{7,15},{8,0},{9,1},... | collective-permute-start | bytes 1179656 | tf_op jit(solution)/shard_map/ppermute | solution.py:356
  44.0 0.2 maximum_select_fusion.1
  44.2 1.6 %collective-permute-start.17 = (bf16[38,3,384]{2,1,0:T(4,128)(2,1)S(1)}, bf16[38,3,384]{2,1,0:T(4,128)(2,1)S(1)}, u32[]{:S(2)}, u32[]{:S(2)}) collective-permute-start(bf16[38,3,384]{2,1,0:T(4,128)(2,1)S(1)} %maximum_select_fusion.1), channel_id=1, source_target_pairs={{0,4},{4,0},{1,5},{5,1},{2,6},{6,2},{3,7},{7,3},{8,12},{12,8},{9,1... | collective-permute-start | bytes 262664 | tf_op jit(solution)/shard_map/ppermute | solution.py:45
  45.8 6.9 %shard_map.198 = (bf16[128,128]{1,0:T(8,128)(2,1)S(1)}, bf16[128,128]{1,0:T(8,128)(2,1)S(1)}) custom-call(s32[1]{0:T(128)} %bitcast.refs_0_.core, bf16[32,32,384]{2,1,0:T(8,128)(2,1)S(1)} %bitcast.13, bf16[3,32,384]{2,1,0:T(8,128)(2,1)S(1)} %get-tuple-element.160.refs_1_.refs_2_, bf16[3,32,384]{2,1,0:T(8,128)(2,1)S(1)} %get-tuple-element.159.refs_2_.refs_3_, ...), custom_call_target="tpu_custom_call" | custom-call | flops 2312110080 | bytes 2257920 | tf_op jit(solution)/shard_map/pallas_call | solution.py:323
  52.7 0.1 collective-permute-start.9
  52.8 0.1 shard_map.199.refs_0_
  52.9 1.6 %collective-permute-start.8 = (bf16[768,128]{1,0:T(8,128)(2,1)S(1)}, bf16[768,128]{1,0:T(8,128)(2,1)S(1)}, u32[]{:S(2)}, u32[]{:S(2)}) collective-permute-start(bf16[768,128]{1,0:T(8,128)(2,1)S(1)} %shard_map.199.refs_0_), channel_id=1, source_target_pairs={{0,1},{1,0},{2,3},{3,2},{4,5},{5,4},{6,7},{7,6},{8,9},{9,8},{10,11... | collective-permute-start | bytes 589832 | tf_op jit(solution)/shard_map/ppermute | solution.py:356
  54.6 0.1 shard_map.200
  54.7 1.2 %collective-permute-start.10 = (bf16[416,128]{1,0:T(8,128)(2,1)S(1)}, bf16[416,128]{1,0:T(8,128)(2,1)S(1)}, u32[]{:S(2)}, u32[]{:S(2)}) collective-permute-start(bf16[416,128]{1,0:T(8,128)(2,1)S(1)} %get-tuple-element.118), channel_id=1, source_target_pairs={{0,16},{1,17},{2,18},{3,19},{4,20},{5,21},{6,22},{7,23},{8,24},{9,... | collective-permute-start | bytes 319496 | tf_op jit(solution)/shard_map/ppermute | solution.py:356
  55.9 0.6 collective-permute-start.11
  56.5 1.8 %collective-permute-start.12 = (bf16[416,128]{1,0:T(8,128)(2,1)S(1)}, bf16[416,128]{1,0:T(8,128)(2,1)S(1)}, u32[]{:S(2)}, u32[]{:S(2)}) collective-permute-start(bf16[416,128]{1,0:T(8,128)(2,1)S(1)} %get-tuple-element.120), channel_id=1, source_target_pairs={{0,20},{1,21},{2,22},{3,23},{4,16},{5,17},{6,18},{7,19},{8,28},{9,... | collective-permute-start | bytes 319496 | tf_op jit(solution)/shard_map/ppermute | solution.py:356
  58.2 0.1 broadcast_select_fusion
  58.3 1.7 %collective-permute-done.10.refs_1_ = bf16[416,128]{1,0:T(8,128)(2,1)S(1)} collective-permute-done((bf16[416,128]{1,0:T(8,128)(2,1)S(1)}, bf16[416,128]{1,0:T(8,128)(2,1)S(1)}, u32[]{:S(2)}, u32[]{:S(2)}) %collective-permute-start.10) | collective-permute-done | bytes 106528 | tf_op jit(solution)/shard_map/ppermute | solution.py:356
  60.1 2.9 %collective-permute-done.11.refs_2_ = bf16[416,128]{1,0:T(8,128)(2,1)S(1)} collective-permute-done((bf16[416,128]{1,0:T(8,128)(2,1)S(1)}, bf16[416,128]{1,0:T(8,128)(2,1)S(1)}, u32[]{:S(2)}, u32[]{:S(2)}) %collective-permute-start.11) | collective-permute-done | bytes 106528 | tf_op jit(solution)/shard_map/ppermute | solution.py:356
  63.0 0.1 shard_map.201.refs_7_.refs_0_
  63.0 0.1 shard_map.202.refs_8_.refs_0_
  63.1 1.0 %collective-permute-start.14 = (bf16[416,128]{1,0:T(8,128)(2,1)S(1)}, bf16[416,128]{1,0:T(8,128)(2,1)S(1)}, u32[]{:S(2)}, u32[]{:S(2)}) collective-permute-start(bf16[416,128]{1,0:T(8,128)(2,1)S(1)} %shard_map.202.refs_8_.refs_0_), channel_id=1, source_target_pairs={{0,1},{1,0},{2,3},{3,2},{4,5},{5,4},{6,7},{7,6},{8,9},{9,8},{10,11... | collective-permute-start | bytes 319496 | tf_op jit(solution)/shard_map/ppermute | solution.py:356
  64.2 2.6 %collective-permute-start.13 = (bf16[768,128]{1,0:T(8,128)(2,1)S(1)}, bf16[768,128]{1,0:T(8,128)(2,1)S(1)}, u32[]{:S(2)}, u32[]{:S(2)}) collective-permute-start(bf16[768,128]{1,0:T(8,128)(2,1)S(1)} %shard_map.201.refs_7_.refs_0_), channel_id=1, source_target_pairs={{0,2},{1,3},{2,0},{3,1},{4,6},{5,7},{6,4},{7,5},{8,10},{9,11},{10,... | collective-permute-start | bytes 589832 | tf_op jit(solution)/shard_map/ppermute | solution.py:356
  66.7 6.7 %shard_map.203 = bf16[1024,384]{1,0:T(8,128)(2,1)} custom-call(bf16[32,32,384]{2,1,0:T(8,128)(2,1)S(1)} %bitcast.16, bf16[3,32,384]{2,1,0:T(8,128)(2,1)S(1)} %get-tuple-element.158.refs_1_, bf16[3,32,384]{2,1,0:T(8,128)(2,1)S(1)} %get-tuple-element.157.refs_2_, bf16[38,3,384]{2,1,0:T(4,128)(2,1)S(1)} %get-tuple-element.162.refs_3_, ...), custom_call_target="tpu_custom_call" | custom-call | flops 2312110080 | bytes 2257920 | tf_op jit(solution)/shard_map/pallas_call | solution.py:323
  73.5 0.2 collective-permute-done.13.refs_1_
  73.7 0.1 shard_map.204.refs_1_
  73.7 2.5 %collective-permute-start.20 = (bf16[768,128]{1,0:T(8,128)(2,1)S(1)}, bf16[768,128]{1,0:T(8,128)(2,1)S(1)}, u32[]{:S(2)}, u32[]{:S(2)}) collective-permute-start(bf16[768,128]{1,0:T(8,128)(2,1)S(1)} %shard_map.204.refs_1_), channel_id=1, source_target_pairs={{0,20},{1,21},{2,22},{3,23},{4,16},{5,17},{6,18},{7,19},{8,28},{9,... | collective-permute-start | bytes 589832 | tf_op jit(solution)/shard_map/ppermute | solution.py:356
  76.3 0.7 collective-permute-start.19
  77.0 0.3 collective-permute-start.18
  77.3 0.2 collective-permute-start.21
  77.5 6.6 %collective-permute-done.21.refs_1_ = bf16[416,128]{1,0:T(8,128)(2,1)S(1)} collective-permute-done((bf16[416,128]{1,0:T(8,128)(2,1)S(1)}, bf16[416,128]{1,0:T(8,128)(2,1)S(1)}, u32[]{:S(2)}, u32[]{:S(2)}) %collective-permute-start.21) | collective-permute-done | bytes 106528 | tf_op jit(solution)/shard_map/ppermute | solution.py:356
  84.2 0.1 shard_map.206.own_a
  84.2 0.1 collective-permute-start.22
  84.3 0.1 shard_map.207.refs_1_
  84.4 2.5 %collective-permute-start.25 = (bf16[416,128]{1,0:T(8,128)(2,1)S(1)}, bf16[416,128]{1,0:T(8,128)(2,1)S(1)}, u32[]{:S(2)}, u32[]{:S(2)}) collective-permute-start(bf16[416,128]{1,0:T(8,128)(2,1)S(1)} %shard_map.207.refs_1_), channel_id=1, source_target_pairs={{0,20},{1,21},{2,22},{3,23},{4,16},{5,17},{6,18},{7,19},{8,28},{9,... | collective-permute-start | bytes 319496 | tf_op jit(solution)/shard_map/ppermute | solution.py:356
  86.9 0.7 collective-permute-start.24
  87.6 0.3 collective-permute-start.23
  87.9 2.9 %collective-permute-done.25.refs_4_ = bf16[416,128]{1,0:T(8,128)(2,1)S(1)} collective-permute-done((bf16[416,128]{1,0:T(8,128)(2,1)S(1)}, bf16[416,128]{1,0:T(8,128)(2,1)S(1)}, u32[]{:S(2)}, u32[]{:S(2)}) %collective-permute-start.25) | collective-permute-done | bytes 106528 | tf_op jit(solution)/shard_map/ppermute | solution.py:356
  90.8 2.2 %collective-permute-done.24.refs_3_ = bf16[416,128]{1,0:T(8,128)(2,1)S(1)} collective-permute-done((bf16[416,128]{1,0:T(8,128)(2,1)S(1)}, bf16[416,128]{1,0:T(8,128)(2,1)S(1)}, u32[]{:S(2)}, u32[]{:S(2)}) %collective-permute-start.24) | collective-permute-done | bytes 106528 | tf_op jit(solution)/shard_map/ppermute | solution.py:356
  93.0 0.1 collective-permute-start.26
  93.1 1.7 %collective-permute-done.26.other_b = bf16[1664,128]{1,0:T(8,128)(2,1)S(1)} collective-permute-done((bf16[1664,128]{1,0:T(8,128)(2,1)S(1)}, bf16[1664,128]{1,0:T(8,128)(2,1)S(1)}, u32[]{:S(2)}, u32[]{:S(2)}) %collective-permute-start.26) | collective-permute-done | bytes 426016 | tf_op jit(solution)/shard_map/ppermute | solution.py:356
  94.9 2.7 %shard_map.209 = (f32[1536,384]{1,0:T(8,128)}, f32[384,1536]{1,0:T(8,128)}, f32[7,7,384]{2,1,0:T(8,128)}, f32[384]{0:T(512)}, f32[384]{0:T(512)}, /*index=5*/f32...) custom-call(s32[1]{0:T(128)} %bitcast.refs_0_.core, bf16[3072,128]{1,0:T(8,128)(2,1)S(1)} %shard_map.206.own_a, ...), custom_call_target="tpu_custom_call" | custom-call | tf_op jit(solution)/shard_map/pallas_call | solution.py:495
  (41 shorter events, 0.3 us)
Async XLA Ops:
  0.6 9.1 %copy-start = (bf16[1,32,32,384]{3,2,1,0:T(8,128)(2,1)S(1)}, bf16[1,32,32,384]{3,2,1,0:T(8,128)(2,1)}, u32[]{:S(2)}) copy-start(bf16[1,32,32,384]{3,2,1,0:T(8,128)(2,1)} %param.11) | copy-start | bytes 2359300
  0.7 9.1 %copy-start.8 = (f32[384]{0:T(512)S(1)}, f32[384]{0:T(512)}, u32[]{:S(2)}) copy-start(f32[384]{0:T(512)} %refs_8_.3) | copy-start | bytes 4612
  0.7 9.1 %copy-start.4 = (f32[7,7,384]{2,1,0:T(8,128)S(1)}, f32[7,7,384]{2,1,0:T(8,128)}, u32[]{:S(2)}) copy-start(f32[7,7,384]{2,1,0:T(8,128)} %refs_5_.7) | copy-start | bytes 225796
  0.7 9.1 %copy-start.7 = (f32[384]{0:T(512)S(1)}, f32[384]{0:T(512)}, u32[]{:S(2)}) copy-start(f32[384]{0:T(512)} %refs_8_.2) | copy-start | bytes 4612
  0.7 9.1 %copy-start.6 = (f32[384]{0:T(512)S(1)}, f32[384]{0:T(512)}, u32[]{:S(2)}) copy-start(f32[384]{0:T(512)} %refs_6_.3) | copy-start | bytes 4612
  1.8 2.3 %collective-permute-start.1 = (bf16[3,32,384]{2,1,0:T(8,128)(2,1)S(1)}, bf16[3,32,384]{2,1,0:T(8,128)(2,1)S(1)}, u32[]{:S(2)}, u32[]{:S(2)}) collective-permute-start(bf16[3,32,384]{2,1,0:T(8,128)(2,1)S(1)} %get-tuple-element.155), channel_id=1, source_target_pairs={{0,8},{16,24},{8,0},{24,16},{1,9},{17,25},{9,1},{25,17},{2,10},{18... | collective-permute-start | bytes 221192 | tf_op jit(solution)/shard_map/ppermute | solution.py:45
  2.3 1.8 %collective-permute-start = (bf16[3,32,384]{2,1,0:T(8,128)(2,1)S(1)}, bf16[3,32,384]{2,1,0:T(8,128)(2,1)S(1)}, u32[]{:S(2)}, u32[]{:S(2)}) collective-permute-start(bf16[3,32,384]{2,1,0:T(8,128)(2,1)S(1)} %get-tuple-element.156), channel_id=1, source_target_pairs={{8,16},{16,8},{9,17},{17,9},{10,18},{18,10},{11,19},{19,11},{12,20... | collective-permute-start | bytes 221192 | tf_op jit(solution)/shard_map/ppermute | solution.py:45
  4.3 5.4 %collective-permute-start.2 = (bf16[38,3,384]{2,1,0:T(4,128)(2,1)S(1)}, bf16[38,3,384]{2,1,0:T(4,128)(2,1)S(1)}, u32[]{:S(2)}, u32[]{:S(2)}) collective-permute-start(bf16[38,3,384]{2,1,0:T(4,128)(2,1)S(1)} %maximum_select_fusion), channel_id=1, source_target_pairs={{0,4},{4,0},{1,5},{5,1},{2,6},{6,2},{3,7},{7,3},{8,12},{12,8},{9,1... | collective-permute-start | bytes 262664 | tf_op jit(solution)/shard_map/ppermute | solution.py:45
  9.8 7.4 %copy-start.1 = (bf16[1536,384]{1,0:T(8,128)(2,1)S(1)}, bf16[1536,384]{1,0:T(8,128)(2,1)}, u32[]{:S(2)}) copy-start(bf16[1536,384]{1,0:T(8,128)(2,1)} %refs_3_.3) | copy-start | bytes 3538948
  9.8 7.4 %copy-start.2 = (bf16[384,1536]{1,0:T(8,128)(2,1)S(1)}, bf16[384,1536]{1,0:T(8,128)(2,1)}, u32[]{:S(2)}) copy-start(bf16[384,1536]{1,0:T(8,128)(2,1)} %refs_4_.3) | copy-start | bytes 3538948
  9.8 7.4 %copy-start.3 = (bf16[1,32,32,384]{3,2,1,0:T(8,128)(2,1)S(1)}, bf16[1,32,32,384]{3,2,1,0:T(8,128)(2,1)}, u32[]{:S(2)}) copy-start(bf16[1,32,32,384]{3,2,1,0:T(8,128)(2,1)} %param.12) | copy-start | bytes 2359300
  9.9 7.4 %copy-start.5 = (f32[1536]{0:T(1024)S(1)}, f32[1536]{0:T(1024)}, u32[]{:S(2)}) copy-start(f32[1536]{0:T(1024)} %refs_5_.6) | copy-start | bytes 18436
  9.9 7.4 %copy-start.9 = (f32[384]{0:T(512)S(1)}, f32[384]{0:T(512)}, u32[]{:S(2)}) copy-start(f32[384]{0:T(512)} %refs_6_.5) | copy-start | bytes 4612
  17.3 12.4 %copy-start.10 = (f32[384]{0:T(512)S(1)}, f32[384]{0:T(512)}, u32[]{:S(2)}) copy-start(f32[384]{0:T(512)} %refs_7_.3) | copy-start | bytes 4612
  25.8 10.4 %collective-permute-start.3 = (bf16[3072,128]{1,0:T(8,128)(2,1)S(1)}, bf16[3072,128]{1,0:T(8,128)(2,1)S(1)}, u32[]{:S(2)}, u32[]{:S(2)}) collective-permute-start(bf16[3072,128]{1,0:T(8,128)(2,1)S(1)} %get-tuple-element.93), channel_id=1, source_target_pairs={{0,8},{1,9},{2,10},{3,11},{4,12},{5,13},{6,14},{7,15},{8,0},{9,1},... | collective-permute-start | bytes 2359304 | tf_op jit(solution)/shard_map/ppermute | solution.py:356
  36.2 6.5 %collective-permute-start.16 = (bf16[3,32,384]{2,1,0:T(8,128)(2,1)S(1)}, bf16[3,32,384]{2,1,0:T(8,128)(2,1)S(1)}, u32[]{:S(2)}, u32[]{:S(2)}) collective-permute-start(bf16[3,32,384]{2,1,0:T(8,128)(2,1)S(1)} %get-tuple-element.151), channel_id=1, source_target_pairs={{0,8},{16,24},{8,0},{24,16},{1,9},{17,25},{9,1},{25,17},{2,10},{18... | collective-permute-start | bytes 221192 | tf_op jit(solution)/shard_map/ppermute | solution.py:45
  36.3 7.7 %collective-permute-start.15 = (bf16[3,32,384]{2,1,0:T(8,128)(2,1)S(1)}, bf16[3,32,384]{2,1,0:T(8,128)(2,1)S(1)}, u32[]{:S(2)}, u32[]{:S(2)}) collective-permute-start(bf16[3,32,384]{2,1,0:T(8,128)(2,1)S(1)} %get-tuple-element.152), channel_id=1, source_target_pairs={{8,16},{16,8},{9,17},{17,9},{10,18},{18,10},{11,19},{19,11},{12,20... | collective-permute-start | bytes 221192 | tf_op jit(solution)/shard_map/ppermute | solution.py:45
  37.4 15.3 %collective-permute-start.5 = (bf16[768,128]{1,0:T(8,128)(2,1)S(1)}, bf16[768,128]{1,0:T(8,128)(2,1)S(1)}, u32[]{:S(2)}, u32[]{:S(2)}) collective-permute-start(bf16[768,128]{1,0:T(8,128)(2,1)S(1)} %get-tuple-element.100), channel_id=1, source_target_pairs={{0,4},{1,5},{2,6},{3,7},{4,0},{5,1},{6,2},{7,3},{8,12},{9,13},{10,... | collective-permute-start | bytes 589832 | tf_op jit(solution)/shard_map/ppermute | solution.py:356
  39.2 13.6 %collective-permute-start.6 = (bf16[768,128]{1,0:T(8,128)(2,1)S(1)}, bf16[768,128]{1,0:T(8,128)(2,1)S(1)}, u32[]{:S(2)}, u32[]{:S(2)}) collective-permute-start(bf16[768,128]{1,0:T(8,128)(2,1)S(1)} %get-tuple-element.101), channel_id=1, source_target_pairs={{0,20},{1,21},{2,22},{3,23},{4,16},{5,17},{6,18},{7,19},{8,28},{9,... | collective-permute-start | bytes 589832 | tf_op jit(solution)/shard_map/ppermute | solution.py:356
  42.7 10.0 %collective-permute-start.4 = (bf16[768,128]{1,0:T(8,128)(2,1)S(1)}, bf16[768,128]{1,0:T(8,128)(2,1)S(1)}, u32[]{:S(2)}, u32[]{:S(2)}) collective-permute-start(bf16[768,128]{1,0:T(8,128)(2,1)S(1)} %get-tuple-element.99.refs_10_), channel_id=1, source_target_pairs={{0,16},{1,17},{2,18},{3,19},{4,20},{5,21},{6,22},{7,23},{8,24},{9,... | collective-permute-start | bytes 589832 | tf_op jit(solution)/shard_map/ppermute | solution.py:356
  42.8 10.0 %collective-permute-start.7 = (bf16[1536,128]{1,0:T(8,128)(2,1)S(1)}, bf16[1536,128]{1,0:T(8,128)(2,1)S(1)}, u32[]{:S(2)}, u32[]{:S(2)}) collective-permute-start(bf16[1536,128]{1,0:T(8,128)(2,1)S(1)} %get-tuple-element.108), channel_id=1, source_target_pairs={{0,8},{1,9},{2,10},{3,11},{4,12},{5,13},{6,14},{7,15},{8,0},{9,1},... | collective-permute-start | bytes 1179656 | tf_op jit(solution)/shard_map/ppermute | solution.py:356
  44.2 14.0 %collective-permute-start.17 = (bf16[38,3,384]{2,1,0:T(4,128)(2,1)S(1)}, bf16[38,3,384]{2,1,0:T(4,128)(2,1)S(1)}, u32[]{:S(2)}, u32[]{:S(2)}) collective-permute-start(bf16[38,3,384]{2,1,0:T(4,128)(2,1)S(1)} %maximum_select_fusion.1), channel_id=1, source_target_pairs={{0,4},{4,0},{1,5},{5,1},{2,6},{6,2},{3,7},{7,3},{8,12},{12,8},{9,1... | collective-permute-start | bytes 262664 | tf_op jit(solution)/shard_map/ppermute | solution.py:45
  52.7 1.8 %collective-permute-start.9 = (bf16[128,128]{1,0:T(8,128)(2,1)S(1)}, bf16[128,128]{1,0:T(8,128)(2,1)S(1)}, u32[]{:S(2)}, u32[]{:S(2)}) collective-permute-start(bf16[128,128]{1,0:T(8,128)(2,1)S(1)} %get-tuple-element.116), channel_id=1, source_target_pairs={{0,8},{1,9},{2,10},{3,11},{4,12},{5,13},{6,14},{7,15},{8,0},{9,1},... | collective-permute-start | bytes 98312 | tf_op jit(solution)/shard_map/ppermute | solution.py:356
  52.9 10.0 %collective-permute-start.8 = (bf16[768,128]{1,0:T(8,128)(2,1)S(1)}, bf16[768,128]{1,0:T(8,128)(2,1)S(1)}, u32[]{:S(2)}, u32[]{:S(2)}) collective-permute-start(bf16[768,128]{1,0:T(8,128)(2,1)S(1)} %shard_map.199.refs_0_), channel_id=1, source_target_pairs={{0,1},{1,0},{2,3},{3,2},{4,5},{5,4},{6,7},{7,6},{8,9},{9,8},{10,11... | collective-permute-start | bytes 589832 | tf_op jit(solution)/shard_map/ppermute | solution.py:356
  54.7 5.4 %collective-permute-start.10 = (bf16[416,128]{1,0:T(8,128)(2,1)S(1)}, bf16[416,128]{1,0:T(8,128)(2,1)S(1)}, u32[]{:S(2)}, u32[]{:S(2)}) collective-permute-start(bf16[416,128]{1,0:T(8,128)(2,1)S(1)} %get-tuple-element.118), channel_id=1, source_target_pairs={{0,16},{1,17},{2,18},{3,19},{4,20},{5,21},{6,22},{7,23},{8,24},{9,... | collective-permute-start | bytes 319496 | tf_op jit(solution)/shard_map/ppermute | solution.py:356
  55.9 7.1 %collective-permute-start.11 = (bf16[416,128]{1,0:T(8,128)(2,1)S(1)}, bf16[416,128]{1,0:T(8,128)(2,1)S(1)}, u32[]{:S(2)}, u32[]{:S(2)}) collective-permute-start(bf16[416,128]{1,0:T(8,128)(2,1)S(1)} %get-tuple-element.119), channel_id=1, source_target_pairs={{0,4},{1,5},{2,6},{3,7},{4,0},{5,1},{6,2},{7,3},{8,12},{9,13},{10,... | collective-permute-start | bytes 319496 | tf_op jit(solution)/shard_map/ppermute | solution.py:356
  56.5 6.5 %collective-permute-start.12 = (bf16[416,128]{1,0:T(8,128)(2,1)S(1)}, bf16[416,128]{1,0:T(8,128)(2,1)S(1)}, u32[]{:S(2)}, u32[]{:S(2)}) collective-permute-start(bf16[416,128]{1,0:T(8,128)(2,1)S(1)} %get-tuple-element.120), channel_id=1, source_target_pairs={{0,20},{1,21},{2,22},{3,23},{4,16},{5,17},{6,18},{7,19},{8,28},{9,... | collective-permute-start | bytes 319496 | tf_op jit(solution)/shard_map/ppermute | solution.py:356
  63.1 10.3 %collective-permute-start.14 = (bf16[416,128]{1,0:T(8,128)(2,1)S(1)}, bf16[416,128]{1,0:T(8,128)(2,1)S(1)}, u32[]{:S(2)}, u32[]{:S(2)}) collective-permute-start(bf16[416,128]{1,0:T(8,128)(2,1)S(1)} %shard_map.202.refs_8_.refs_0_), channel_id=1, source_target_pairs={{0,1},{1,0},{2,3},{3,2},{4,5},{5,4},{6,7},{7,6},{8,9},{9,8},{10,11... | collective-permute-start | bytes 319496 | tf_op jit(solution)/shard_map/ppermute | solution.py:356
  64.2 9.5 %collective-permute-start.13 = (bf16[768,128]{1,0:T(8,128)(2,1)S(1)}, bf16[768,128]{1,0:T(8,128)(2,1)S(1)}, u32[]{:S(2)}, u32[]{:S(2)}) collective-permute-start(bf16[768,128]{1,0:T(8,128)(2,1)S(1)} %shard_map.201.refs_7_.refs_0_), channel_id=1, source_target_pairs={{0,2},{1,3},{2,0},{3,1},{4,6},{5,7},{6,4},{7,5},{8,10},{9,11},{10,... | collective-permute-start | bytes 589832 | tf_op jit(solution)/shard_map/ppermute | solution.py:356
  73.7 10.4 %collective-permute-start.20 = (bf16[768,128]{1,0:T(8,128)(2,1)S(1)}, bf16[768,128]{1,0:T(8,128)(2,1)S(1)}, u32[]{:S(2)}, u32[]{:S(2)}) collective-permute-start(bf16[768,128]{1,0:T(8,128)(2,1)S(1)} %shard_map.204.refs_1_), channel_id=1, source_target_pairs={{0,20},{1,21},{2,22},{3,23},{4,16},{5,17},{6,18},{7,19},{8,28},{9,... | collective-permute-start | bytes 589832 | tf_op jit(solution)/shard_map/ppermute | solution.py:356
  76.3 7.9 %collective-permute-start.19 = (bf16[768,128]{1,0:T(8,128)(2,1)S(1)}, bf16[768,128]{1,0:T(8,128)(2,1)S(1)}, u32[]{:S(2)}, u32[]{:S(2)}) collective-permute-start(bf16[768,128]{1,0:T(8,128)(2,1)S(1)} %shard_map.204.refs_1_), channel_id=1, source_target_pairs={{0,4},{1,5},{2,6},{3,7},{4,0},{5,1},{6,2},{7,3},{8,12},{9,13},{10,... | collective-permute-start | bytes 589832 | tf_op jit(solution)/shard_map/ppermute | solution.py:356
  77.0 7.2 %collective-permute-start.18 = (bf16[768,128]{1,0:T(8,128)(2,1)S(1)}, bf16[768,128]{1,0:T(8,128)(2,1)S(1)}, u32[]{:S(2)}, u32[]{:S(2)}) collective-permute-start(bf16[768,128]{1,0:T(8,128)(2,1)S(1)} %shard_map.204.refs_1_), channel_id=1, source_target_pairs={{0,16},{1,17},{2,18},{3,19},{4,20},{5,21},{6,22},{7,23},{8,24},{9,... | collective-permute-start | bytes 589832 | tf_op jit(solution)/shard_map/ppermute | solution.py:356
  77.3 6.8 %collective-permute-start.21 = (bf16[416,128]{1,0:T(8,128)(2,1)S(1)}, bf16[416,128]{1,0:T(8,128)(2,1)S(1)}, u32[]{:S(2)}, u32[]{:S(2)}) collective-permute-start(bf16[416,128]{1,0:T(8,128)(2,1)S(1)} %shard_map.205.refs_0_), channel_id=1, source_target_pairs={{0,2},{1,3},{2,0},{3,1},{4,6},{5,7},{6,4},{7,5},{8,10},{9,11},{10,... | collective-permute-start | bytes 319496 | tf_op jit(solution)/shard_map/ppermute | solution.py:356
  84.2 8.8 %collective-permute-start.22 = (bf16[3072,128]{1,0:T(8,128)(2,1)S(1)}, bf16[3072,128]{1,0:T(8,128)(2,1)S(1)}, u32[]{:S(2)}, u32[]{:S(2)}) collective-permute-start(bf16[3072,128]{1,0:T(8,128)(2,1)S(1)} %shard_map.206.own_a), channel_id=1, source_target_pairs={{0,8},{1,9},{2,10},{3,11},{4,12},{5,13},{6,14},{7,15},{8,0},{9,1},... | collective-permute-start | bytes 2359304 | tf_op jit(solution)/shard_map/ppermute | solution.py:356
  84.4 6.4 %collective-permute-start.25 = (bf16[416,128]{1,0:T(8,128)(2,1)S(1)}, bf16[416,128]{1,0:T(8,128)(2,1)S(1)}, u32[]{:S(2)}, u32[]{:S(2)}) collective-permute-start(bf16[416,128]{1,0:T(8,128)(2,1)S(1)} %shard_map.207.refs_1_), channel_id=1, source_target_pairs={{0,20},{1,21},{2,22},{3,23},{4,16},{5,17},{6,18},{7,19},{8,28},{9,... | collective-permute-start | bytes 319496 | tf_op jit(solution)/shard_map/ppermute | solution.py:356
  86.9 6.1 %collective-permute-start.24 = (bf16[416,128]{1,0:T(8,128)(2,1)S(1)}, bf16[416,128]{1,0:T(8,128)(2,1)S(1)}, u32[]{:S(2)}, u32[]{:S(2)}) collective-permute-start(bf16[416,128]{1,0:T(8,128)(2,1)S(1)} %shard_map.207.refs_1_), channel_id=1, source_target_pairs={{0,4},{1,5},{2,6},{3,7},{4,0},{5,1},{6,2},{7,3},{8,12},{9,13},{10,... | collective-permute-start | bytes 319496 | tf_op jit(solution)/shard_map/ppermute | solution.py:356
  87.6 5.4 %collective-permute-start.23 = (bf16[416,128]{1,0:T(8,128)(2,1)S(1)}, bf16[416,128]{1,0:T(8,128)(2,1)S(1)}, u32[]{:S(2)}, u32[]{:S(2)}) collective-permute-start(bf16[416,128]{1,0:T(8,128)(2,1)S(1)} %shard_map.207.refs_1_), channel_id=1, source_target_pairs={{0,16},{1,17},{2,18},{3,19},{4,20},{5,21},{6,22},{7,23},{8,24},{9,... | collective-permute-start | bytes 319496 | tf_op jit(solution)/shard_map/ppermute | solution.py:356
  93.0 1.8 %collective-permute-start.26 = (bf16[1664,128]{1,0:T(8,128)(2,1)S(1)}, bf16[1664,128]{1,0:T(8,128)(2,1)S(1)}, u32[]{:S(2)}, u32[]{:S(2)}) collective-permute-start(bf16[1664,128]{1,0:T(8,128)(2,1)S(1)} %shard_map.208.own_b), channel_id=1, source_target_pairs={{0,8},{1,9},{2,10},{3,11},{4,12},{5,13},{6,14},{7,15},{8,0},{9,1},... | collective-permute-start | bytes 1277960 | tf_op jit(solution)/shard_map/ppermute | solution.py:356

commit v8 on v7

--- a/solution.py
+++ b/solution.py
@@ -53,6 +53,75 @@
     ]
     left, right = swap_edges(*column, "gx", even_x)
     return top, bottom, left, right
+
+
+def whole_halo(tile, even_y, even_x):
+    rows, cols, _ = tile.shape
+    rounds_y = list(enumerate(pair_rounds(lax.axis_size("gy"))))
+    rounds_x = list(enumerate(pair_rounds(lax.axis_size("gx"))))
+    high_y, high_x = (even_y, ~even_y), (even_x, ~even_x)
+    received = {}
+    for y, pairs in rounds_y:
+        strip = jnp.where(high_y[y], tile[rows - 3 :], tile[:3])
+        if pairs:
+            received[y, None] = lax.ppermute(strip, "gy", pairs)
+    for x, pairs in rounds_x:
+        strip = jnp.where(high_x[x], tile[:, cols - 3 :], tile[:, :3])
+        if pairs:
+            received[None, x] = lax.ppermute(strip, "gx", pairs)
+    count = lax.axis_size("gx")
+    for y, pairs_y in rounds_y:
+        for x, pairs_x in rounds_x:
+            pairs = [(a * count + c, b * count + d) for a, b in pairs_y for c, d in pairs_x]
+            if pairs:
+                strip = jnp.where(high_y[y], tile[rows - 3 :], tile[:3])
+                strip = jnp.where(high_x[x], strip[:, cols - 3 :], strip[:, :3])
+                received[y, x] = lax.ppermute(strip, ("gy", "gx"), pairs)
+    return received
+
+
+def fill_tile(pad, tile, at, slab):
+    rows, cols, _ = tile.shape
+
+    def body(row, _):
+        pad[slab, row + 3, EDGE : EDGE + cols, :] = tile[row, :, at].astype(f32)
+        return _
+
+    lax.fori_loop(0, rows, body, 0, unroll=4)
+
+
+def fill_around(pad, even, tile, received):
+    rows, cols, channels = tile.shape
+    even_y, even_x = even[0] == 1, even[1] == 1
+    tall = {False: slice(0, 3), None: slice(3, rows + 3), True: slice(rows + 3, rows + 6)}
+    wide = {
+        False: slice(EDGE - 3, EDGE),
+        None: slice(EDGE, EDGE + cols),
+        True: slice(EDGE + cols, EDGE + cols + 3),
+    }
+    for slab in range(channels // LANES):
+        at = slice(slab * LANES, (slab + 1) * LANES)
+        fill_tile(pad, tile, at, slab)
+
+        def value(y, x, shape):
+            if (y, x) in received:
+                return received[y, x][:, :, at].astype(f32)
+            return jnp.zeros(shape, f32)
+
+        def pick(even, high, first, second):
+            return jnp.where(even, first, second) if high else jnp.where(even, second, first)
+
+        for high_y in (None, False, True):
+            for high_x in (None, False, True):
+                if high_y is None and high_x is None:
+                    continue
+                shape = (rows if high_y is None else 3, cols if high_x is None else 3, LANES)
+                found = []
+                for y in (None,) if high_y is None else (0, 1):
+                    line_x = [value(y, x, shape) for x in ((None,) if high_x is None else (0, 1))]
+                    found.append(line_x[0] if high_x is None else pick(even_x, high_x, *line_x))
+                part = found[0] if high_y is None else pick(even_y, high_y, *found)
+                pad[slab, tall[high_y], wide[high_x], :] = part
 
 
 def fill(pad, tile, top, bottom, left, right):
@@ -107,18 +176,64 @@
     return ref[at].reshape(1, -1)
 
 
-def conv_norm_kernel(
-    tile, top, bottom, left, right, kernel, bias, gain, shift, normed_ref, inv_ref, ln_ref, pad, depth
-):
+def inner(cols, col):
+    return (col > 0) & (col < cols - 8)
+
+
+def conv_inner_kernel(tile, kernel, depth, pad):
     rows, cols, channels = tile.shape
-    fill(pad, tile, top, bottom, left, right)
+    for slab in range(channels // LANES):
+        fill_tile(pad, tile, slice(slab * LANES, (slab + 1) * LANES), slab)
+    for edge in (pl.ds(0, 3), pl.ds(rows + 3, 3)):
+        pad[:, edge, :, :] = jnp.zeros((channels // LANES, 3, pad.shape[2], LANES), f32)
 
     def piece(slab, col, row):
-        acc = taps(pad, kernel, slab, col, row, False)
+        @pl.when(inner(cols, col))
+        def _():
+            acc = taps(pad, kernel, slab, col, row, False)
+            for i in range(BAND):
+                at = pl.ds(pl.multiple_of((row + i) * cols + col, 8), 8)
+                depth[at, lanes(slab)] = acc[i]
+
+    steps(rows, cols, channels, piece)
+
+
+def edge_taps(pad, kernel, slab, col, rows):
+    acc = {}
+    for b in range(7):
+        for r in (0, 1, 2, rows + 3, rows + 4, rows + 5):
+            x = pad[slab, r, pl.ds(col + EDGE - 3 + b, 8), :]
+            for a in range(7):
+                i = r - a
+                if 0 <= i < rows:
+                    term = x * jnp.broadcast_to(kernel[a, b : b + 1, lanes(slab)], (8, LANES))
+                    acc[i] = acc[i] + term if i in acc else term
+    return acc
+
+
+def conv_norm_kernel(keys, even, tile, depth_in, kernel, bias, gain, shift, *refs):
+    received = dict(zip(keys, refs))
+    normed_ref, inv_ref, ln_ref, pad, depth = refs[len(keys) :]
+    rows, cols, channels = tile.shape
+    fill_around(pad, even, tile, received)
+
+    def piece(slab, col, row):
         add = jnp.broadcast_to(line(bias, lanes(slab)), (8, LANES))
-        for i in range(BAND):
-            at = pl.ds(pl.multiple_of((row + i) * cols + col, 8), 8)
-            depth[at, lanes(slab)] = acc[i] + add
+
+        @pl.when(~inner(cols, col))
+        def _():
+            acc = taps(pad, kernel, slab, col, row, False)
+            for i in range(BAND):
+                at = pl.ds(pl.multiple_of((row + i) * cols + col, 8), 8)
+                depth[at, lanes(slab)] = acc[i] + add
+
+        @pl.when(inner(cols, col) & (row == 0))
+        def _():
+            acc = edge_taps(pad, kernel, slab, col, rows)
+            for i in range(rows):
+                at = pl.ds(pl.multiple_of(i * cols + col, 8), 8)
+                value = depth_in[at, lanes(slab)] + add
+                depth[at, lanes(slab)] = value + acc[i] if i in acc else value
 
     steps(rows, cols, channels, piece)
     block = 128
@@ -244,11 +359,11 @@
 SMALL = 64
 
 
-def kernel_grad_kernel(
-    core, tile, top, bottom, left, right, d_depth, sums, gbin_a, gbin_b, keep, send, pad, d32, acc_ref
-):
+def kernel_grad_kernel(keys, core, even, tile, d_depth, sums, gbin_a, gbin_b, *refs):
+    received = dict(zip(keys, refs))
+    keep, send, pad, d32, acc_ref = refs[len(keys) :]
     rows, cols, channels = tile.shape
-    fill(pad, tile, top, bottom, left, right)
+    fill_around(pad, even, tile, received)
     d32[...] = d_depth[...].astype(f32)
     acc_ref[...] = jnp.zeros_like(acc_ref)
 
@@ -532,15 +647,18 @@
     even_x = lax.axis_index("gx") % 2 == 0
     core = (lax.axis_index("gy") % 2).astype(jnp.int32).reshape(1)
     mine = (lax.axis_index("gy") // 2 % 2 + lax.axis_index("gx") % 2 * 2).astype(jnp.int32).reshape(1)
-    even_y, even_x, core, mine, tile = hold((even_y, even_x, core, mine, tile))
-    around = halo(tile, even_y, even_x)
+    even = jnp.stack([even_y, even_x]).astype(jnp.int32)
+    even_y, even_x, even, core, mine, tile = hold((even_y, even_x, even, core, mine, tile))
+    around = whole_halo(tile, even_y, even_x)
     conv_flops = 2 * 49 * pixels * channels * 60
+    (inner_depth,) = call(conv_inner_kernel, [(full, f32)], [pad], (tile, conv_kernel), conv_flops)
     normed, inv, ln_out = call(
-        conv_norm_kernel,
+        functools.partial(conv_norm_kernel, tuple(around)),
         [(full, f32), ((pixels, LANES), f32), (full, bf16)],
         [pad, (full, f32)],
-        (tile, *around, conv_kernel, conv_bias, norm_gain, norm_bias),
+        (even, tile, inner_depth, conv_kernel, conv_bias, norm_gain, norm_bias, *around.values()),
         conv_flops,
+        1,
     )
     acts = lambda width: [((pixels, width), bf16)] * 2
     packed = lambda width: [((width * channels // LANES, LANES), bf16)] * 2 + [((1, width), f32)]
@@ -573,12 +691,12 @@
     d_around = halo(d_tile, even_y, even_x)
     small_rows = ((2 * SMALL, LANES), bf16)
     keep_s, send_s = call(
-        kernel_grad_kernel,
+        functools.partial(kernel_grad_kernel, tuple(around)),
         [small_rows, small_rows],
         [pad, (full, f32), ((channels // LANES, 49, 8, LANES), f32)],
-        (core, tile, *around, d_tile.reshape(full), sums, gbin_a, gbin_b),
+        (core, even, tile, d_tile.reshape(full), sums, gbin_a, gbin_b, *around.values()),
         conv_flops,
-        1,
+        2,
         (parts_a[1],),
     )
     got_a, keep_s, send_s, other_b = hold((got_a, keep_s, send_s, other_b))

time: 97.9 us -> 102 us (1.042)
  Pallas kernels: 39.6 us -> 41.7 us
  waiting for transfers between devices: 21.1 us -> 19.8 us
    ppermute x6 -> x3, starting transfers between devices: 6.11 us -> 1.33 us  [swap_edges(): got.append(lax.ppermute(jnp.where(is_high, high, low), axis, pairs))]
    ppermute x0 -> x5, starting transfers between devices: none -> 4.6 us  [the longest x1 3.03 us: whole_halo(): received[None, x] = lax.ppermute(strip, 'gx', pairs)]
    ppermute x6 -> x3, waiting for transfers between devices: 2.81 us -> 0.01 us  [swap_edges(): got.append(lax.ppermute(jnp.where(is_high, high, low), axis, pairs))]
    pallas_call x15 -> x16, Pallas kernels: 36.9 us -> 39 us  [call(): pl.pallas_call(kernel, out_shape=[jax.ShapeDtypeStruct(shape, dtype) for...]
    select_n x0 -> x4, other arithmetic: none -> 2.07 us  [the longest x1 1.1 us: whole_halo(): strip = jnp.where(high_x[x], tile[:, cols - 3:], tile[:, :3])]
    unnamed x22 -> x26, local copies, waits for them, and re-layouts: 0.06 us -> 2.08 us
    ppermute x21, waiting for transfers between devices: 18.3 us -> 19.8 us  [exchange(): return lax.ppermute(x, AXES, perm)]
    ppermute x21, starting transfers between devices: 26.8 us -> 28 us  [exchange(): return lax.ppermute(x, AXES, perm)]
  transfers between devices with their start and end apart: 27 -> 29, of which waited for: 8 -> 8; matrix products, arithmetic and copies ran while one was open for 2% -> 1% of each run, Pallas kernels for 21% -> 24%
where the time goes in v8:
time: 102 us; the launch traced here: 101 us
  Pallas kernels  41.7 us (41%)
  starting transfers between devices  33.9 us (33%)
  waiting for transfers between devices  19.8 us (19%)
  other arithmetic  2.43 us (2%)
  local copies, waits for them, and re-layouts  2.18 us (2%)
  between operations  1.31 us (1%)
    pallas_call x16, Pallas kernels, call(): pl.pallas_call(kernel, out_shape=[jax.ShapeDtypeStruct(shape, dtype) for...  39 us
    ppermute x21, starting transfers between devices, exchange(): return lax.ppermute(x, AXES, perm)  28 us
    ppermute x21, waiting for transfers between devices, exchange(): return lax.ppermute(x, AXES, perm)  19.8 us
    ppermute x1, starting transfers between devices, whole_halo(): received[None, x] = lax.ppermute(strip, 'gx', pairs)  3.03 us
    pallas_call x1, Pallas kernels, finish(): pl.pallas_call(functools.partial(finish_kernel, factor, widths), grid=(hi...  2.69 us
    unnamed x26, local copies, waits for them, and re-layouts  2.08 us
  transfers between devices with their start and end apart: 29, of which 8 were waited for; matrix products, arithmetic and copies ran while one was open for 1% of the time, Pallas kernels for 24%

profile of v8, /device:TPU:0, one launch (start us, length us, event | category | flops | bytes accessed | tf_op | source)
XLA Modules:
  0.0 101.3 jit_solution(5088160604444532525)
XLA Ops:
  0.7 0.1 add_convert_fusion.refs_0_.refs_1_
  0.8 1.1 %slice_select_fusion = bf16[32,3,384]{2,1,0:T(4,128)(2,1)S(1)} fusion(bf16[32,32,384]{2,1,0:T(8,128)(2,1)} %bitcast.11, pred[]{:T(512)} %eq.13), kind=kLoop, calls=%fused_computation.3 | loop fusion | flops 36864 | bytes 221185 | tf_op jit(solution)/shard_map/jit(_where)/select_n | solution.py:69
  1.9 3.0 %collective-permute-start.2 = (bf16[32,3,384]{2,1,0:T(4,128)(2,1)S(1)}, bf16[32,3,384]{2,1,0:T(4,128)(2,1)S(1)}, u32[]{:S(2)}, u32[]{:S(2)}) collective-permute-start(bf16[32,3,384]{2,1,0:T(4,128)(2,1)S(1)} %slice_select_fusion), channel_id=1, source_target_pairs={{0,4},{4,0},{1,5},{5,1},{2,6},{6,2},{3,7},{7,3},{8,12},{12,8},{9,1... | collective-permute-start | bytes 221192 | tf_op jit(solution)/shard_map/ppermute | solution.py:71
  4.9 0.9 broadcast_select_fusion.3
  5.8 0.1 collective-permute-start
  5.9 0.2 collective-permute-start.3
  6.1 0.7 collective-permute-start.1
  6.8 0.7 collective-permute-start.4
  7.5 0.0 copy-start
  7.5 1.1 %copy-done = bf16[1,32,32,384]{3,2,1,0:T(8,128)(2,1)S(1)} copy-done((bf16[1,32,32,384]{3,2,1,0:T(8,128)(2,1)S(1)}, bf16[1,32,32,384]{3,2,1,0:T(8,128)(2,1)}, u32[]{:S(2)}) %copy-start) | copy-done | bytes 786456
  8.6 0.9 copy-done.5
  9.5 3.0 %shard_map.194.refs_2_ = f32[1024,384]{1,0:T(8,128)S(1)} custom-call(bf16[32,32,384]{2,1,0:T(8,128)(2,1)S(1)} %bitcast.13, f32[7,7,384]{2,1,0:T(8,128)S(1)} %copy-done.5), custom_call_target="tpu_custom_call" | custom-call | flops 2312110080 | bytes 2257920 | tf_op jit(solution)/shard_map/pallas_call | solution.py:438
  12.6 0.0 copy-start.2
  12.6 0.0 copy-start.3
  12.6 0.0 copy-start.11
  12.7 5.8 %shard_map.195 = (f32[1024,384]{1,0:T(8,128)S(1)}, f32[1024,128]{1,0:T(8,128)S(1)}, bf16[1024,384]{1,0:T(8,128)(2,1)S(1)}) custom-call(s32[2]{0:T(128)S(1)} %add_convert_fusion.refs_0_.refs_1_, bf16[32,32,384]{2,1,0:T(8,128)(2,1)S(1)} %bitcast.14, f32[1024,384]{1,0:T(8,128)S(1)} %shard_map.194.refs_2_, f32[7,7,384]{2,1,0:T(8,128)S(1)} %copy-done.5, ...), custom_call_target="tpu_custom_call" | custom-call | flops 2312110080 | bytes 2257920 | tf_op jit(solution)/shard_map/pallas_call | solution.py:438
  18.5 0.0 copy-start.1
  18.5 8.5 %shard_map.196 = (f32[1024,384]{1,0:T(8,128)S(1)}, f32[1024,384]{1,0:T(8,128)S(1)}, bf16[1024,384]{1,0:T(8,128)(2,1)S(1)}, bf16[3072,128]{1,0:T(8,128)(2,1)S(1)}...) custom-call(s32[1]{0:T(128)} %bitcast.2.refs_0_.core, bf16[1024,384]{1,0:T(8,128)(2,1)S(1)} %get-tuple-element.86.refs_1_, ...), custom_call_target="tpu_custom_call" | custom-call | flops 7247757312 | bytes 7077888 | tf_op jit(solution)/shard_map/pallas_call | solution.py:438
  27.1 5.8 %collective-permute-start.5 = (bf16[3072,128]{1,0:T(8,128)(2,1)S(1)}, bf16[3072,128]{1,0:T(8,128)(2,1)S(1)}, u32[]{:S(2)}, u32[]{:S(2)}) collective-permute-start(bf16[3072,128]{1,0:T(8,128)(2,1)S(1)} %get-tuple-element.95), channel_id=1, source_target_pairs={{0,8},{1,9},{2,10},{3,11},{4,12},{5,13},{6,14},{7,15},{8,0},{9,1},... | collective-permute-start | bytes 2359304 | tf_op jit(solution)/shard_map/ppermute | solution.py:471
  32.9 6.6 %shard_map.197 = (bf16[1024,384]{1,0:T(8,128)(2,1)}, bf16[1024,384]{1,0:T(8,128)(2,1)S(1)}, bf16[1536,128]{1,0:T(8,128)(2,1)S(1)}, bf16[1536,128]{1,0:T(8,128)(2...) custom-call(s32[1]{0:T(128)} %bitcast.2.refs_0_.core, bf16[1024,384]{1,0:T(8,128)(2,1)S(1)} %get-tuple-element.86.refs_1_, ...), custom_call_target="tpu_custom_call" | custom-call | flops 7247757312 | bytes 7077888 | tf_op jit(solution)/shard_map/pallas_call | solution.py:438
  39.5 0.1 collective-permute-start.18
  39.6 0.7 collective-permute-start.17
  40.2 0.1 fusion
  40.3 0.3 shard_map.198
  40.6 0.5 collective-permute-start.7
  41.1 4.4 %collective-permute-start.8 = (bf16[768,128]{1,0:T(8,128)(2,1)S(1)}, bf16[768,128]{1,0:T(8,128)(2,1)S(1)}, u32[]{:S(2)}, u32[]{:S(2)}) collective-permute-start(bf16[768,128]{1,0:T(8,128)(2,1)S(1)} %get-tuple-element.103), channel_id=1, source_target_pairs={{0,20},{1,21},{2,22},{3,23},{4,16},{5,17},{6,18},{7,19},{8,28},{9,... | collective-permute-start | bytes 589832 | tf_op jit(solution)/shard_map/ppermute | solution.py:471
  45.5 1.1 %collective-permute-start.9 = (bf16[1536,128]{1,0:T(8,128)(2,1)S(1)}, bf16[1536,128]{1,0:T(8,128)(2,1)S(1)}, u32[]{:S(2)}, u32[]{:S(2)}) collective-permute-start(bf16[1536,128]{1,0:T(8,128)(2,1)S(1)} %get-tuple-element.110), channel_id=1, source_target_pairs={{0,8},{1,9},{2,10},{3,11},{4,12},{5,13},{6,14},{7,15},{8,0},{9,1},... | collective-permute-start | bytes 1179656 | tf_op jit(solution)/shard_map/ppermute | solution.py:471
  46.7 0.2 maximum_select_fusion
  46.8 0.6 collective-permute-start.19
  47.4 7.5 %shard_map.199 = (bf16[128,128]{1,0:T(8,128)(2,1)S(1)}, bf16[128,128]{1,0:T(8,128)(2,1)S(1)}) custom-call(s32[1]{0:T(128)} %bitcast.2.refs_0_.core, s32[2]{0:T(128)S(1)} %add_convert_fusion.refs_0_.refs_1_, bf16[32,32,384]{2,1,0:T(8,128)(2,1)S(1)} %bitcast.16, bf16[1024,384]{1,0:T(8,128)(2,1)S(1)} %get-tuple-element.96, ...), custom_call_target="tpu_custom_call" | custom-call | flops 2312110080 | bytes 2257920 | tf_op jit(solution)/shard_map/pallas_call | solution.py:438
  54.9 0.1 collective-permute-start.11
  55.0 0.1 shard_map.200.refs_0_
  55.1 1.6 %collective-permute-start.10 = (bf16[768,128]{1,0:T(8,128)(2,1)S(1)}, bf16[768,128]{1,0:T(8,128)(2,1)S(1)}, u32[]{:S(2)}, u32[]{:S(2)}) collective-permute-start(bf16[768,128]{1,0:T(8,128)(2,1)S(1)} %shard_map.200.refs_0_), channel_id=1, source_target_pairs={{0,1},{1,0},{2,3},{3,2},{4,5},{5,4},{6,7},{7,6},{8,9},{9,8},{10,11... | collective-permute-start | bytes 589832 | tf_op jit(solution)/shard_map/ppermute | solution.py:471
  56.8 0.1 shard_map.201
  56.9 1.1 %collective-permute-start.12 = (bf16[416,128]{1,0:T(8,128)(2,1)S(1)}, bf16[416,128]{1,0:T(8,128)(2,1)S(1)}, u32[]{:S(2)}, u32[]{:S(2)}) collective-permute-start(bf16[416,128]{1,0:T(8,128)(2,1)S(1)} %get-tuple-element.120), channel_id=1, source_target_pairs={{0,16},{1,17},{2,18},{3,19},{4,20},{5,21},{6,22},{7,23},{8,24},{9,... | collective-permute-start | bytes 319496 | tf_op jit(solution)/shard_map/ppermute | solution.py:471
  58.0 1.5 %collective-permute-start.13 = (bf16[416,128]{1,0:T(8,128)(2,1)S(1)}, bf16[416,128]{1,0:T(8,128)(2,1)S(1)}, u32[]{:S(2)}, u32[]{:S(2)}) collective-permute-start(bf16[416,128]{1,0:T(8,128)(2,1)S(1)} %get-tuple-element.121), channel_id=1, source_target_pairs={{0,4},{1,5},{2,6},{3,7},{4,0},{5,1},{6,2},{7,3},{8,12},{9,13},{10,... | collective-permute-start | bytes 319496 | tf_op jit(solution)/shard_map/ppermute | solution.py:471
  59.5 0.9 collective-permute-start.14
  60.4 0.1 broadcast_select_fusion
  60.5 2.0 %collective-permute-done.12.refs_1_ = bf16[416,128]{1,0:T(8,128)(2,1)S(1)} collective-permute-done((bf16[416,128]{1,0:T(8,128)(2,1)S(1)}, bf16[416,128]{1,0:T(8,128)(2,1)S(1)}, u32[]{:S(2)}, u32[]{:S(2)}) %collective-permute-start.12) | collective-permute-done | bytes 106528 | tf_op jit(solution)/shard_map/ppermute | solution.py:471
  62.5 1.5 %collective-permute-done.13.refs_2_ = bf16[416,128]{1,0:T(8,128)(2,1)S(1)} collective-permute-done((bf16[416,128]{1,0:T(8,128)(2,1)S(1)}, bf16[416,128]{1,0:T(8,128)(2,1)S(1)}, u32[]{:S(2)}, u32[]{:S(2)}) %collective-permute-start.13) | collective-permute-done | bytes 106528 | tf_op jit(solution)/shard_map/ppermute | solution.py:471
  64.0 1.2 %collective-permute-done.14.refs_3_ = bf16[416,128]{1,0:T(8,128)(2,1)S(1)} collective-permute-done((bf16[416,128]{1,0:T(8,128)(2,1)S(1)}, bf16[416,128]{1,0:T(8,128)(2,1)S(1)}, u32[]{:S(2)}, u32[]{:S(2)}) %collective-permute-start.14) | collective-permute-done | bytes 106528 | tf_op jit(solution)/shard_map/ppermute | solution.py:471
  65.3 0.1 shard_map.202.refs_7_.refs_0_
  65.3 0.1 shard_map.203.refs_8_.refs_0_
  65.4 1.0 %collective-permute-start.16 = (bf16[416,128]{1,0:T(8,128)(2,1)S(1)}, bf16[416,128]{1,0:T(8,128)(2,1)S(1)}, u32[]{:S(2)}, u32[]{:S(2)}) collective-permute-start(bf16[416,128]{1,0:T(8,128)(2,1)S(1)} %shard_map.203.refs_8_.refs_0_), channel_id=1, source_target_pairs={{0,1},{1,0},{2,3},{3,2},{4,5},{5,4},{6,7},{7,6},{8,9},{9,8},{10,11... | collective-permute-start | bytes 319496 | tf_op jit(solution)/shard_map/ppermute | solution.py:471
  66.4 2.6 %collective-permute-start.15 = (bf16[768,128]{1,0:T(8,128)(2,1)S(1)}, bf16[768,128]{1,0:T(8,128)(2,1)S(1)}, u32[]{:S(2)}, u32[]{:S(2)}) collective-permute-start(bf16[768,128]{1,0:T(8,128)(2,1)S(1)} %shard_map.202.refs_7_.refs_0_), channel_id=1, source_target_pairs={{0,2},{1,3},{2,0},{3,1},{4,6},{5,7},{6,4},{7,5},{8,10},{9,11},{10,... | collective-permute-start | bytes 589832 | tf_op jit(solution)/shard_map/ppermute | solution.py:471
  69.0 6.7 %shard_map.204 = bf16[1024,384]{1,0:T(8,128)(2,1)} custom-call(bf16[32,32,384]{2,1,0:T(8,128)(2,1)S(1)} %bitcast.19, bf16[3,32,384]{2,1,0:T(8,128)(2,1)S(1)} %get-tuple-element.158.refs_1_, bf16[3,32,384]{2,1,0:T(8,128)(2,1)S(1)} %get-tuple-element.157.refs_2_, bf16[38,3,384]{2,1,0:T(4,128)(2,1)S(1)} %get-tuple-element.160.refs_3_, ...), custom_call_target="tpu_custom_call" | custom-call | flops 2312110080 | bytes 2257920 | tf_op jit(solution)/shard_map/pallas_call | solution.py:438
  75.8 1.5 %collective-permute-done.15.refs_1_ = bf16[768,128]{1,0:T(8,128)(2,1)S(1)} collective-permute-done((bf16[768,128]{1,0:T(8,128)(2,1)S(1)}, bf16[768,128]{1,0:T(8,128)(2,1)S(1)}, u32[]{:S(2)}, u32[]{:S(2)}) %collective-permute-start.15) | collective-permute-done | bytes 196640 | tf_op jit(solution)/shard_map/ppermute | solution.py:471
  77.3 0.1 shard_map.205.refs_1_
  77.3 0.8 collective-permute-start.22
  78.1 1.5 %collective-permute-start.21 = (bf16[768,128]{1,0:T(8,128)(2,1)S(1)}, bf16[768,128]{1,0:T(8,128)(2,1)S(1)}, u32[]{:S(2)}, u32[]{:S(2)}) collective-permute-start(bf16[768,128]{1,0:T(8,128)(2,1)S(1)} %shard_map.205.refs_1_), channel_id=1, source_target_pairs={{0,4},{1,5},{2,6},{3,7},{4,0},{5,1},{6,2},{7,3},{8,12},{9,13},{10,... | collective-permute-start | bytes 589832 | tf_op jit(solution)/shard_map/ppermute | solution.py:471
  79.6 1.3 %collective-permute-start.20 = (bf16[768,128]{1,0:T(8,128)(2,1)S(1)}, bf16[768,128]{1,0:T(8,128)(2,1)S(1)}, u32[]{:S(2)}, u32[]{:S(2)}) collective-permute-start(bf16[768,128]{1,0:T(8,128)(2,1)S(1)} %shard_map.205.refs_1_), channel_id=1, source_target_pairs={{0,16},{1,17},{2,18},{3,19},{4,20},{5,21},{6,22},{7,23},{8,24},{9,... | collective-permute-start | bytes 589832 | tf_op jit(solution)/shard_map/ppermute | solution.py:471
  80.9 0.1 collective-permute-start.23
  81.0 6.7 %collective-permute-done.23.refs_1_ = bf16[416,128]{1,0:T(8,128)(2,1)S(1)} collective-permute-done((bf16[416,128]{1,0:T(8,128)(2,1)S(1)}, bf16[416,128]{1,0:T(8,128)(2,1)S(1)}, u32[]{:S(2)}, u32[]{:S(2)}) %collective-permute-start.23) | collective-permute-done | bytes 106528 | tf_op jit(solution)/shard_map/ppermute | solution.py:471
  87.8 0.1 shard_map.207.own_a
  87.8 0.1 collective-permute-start.24
  87.9 0.1 shard_map.208.refs_1_
  88.0 1.2 %collective-permute-start.27 = (bf16[416,128]{1,0:T(8,128)(2,1)S(1)}, bf16[416,128]{1,0:T(8,128)(2,1)S(1)}, u32[]{:S(2)}, u32[]{:S(2)}) collective-permute-start(bf16[416,128]{1,0:T(8,128)(2,1)S(1)} %shard_map.208.refs_1_), channel_id=1, source_target_pairs={{0,20},{1,21},{2,22},{3,23},{4,16},{5,17},{6,18},{7,19},{8,28},{9,... | collective-permute-start | bytes 319496 | tf_op jit(solution)/shard_map/ppermute | solution.py:471
  89.2 0.9 collective-permute-start.26
  90.1 1.5 %collective-permute-start.25 = (bf16[416,128]{1,0:T(8,128)(2,1)S(1)}, bf16[416,128]{1,0:T(8,128)(2,1)S(1)}, u32[]{:S(2)}, u32[]{:S(2)}) collective-permute-start(bf16[416,128]{1,0:T(8,128)(2,1)S(1)} %shard_map.208.refs_1_), channel_id=1, source_target_pairs={{0,16},{1,17},{2,18},{3,19},{4,20},{5,21},{6,22},{7,23},{8,24},{9,... | collective-permute-start | bytes 319496 | tf_op jit(solution)/shard_map/ppermute | solution.py:471
  91.5 3.2 %collective-permute-done.27.refs_4_ = bf16[416,128]{1,0:T(8,128)(2,1)S(1)} collective-permute-done((bf16[416,128]{1,0:T(8,128)(2,1)S(1)}, bf16[416,128]{1,0:T(8,128)(2,1)S(1)}, u32[]{:S(2)}, u32[]{:S(2)}) %collective-permute-start.27) | collective-permute-done | bytes 106528 | tf_op jit(solution)/shard_map/ppermute | solution.py:471
  94.8 1.8 %collective-permute-done.26.refs_3_ = bf16[416,128]{1,0:T(8,128)(2,1)S(1)} collective-permute-done((bf16[416,128]{1,0:T(8,128)(2,1)S(1)}, bf16[416,128]{1,0:T(8,128)(2,1)S(1)}, u32[]{:S(2)}, u32[]{:S(2)}) %collective-permute-start.26) | collective-permute-done | bytes 106528 | tf_op jit(solution)/shard_map/ppermute | solution.py:471
  96.6 0.1 collective-permute-start.28
  96.6 1.8 %collective-permute-done.28.other_b = bf16[1664,128]{1,0:T(8,128)(2,1)S(1)} collective-permute-done((bf16[1664,128]{1,0:T(8,128)(2,1)S(1)}, bf16[1664,128]{1,0:T(8,128)(2,1)S(1)}, u32[]{:S(2)}, u32[]{:S(2)}) %collective-permute-start.28) | collective-permute-done | bytes 426016 | tf_op jit(solution)/shard_map/ppermute | solution.py:471
  98.4 2.7 %shard_map.210 = (f32[1536,384]{1,0:T(8,128)}, f32[384,1536]{1,0:T(8,128)}, f32[7,7,384]{2,1,0:T(8,128)}, f32[384]{0:T(512)}, f32[384]{0:T(512)}, /*index=5*/f32...) custom-call(s32[1]{0:T(128)} %bitcast.2.refs_0_.core, bf16[3072,128]{1,0:T(8,128)(2,1)S(1)} %shard_map.207.own_a, ...), custom_call_target="tpu_custom_call" | custom-call | tf_op jit(solution)/shard_map/pallas_call | solution.py:610
  (48 shorter events, 0.3 us)
Async XLA Ops:
  1.9 10.8 %collective-permute-start.2 = (bf16[32,3,384]{2,1,0:T(4,128)(2,1)S(1)}, bf16[32,3,384]{2,1,0:T(4,128)(2,1)S(1)}, u32[]{:S(2)}, u32[]{:S(2)}) collective-permute-start(bf16[32,3,384]{2,1,0:T(4,128)(2,1)S(1)} %slice_select_fusion), channel_id=1, source_target_pairs={{0,4},{4,0},{1,5},{5,1},{2,6},{6,2},{3,7},{7,3},{8,12},{12,8},{9,1... | collective-permute-start | bytes 221192 | tf_op jit(solution)/shard_map/ppermute | solution.py:71
  5.8 6.8 %collective-permute-start = (bf16[3,32,384]{2,1,0:T(8,128)(2,1)S(1)}, bf16[3,32,384]{2,1,0:T(8,128)(2,1)S(1)}, u32[]{:S(2)}, u32[]{:S(2)}) collective-permute-start(bf16[3,32,384]{2,1,0:T(8,128)(2,1)S(1)} %get-tuple-element.156), channel_id=1, source_target_pairs={{0,8},{16,24},{8,0},{24,16},{1,9},{17,25},{9,1},{25,17},{2,10},{18... | collective-permute-start | bytes 221192 | tf_op jit(solution)/shard_map/ppermute | solution.py:67
  5.9 6.7 %collective-permute-start.3 = (bf16[3,3,384]{2,1,0:T(4,128)(2,1)S(1)}, bf16[3,3,384]{2,1,0:T(4,128)(2,1)S(1)}, u32[]{:S(2)}, u32[]{:S(2)}) collective-permute-start(bf16[3,3,384]{2,1,0:T(4,128)(2,1)S(1)} %slice_select_fusion.2), channel_id=1, source_target_pairs={{0,12},{4,8},{16,28},{20,24},{8,4},{12,0},{24,20},{28,16},{1,13},{... | collective-permute-start | bytes 20744 | tf_op jit(solution)/shard_map/ppermute | solution.py:79
  6.1 6.5 %collective-permute-start.1 = (bf16[3,32,384]{2,1,0:T(8,128)(2,1)S(1)}, bf16[3,32,384]{2,1,0:T(8,128)(2,1)S(1)}, u32[]{:S(2)}, u32[]{:S(2)}) collective-permute-start(bf16[3,32,384]{2,1,0:T(8,128)(2,1)S(1)} %get-tuple-element.155), channel_id=1, source_target_pairs={{8,16},{16,8},{9,17},{17,9},{10,18},{18,10},{11,19},{19,11},{12,20... | collective-permute-start | bytes 221192 | tf_op jit(solution)/shard_map/ppermute | solution.py:67
  6.8 5.8 %collective-permute-start.4 = (bf16[3,3,384]{2,1,0:T(4,128)(2,1)S(1)}, bf16[3,3,384]{2,1,0:T(4,128)(2,1)S(1)}, u32[]{:S(2)}, u32[]{:S(2)}) collective-permute-start(bf16[3,3,384]{2,1,0:T(4,128)(2,1)S(1)} %slice_select_fusion.1), channel_id=1, source_target_pairs={{8,20},{12,16},{16,12},{20,8},{9,21},{13,17},{17,13},{21,9},{10,22... | collective-permute-start | bytes 20744 | tf_op jit(solution)/shard_map/ppermute | solution.py:79
  7.5 1.1 %copy-start = (bf16[1,32,32,384]{3,2,1,0:T(8,128)(2,1)S(1)}, bf16[1,32,32,384]{3,2,1,0:T(8,128)(2,1)}, u32[]{:S(2)}) copy-start(bf16[1,32,32,384]{3,2,1,0:T(8,128)(2,1)} %param.11) | copy-start | bytes 2359300
  8.6 0.9 copy-start.5
  9.5 3.2 %copy-start.8 = (f32[384]{0:T(512)S(1)}, f32[384]{0:T(512)}, u32[]{:S(2)}) copy-start(f32[384]{0:T(512)} %refs_4_.3) | copy-start | bytes 4612
  9.5 3.2 %copy-start.9 = (f32[384]{0:T(512)S(1)}, f32[384]{0:T(512)}, u32[]{:S(2)}) copy-start(f32[384]{0:T(512)} %refs_6_.3) | copy-start | bytes 4612
  9.5 3.2 %copy-start.10 = (f32[384]{0:T(512)S(1)}, f32[384]{0:T(512)}, u32[]{:S(2)}) copy-start(f32[384]{0:T(512)} %refs_8_.1) | copy-start | bytes 4612
  12.6 5.9 %copy-start.2 = (bf16[1536,384]{1,0:T(8,128)(2,1)S(1)}, bf16[1536,384]{1,0:T(8,128)(2,1)}, u32[]{:S(2)}) copy-start(bf16[1536,384]{1,0:T(8,128)(2,1)} %refs_3_.5) | copy-start | bytes 3538948
  12.6 5.9 %copy-start.3 = (bf16[384,1536]{1,0:T(8,128)(2,1)S(1)}, bf16[384,1536]{1,0:T(8,128)(2,1)}, u32[]{:S(2)}) copy-start(bf16[384,1536]{1,0:T(8,128)(2,1)} %refs_4_.5) | copy-start | bytes 3538948
  12.6 5.9 %copy-start.4 = (bf16[1,32,32,384]{3,2,1,0:T(8,128)(2,1)S(1)}, bf16[1,32,32,384]{3,2,1,0:T(8,128)(2,1)}, u32[]{:S(2)}) copy-start(bf16[1,32,32,384]{3,2,1,0:T(8,128)(2,1)} %param.12) | copy-start | bytes 2359300
  12.6 5.9 %copy-start.7 = (f32[1536]{0:T(1024)S(1)}, f32[1536]{0:T(1024)}, u32[]{:S(2)}) copy-start(f32[1536]{0:T(1024)} %refs_5_.6) | copy-start | bytes 18436
  12.6 5.9 %copy-start.11 = (f32[384]{0:T(512)S(1)}, f32[384]{0:T(512)}, u32[]{:S(2)}) copy-start(f32[384]{0:T(512)} %refs_6_.5) | copy-start | bytes 4612
  18.5 14.3 %copy-start.1 = (bf16[1,32,32,384]{3,2,1,0:T(8,128)(2,1)S(1)}, bf16[1,32,32,384]{3,2,1,0:T(8,128)(2,1)}, u32[]{:S(2)}) copy-start(bf16[1,32,32,384]{3,2,1,0:T(8,128)(2,1)} %param.11) | copy-start | bytes 2359300
  18.5 14.3 %copy-start.12 = (f32[384]{0:T(512)S(1)}, f32[384]{0:T(512)}, u32[]{:S(2)}) copy-start(f32[384]{0:T(512)} %refs_7_.1) | copy-start | bytes 4612
  27.1 12.3 %collective-permute-start.5 = (bf16[3072,128]{1,0:T(8,128)(2,1)S(1)}, bf16[3072,128]{1,0:T(8,128)(2,1)S(1)}, u32[]{:S(2)}, u32[]{:S(2)}) collective-permute-start(bf16[3072,128]{1,0:T(8,128)(2,1)S(1)} %get-tuple-element.95), channel_id=1, source_target_pairs={{0,8},{1,9},{2,10},{3,11},{4,12},{5,13},{6,14},{7,15},{8,0},{9,1},... | collective-permute-start | bytes 2359304 | tf_op jit(solution)/shard_map/ppermute | solution.py:471
  39.5 6.0 %collective-permute-start.18 = (bf16[3,32,384]{2,1,0:T(8,128)(2,1)S(1)}, bf16[3,32,384]{2,1,0:T(8,128)(2,1)S(1)}, u32[]{:S(2)}, u32[]{:S(2)}) collective-permute-start(bf16[3,32,384]{2,1,0:T(8,128)(2,1)S(1)} %get-tuple-element.153), channel_id=1, source_target_pairs={{0,8},{16,24},{8,0},{24,16},{1,9},{17,25},{9,1},{25,17},{2,10},{18... | collective-permute-start | bytes 221192 | tf_op jit(solution)/shard_map/ppermute | solution.py:45
  39.6 7.1 %collective-permute-start.17 = (bf16[3,32,384]{2,1,0:T(8,128)(2,1)S(1)}, bf16[3,32,384]{2,1,0:T(8,128)(2,1)S(1)}, u32[]{:S(2)}, u32[]{:S(2)}) collective-permute-start(bf16[3,32,384]{2,1,0:T(8,128)(2,1)S(1)} %get-tuple-element.154), channel_id=1, source_target_pairs={{8,16},{16,8},{9,17},{17,9},{10,18},{18,10},{11,19},{19,11},{12,20... | collective-permute-start | bytes 221192 | tf_op jit(solution)/shard_map/ppermute | solution.py:45
  40.6 14.3 %collective-permute-start.7 = (bf16[768,128]{1,0:T(8,128)(2,1)S(1)}, bf16[768,128]{1,0:T(8,128)(2,1)S(1)}, u32[]{:S(2)}, u32[]{:S(2)}) collective-permute-start(bf16[768,128]{1,0:T(8,128)(2,1)S(1)} %get-tuple-element.102), channel_id=1, source_target_pairs={{0,4},{1,5},{2,6},{3,7},{4,0},{5,1},{6,2},{7,3},{8,12},{9,13},{10,... | collective-permute-start | bytes 589832 | tf_op jit(solution)/shard_map/ppermute | solution.py:471
  41.1 13.8 %collective-permute-start.8 = (bf16[768,128]{1,0:T(8,128)(2,1)S(1)}, bf16[768,128]{1,0:T(8,128)(2,1)S(1)}, u32[]{:S(2)}, u32[]{:S(2)}) collective-permute-start(bf16[768,128]{1,0:T(8,128)(2,1)S(1)} %get-tuple-element.103), channel_id=1, source_target_pairs={{0,20},{1,21},{2,22},{3,23},{4,16},{5,17},{6,18},{7,19},{8,28},{9,... | collective-permute-start | bytes 589832 | tf_op jit(solution)/shard_map/ppermute | solution.py:471
  45.5 9.4 %collective-permute-start.6 = (bf16[768,128]{1,0:T(8,128)(2,1)S(1)}, bf16[768,128]{1,0:T(8,128)(2,1)S(1)}, u32[]{:S(2)}, u32[]{:S(2)}) collective-permute-start(bf16[768,128]{1,0:T(8,128)(2,1)S(1)} %get-tuple-element.101.refs_12_), channel_id=1, source_target_pairs={{0,16},{1,17},{2,18},{3,19},{4,20},{5,21},{6,22},{7,23},{8,24},{9,... | collective-permute-start | bytes 589832 | tf_op jit(solution)/shard_map/ppermute | solution.py:471
  45.5 9.4 %collective-permute-start.9 = (bf16[1536,128]{1,0:T(8,128)(2,1)S(1)}, bf16[1536,128]{1,0:T(8,128)(2,1)S(1)}, u32[]{:S(2)}, u32[]{:S(2)}) collective-permute-start(bf16[1536,128]{1,0:T(8,128)(2,1)S(1)} %get-tuple-element.110), channel_id=1, source_target_pairs={{0,8},{1,9},{2,10},{3,11},{4,12},{5,13},{6,14},{7,15},{8,0},{9,1},... | collective-permute-start | bytes 1179656 | tf_op jit(solution)/shard_map/ppermute | solution.py:471
  46.8 13.6 %collective-permute-start.19 = (bf16[38,3,384]{2,1,0:T(4,128)(2,1)S(1)}, bf16[38,3,384]{2,1,0:T(4,128)(2,1)S(1)}, u32[]{:S(2)}, u32[]{:S(2)}) collective-permute-start(bf16[38,3,384]{2,1,0:T(4,128)(2,1)S(1)} %maximum_select_fusion), channel_id=1, source_target_pairs={{0,4},{4,0},{1,5},{5,1},{2,6},{6,2},{3,7},{7,3},{8,12},{12,8},{9,1... | collective-permute-start | bytes 262664 | tf_op jit(solution)/shard_map/ppermute | solution.py:45
  54.9 14.1 %copy-start.6 = (f32[7,7,384]{2,1,0:T(8,128)S(1)}, f32[7,7,384]{2,1,0:T(8,128)}, u32[]{:S(2)}) copy-start(f32[7,7,384]{2,1,0:T(8,128)} %refs_5_.7) | copy-start | bytes 225796
  54.9 1.9 %collective-permute-start.11 = (bf16[128,128]{1,0:T(8,128)(2,1)S(1)}, bf16[128,128]{1,0:T(8,128)(2,1)S(1)}, u32[]{:S(2)}, u32[]{:S(2)}) collective-permute-start(bf16[128,128]{1,0:T(8,128)(2,1)S(1)} %get-tuple-element.118), channel_id=1, source_target_pairs={{0,8},{1,9},{2,10},{3,11},{4,12},{5,13},{6,14},{7,15},{8,0},{9,1},... | collective-permute-start | bytes 98312 | tf_op jit(solution)/shard_map/ppermute | solution.py:471
  55.1 10.1 %collective-permute-start.10 = (bf16[768,128]{1,0:T(8,128)(2,1)S(1)}, bf16[768,128]{1,0:T(8,128)(2,1)S(1)}, u32[]{:S(2)}, u32[]{:S(2)}) collective-permute-start(bf16[768,128]{1,0:T(8,128)(2,1)S(1)} %shard_map.200.refs_0_), channel_id=1, source_target_pairs={{0,1},{1,0},{2,3},{3,2},{4,5},{5,4},{6,7},{7,6},{8,9},{9,8},{10,11... | collective-permute-start | bytes 589832 | tf_op jit(solution)/shard_map/ppermute | solution.py:471
  56.9 5.6 %collective-permute-start.12 = (bf16[416,128]{1,0:T(8,128)(2,1)S(1)}, bf16[416,128]{1,0:T(8,128)(2,1)S(1)}, u32[]{:S(2)}, u32[]{:S(2)}) collective-permute-start(bf16[416,128]{1,0:T(8,128)(2,1)S(1)} %get-tuple-element.120), channel_id=1, source_target_pairs={{0,16},{1,17},{2,18},{3,19},{4,20},{5,21},{6,22},{7,23},{8,24},{9,... | collective-permute-start | bytes 319496 | tf_op jit(solution)/shard_map/ppermute | solution.py:471
  58.0 6.0 %collective-permute-start.13 = (bf16[416,128]{1,0:T(8,128)(2,1)S(1)}, bf16[416,128]{1,0:T(8,128)(2,1)S(1)}, u32[]{:S(2)}, u32[]{:S(2)}) collective-permute-start(bf16[416,128]{1,0:T(8,128)(2,1)S(1)} %get-tuple-element.121), channel_id=1, source_target_pairs={{0,4},{1,5},{2,6},{3,7},{4,0},{5,1},{6,2},{7,3},{8,12},{9,13},{10,... | collective-permute-start | bytes 319496 | tf_op jit(solution)/shard_map/ppermute | solution.py:471
  59.5 5.7 %collective-permute-start.14 = (bf16[416,128]{1,0:T(8,128)(2,1)S(1)}, bf16[416,128]{1,0:T(8,128)(2,1)S(1)}, u32[]{:S(2)}, u32[]{:S(2)}) collective-permute-start(bf16[416,128]{1,0:T(8,128)(2,1)S(1)} %get-tuple-element.122), channel_id=1, source_target_pairs={{0,20},{1,21},{2,22},{3,23},{4,16},{5,17},{6,18},{7,19},{8,28},{9,... | collective-permute-start | bytes 319496 | tf_op jit(solution)/shard_map/ppermute | solution.py:471
  65.4 10.3 %collective-permute-start.16 = (bf16[416,128]{1,0:T(8,128)(2,1)S(1)}, bf16[416,128]{1,0:T(8,128)(2,1)S(1)}, u32[]{:S(2)}, u32[]{:S(2)}) collective-permute-start(bf16[416,128]{1,0:T(8,128)(2,1)S(1)} %shard_map.203.refs_8_.refs_0_), channel_id=1, source_target_pairs={{0,1},{1,0},{2,3},{3,2},{4,5},{5,4},{6,7},{7,6},{8,9},{9,8},{10,11... | collective-permute-start | bytes 319496 | tf_op jit(solution)/shard_map/ppermute | solution.py:471
  66.4 10.8 %collective-permute-start.15 = (bf16[768,128]{1,0:T(8,128)(2,1)S(1)}, bf16[768,128]{1,0:T(8,128)(2,1)S(1)}, u32[]{:S(2)}, u32[]{:S(2)}) collective-permute-start(bf16[768,128]{1,0:T(8,128)(2,1)S(1)} %shard_map.202.refs_7_.refs_0_), channel_id=1, source_target_pairs={{0,2},{1,3},{2,0},{3,1},{4,6},{5,7},{6,4},{7,5},{8,10},{9,11},{10,... | collective-permute-start | bytes 589832 | tf_op jit(solution)/shard_map/ppermute | solution.py:471
  77.3 10.4 %collective-permute-start.22 = (bf16[768,128]{1,0:T(8,128)(2,1)S(1)}, bf16[768,128]{1,0:T(8,128)(2,1)S(1)}, u32[]{:S(2)}, u32[]{:S(2)}) collective-permute-start(bf16[768,128]{1,0:T(8,128)(2,1)S(1)} %shard_map.205.refs_1_), channel_id=1, source_target_pairs={{0,20},{1,21},{2,22},{3,23},{4,16},{5,17},{6,18},{7,19},{8,28},{9,... | collective-permute-start | bytes 589832 | tf_op jit(solution)/shard_map/ppermute | solution.py:471
  78.1 9.7 %collective-permute-start.21 = (bf16[768,128]{1,0:T(8,128)(2,1)S(1)}, bf16[768,128]{1,0:T(8,128)(2,1)S(1)}, u32[]{:S(2)}, u32[]{:S(2)}) collective-permute-start(bf16[768,128]{1,0:T(8,128)(2,1)S(1)} %shard_map.205.refs_1_), channel_id=1, source_target_pairs={{0,4},{1,5},{2,6},{3,7},{4,0},{5,1},{6,2},{7,3},{8,12},{9,13},{10,... | collective-permute-start | bytes 589832 | tf_op jit(solution)/shard_map/ppermute | solution.py:471
  79.6 8.1 %collective-permute-start.20 = (bf16[768,128]{1,0:T(8,128)(2,1)S(1)}, bf16[768,128]{1,0:T(8,128)(2,1)S(1)}, u32[]{:S(2)}, u32[]{:S(2)}) collective-permute-start(bf16[768,128]{1,0:T(8,128)(2,1)S(1)} %shard_map.205.refs_1_), channel_id=1, source_target_pairs={{0,16},{1,17},{2,18},{3,19},{4,20},{5,21},{6,22},{7,23},{8,24},{9,... | collective-permute-start | bytes 589832 | tf_op jit(solution)/shard_map/ppermute | solution.py:471
  80.9 6.8 %collective-permute-start.23 = (bf16[416,128]{1,0:T(8,128)(2,1)S(1)}, bf16[416,128]{1,0:T(8,128)(2,1)S(1)}, u32[]{:S(2)}, u32[]{:S(2)}) collective-permute-start(bf16[416,128]{1,0:T(8,128)(2,1)S(1)} %shard_map.206.refs_0_), channel_id=1, source_target_pairs={{0,2},{1,3},{2,0},{3,1},{4,6},{5,7},{6,4},{7,5},{8,10},{9,11},{10,... | collective-permute-start | bytes 319496 | tf_op jit(solution)/shard_map/ppermute | solution.py:471
  87.8 8.7 %collective-permute-start.24 = (bf16[3072,128]{1,0:T(8,128)(2,1)S(1)}, bf16[3072,128]{1,0:T(8,128)(2,1)S(1)}, u32[]{:S(2)}, u32[]{:S(2)}) collective-permute-start(bf16[3072,128]{1,0:T(8,128)(2,1)S(1)} %shard_map.207.own_a), channel_id=1, source_target_pairs={{0,8},{1,9},{2,10},{3,11},{4,12},{5,13},{6,14},{7,15},{8,0},{9,1},... | collective-permute-start | bytes 2359304 | tf_op jit(solution)/shard_map/ppermute | solution.py:471
  88.0 6.8 %collective-permute-start.27 = (bf16[416,128]{1,0:T(8,128)(2,1)S(1)}, bf16[416,128]{1,0:T(8,128)(2,1)S(1)}, u32[]{:S(2)}, u32[]{:S(2)}) collective-permute-start(bf16[416,128]{1,0:T(8,128)(2,1)S(1)} %shard_map.208.refs_1_), channel_id=1, source_target_pairs={{0,20},{1,21},{2,22},{3,23},{4,16},{5,17},{6,18},{7,19},{8,28},{9,... | collective-permute-start | bytes 319496 | tf_op jit(solution)/shard_map/ppermute | solution.py:471
  89.2 7.4 %collective-permute-start.26 = (bf16[416,128]{1,0:T(8,128)(2,1)S(1)}, bf16[416,128]{1,0:T(8,128)(2,1)S(1)}, u32[]{:S(2)}, u32[]{:S(2)}) collective-permute-start(bf16[416,128]{1,0:T(8,128)(2,1)S(1)} %shard_map.208.refs_1_), channel_id=1, source_target_pairs={{0,4},{1,5},{2,6},{3,7},{4,0},{5,1},{6,2},{7,3},{8,12},{9,13},{10,... | collective-permute-start | bytes 319496 | tf_op jit(solution)/shard_map/ppermute | solution.py:471
  90.1 6.5 %collective-permute-start.25 = (bf16[416,128]{1,0:T(8,128)(2,1)S(1)}, bf16[416,128]{1,0:T(8,128)(2,1)S(1)}, u32[]{:S(2)}, u32[]{:S(2)}) collective-permute-start(bf16[416,128]{1,0:T(8,128)(2,1)S(1)} %shard_map.208.refs_1_), channel_id=1, source_target_pairs={{0,16},{1,17},{2,18},{3,19},{4,20},{5,21},{6,22},{7,23},{8,24},{9,... | collective-permute-start | bytes 319496 | tf_op jit(solution)/shard_map/ppermute | solution.py:471
  96.6 1.8 %collective-permute-start.28 = (bf16[1664,128]{1,0:T(8,128)(2,1)S(1)}, bf16[1664,128]{1,0:T(8,128)(2,1)S(1)}, u32[]{:S(2)}, u32[]{:S(2)}) collective-permute-start(bf16[1664,128]{1,0:T(8,128)(2,1)S(1)} %shard_map.209.own_b), channel_id=1, source_target_pairs={{0,8},{1,9},{2,10},{3,11},{4,12},{5,13},{6,14},{7,15},{8,0},{9,1},... | collective-permute-start | bytes 1277960 | tf_op jit(solution)/shard_map/ppermute | solution.py:471

commit v9 on v7

--- a/solution.py
+++ b/solution.py
@@ -35,40 +35,48 @@
     return [pairs + [(b, a) for a, b in pairs] for pairs in (first, second)]
 
 
-def halo(tile, even_y, even_x):
-    rows, cols, _ = tile.shape
-
-    def swap_edges(low, high, axis, even):
-        got = []
-        for pairs, is_high in zip(pair_rounds(lax.axis_size(axis)), (even, ~even)):
-            if pairs:
-                got.append(lax.ppermute(jnp.where(is_high, high, low), axis, pairs))
-            else:
-                got.append(jnp.zeros_like(low))
-        return jnp.where(even, got[1], got[0]), jnp.where(even, got[0], got[1])
-
-    top, bottom = swap_edges(tile[:3], tile[rows - 3 :], "gy", even_y)
+def swap_edges(low, high, axis, even):
+    got = []
+    for pairs, is_high in zip(pair_rounds(lax.axis_size(axis)), (even, ~even)):
+        if pairs:
+            got.append(lax.ppermute(jnp.where(is_high, high, low), axis, pairs))
+        else:
+            got.append(jnp.zeros_like(low))
+    return jnp.where(even, got[1], got[0]), jnp.where(even, got[0], got[1])
+
+
+def halo_rows(tile, even):
+    return swap_edges(tile[:3], tile[tile.shape[0] - 3 :], "gy", even)
+
+
+def halo_cols(tile, top, bottom, even):
     column = [
-        jnp.concatenate([part[:, at : at + 3] for part in (top, tile, bottom)], axis=0) for at in (0, cols - 3)
+        jnp.concatenate([part[:, at : at + 3] for part in (top, tile, bottom)], axis=0)
+        for at in (0, tile.shape[1] - 3)
     ]
-    left, right = swap_edges(*column, "gx", even_x)
-    return top, bottom, left, right
+    return swap_edges(*column, "gx", even)
+
+
+def fill_tile(pad, tile):
+    rows, cols, channels = tile.shape
+    for slab in range(channels // LANES):
+
+        def body(row, _):
+            pad[slab, row + 3, EDGE : EDGE + cols, :] = tile[row, :, slab * LANES : (slab + 1) * LANES].astype(f32)
+            return _
+
+        lax.fori_loop(0, rows, body, 0, unroll=4)
 
 
 def fill(pad, tile, top, bottom, left, right):
     rows, cols, channels = tile.shape
+    fill_tile(pad, tile)
     for slab in range(channels // LANES):
         at = slice(slab * LANES, (slab + 1) * LANES)
         pad[slab, 0:3, EDGE : EDGE + cols, :] = top[:, :, at].astype(f32)
         pad[slab, 3 + rows :, EDGE : EDGE + cols, :] = bottom[:, :, at].astype(f32)
         pad[slab, :, EDGE - 3 : EDGE, :] = left[:, :, at].astype(f32)
         pad[slab, :, EDGE + cols : EDGE + cols + 3, :] = right[:, :, at].astype(f32)
-
-        def body(row, _):
-            pad[slab, row + 3, EDGE : EDGE + cols, :] = tile[row, :, at].astype(f32)
-            return _
-
-        lax.fori_loop(0, rows, body, 0, unroll=4)
 
 
 def steps(rows, cols, channels, body):
@@ -107,18 +115,63 @@
     return ref[at].reshape(1, -1)
 
 
+def inner(cols, col):
+    return (col > 0) & (col < cols - 8)
+
+
+def conv_inner_kernel(tile, kernel, depth, pad):
+    rows, cols, channels = tile.shape
+    fill_tile(pad, tile)
+    for edge in (pl.ds(0, 3), pl.ds(rows + 3, 3)):
+        pad[:, edge, :, :] = jnp.zeros((channels // LANES, 3, pad.shape[2], LANES), f32)
+
+    def piece(slab, col, row):
+        @pl.when(inner(cols, col))
+        def _():
+            acc = taps(pad, kernel, slab, col, row, False)
+            for i in range(BAND):
+                at = pl.ds(pl.multiple_of((row + i) * cols + col, 8), 8)
+                depth[at, lanes(slab)] = acc[i]
+
+    steps(rows, cols, channels, piece)
+
+
+def edge_taps(pad, kernel, slab, col, rows):
+    acc = {}
+    for b in range(7):
+        for r in (0, 1, 2, rows + 3, rows + 4, rows + 5):
+            x = pad[slab, r, pl.ds(col + EDGE - 3 + b, 8), :]
+            for a in range(7):
+                i = r - a
+                if 0 <= i < rows:
+                    term = x * jnp.broadcast_to(kernel[a, b : b + 1, lanes(slab)], (8, LANES))
+                    acc[i] = acc[i] + term if i in acc else term
+    return acc
+
+
 def conv_norm_kernel(
-    tile, top, bottom, left, right, kernel, bias, gain, shift, normed_ref, inv_ref, ln_ref, pad, depth
+    tile, top, bottom, left, right, depth_in, kernel, bias, gain, shift, normed_ref, inv_ref, ln_ref, pad, depth
 ):
     rows, cols, channels = tile.shape
     fill(pad, tile, top, bottom, left, right)
 
     def piece(slab, col, row):
-        acc = taps(pad, kernel, slab, col, row, False)
         add = jnp.broadcast_to(line(bias, lanes(slab)), (8, LANES))
-        for i in range(BAND):
-            at = pl.ds(pl.multiple_of((row + i) * cols + col, 8), 8)
-            depth[at, lanes(slab)] = acc[i] + add
+
+        @pl.when(~inner(cols, col))
+        def _():
+            acc = taps(pad, kernel, slab, col, row, False)
+            for i in range(BAND):
+                at = pl.ds(pl.multiple_of((row + i) * cols + col, 8), 8)
+                depth[at, lanes(slab)] = acc[i] + add
+
+        @pl.when(inner(cols, col) & (row == 0))
+        def _():
+            acc = edge_taps(pad, kernel, slab, col, rows)
+            for i in range(rows):
+                at = pl.ds(pl.multiple_of(i * cols + col, 8), 8)
+                value = depth_in[at, lanes(slab)] + add
+                depth[at, lanes(slab)] = value + acc[i] if i in acc else value
 
     steps(rows, cols, channels, piece)
     block = 128
@@ -147,7 +200,7 @@
     return jnp.sum(x.reshape(-1, 8, x.shape[1]), axis=0)
 
 
-def mlp(core, ln_ref, d_branch, w_in, w_out, b_in, base, width, hid_ref, dpre_ref, keep, send, gbin_ref):
+def mlp(core, ln_ref, d_branch, w_in, w_out, b_in, base, width, hid_ref, dpre_ref, first, second, keep, send, gbin_ref):
     sub = 256
     count = width // sub
     channels = ln_ref.shape[1]
@@ -168,18 +221,18 @@
         gbin_ref[:, at] = jnp.sum(d_pre, axis=0, keepdims=True)
         hid_ref[:, at] = act.astype(bf16)
         dpre_ref[:, at] = d_pre.astype(bf16)
-
-    def store(first, second):
-        for s in range(count):
-            at = slice(s * sub, (s + 1) * sub)
-            gwin = dot(dpre_ref[:, at], ln_ref[...], TN).astype(bf16)
-            for j in range(channels // LANES):
-                start = j * width + s * sub
-                first[start : start + sub, :] = gwin[:, j * LANES : (j + 1) * LANES]
-            gwout = dot(d_branch[...], hid_ref[:, at], TN).astype(bf16)
-            for j in range(sub // LANES):
-                start = (s * sub // LANES + j) * channels
-                second[start : start + channels, :] = gwout[:, j * LANES : (j + 1) * LANES]
+        gwin = dot(dpre_ref[:, at], ln, TN).astype(bf16)
+        for j in range(channels // LANES):
+            start = j * width + s * sub
+            first[start : start + sub, :] = gwin[:, j * LANES : (j + 1) * LANES]
+        gwout = dot(d_branch[...], hid_ref[:, at], TN).astype(bf16)
+        for j in range(sub // LANES):
+            start = (s * sub // LANES + j) * channels
+            second[start : start + channels, :] = gwout[:, j * LANES : (j + 1) * LANES]
+
+    def store(one, two):
+        one[...] = first[...]
+        two[...] = second[...]
 
     pl.when(core[0] == 0)(lambda: store(keep, send))
     pl.when(core[0] != 0)(lambda: store(send, keep))
@@ -190,10 +243,10 @@
 
 def mlp_first_kernel(
     base, width, core, ln_ref, cot, w_in, w_out, b_in, scale, branch_ref, dnorm_ref, d_branch_ref,
-    keep, send, gbin_ref, hid_ref, dpre_ref,
+    keep, send, gbin_ref, hid_ref, dpre_ref, gwin, gwout,
 ):
     d_branch_ref[...] = (line(scale) * cot[...].astype(f32)).astype(bf16)
-    mlp(core, ln_ref, d_branch_ref, w_in, w_out, b_in, base, width, hid_ref, dpre_ref, keep, send, gbin_ref)
+    mlp(core, ln_ref, d_branch_ref, w_in, w_out, b_in, base, width, hid_ref, dpre_ref, gwin, gwout, keep, send, gbin_ref)
     at = pl.ds(base, width)
 
     def step(i, _):
@@ -209,10 +262,10 @@
     base, width, core, ln_ref, cot, w_in, w_out, b_in, scale, b_out, gain, page, normed_ref, inv_ref,
     branch_ref, dnorm_ref, d_branch_ref,
     result, d_depth_ref, keep, send, gbin_ref, sums_ref,
-    hid_ref, dpre_ref, sums,
+    hid_ref, dpre_ref, gwin, gwout, sums,
 ):
     sums[...] = jnp.zeros_like(sums)
-    mlp(core, ln_ref, d_branch_ref, w_in, w_out, b_in, base, width, hid_ref, dpre_ref, keep, send, gbin_ref)
+    mlp(core, ln_ref, d_branch_ref, w_in, w_out, b_in, base, width, hid_ref, dpre_ref, gwin, gwout, keep, send, gbin_ref)
     units = pl.ds(base, width)
 
     def step(i, _):
@@ -439,32 +492,30 @@
     return x
 
 
-def finish_kernel(
-    factor, widths, core, own_a, other_a, own_b, other_b,
-    win, wout, gk, scale, b_out, gain, shift, bias, b_in,
-):
+def finish_kernel(factor, width, core, own, other, win, wout, *smalls):
     channels, unit = wout.shape
     slabs = channels // LANES
 
-    def rows(ref, width, at):
+    def rows(ref, at):
         part, block = ref.shape[0] // 4, width * slabs // 4
         start = at // block * part + at % block
         return ref[start : start + LANES, :].astype(f32) * factor
 
-    def store(first, second, width, offset):
+    def store(first, second, offset):
         for j in range(slabs):
             for i in range(0, unit, LANES):
-                win[i : i + LANES, j * LANES : (j + 1) * LANES] = rows(first, width, j * width + offset + i)
+                win[i : i + LANES, j * LANES : (j + 1) * LANES] = rows(first, j * width + offset + i)
         for j in range(unit // LANES):
             for i in range(0, channels, LANES):
                 wout[i : i + LANES, j * LANES : (j + 1) * LANES] = rows(
-                    second, width, (offset // LANES + j) * channels + i
+                    second, (offset // LANES + j) * channels + i
                 )
 
     def store_small(*halves):
+        gk, scale, b_out, gain, shift, bias, b_in = smalls
         for slab in range(slabs):
             at = slice(slab * LANES, (slab + 1) * LANES)
-            start = slab * (halves[0].shape[0] // 4) + widths[1] * slabs // 4
+            start = slab * (halves[0].shape[0] // 4) + width * slabs // 4
             values = jnp.concatenate([ref[start : start + SMALL // 2, :].astype(f32) for ref in halves]) * factor
             for j in range(7):
                 gk[j, :, at] = values[7 * j : 7 * j + 7]
@@ -476,34 +527,38 @@
 
     is_first = core[0] == 0
     step = pl.program_id(0)
-    for i in range(sum(widths) // unit):
-        offset, halves = i * unit, (own_a, other_a)
-        width = widths[0]
-        if offset >= widths[0]:
-            offset, halves, width = offset - widths[0], (own_b, other_b), widths[1]
+    for i in range(width // unit):
         here = step == i
-        pl.when(here & is_first)(functools.partial(store, *halves, width, offset))
-        pl.when(here & ~is_first)(functools.partial(store, *halves[::-1], width, offset))
-    pl.when((step == 0) & is_first)(lambda: store_small(own_b, other_b))
-    pl.when((step == 0) & ~is_first)(lambda: store_small(other_b, own_b))
-
-
-def finish(factor, widths, channels, core, *halves):
-    hid, unit = sum(widths), widths[1]
+        pl.when(here & is_first)(functools.partial(store, own, other, i * unit))
+        pl.when(here & ~is_first)(functools.partial(store, other, own, i * unit))
+    if smalls:
+        pl.when(is_first)(lambda: store_small(own, other))
+        pl.when(~is_first)(lambda: store_small(other, own))
+
+
+def finish(factor, base, width, unit, hid, channels, core, own, other, whole=()):
     vmem = pl.BlockSpec(memory_space=pltpu.VMEM)
-    outs = [(hid, channels), (channels, hid), (7, 7, channels)] + [(channels,)] * 5 + [(hid,)]
+    start = base // unit
+    outs = [(hid, channels), (channels, hid)]
+    smalls = [(7, 7, channels)] + [(channels,)] * 5 + [(hid,)] if whole else []
+
+    def kernel(core, own, other, *refs):
+        finish_kernel(factor, width, core, own, other, *refs[len(whole) :])
+
     return pl.pallas_call(
-        functools.partial(finish_kernel, factor, widths),
-        grid=(hid // unit,),
-        out_shape=[jax.ShapeDtypeStruct(shape, f32) for shape in outs],
-        in_specs=[pl.BlockSpec(memory_space=pltpu.SMEM)] + [vmem] * len(halves),
+        kernel,
+        grid=(width // unit,),
+        out_shape=[jax.ShapeDtypeStruct(shape, f32) for shape in outs + smalls],
+        in_specs=[pl.BlockSpec(memory_space=pltpu.SMEM), vmem, vmem]
+        + [pl.BlockSpec(memory_space=pl.ANY)] * len(whole),
         out_specs=[
-            pl.BlockSpec((unit, channels), lambda i: (i, 0)),
-            pl.BlockSpec((channels, unit), lambda i: (0, i)),
+            pl.BlockSpec((unit, channels), lambda i: (start + i, 0)),
+            pl.BlockSpec((channels, unit), lambda i: (0, start + i)),
         ]
-        + [vmem] * 7,
+        + [vmem] * len(smalls),
+        input_output_aliases={3: 0, 4: 1} if whole else {},
         compiler_params=pltpu.CompilerParams(vmem_limit_bytes=24 << 20),
-    )(core, *halves)
+    )(core, own, other, *whole)
 
 
 def shards(
@@ -533,16 +588,18 @@
     core = (lax.axis_index("gy") % 2).astype(jnp.int32).reshape(1)
     mine = (lax.axis_index("gy") // 2 % 2 + lax.axis_index("gx") % 2 * 2).astype(jnp.int32).reshape(1)
     even_y, even_x, core, mine, tile = hold((even_y, even_x, core, mine, tile))
-    around = halo(tile, even_y, even_x)
+    around = halo_rows(tile, even_y)
+    around += halo_cols(tile, *around, even_x)
     conv_flops = 2 * 49 * pixels * channels * 60
+    (inner_depth,) = call(conv_inner_kernel, [(full, f32)], [pad], (tile, conv_kernel), conv_flops)
     normed, inv, ln_out = call(
         conv_norm_kernel,
         [(full, f32), ((pixels, LANES), f32), (full, bf16)],
         [pad, (full, f32)],
-        (tile, *around, conv_kernel, conv_bias, norm_gain, norm_bias),
+        (tile, *around, inner_depth, conv_kernel, conv_bias, norm_gain, norm_bias),
         conv_flops,
     )
-    acts = lambda width: [((pixels, width), bf16)] * 2
+    acts = lambda width: [((pixels, width), bf16)] * 2 + [((width * channels // LANES, LANES), bf16)] * 2
     packed = lambda width: [((width * channels // LANES, LANES), bf16)] * 2 + [((1, width), f32)]
     core_flip = [("gy", 0)]
     mlp_flops = 12 * pixels * channels * hid
@@ -570,7 +627,6 @@
     parts_a = add_halves(mine, keep_a, other_a)
     got_a = spread(parts_a)
     other_b = exchange(send_b, core_flip)
-    d_around = halo(d_tile, even_y, even_x)
     small_rows = ((2 * SMALL, LANES), bf16)
     keep_s, send_s = call(
         kernel_grad_kernel,
@@ -586,9 +642,13 @@
     part_a = add(*got_a)
     parts_b = add_halves(mine, keep_b, other_b, keep_s, other_s)
     flips = [[bit] for bit in beyond()]
-    got_a, got_b = exchange(part_a, flips[0]), spread(parts_b)
-    got_a, got_b = hold((got_a, got_b))
+    parts_b, d_tile = hold((parts_b, d_tile))
+    got_a, got_b, d_rows = hold((exchange(part_a, flips[0]), spread(parts_b), halo_rows(d_tile, even_y)))
     part_a, part_b = add(part_a, got_a), add(*got_b)
+    d_around = d_rows + halo_cols(d_tile, *d_rows, even_x)
+    for ahead, behind in zip(flips[1:], flips):
+        got_a, got_b, d_around = hold((exchange(part_a, ahead), exchange(part_b, behind), d_around))
+        part_a, part_b = add(part_a, got_a), add(part_b, got_b)
     (grad_pages,) = call(
         conv_grad_kernel,
         [(full, bf16)],
@@ -598,17 +658,15 @@
         0,
         (part_a, part_b),
     )
-    for ahead, behind in zip(flips[1:], flips):
-        got_a, got_b, grad_pages = hold((exchange(part_a, ahead), exchange(part_b, behind), grad_pages))
-        part_a, part_b = add(part_a, got_a), add(part_b, got_b)
-    got_a, got_b = hold((spread([part_a] * 4), exchange(part_b, flips[-1])))
+    got_a, got_b, grad_pages = hold((spread([part_a] * 4), exchange(part_b, flips[-1]), grad_pages))
     half_a, part_b = join(mine, *got_a), add(part_b, got_b)
     got_a, got_b = hold(([half_a, exchange(half_a, core_flip)], spread([part_b] * 4)))
     half_b = join(mine, *got_b)
     got_b = [half_b, exchange(half_b, core_flip)]
     factor = float(pixels * lax.axis_size("gy") * lax.axis_size("gx") * lax.axis_size("rep")) ** (-0.5)
+    begun = finish(factor, 0, first, second, hid, channels, core, *got_a)
     win, wout, gk, g_scale, g_bout, g_gain, g_shift, g_bias, g_bin = finish(
-        factor, (first, second), channels, core, *got_a, *got_b
+        factor, first, second, second, hid, channels, core, *got_b, begun
     )
     return (
         result.reshape(pages.shape),

time: 97.9 us -> 102 us (1.042); the launches traced: 97.7 us -> 100 us
  Pallas kernels: 39.6 us -> 41.9 us
  local copies, waits for them, and re-layouts: 1.29 us -> 3.31 us
  starting transfers between devices: 32.9 us -> 31.5 us
    ppermute x6, waiting for transfers between devices: 2.81 us -> 0.02 us  [swap_edges(): got.append(lax.ppermute(jnp.where(is_high, high, low), axis, pairs))]
    ppermute x21, waiting for transfers between devices: 18.3 us -> 21 us  [exchange(): return lax.ppermute(x, AXES, perm)]
    unnamed x22 -> x26, local copies, waits for them, and re-layouts: 0.06 us -> 2.08 us
    pallas_call x15 -> x16, Pallas kernels: 36.9 us -> 38.8 us  [call(): pl.pallas_call(kernel, out_shape=[jax.ShapeDtypeStruct(shape, dtype) for...]
    ppermute x21, starting transfers between devices: 26.8 us -> 25.6 us  [exchange(): return lax.ppermute(x, AXES, perm)]
    pallas_call x1 -> x2, Pallas kernels: 2.69 us -> 3.19 us  [finish(): pl.pallas_call(kernel, grid=(width // unit,), out_shape=[jax.ShapeDtypeSt...]
  transfers between devices with their start and end apart: 27 -> 27, of which waited for: 8 -> 9; matrix products, arithmetic and copies ran while one was open for 2% -> 1% of each run, Pallas kernels for 21% -> 26%
where the time goes in v9:
time: 102 us; the launch traced here: 100 us
  Pallas kernels  41.9 us (41%)
  starting transfers between devices  31.5 us (31%)
  waiting for transfers between devices  21 us (21%)
  local copies, waits for them, and re-layouts  3.31 us (3%)
  other arithmetic  1.5 us (1%)
  between operations  1.09 us (1%)
    pallas_call x16, Pallas kernels, call(): pl.pallas_call(kernel, out_shape=[jax.ShapeDtypeStruct(shape, dtype) for...  38.8 us
    ppermute x21, starting transfers between devices, exchange(): return lax.ppermute(x, AXES, perm)  25.6 us
    ppermute x21, waiting for transfers between devices, exchange(): return lax.ppermute(x, AXES, perm)  21 us
    ppermute x6, starting transfers between devices, swap_edges(): got.append(lax.ppermute(jnp.where(is_high, high, low), axis, pairs))  5.96 us
    pallas_call x2, Pallas kernels, finish(): pl.pallas_call(kernel, grid=(width // unit,), out_shape=[jax.ShapeDtypeSt...  3.19 us
    unnamed x26, local copies, waits for them, and re-layouts  2.08 us
  transfers between devices with their start and end apart: 27, of which 9 were waited for; matrix products, arithmetic and copies ran while one was open for 1% of the time, Pallas kernels for 26%

profile of v9, /device:TPU:0, one launch (start us, length us, event | category | flops | bytes accessed | tf_op | source)
XLA Modules:
  0.0 100.4 jit_solution(4786950979865931057)
XLA Ops:
  0.7 0.9 broadcast_select_fusion.11
  1.6 0.5 collective-permute-start.1
  2.2 0.7 collective-permute-start
  2.8 1.1 %fusion.1 = (bf16[32,3,384]{2,1,0:T(4,128)(2,1)S(1)}, bf16[32,3,384]{2,1,0:T(4,128)(2,1)S(1)}) fusion(bf16[32,32,384]{2,1,0:T(8,128)(2,1)} %bitcast.10), kind=kLoop, calls=%fused_computation.15 | loop fusion | bytes 294912 | tf_op jit(solution)/shard_map/slice | solution.py:54
  4.0 0.2 maximum_select_fusion
  4.2 2.6 %collective-permute-start.2 = (bf16[38,3,384]{2,1,0:T(4,128)(2,1)S(1)}, bf16[38,3,384]{2,1,0:T(4,128)(2,1)S(1)}, u32[]{:S(2)}, u32[]{:S(2)}) collective-permute-start(bf16[38,3,384]{2,1,0:T(4,128)(2,1)S(1)} %maximum_select_fusion), channel_id=1, source_target_pairs={{0,4},{4,0},{1,5},{5,1},{2,6},{6,2},{3,7},{7,3},{8,12},{12,8},{9,1... | collective-permute-start | bytes 262664 | tf_op jit(solution)/shard_map/ppermute | solution.py:42
  6.8 1.1 %copy-done = bf16[1,32,32,384]{3,2,1,0:T(8,128)(2,1)S(1)} copy-done((bf16[1,32,32,384]{3,2,1,0:T(8,128)(2,1)S(1)}, bf16[1,32,32,384]{3,2,1,0:T(8,128)(2,1)}, u32[]{:S(2)}) %copy-start) | copy-done | bytes 786456
  7.9 0.9 copy-done.5
  8.8 3.0 %shard_map.194.refs_5_ = f32[1024,384]{1,0:T(8,128)S(1)} custom-call(bf16[32,32,384]{2,1,0:T(8,128)(2,1)S(1)} %bitcast.11, f32[7,7,384]{2,1,0:T(8,128)S(1)} %copy-done.5), custom_call_target="tpu_custom_call" | custom-call | flops 2312110080 | bytes 2257920 | tf_op jit(solution)/shard_map/pallas_call | solution.py:376
  11.8 0.1 broadcast_select_fusion.2
  12.0 0.0 copy-start.4
  12.0 0.0 copy-start.7
  12.0 5.2 %shard_map.195 = (f32[1024,384]{1,0:T(8,128)S(1)}, f32[1024,128]{1,0:T(8,128)S(1)}, bf16[1024,384]{1,0:T(8,128)(2,1)S(1)}) custom-call(bf16[32,32,384]{2,1,0:T(8,128)(2,1)S(1)} %bitcast.12, bf16[3,32,384]{2,1,0:T(8,128)(2,1)S(1)} %get-tuple-element.186.refs_1_.refs_2_, bf16[3,32,384]{2,1,0:T(8,128)(2,1)S(1)} %get-tuple-element.185.refs_2_.refs_3_, ...), custom_call_target="tpu_custom_call" | custom-call | flops 2312110080 | bytes 2257920 | tf_op jit(solution)/shard_map/pallas_call | solution.py:376
  17.3 0.0 copy-start.1
  17.3 0.0 copy-start.12
  17.3 9.2 %shard_map.196 = (f32[1024,384]{1,0:T(8,128)S(1)}, f32[1024,384]{1,0:T(8,128)S(1)}, bf16[1024,384]{1,0:T(8,128)(2,1)S(1)}, bf16[3072,128]{1,0:T(8,128)(2,1)S(1)}...) custom-call(s32[1]{0:T(128)} %bitcast.refs_0_.core, bf16[1024,384]{1,0:T(8,128)(2,1)S(1)} %get-tuple-element.97.refs_1_, ...), custom_call_target="tpu_custom_call" | custom-call | flops 7247757312 | bytes 7077888 | tf_op jit(solution)/shard_map/pallas_call | solution.py:376
  26.6 4.5 %collective-permute-start.3 = (bf16[3072,128]{1,0:T(8,128)(2,1)S(1)}, bf16[3072,128]{1,0:T(8,128)(2,1)S(1)}, u32[]{:S(2)}, u32[]{:S(2)}) collective-permute-start(bf16[3072,128]{1,0:T(8,128)(2,1)S(1)} %get-tuple-element.106), channel_id=1, source_target_pairs={{0,8},{1,9},{2,10},{3,11},{4,12},{5,13},{6,14},{7,15},{8,0},{9,1},... | collective-permute-start | bytes 2359304 | tf_op jit(solution)/shard_map/ppermute | solution.py:409
  31.0 6.8 %shard_map.197 = (bf16[1024,384]{1,0:T(8,128)(2,1)}, bf16[1024,384]{1,0:T(8,128)(2,1)S(1)}, bf16[1536,128]{1,0:T(8,128)(2,1)S(1)}, bf16[1536,128]{1,0:T(8,128)(2...) custom-call(s32[1]{0:T(128)} %bitcast.refs_0_.core, bf16[1024,384]{1,0:T(8,128)(2,1)S(1)} %get-tuple-element.97.refs_1_, ...), custom_call_target="tpu_custom_call" | custom-call | flops 7247757312 | bytes 7077888 | tf_op jit(solution)/shard_map/pallas_call | solution.py:376
  37.8 0.1 collective-permute-start.7
  37.9 0.3 shard_map.198
  38.2 0.4 collective-permute-start.5
  38.5 2.6 %collective-permute-start.6 = (bf16[768,128]{1,0:T(8,128)(2,1)S(1)}, bf16[768,128]{1,0:T(8,128)(2,1)S(1)}, u32[]{:S(2)}, u32[]{:S(2)}) collective-permute-start(bf16[768,128]{1,0:T(8,128)(2,1)S(1)} %get-tuple-element.114), channel_id=1, source_target_pairs={{0,20},{1,21},{2,22},{3,23},{4,16},{5,17},{6,18},{7,19},{8,28},{9,... | collective-permute-start | bytes 589832 | tf_op jit(solution)/shard_map/ppermute | solution.py:409
  41.1 0.6 collective-permute-start.4
  41.7 6.9 %shard_map.199 = (bf16[128,128]{1,0:T(8,128)(2,1)S(1)}, bf16[128,128]{1,0:T(8,128)(2,1)S(1)}) custom-call(s32[1]{0:T(128)} %bitcast.refs_0_.core, bf16[32,32,384]{2,1,0:T(8,128)(2,1)S(1)} %bitcast.14, bf16[3,32,384]{2,1,0:T(8,128)(2,1)S(1)} %get-tuple-element.186.refs_1_.refs_2_, bf16[3,32,384]{2,1,0:T(8,128)(2,1)S(1)} %get-tuple-element.185.refs_2_.refs_3_, ...), custom_call_target="tpu_custom_call" | custom-call | flops 2312110080 | bytes 2257920 | tf_op jit(solution)/shard_map/pallas_call | solution.py:376
  48.6 1.1 %collective-permute-done.5.refs_2_ = bf16[768,128]{1,0:T(8,128)(2,1)S(1)} collective-permute-done((bf16[768,128]{1,0:T(8,128)(2,1)S(1)}, bf16[768,128]{1,0:T(8,128)(2,1)S(1)}, u32[]{:S(2)}, u32[]{:S(2)}) %collective-permute-start.5) | collective-permute-done | bytes 196640 | tf_op jit(solution)/shard_map/ppermute | solution.py:409
  49.7 1.2 %collective-permute-done.4.refs_1_ = bf16[768,128]{1,0:T(8,128)(2,1)S(1)} collective-permute-done((bf16[768,128]{1,0:T(8,128)(2,1)S(1)}, bf16[768,128]{1,0:T(8,128)(2,1)S(1)}, u32[]{:S(2)}, u32[]{:S(2)}) %collective-permute-start.4) | collective-permute-done | bytes 196640 | tf_op jit(solution)/shard_map/ppermute | solution.py:409
  50.9 0.1 shard_map.200.refs_0_
  51.1 1.6 %collective-permute-start.8 = (bf16[768,128]{1,0:T(8,128)(2,1)S(1)}, bf16[768,128]{1,0:T(8,128)(2,1)S(1)}, u32[]{:S(2)}, u32[]{:S(2)}) collective-permute-start(bf16[768,128]{1,0:T(8,128)(2,1)S(1)} %shard_map.200.refs_0_), channel_id=1, source_target_pairs={{0,1},{1,0},{2,3},{3,2},{4,5},{5,4},{6,7},{7,6},{8,9},{9,8},{10,11... | collective-permute-start | bytes 589832 | tf_op jit(solution)/shard_map/ppermute | solution.py:409
  52.7 0.1 shard_map.201
  52.9 0.3 collective-permute-start.14
  53.1 0.7 collective-permute-start.13
  53.8 0.1 fusion
  53.9 3.2 %collective-permute-start.10 = (bf16[416,128]{1,0:T(8,128)(2,1)S(1)}, bf16[416,128]{1,0:T(8,128)(2,1)S(1)}, u32[]{:S(2)}, u32[]{:S(2)}) collective-permute-start(bf16[416,128]{1,0:T(8,128)(2,1)S(1)} %get-tuple-element.135), channel_id=1, source_target_pairs={{0,16},{1,17},{2,18},{3,19},{4,20},{5,21},{6,22},{7,23},{8,24},{9,... | collective-permute-start | bytes 319496 | tf_op jit(solution)/shard_map/ppermute | solution.py:409
  57.1 0.5 collective-permute-start.11
  57.6 1.0 %collective-permute-start.12 = (bf16[416,128]{1,0:T(8,128)(2,1)S(1)}, bf16[416,128]{1,0:T(8,128)(2,1)S(1)}, u32[]{:S(2)}, u32[]{:S(2)}) collective-permute-start(bf16[416,128]{1,0:T(8,128)(2,1)S(1)} %get-tuple-element.137), channel_id=1, source_target_pairs={{0,20},{1,21},{2,22},{3,23},{4,16},{5,17},{6,18},{7,19},{8,28},{9,... | collective-permute-start | bytes 319496 | tf_op jit(solution)/shard_map/ppermute | solution.py:409
  58.7 3.3 %collective-permute-done.10.refs_1_ = bf16[416,128]{1,0:T(8,128)(2,1)S(1)} collective-permute-done((bf16[416,128]{1,0:T(8,128)(2,1)S(1)}, bf16[416,128]{1,0:T(8,128)(2,1)S(1)}, u32[]{:S(2)}, u32[]{:S(2)}) %collective-permute-start.10) | collective-permute-done | bytes 106528 | tf_op jit(solution)/shard_map/ppermute | solution.py:409
  62.0 2.2 %collective-permute-done.11.refs_2_ = bf16[416,128]{1,0:T(8,128)(2,1)S(1)} collective-permute-done((bf16[416,128]{1,0:T(8,128)(2,1)S(1)}, bf16[416,128]{1,0:T(8,128)(2,1)S(1)}, u32[]{:S(2)}, u32[]{:S(2)}) %collective-permute-start.11) | collective-permute-done | bytes 106528 | tf_op jit(solution)/shard_map/ppermute | solution.py:409
  64.2 0.2 maximum_select_fusion.1
  64.3 1.2 %collective-permute-start.17 = (bf16[38,3,384]{2,1,0:T(4,128)(2,1)S(1)}, bf16[38,3,384]{2,1,0:T(4,128)(2,1)S(1)}, u32[]{:S(2)}, u32[]{:S(2)}) collective-permute-start(bf16[38,3,384]{2,1,0:T(4,128)(2,1)S(1)} %maximum_select_fusion.1), channel_id=1, source_target_pairs={{0,4},{4,0},{1,5},{5,1},{2,6},{6,2},{3,7},{7,3},{8,12},{12,8},{9,1... | collective-permute-start | bytes 262664 | tf_op jit(solution)/shard_map/ppermute | solution.py:42
  65.6 0.1 shard_map.203.refs_0_
  65.6 1.1 %collective-permute-start.16 = (bf16[416,128]{1,0:T(8,128)(2,1)S(1)}, bf16[416,128]{1,0:T(8,128)(2,1)S(1)}, u32[]{:S(2)}, u32[]{:S(2)}) collective-permute-start(bf16[416,128]{1,0:T(8,128)(2,1)S(1)} %shard_map.203.refs_0_), channel_id=1, source_target_pairs={{0,1},{1,0},{2,3},{3,2},{4,5},{5,4},{6,7},{7,6},{8,9},{9,8},{10,11... | collective-permute-start | bytes 319496 | tf_op jit(solution)/shard_map/ppermute | solution.py:409
  66.7 0.1 shard_map.202.refs_0_
  66.8 2.6 %collective-permute-start.15 = (bf16[768,128]{1,0:T(8,128)(2,1)S(1)}, bf16[768,128]{1,0:T(8,128)(2,1)S(1)}, u32[]{:S(2)}, u32[]{:S(2)}) collective-permute-start(bf16[768,128]{1,0:T(8,128)(2,1)S(1)} %shard_map.202.refs_0_), channel_id=1, source_target_pairs={{0,2},{1,3},{2,0},{3,1},{4,6},{5,7},{6,4},{7,5},{8,10},{9,11},{10,... | collective-permute-start | bytes 589832 | tf_op jit(solution)/shard_map/ppermute | solution.py:409
  69.4 0.1 broadcast_select_fusion
  69.5 2.6 %collective-permute-done.16.refs_1_ = bf16[416,128]{1,0:T(8,128)(2,1)S(1)} collective-permute-done((bf16[416,128]{1,0:T(8,128)(2,1)S(1)}, bf16[416,128]{1,0:T(8,128)(2,1)S(1)}, u32[]{:S(2)}, u32[]{:S(2)}) %collective-permute-start.16) | collective-permute-done | bytes 106528 | tf_op jit(solution)/shard_map/ppermute | solution.py:409
  72.2 5.5 %collective-permute-done.15.refs_1_ = bf16[768,128]{1,0:T(8,128)(2,1)S(1)} collective-permute-done((bf16[768,128]{1,0:T(8,128)(2,1)S(1)}, bf16[768,128]{1,0:T(8,128)(2,1)S(1)}, u32[]{:S(2)}, u32[]{:S(2)}) %collective-permute-start.15) | collective-permute-done | bytes 196640 | tf_op jit(solution)/shard_map/ppermute | solution.py:409
  77.7 0.1 shard_map.204.refs_7_.refs_1_
  77.7 2.0 %collective-permute-start.20 = (bf16[768,128]{1,0:T(8,128)(2,1)S(1)}, bf16[768,128]{1,0:T(8,128)(2,1)S(1)}, u32[]{:S(2)}, u32[]{:S(2)}) collective-permute-start(bf16[768,128]{1,0:T(8,128)(2,1)S(1)} %shard_map.204.refs_7_.refs_1_), channel_id=1, source_target_pairs={{0,20},{1,21},{2,22},{3,23},{4,16},{5,17},{6,18},{7,19},{8,28},{9,... | collective-permute-start | bytes 589832 | tf_op jit(solution)/shard_map/ppermute | solution.py:409
  79.7 0.5 collective-permute-start.19
  80.2 1.0 %collective-permute-start.18 = (bf16[768,128]{1,0:T(8,128)(2,1)S(1)}, bf16[768,128]{1,0:T(8,128)(2,1)S(1)}, u32[]{:S(2)}, u32[]{:S(2)}) collective-permute-start(bf16[768,128]{1,0:T(8,128)(2,1)S(1)} %shard_map.204.refs_7_.refs_1_), channel_id=1, source_target_pairs={{0,16},{1,17},{2,18},{3,19},{4,20},{5,21},{6,22},{7,23},{8,24},{9,... | collective-permute-start | bytes 589832 | tf_op jit(solution)/shard_map/ppermute | solution.py:409
  81.3 0.1 collective-permute-start.21
  81.4 6.7 %shard_map.206 = bf16[1024,384]{1,0:T(8,128)(2,1)} custom-call(bf16[32,32,384]{2,1,0:T(8,128)(2,1)S(1)} %bitcast.17, bf16[3,32,384]{2,1,0:T(8,128)(2,1)S(1)} %get-tuple-element.148.refs_1_, bf16[3,32,384]{2,1,0:T(8,128)(2,1)S(1)} %get-tuple-element.149.refs_2_, bf16[38,3,384]{2,1,0:T(4,128)(2,1)S(1)} %get-tuple-element.150.refs_3_, ...), custom_call_target="tpu_custom_call" | custom-call | flops 2312110080 | bytes 2257920 | tf_op jit(solution)/shard_map/pallas_call | solution.py:376
  88.1 0.1 collective-permute-done.19.refs_3_
  88.3 0.1 shard_map.207.own
  88.3 0.1 collective-permute-start.22
  88.4 0.1 shard_map.208.refs_1_
  88.5 1.9 %collective-permute-start.25 = (bf16[416,128]{1,0:T(8,128)(2,1)S(1)}, bf16[416,128]{1,0:T(8,128)(2,1)S(1)}, u32[]{:S(2)}, u32[]{:S(2)}) collective-permute-start(bf16[416,128]{1,0:T(8,128)(2,1)S(1)} %shard_map.208.refs_1_), channel_id=1, source_target_pairs={{0,20},{1,21},{2,22},{3,23},{4,16},{5,17},{6,18},{7,19},{8,28},{9,... | collective-permute-start | bytes 319496 | tf_op jit(solution)/shard_map/ppermute | solution.py:409
  90.3 0.7 collective-permute-start.24
  91.0 1.0 collective-permute-start.23
  92.0 3.2 %collective-permute-done.25.refs_4_ = bf16[416,128]{1,0:T(8,128)(2,1)S(1)} collective-permute-done((bf16[416,128]{1,0:T(8,128)(2,1)S(1)}, bf16[416,128]{1,0:T(8,128)(2,1)S(1)}, u32[]{:S(2)}, u32[]{:S(2)}) %collective-permute-start.25) | collective-permute-done | bytes 106528 | tf_op jit(solution)/shard_map/ppermute | solution.py:409
  95.2 1.9 %collective-permute-done.24.refs_3_ = bf16[416,128]{1,0:T(8,128)(2,1)S(1)} collective-permute-done((bf16[416,128]{1,0:T(8,128)(2,1)S(1)}, bf16[416,128]{1,0:T(8,128)(2,1)S(1)}, u32[]{:S(2)}, u32[]{:S(2)}) %collective-permute-start.24) | collective-permute-done | bytes 106528 | tf_op jit(solution)/shard_map/ppermute | solution.py:409
  97.1 0.1 collective-permute-start.26
  97.2 1.8 %shard_map.210 = (f32[1536,384]{1,0:T(8,128)}, f32[384,1536]{1,0:T(8,128)}) custom-call(s32[1]{0:T(128)} %bitcast.refs_0_.core, bf16[3072,128]{1,0:T(8,128)(2,1)S(1)} %shard_map.207.own, bf16[3072,128]{1,0:T(8,128)(2,1)S(1)} %collective-permute-done.22.other), custom_call_target="tpu_custom_call" | custom-call | tf_op jit(solution)/shard_map/pallas_call | solution.py:548
  99.1 1.4 %shard_map.211 = (f32[1536,384]{1,0:T(8,128)}, f32[384,1536]{1,0:T(8,128)}, f32[7,7,384]{2,1,0:T(8,128)}, f32[384]{0:T(512)}, f32[384]{0:T(512)}, /*index=5*/f32...) custom-call(s32[1]{0:T(128)} %bitcast.refs_0_.core, ...), custom_call_target="tpu_custom_call", output_to_operand_aliasing={{0}: (3, {}), {1}: (4, {})} | custom-call | tf_op jit(solution)/shard_map/pallas_call | solution.py:548
  (47 shorter events, 0.3 us)
Async XLA Ops:
  1.6 2.3 %collective-permute-start.1 = (bf16[3,32,384]{2,1,0:T(8,128)(2,1)S(1)}, bf16[3,32,384]{2,1,0:T(8,128)(2,1)S(1)}, u32[]{:S(2)}, u32[]{:S(2)}) collective-permute-start(bf16[3,32,384]{2,1,0:T(8,128)(2,1)S(1)} %get-tuple-element.181), channel_id=1, source_target_pairs={{0,8},{16,24},{8,0},{24,16},{1,9},{17,25},{9,1},{25,17},{2,10},{18... | collective-permute-start | bytes 221192 | tf_op jit(solution)/shard_map/ppermute | solution.py:42
  2.2 1.8 %collective-permute-start = (bf16[3,32,384]{2,1,0:T(8,128)(2,1)S(1)}, bf16[3,32,384]{2,1,0:T(8,128)(2,1)S(1)}, u32[]{:S(2)}, u32[]{:S(2)}) collective-permute-start(bf16[3,32,384]{2,1,0:T(8,128)(2,1)S(1)} %get-tuple-element.182), channel_id=1, source_target_pairs={{8,16},{16,8},{9,17},{17,9},{10,18},{18,10},{11,19},{19,11},{12,20... | collective-permute-start | bytes 221192 | tf_op jit(solution)/shard_map/ppermute | solution.py:42
  4.2 7.7 %collective-permute-start.2 = (bf16[38,3,384]{2,1,0:T(4,128)(2,1)S(1)}, bf16[38,3,384]{2,1,0:T(4,128)(2,1)S(1)}, u32[]{:S(2)}, u32[]{:S(2)}) collective-permute-start(bf16[38,3,384]{2,1,0:T(4,128)(2,1)S(1)} %maximum_select_fusion), channel_id=1, source_target_pairs={{0,4},{4,0},{1,5},{5,1},{2,6},{6,2},{3,7},{7,3},{8,12},{12,8},{9,1... | collective-permute-start | bytes 262664 | tf_op jit(solution)/shard_map/ppermute | solution.py:42
  6.8 1.1 %copy-start = (bf16[1,32,32,384]{3,2,1,0:T(8,128)(2,1)S(1)}, bf16[1,32,32,384]{3,2,1,0:T(8,128)(2,1)}, u32[]{:S(2)}) copy-start(bf16[1,32,32,384]{3,2,1,0:T(8,128)(2,1)} %param.11) | copy-start | bytes 2359300
  7.9 0.9 copy-start.5
  8.8 3.2 %copy-start.8 = (f32[384]{0:T(512)S(1)}, f32[384]{0:T(512)}, u32[]{:S(2)}) copy-start(f32[384]{0:T(512)} %refs_7_.2) | copy-start | bytes 4612
  8.8 3.2 %copy-start.9 = (f32[384]{0:T(512)S(1)}, f32[384]{0:T(512)}, u32[]{:S(2)}) copy-start(f32[384]{0:T(512)} %refs_9_.1) | copy-start | bytes 4612
  8.8 3.2 %copy-start.10 = (f32[384]{0:T(512)S(1)}, f32[384]{0:T(512)}, u32[]{:S(2)}) copy-start(f32[384]{0:T(512)} %refs_8_.3) | copy-start | bytes 4612
  12.0 5.3 %copy-start.2 = (bf16[1536,384]{1,0:T(8,128)(2,1)S(1)}, bf16[1536,384]{1,0:T(8,128)(2,1)}, u32[]{:S(2)}) copy-start(bf16[1536,384]{1,0:T(8,128)(2,1)} %refs_3_.3) | copy-start | bytes 3538948
  12.0 5.3 %copy-start.3 = (bf16[384,1536]{1,0:T(8,128)(2,1)S(1)}, bf16[384,1536]{1,0:T(8,128)(2,1)}, u32[]{:S(2)}) copy-start(bf16[384,1536]{1,0:T(8,128)(2,1)} %refs_4_.3) | copy-start | bytes 3538948
  12.0 5.3 %copy-start.4 = (bf16[1,32,32,384]{3,2,1,0:T(8,128)(2,1)S(1)}, bf16[1,32,32,384]{3,2,1,0:T(8,128)(2,1)}, u32[]{:S(2)}) copy-start(bf16[1,32,32,384]{3,2,1,0:T(8,128)(2,1)} %param.12) | copy-start | bytes 2359300
  12.0 5.3 %copy-start.7 = (f32[1536]{0:T(1024)S(1)}, f32[1536]{0:T(1024)}, u32[]{:S(2)}) copy-start(f32[1536]{0:T(1024)} %refs_5_.4) | copy-start | bytes 18436
  12.0 5.3 %copy-start.11 = (f32[384]{0:T(512)S(1)}, f32[384]{0:T(512)}, u32[]{:S(2)}) copy-start(f32[384]{0:T(512)} %refs_6_.5) | copy-start | bytes 4612
  17.3 13.7 %copy-start.1 = (bf16[1,32,32,384]{3,2,1,0:T(8,128)(2,1)S(1)}, bf16[1,32,32,384]{3,2,1,0:T(8,128)(2,1)}, u32[]{:S(2)}) copy-start(bf16[1,32,32,384]{3,2,1,0:T(8,128)(2,1)} %param.11) | copy-start | bytes 2359300
  17.3 13.7 %copy-start.12 = (f32[384]{0:T(512)S(1)}, f32[384]{0:T(512)}, u32[]{:S(2)}) copy-start(f32[384]{0:T(512)} %refs_7_.3) | copy-start | bytes 4612
  26.6 11.3 %collective-permute-start.3 = (bf16[3072,128]{1,0:T(8,128)(2,1)S(1)}, bf16[3072,128]{1,0:T(8,128)(2,1)S(1)}, u32[]{:S(2)}, u32[]{:S(2)}) collective-permute-start(bf16[3072,128]{1,0:T(8,128)(2,1)S(1)} %get-tuple-element.106), channel_id=1, source_target_pairs={{0,8},{1,9},{2,10},{3,11},{4,12},{5,13},{6,14},{7,15},{8,0},{9,1},... | collective-permute-start | bytes 2359304 | tf_op jit(solution)/shard_map/ppermute | solution.py:409
  37.8 13.1 %collective-permute-start.7 = (bf16[1536,128]{1,0:T(8,128)(2,1)S(1)}, bf16[1536,128]{1,0:T(8,128)(2,1)S(1)}, u32[]{:S(2)}, u32[]{:S(2)}) collective-permute-start(bf16[1536,128]{1,0:T(8,128)(2,1)S(1)} %get-tuple-element.121), channel_id=1, source_target_pairs={{0,8},{1,9},{2,10},{3,11},{4,12},{5,13},{6,14},{7,15},{8,0},{9,1},... | collective-permute-start | bytes 1179656 | tf_op jit(solution)/shard_map/ppermute | solution.py:409
  38.2 11.5 %collective-permute-start.5 = (bf16[768,128]{1,0:T(8,128)(2,1)S(1)}, bf16[768,128]{1,0:T(8,128)(2,1)S(1)}, u32[]{:S(2)}, u32[]{:S(2)}) collective-permute-start(bf16[768,128]{1,0:T(8,128)(2,1)S(1)} %get-tuple-element.113), channel_id=1, source_target_pairs={{0,4},{1,5},{2,6},{3,7},{4,0},{5,1},{6,2},{7,3},{8,12},{9,13},{10,... | collective-permute-start | bytes 589832 | tf_op jit(solution)/shard_map/ppermute | solution.py:409
  38.5 11.2 %collective-permute-start.6 = (bf16[768,128]{1,0:T(8,128)(2,1)S(1)}, bf16[768,128]{1,0:T(8,128)(2,1)S(1)}, u32[]{:S(2)}, u32[]{:S(2)}) collective-permute-start(bf16[768,128]{1,0:T(8,128)(2,1)S(1)} %get-tuple-element.114), channel_id=1, source_target_pairs={{0,20},{1,21},{2,22},{3,23},{4,16},{5,17},{6,18},{7,19},{8,28},{9,... | collective-permute-start | bytes 589832 | tf_op jit(solution)/shard_map/ppermute | solution.py:409
  41.1 9.8 %collective-permute-start.4 = (bf16[768,128]{1,0:T(8,128)(2,1)S(1)}, bf16[768,128]{1,0:T(8,128)(2,1)S(1)}, u32[]{:S(2)}, u32[]{:S(2)}) collective-permute-start(bf16[768,128]{1,0:T(8,128)(2,1)S(1)} %get-tuple-element.112.refs_10_), channel_id=1, source_target_pairs={{0,16},{1,17},{2,18},{3,19},{4,20},{5,21},{6,22},{7,23},{8,24},{9,... | collective-permute-start | bytes 589832 | tf_op jit(solution)/shard_map/ppermute | solution.py:409
  50.9 1.8 %collective-permute-start.9 = (bf16[128,128]{1,0:T(8,128)(2,1)S(1)}, bf16[128,128]{1,0:T(8,128)(2,1)S(1)}, u32[]{:S(2)}, u32[]{:S(2)}) collective-permute-start(bf16[128,128]{1,0:T(8,128)(2,1)S(1)} %get-tuple-element.129), channel_id=1, source_target_pairs={{0,8},{1,9},{2,10},{3,11},{4,12},{5,13},{6,14},{7,15},{8,0},{9,1},... | collective-permute-start | bytes 98312 | tf_op jit(solution)/shard_map/ppermute | solution.py:409
  51.1 13.1 %collective-permute-start.8 = (bf16[768,128]{1,0:T(8,128)(2,1)S(1)}, bf16[768,128]{1,0:T(8,128)(2,1)S(1)}, u32[]{:S(2)}, u32[]{:S(2)}) collective-permute-start(bf16[768,128]{1,0:T(8,128)(2,1)S(1)} %shard_map.200.refs_0_), channel_id=1, source_target_pairs={{0,1},{1,0},{2,3},{3,2},{4,5},{5,4},{6,7},{7,6},{8,9},{9,8},{10,11... | collective-permute-start | bytes 589832 | tf_op jit(solution)/shard_map/ppermute | solution.py:409
  52.9 4.8 %collective-permute-start.14 = (bf16[3,32,384]{2,1,0:T(8,128)(2,1)S(1)}, bf16[3,32,384]{2,1,0:T(8,128)(2,1)S(1)}, u32[]{:S(2)}, u32[]{:S(2)}) collective-permute-start(bf16[3,32,384]{2,1,0:T(8,128)(2,1)S(1)} %get-tuple-element.177), channel_id=1, source_target_pairs={{0,8},{16,24},{8,0},{24,16},{1,9},{17,25},{9,1},{25,17},{2,10},{18... | collective-permute-start | bytes 221192 | tf_op jit(solution)/shard_map/ppermute | solution.py:42
  53.1 5.5 %collective-permute-start.13 = (bf16[3,32,384]{2,1,0:T(8,128)(2,1)S(1)}, bf16[3,32,384]{2,1,0:T(8,128)(2,1)S(1)}, u32[]{:S(2)}, u32[]{:S(2)}) collective-permute-start(bf16[3,32,384]{2,1,0:T(8,128)(2,1)S(1)} %get-tuple-element.178), channel_id=1, source_target_pairs={{8,16},{16,8},{9,17},{17,9},{10,18},{18,10},{11,19},{19,11},{12,20... | collective-permute-start | bytes 221192 | tf_op jit(solution)/shard_map/ppermute | solution.py:42
  53.9 27.5 %copy-start.6 = (f32[7,7,384]{2,1,0:T(8,128)S(1)}, f32[7,7,384]{2,1,0:T(8,128)}, u32[]{:S(2)}) copy-start(f32[7,7,384]{2,1,0:T(8,128)} %refs_5_.5) | copy-start | bytes 225796
  53.9 8.1 %collective-permute-start.10 = (bf16[416,128]{1,0:T(8,128)(2,1)S(1)}, bf16[416,128]{1,0:T(8,128)(2,1)S(1)}, u32[]{:S(2)}, u32[]{:S(2)}) collective-permute-start(bf16[416,128]{1,0:T(8,128)(2,1)S(1)} %get-tuple-element.135), channel_id=1, source_target_pairs={{0,16},{1,17},{2,18},{3,19},{4,20},{5,21},{6,22},{7,23},{8,24},{9,... | collective-permute-start | bytes 319496 | tf_op jit(solution)/shard_map/ppermute | solution.py:409
  57.1 7.0 %collective-permute-start.11 = (bf16[416,128]{1,0:T(8,128)(2,1)S(1)}, bf16[416,128]{1,0:T(8,128)(2,1)S(1)}, u32[]{:S(2)}, u32[]{:S(2)}) collective-permute-start(bf16[416,128]{1,0:T(8,128)(2,1)S(1)} %get-tuple-element.136), channel_id=1, source_target_pairs={{0,4},{1,5},{2,6},{3,7},{4,0},{5,1},{6,2},{7,3},{8,12},{9,13},{10,... | collective-permute-start | bytes 319496 | tf_op jit(solution)/shard_map/ppermute | solution.py:409
  57.6 6.5 %collective-permute-start.12 = (bf16[416,128]{1,0:T(8,128)(2,1)S(1)}, bf16[416,128]{1,0:T(8,128)(2,1)S(1)}, u32[]{:S(2)}, u32[]{:S(2)}) collective-permute-start(bf16[416,128]{1,0:T(8,128)(2,1)S(1)} %get-tuple-element.137), channel_id=1, source_target_pairs={{0,20},{1,21},{2,22},{3,23},{4,16},{5,17},{6,18},{7,19},{8,28},{9,... | collective-permute-start | bytes 319496 | tf_op jit(solution)/shard_map/ppermute | solution.py:409
  64.3 5.1 %collective-permute-start.17 = (bf16[38,3,384]{2,1,0:T(4,128)(2,1)S(1)}, bf16[38,3,384]{2,1,0:T(4,128)(2,1)S(1)}, u32[]{:S(2)}, u32[]{:S(2)}) collective-permute-start(bf16[38,3,384]{2,1,0:T(4,128)(2,1)S(1)} %maximum_select_fusion.1), channel_id=1, source_target_pairs={{0,4},{4,0},{1,5},{5,1},{2,6},{6,2},{3,7},{7,3},{8,12},{12,8},{9,1... | collective-permute-start | bytes 262664 | tf_op jit(solution)/shard_map/ppermute | solution.py:42
  65.6 6.5 %collective-permute-start.16 = (bf16[416,128]{1,0:T(8,128)(2,1)S(1)}, bf16[416,128]{1,0:T(8,128)(2,1)S(1)}, u32[]{:S(2)}, u32[]{:S(2)}) collective-permute-start(bf16[416,128]{1,0:T(8,128)(2,1)S(1)} %shard_map.203.refs_0_), channel_id=1, source_target_pairs={{0,1},{1,0},{2,3},{3,2},{4,5},{5,4},{6,7},{7,6},{8,9},{9,8},{10,11... | collective-permute-start | bytes 319496 | tf_op jit(solution)/shard_map/ppermute | solution.py:409
  66.8 10.9 %collective-permute-start.15 = (bf16[768,128]{1,0:T(8,128)(2,1)S(1)}, bf16[768,128]{1,0:T(8,128)(2,1)S(1)}, u32[]{:S(2)}, u32[]{:S(2)}) collective-permute-start(bf16[768,128]{1,0:T(8,128)(2,1)S(1)} %shard_map.202.refs_0_), channel_id=1, source_target_pairs={{0,2},{1,3},{2,0},{3,1},{4,6},{5,7},{6,4},{7,5},{8,10},{9,11},{10,... | collective-permute-start | bytes 589832 | tf_op jit(solution)/shard_map/ppermute | solution.py:409
  77.7 10.4 %collective-permute-start.20 = (bf16[768,128]{1,0:T(8,128)(2,1)S(1)}, bf16[768,128]{1,0:T(8,128)(2,1)S(1)}, u32[]{:S(2)}, u32[]{:S(2)}) collective-permute-start(bf16[768,128]{1,0:T(8,128)(2,1)S(1)} %shard_map.204.refs_7_.refs_1_), channel_id=1, source_target_pairs={{0,20},{1,21},{2,22},{3,23},{4,16},{5,17},{6,18},{7,19},{8,28},{9,... | collective-permute-start | bytes 589832 | tf_op jit(solution)/shard_map/ppermute | solution.py:409
  79.7 8.6 %collective-permute-start.19 = (bf16[768,128]{1,0:T(8,128)(2,1)S(1)}, bf16[768,128]{1,0:T(8,128)(2,1)S(1)}, u32[]{:S(2)}, u32[]{:S(2)}) collective-permute-start(bf16[768,128]{1,0:T(8,128)(2,1)S(1)} %shard_map.204.refs_7_.refs_1_), channel_id=1, source_target_pairs={{0,4},{1,5},{2,6},{3,7},{4,0},{5,1},{6,2},{7,3},{8,12},{9,13},{10,... | collective-permute-start | bytes 589832 | tf_op jit(solution)/shard_map/ppermute | solution.py:409
  80.2 8.0 %collective-permute-start.18 = (bf16[768,128]{1,0:T(8,128)(2,1)S(1)}, bf16[768,128]{1,0:T(8,128)(2,1)S(1)}, u32[]{:S(2)}, u32[]{:S(2)}) collective-permute-start(bf16[768,128]{1,0:T(8,128)(2,1)S(1)} %shard_map.204.refs_7_.refs_1_), channel_id=1, source_target_pairs={{0,16},{1,17},{2,18},{3,19},{4,20},{5,21},{6,22},{7,23},{8,24},{9,... | collective-permute-start | bytes 589832 | tf_op jit(solution)/shard_map/ppermute | solution.py:409
  81.3 6.8 %collective-permute-start.21 = (bf16[416,128]{1,0:T(8,128)(2,1)S(1)}, bf16[416,128]{1,0:T(8,128)(2,1)S(1)}, u32[]{:S(2)}, u32[]{:S(2)}) collective-permute-start(bf16[416,128]{1,0:T(8,128)(2,1)S(1)} %shard_map.205.refs_8_.refs_0_), channel_id=1, source_target_pairs={{0,2},{1,3},{2,0},{3,1},{4,6},{5,7},{6,4},{7,5},{8,10},{9,11},{10,... | collective-permute-start | bytes 319496 | tf_op jit(solution)/shard_map/ppermute | solution.py:409
  88.3 8.8 %collective-permute-start.22 = (bf16[3072,128]{1,0:T(8,128)(2,1)S(1)}, bf16[3072,128]{1,0:T(8,128)(2,1)S(1)}, u32[]{:S(2)}, u32[]{:S(2)}) collective-permute-start(bf16[3072,128]{1,0:T(8,128)(2,1)S(1)} %shard_map.207.own), channel_id=1, source_target_pairs={{0,8},{1,9},{2,10},{3,11},{4,12},{5,13},{6,14},{7,15},{8,0},{9,1},... | collective-permute-start | bytes 2359304 | tf_op jit(solution)/shard_map/ppermute | solution.py:409
  88.5 6.7 %collective-permute-start.25 = (bf16[416,128]{1,0:T(8,128)(2,1)S(1)}, bf16[416,128]{1,0:T(8,128)(2,1)S(1)}, u32[]{:S(2)}, u32[]{:S(2)}) collective-permute-start(bf16[416,128]{1,0:T(8,128)(2,1)S(1)} %shard_map.208.refs_1_), channel_id=1, source_target_pairs={{0,20},{1,21},{2,22},{3,23},{4,16},{5,17},{6,18},{7,19},{8,28},{9,... | collective-permute-start | bytes 319496 | tf_op jit(solution)/shard_map/ppermute | solution.py:409
  90.3 6.7 %collective-permute-start.24 = (bf16[416,128]{1,0:T(8,128)(2,1)S(1)}, bf16[416,128]{1,0:T(8,128)(2,1)S(1)}, u32[]{:S(2)}, u32[]{:S(2)}) collective-permute-start(bf16[416,128]{1,0:T(8,128)(2,1)S(1)} %shard_map.208.refs_1_), channel_id=1, source_target_pairs={{0,4},{1,5},{2,6},{3,7},{4,0},{5,1},{6,2},{7,3},{8,12},{9,13},{10,... | collective-permute-start | bytes 319496 | tf_op jit(solution)/shard_map/ppermute | solution.py:409
  91.0 6.1 %collective-permute-start.23 = (bf16[416,128]{1,0:T(8,128)(2,1)S(1)}, bf16[416,128]{1,0:T(8,128)(2,1)S(1)}, u32[]{:S(2)}, u32[]{:S(2)}) collective-permute-start(bf16[416,128]{1,0:T(8,128)(2,1)S(1)} %shard_map.208.refs_1_), channel_id=1, source_target_pairs={{0,16},{1,17},{2,18},{3,19},{4,20},{5,21},{6,22},{7,23},{8,24},{9,... | collective-permute-start | bytes 319496 | tf_op jit(solution)/shard_map/ppermute | solution.py:409
  97.1 1.9 %collective-permute-start.26 = (bf16[1664,128]{1,0:T(8,128)(2,1)S(1)}, bf16[1664,128]{1,0:T(8,128)(2,1)S(1)}, u32[]{:S(2)}, u32[]{:S(2)}) collective-permute-start(bf16[1664,128]{1,0:T(8,128)(2,1)S(1)} %shard_map.209.own), channel_id=1, source_target_pairs={{0,8},{1,9},{2,10},{3,11},{4,12},{5,13},{6,14},{7,15},{8,0},{9,1},... | collective-permute-start | bytes 1277960 | tf_op jit(solution)/shard_map/ppermute | solution.py:409

commit v10 on v7

--- a/solution.py
+++ b/solution.py
@@ -188,21 +188,74 @@
 PIXELS = 256
 
 
+def mlp_block(ln, d_branch, w_in, w_out, b_in, base, width, hid_ref, dpre_ref, gbin):
+    sub = 256
+    count = width // sub
+
+    def products(s):
+        at = pl.ds(base + s * sub, sub)
+        return dot(ln, w_in[at, :], NT), dot(d_branch, w_out[:, at], NN)
+
+    ahead = products(0)
+    for s in range(count):
+        pre, d_hidden = ahead
+        if s + 1 < count:
+            ahead = products(s + 1)
+        act, slope = gelu_pair(pre + line(b_in, pl.ds(base + s * sub, sub)))
+        d_pre = d_hidden * slope
+        gbin[:, s * sub : (s + 1) * sub] += fold(d_pre)
+        hid_ref[:, s * sub : (s + 1) * sub] = act.astype(bf16)
+        dpre_ref[:, s * sub : (s + 1) * sub] = d_pre.astype(bf16)
+    at = pl.ds(base, width)
+    hidden, d_pre = hid_ref[...], dpre_ref[...]
+    branch = dot(hidden, w_out[:, at], NT)
+    d_norm = dot(d_pre, w_in[at, :], NN)
+    return hidden, d_pre, branch, d_norm
+
+
+def pack_grads(core, keep, send, gwin, gwout, gbin_ref, gbin):
+    width, channels = gwin.shape
+
+    def store(first, second):
+        for j in range(channels // LANES):
+            first[j * width : (j + 1) * width, :] = gwin[:, j * LANES : (j + 1) * LANES].astype(bf16)
+        for j in range(width // LANES):
+            second[j * channels : (j + 1) * channels, :] = gwout[
+                :, j * LANES : (j + 1) * LANES
+            ].astype(bf16)
+
+    pl.when(core[0] == 0)(lambda: store(keep, send))
+    pl.when(core[0] != 0)(lambda: store(send, keep))
+    gbin_ref[...] = jnp.sum(gbin[...], axis=0, keepdims=True)
+
+
+MLP_BLOCK = 256
+
+
 def mlp_first_kernel(
-    base, width, core, ln_ref, cot, w_in, w_out, b_in, scale, branch_ref, dnorm_ref, d_branch_ref,
-    keep, send, gbin_ref, hid_ref, dpre_ref,
+    base, width, core, ln_ref, cot, w_in, w_out, b_in, scale, branch_ref, dnorm_ref, d_branch_ref, keep, send, gbin_ref,
+    hid_ref, dpre_ref, gwin, gwout, gbin,
 ):
-    d_branch_ref[...] = (line(scale) * cot[...].astype(f32)).astype(bf16)
-    mlp(core, ln_ref, d_branch_ref, w_in, w_out, b_in, base, width, hid_ref, dpre_ref, keep, send, gbin_ref)
-    at = pl.ds(base, width)
+    gwin[...] = jnp.zeros_like(gwin)
+    gwout[...] = jnp.zeros_like(gwout)
+    gbin[...] = jnp.zeros_like(gbin)
 
     def step(i, _):
-        to = pl.ds(pl.multiple_of(i * PIXELS, PIXELS), PIXELS)
-        branch_ref[to, :] = dot(hid_ref[to, :], w_out[:, at], NT)
-        dnorm_ref[to, :] = dot(dpre_ref[to, :], w_in[at, :], NN)
+        at = pl.ds(pl.multiple_of(i * MLP_BLOCK, MLP_BLOCK), MLP_BLOCK)
+        ln = ln_ref[at, :]
+        d_branch = (line(scale) * cot[at, :].astype(f32)).astype(bf16)
+        hidden, d_pre, branch, d_norm = mlp_block(
+            ln, d_branch, w_in, w_out, b_in, base, width, hid_ref, dpre_ref, gbin
+        )
+        d_branch_ref[at, :] = d_branch
+        branch_ref[at, :] = branch
+        dnorm_ref[at, :] = d_norm
+        gwin[...] += dot(d_pre, ln, TN)
+        gwout[...] += dot(d_branch, hidden, TN)
         return _
 
-    lax.fori_loop(0, ln_ref.shape[0] // PIXELS, step, 0)
+    lax.fori_loop(0, ln_ref.shape[0] // MLP_BLOCK, step, 0)
+    pack_grads(core, keep, send, gwin, gwout, gbin_ref, gbin)
 
 
 def mlp_second_kernel(
@@ -439,32 +492,30 @@
     return x
 
 
-def finish_kernel(
-    factor, widths, core, own_a, other_a, own_b, other_b,
-    win, wout, gk, scale, b_out, gain, shift, bias, b_in,
-):
+def finish_kernel(factor, width, core, own, other, win, wout, *smalls):
     channels, unit = wout.shape
     slabs = channels // LANES
 
-    def rows(ref, width, at):
+    def rows(ref, at):
         part, block = ref.shape[0] // 4, width * slabs // 4
         start = at // block * part + at % block
         return ref[start : start + LANES, :].astype(f32) * factor
 
-    def store(first, second, width, offset):
+    def store(first, second, offset):
         for j in range(slabs):
             for i in range(0, unit, LANES):
-                win[i : i + LANES, j * LANES : (j + 1) * LANES] = rows(first, width, j * width + offset + i)
+                win[i : i + LANES, j * LANES : (j + 1) * LANES] = rows(first, j * width + offset + i)
         for j in range(unit // LANES):
             for i in range(0, channels, LANES):
                 wout[i : i + LANES, j * LANES : (j + 1) * LANES] = rows(
-                    second, width, (offset // LANES + j) * channels + i
+                    second, (offset // LANES + j) * channels + i
                 )
 
     def store_small(*halves):
+        gk, scale, b_out, gain, shift, bias, b_in = smalls
         for slab in range(slabs):
             at = slice(slab * LANES, (slab + 1) * LANES)
-            start = slab * (halves[0].shape[0] // 4) + widths[1] * slabs // 4
+            start = slab * (halves[0].shape[0] // 4) + width * slabs // 4
             values = jnp.concatenate([ref[start : start + SMALL // 2, :].astype(f32) for ref in halves]) * factor
             for j in range(7):
                 gk[j, :, at] = values[7 * j : 7 * j + 7]
@@ -476,34 +527,38 @@
 
     is_first = core[0] == 0
     step = pl.program_id(0)
-    for i in range(sum(widths) // unit):
-        offset, halves = i * unit, (own_a, other_a)
-        width = widths[0]
-        if offset >= widths[0]:
-            offset, halves, width = offset - widths[0], (own_b, other_b), widths[1]
+    for i in range(width // unit):
         here = step == i
-        pl.when(here & is_first)(functools.partial(store, *halves, width, offset))
-        pl.when(here & ~is_first)(functools.partial(store, *halves[::-1], width, offset))
-    pl.when((step == 0) & is_first)(lambda: store_small(own_b, other_b))
-    pl.when((step == 0) & ~is_first)(lambda: store_small(other_b, own_b))
-
-
-def finish(factor, widths, channels, core, *halves):
-    hid, unit = sum(widths), widths[1]
+        pl.when(here & is_first)(functools.partial(store, own, other, i * unit))
+        pl.when(here & ~is_first)(functools.partial(store, other, own, i * unit))
+    if smalls:
+        pl.when(is_first)(lambda: store_small(own, other))
+        pl.when(~is_first)(lambda: store_small(other, own))
+
+
+def finish(factor, base, width, unit, hid, channels, core, own, other, whole=()):
     vmem = pl.BlockSpec(memory_space=pltpu.VMEM)
-    outs = [(hid, channels), (channels, hid), (7, 7, channels)] + [(channels,)] * 5 + [(hid,)]
+    start = base // unit
+    outs = [(hid, channels), (channels, hid)]
+    smalls = [(7, 7, channels)] + [(channels,)] * 5 + [(hid,)] if whole else []
+
+    def kernel(core, own, other, *refs):
+        finish_kernel(factor, width, core, own, other, *refs[len(whole) :])
+
     return pl.pallas_call(
-        functools.partial(finish_kernel, factor, widths),
-        grid=(hid // unit,),
-        out_shape=[jax.ShapeDtypeStruct(shape, f32) for shape in outs],
-        in_specs=[pl.BlockSpec(memory_space=pltpu.SMEM)] + [vmem] * len(halves),
+        kernel,
+        grid=(width // unit,),
+        out_shape=[jax.ShapeDtypeStruct(shape, f32) for shape in outs + smalls],
+        in_specs=[pl.BlockSpec(memory_space=pltpu.SMEM), vmem, vmem]
+        + [pl.BlockSpec(memory_space=pl.ANY)] * len(whole),
         out_specs=[
-            pl.BlockSpec((unit, channels), lambda i: (i, 0)),
-            pl.BlockSpec((channels, unit), lambda i: (0, i)),
+            pl.BlockSpec((unit, channels), lambda i: (start + i, 0)),
+            pl.BlockSpec((channels, unit), lambda i: (0, start + i)),
         ]
-        + [vmem] * 7,
+        + [vmem] * len(smalls),
+        input_output_aliases={3: 0, 4: 1} if whole else {},
         compiler_params=pltpu.CompilerParams(vmem_limit_bytes=24 << 20),
-    )(core, *halves)
+    )(core, own, other, *whole)
 
 
 def shards(
@@ -551,7 +606,13 @@
     branch, d_norm, d_branch, keep_a, send_a, gbin_a = call(
         functools.partial(mlp_first_kernel, 0, first),
         [(full, f32), (full, f32), (full, bf16)] + packed(first),
-        acts(first),
+        [
+            ((MLP_BLOCK, first), bf16),
+            ((MLP_BLOCK, first), bf16),
+            ((first, channels), f32),
+            ((channels, first), f32),
+            ((8, first), f32),
+        ],
         (core, ln_out, cot, *weights),
         mlp_flops,
         1,
@@ -607,8 +668,9 @@
     half_b = join(mine, *got_b)
     got_b = [half_b, exchange(half_b, core_flip)]
     factor = float(pixels * lax.axis_size("gy") * lax.axis_size("gx") * lax.axis_size("rep")) ** (-0.5)
+    begun = finish(factor, 0, first, second, hid, channels, core, *got_a)
     win, wout, gk, g_scale, g_bout, g_gain, g_shift, g_bias, g_bin = finish(
-        factor, (first, second), channels, core, *got_a, *got_b
+        factor, first, second, second, hid, channels, core, *got_b, begun
     )
     return (
         result.reshape(pages.shape),

time: 97.9 us -> 96.5 us (0.986)
  waiting for transfers between devices: 21.1 us -> 19.9 us
    ppermute x21, waiting for transfers between devices: 18.3 us -> 17.1 us  [exchange(): return lax.ppermute(x, AXES, perm)]
    pallas_call x1 -> x2, Pallas kernels: 2.69 us -> 3.22 us  [finish(): pl.pallas_call(kernel, grid=(width // unit,), out_shape=[jax.ShapeDtypeSt...]
  transfers between devices with their start and end apart: 27 -> 27, of which waited for: 8 -> 8; matrix products, arithmetic and copies ran while one was open for 2% -> 2% of each run, Pallas kernels for 21% -> 23%
where the time goes in v10:
time: 96.5 us; the launch traced here: 96.3 us
  Pallas kernels  39.7 us (41%)
  starting transfers between devices  32.8 us (34%)
  waiting for transfers between devices  19.9 us (21%)
  other arithmetic  1.55 us (2%)
  local copies, waits for them, and re-layouts  1.29 us (1%)
  between operations  1.15 us (1%)
    pallas_call x15, Pallas kernels, call(): pl.pallas_call(kernel, out_shape=[jax.ShapeDtypeStruct(shape, dtype) for...  36.4 us
    ppermute x21, starting transfers between devices, exchange(): return lax.ppermute(x, AXES, perm)  26.7 us
    ppermute x21, waiting for transfers between devices, exchange(): return lax.ppermute(x, AXES, perm)  17.1 us
    ppermute x6, starting transfers between devices, swap_edges(): got.append(lax.ppermute(jnp.where(is_high, high, low), axis, pairs))  6.1 us
    pallas_call x2, Pallas kernels, finish(): pl.pallas_call(kernel, grid=(width // unit,), out_shape=[jax.ShapeDtypeSt...  3.22 us
    ppermute x6, waiting for transfers between devices, swap_edges(): got.append(lax.ppermute(jnp.where(is_high, high, low), axis, pairs))  2.81 us
  transfers between devices with their start and end apart: 27, of which 8 were waited for; matrix products, arithmetic and copies ran while one was open for 2% of the time, Pallas kernels for 23%

profile of v10, /device:TPU:0, one launch (start us, length us, event | category | flops | bytes accessed | tf_op | source)
XLA Modules:
  0.0 96.3 jit_solution(17508176955820771804)
XLA Ops:
  0.6 0.0 copy-start
  0.7 1.0 %broadcast_select_fusion.11 = (bf16[3,32,384]{2,1,0:T(8,128)(2,1)S(1)}, bf16[3,32,384]{2,1,0:T(8,128)(2,1)S(1)}) fusion(pred[]{:T(512)S(6)} %eq.12, bf16[32,32,384]{2,1,0:T(8,128)(2,1)} %bitcast.9, pred[]{:T(512)S(6)} %not.4), kind=kLoop, calls=%fused_computation.13 | loop fusion | flops 73728 | bytes 294914 | tf_op jit(solution)/shard_map/jit(_where)/select_n | solution.py:45
  1.8 0.5 collective-permute-start.1
  2.3 0.7 collective-permute-start
  2.9 1.1 %fusion.1 = (bf16[32,3,384]{2,1,0:T(4,128)(2,1)S(1)}, bf16[32,3,384]{2,1,0:T(4,128)(2,1)S(1)}) fusion(bf16[32,32,384]{2,1,0:T(8,128)(2,1)} %bitcast.10), kind=kLoop, calls=%fused_computation.15 | loop fusion | bytes 294912 | tf_op jit(solution)/shard_map/slice | solution.py:52
  4.1 0.2 maximum_select_fusion
  4.3 2.6 %collective-permute-start.2 = (bf16[38,3,384]{2,1,0:T(4,128)(2,1)S(1)}, bf16[38,3,384]{2,1,0:T(4,128)(2,1)S(1)}, u32[]{:S(2)}, u32[]{:S(2)}) collective-permute-start(bf16[38,3,384]{2,1,0:T(4,128)(2,1)S(1)} %maximum_select_fusion), channel_id=1, source_target_pairs={{0,4},{4,0},{1,5},{5,1},{2,6},{6,2},{3,7},{7,3},{8,12},{12,8},{9,1... | collective-permute-start | bytes 262664 | tf_op jit(solution)/shard_map/ppermute | solution.py:45
  6.9 2.8 %collective-permute-done.2 = bf16[38,3,384]{2,1,0:T(4,128)(2,1)S(1)} collective-permute-done((bf16[38,3,384]{2,1,0:T(4,128)(2,1)S(1)}, bf16[38,3,384]{2,1,0:T(4,128)(2,1)S(1)}, u32[]{:S(2)}, u32[]{:S(2)}) %collective-permute-start.2) | collective-permute-done | bytes 87584 | tf_op jit(solution)/shard_map/ppermute | solution.py:45
  9.7 0.1 broadcast_select_fusion.2
  9.8 0.0 copy-start.1
  9.8 0.0 copy-start.2
  9.8 0.0 copy-start.3
  9.9 0.0 copy-start.5
  9.9 0.0 copy-start.9
  9.9 7.3 %shard_map.194 = (f32[1024,384]{1,0:T(8,128)S(1)}, f32[1024,128]{1,0:T(8,128)S(1)}, bf16[1024,384]{1,0:T(8,128)(2,1)S(1)}) custom-call(bf16[32,32,384]{2,1,0:T(8,128)(2,1)S(1)} %bitcast.11, bf16[3,32,384]{2,1,0:T(8,128)(2,1)S(1)} %get-tuple-element.164.refs_1_.refs_2_, bf16[3,32,384]{2,1,0:T(8,128)(2,1)S(1)} %get-tuple-element.163.refs_2_.refs_3_, ...), custom_call_target="tpu_custom_call" | custom-call | flops 2312110080 | bytes 2257920 | tf_op jit(solution)/shard_map/pallas_call | solution.py:376
  17.3 0.0 copy-start.10
  17.3 8.1 %shard_map.195 = (f32[1024,384]{1,0:T(8,128)S(1)}, f32[1024,384]{1,0:T(8,128)S(1)}, bf16[1024,384]{1,0:T(8,128)(2,1)S(1)}, bf16[3072,128]{1,0:T(8,128)(2,1)S(1)}...) custom-call(s32[1]{0:T(128)} %bitcast.refs_0_.core, bf16[1024,384]{1,0:T(8,128)(2,1)S(1)} %get-tuple-element.86.refs_1_, ...), custom_call_target="tpu_custom_call" | custom-call | flops 7247757312 | bytes 7077888 | tf_op jit(solution)/shard_map/pallas_call | solution.py:376
  25.3 3.8 %collective-permute-start.3 = (bf16[3072,128]{1,0:T(8,128)(2,1)S(1)}, bf16[3072,128]{1,0:T(8,128)(2,1)S(1)}, u32[]{:S(2)}, u32[]{:S(2)}) collective-permute-start(bf16[3072,128]{1,0:T(8,128)(2,1)S(1)} %get-tuple-element.95), channel_id=1, source_target_pairs={{0,8},{1,9},{2,10},{3,11},{4,12},{5,13},{6,14},{7,15},{8,0},{9,1},... | collective-permute-start | bytes 2359304 | tf_op jit(solution)/shard_map/ppermute | solution.py:409
  29.2 6.4 %shard_map.196 = (bf16[1024,384]{1,0:T(8,128)(2,1)}, bf16[1024,384]{1,0:T(8,128)(2,1)S(1)}, bf16[1536,128]{1,0:T(8,128)(2,1)S(1)}, bf16[1536,128]{1,0:T(8,128)(2...) custom-call(s32[1]{0:T(128)} %bitcast.refs_0_.core, bf16[1024,384]{1,0:T(8,128)(2,1)S(1)} %get-tuple-element.86.refs_1_, ...), custom_call_target="tpu_custom_call" | custom-call | flops 7247757312 | bytes 7077888 | tf_op jit(solution)/shard_map/pallas_call | solution.py:376
  35.6 0.1 collective-permute-start.16
  35.7 0.7 collective-permute-start.15
  36.3 0.1 fusion
  36.4 0.3 shard_map.197
  36.7 1.8 %collective-permute-start.5 = (bf16[768,128]{1,0:T(8,128)(2,1)S(1)}, bf16[768,128]{1,0:T(8,128)(2,1)S(1)}, u32[]{:S(2)}, u32[]{:S(2)}) collective-permute-start(bf16[768,128]{1,0:T(8,128)(2,1)S(1)} %get-tuple-element.102), channel_id=1, source_target_pairs={{0,4},{1,5},{2,6},{3,7},{4,0},{5,1},{6,2},{7,3},{8,12},{9,13},{10,... | collective-permute-start | bytes 589832 | tf_op jit(solution)/shard_map/ppermute | solution.py:409
  38.5 3.5 %collective-permute-start.6 = (bf16[768,128]{1,0:T(8,128)(2,1)S(1)}, bf16[768,128]{1,0:T(8,128)(2,1)S(1)}, u32[]{:S(2)}, u32[]{:S(2)}) collective-permute-start(bf16[768,128]{1,0:T(8,128)(2,1)S(1)} %get-tuple-element.103), channel_id=1, source_target_pairs={{0,20},{1,21},{2,22},{3,23},{4,16},{5,17},{6,18},{7,19},{8,28},{9,... | collective-permute-start | bytes 589832 | tf_op jit(solution)/shard_map/ppermute | solution.py:409
  42.1 0.1 collective-permute-start.4
  42.1 1.2 %collective-permute-start.7 = (bf16[1536,128]{1,0:T(8,128)(2,1)S(1)}, bf16[1536,128]{1,0:T(8,128)(2,1)S(1)}, u32[]{:S(2)}, u32[]{:S(2)}) collective-permute-start(bf16[1536,128]{1,0:T(8,128)(2,1)S(1)} %get-tuple-element.110), channel_id=1, source_target_pairs={{0,8},{1,9},{2,10},{3,11},{4,12},{5,13},{6,14},{7,15},{8,0},{9,1},... | collective-permute-start | bytes 1179656 | tf_op jit(solution)/shard_map/ppermute | solution.py:409
  43.4 0.2 maximum_select_fusion.1
  43.6 1.6 %collective-permute-start.17 = (bf16[38,3,384]{2,1,0:T(4,128)(2,1)S(1)}, bf16[38,3,384]{2,1,0:T(4,128)(2,1)S(1)}, u32[]{:S(2)}, u32[]{:S(2)}) collective-permute-start(bf16[38,3,384]{2,1,0:T(4,128)(2,1)S(1)} %maximum_select_fusion.1), channel_id=1, source_target_pairs={{0,4},{4,0},{1,5},{5,1},{2,6},{6,2},{3,7},{7,3},{8,12},{12,8},{9,1... | collective-permute-start | bytes 262664 | tf_op jit(solution)/shard_map/ppermute | solution.py:45
  45.2 7.1 %shard_map.198 = (bf16[128,128]{1,0:T(8,128)(2,1)S(1)}, bf16[128,128]{1,0:T(8,128)(2,1)S(1)}) custom-call(s32[1]{0:T(128)} %bitcast.refs_0_.core, bf16[32,32,384]{2,1,0:T(8,128)(2,1)S(1)} %bitcast.13, bf16[3,32,384]{2,1,0:T(8,128)(2,1)S(1)} %get-tuple-element.164.refs_1_.refs_2_, bf16[3,32,384]{2,1,0:T(8,128)(2,1)S(1)} %get-tuple-element.163.refs_2_.refs_3_, ...), custom_call_target="tpu_custom_call" | custom-call | flops 2312110080 | bytes 2257920 | tf_op jit(solution)/shard_map/pallas_call | solution.py:376
  52.3 0.1 collective-permute-start.9
  52.4 0.1 shard_map.199.refs_0_
  52.5 1.6 %collective-permute-start.8 = (bf16[768,128]{1,0:T(8,128)(2,1)S(1)}, bf16[768,128]{1,0:T(8,128)(2,1)S(1)}, u32[]{:S(2)}, u32[]{:S(2)}) collective-permute-start(bf16[768,128]{1,0:T(8,128)(2,1)S(1)} %shard_map.199.refs_0_), channel_id=1, source_target_pairs={{0,1},{1,0},{2,3},{3,2},{4,5},{5,4},{6,7},{7,6},{8,9},{9,8},{10,11... | collective-permute-start | bytes 589832 | tf_op jit(solution)/shard_map/ppermute | solution.py:409
  54.1 0.1 shard_map.200
  54.2 1.0 %collective-permute-start.10 = (bf16[416,128]{1,0:T(8,128)(2,1)S(1)}, bf16[416,128]{1,0:T(8,128)(2,1)S(1)}, u32[]{:S(2)}, u32[]{:S(2)}) collective-permute-start(bf16[416,128]{1,0:T(8,128)(2,1)S(1)} %get-tuple-element.120), channel_id=1, source_target_pairs={{0,16},{1,17},{2,18},{3,19},{4,20},{5,21},{6,22},{7,23},{8,24},{9,... | collective-permute-start | bytes 319496 | tf_op jit(solution)/shard_map/ppermute | solution.py:409
  55.3 0.6 collective-permute-start.11
  55.8 2.0 %collective-permute-start.12 = (bf16[416,128]{1,0:T(8,128)(2,1)S(1)}, bf16[416,128]{1,0:T(8,128)(2,1)S(1)}, u32[]{:S(2)}, u32[]{:S(2)}) collective-permute-start(bf16[416,128]{1,0:T(8,128)(2,1)S(1)} %get-tuple-element.122), channel_id=1, source_target_pairs={{0,20},{1,21},{2,22},{3,23},{4,16},{5,17},{6,18},{7,19},{8,28},{9,... | collective-permute-start | bytes 319496 | tf_op jit(solution)/shard_map/ppermute | solution.py:409
  57.8 0.1 broadcast_select_fusion
  57.9 1.9 %collective-permute-done.10.refs_1_ = bf16[416,128]{1,0:T(8,128)(2,1)S(1)} collective-permute-done((bf16[416,128]{1,0:T(8,128)(2,1)S(1)}, bf16[416,128]{1,0:T(8,128)(2,1)S(1)}, u32[]{:S(2)}, u32[]{:S(2)}) %collective-permute-start.10) | collective-permute-done | bytes 106528 | tf_op jit(solution)/shard_map/ppermute | solution.py:409
  59.8 2.5 %collective-permute-done.11.refs_2_ = bf16[416,128]{1,0:T(8,128)(2,1)S(1)} collective-permute-done((bf16[416,128]{1,0:T(8,128)(2,1)S(1)}, bf16[416,128]{1,0:T(8,128)(2,1)S(1)}, u32[]{:S(2)}, u32[]{:S(2)}) %collective-permute-start.11) | collective-permute-done | bytes 106528 | tf_op jit(solution)/shard_map/ppermute | solution.py:409
  62.4 0.1 shard_map.201.refs_7_.refs_0_
  62.4 0.1 shard_map.202.refs_8_.refs_0_
  62.5 1.0 %collective-permute-start.14 = (bf16[416,128]{1,0:T(8,128)(2,1)S(1)}, bf16[416,128]{1,0:T(8,128)(2,1)S(1)}, u32[]{:S(2)}, u32[]{:S(2)}) collective-permute-start(bf16[416,128]{1,0:T(8,128)(2,1)S(1)} %shard_map.202.refs_8_.refs_0_), channel_id=1, source_target_pairs={{0,1},{1,0},{2,3},{3,2},{4,5},{5,4},{6,7},{7,6},{8,9},{9,8},{10,11... | collective-permute-start | bytes 319496 | tf_op jit(solution)/shard_map/ppermute | solution.py:409
  63.5 2.6 %collective-permute-start.13 = (bf16[768,128]{1,0:T(8,128)(2,1)S(1)}, bf16[768,128]{1,0:T(8,128)(2,1)S(1)}, u32[]{:S(2)}, u32[]{:S(2)}) collective-permute-start(bf16[768,128]{1,0:T(8,128)(2,1)S(1)} %shard_map.201.refs_7_.refs_0_), channel_id=1, source_target_pairs={{0,2},{1,3},{2,0},{3,1},{4,6},{5,7},{6,4},{7,5},{8,10},{9,11},{10,... | collective-permute-start | bytes 589832 | tf_op jit(solution)/shard_map/ppermute | solution.py:409
  66.1 6.7 %shard_map.203 = bf16[1024,384]{1,0:T(8,128)(2,1)} custom-call(bf16[32,32,384]{2,1,0:T(8,128)(2,1)S(1)} %bitcast.16, bf16[3,32,384]{2,1,0:T(8,128)(2,1)S(1)} %get-tuple-element.162.refs_1_, bf16[3,32,384]{2,1,0:T(8,128)(2,1)S(1)} %get-tuple-element.161.refs_2_, bf16[38,3,384]{2,1,0:T(4,128)(2,1)S(1)} %get-tuple-element.166.refs_3_, ...), custom_call_target="tpu_custom_call" | custom-call | flops 2312110080 | bytes 2257920 | tf_op jit(solution)/shard_map/pallas_call | solution.py:376
  72.8 0.7 collective-permute-done.13.refs_1_
  73.5 0.1 shard_map.204.refs_1_
  73.6 1.9 %collective-permute-start.20 = (bf16[768,128]{1,0:T(8,128)(2,1)S(1)}, bf16[768,128]{1,0:T(8,128)(2,1)S(1)}, u32[]{:S(2)}, u32[]{:S(2)}) collective-permute-start(bf16[768,128]{1,0:T(8,128)(2,1)S(1)} %shard_map.204.refs_1_), channel_id=1, source_target_pairs={{0,20},{1,21},{2,22},{3,23},{4,16},{5,17},{6,18},{7,19},{8,28},{9,... | collective-permute-start | bytes 589832 | tf_op jit(solution)/shard_map/ppermute | solution.py:409
  75.5 0.7 collective-permute-start.19
  76.2 1.0 collective-permute-start.18
  77.2 0.1 collective-permute-start.21
  77.3 6.7 %collective-permute-done.21.refs_1_ = bf16[416,128]{1,0:T(8,128)(2,1)S(1)} collective-permute-done((bf16[416,128]{1,0:T(8,128)(2,1)S(1)}, bf16[416,128]{1,0:T(8,128)(2,1)S(1)}, u32[]{:S(2)}, u32[]{:S(2)}) %collective-permute-start.21) | collective-permute-done | bytes 106528 | tf_op jit(solution)/shard_map/ppermute | solution.py:409
  84.0 0.1 shard_map.206.own
  84.1 0.1 collective-permute-start.22
  84.1 0.1 shard_map.207.refs_1_
  84.2 1.9 %collective-permute-start.25 = (bf16[416,128]{1,0:T(8,128)(2,1)S(1)}, bf16[416,128]{1,0:T(8,128)(2,1)S(1)}, u32[]{:S(2)}, u32[]{:S(2)}) collective-permute-start(bf16[416,128]{1,0:T(8,128)(2,1)S(1)} %shard_map.207.refs_1_), channel_id=1, source_target_pairs={{0,20},{1,21},{2,22},{3,23},{4,16},{5,17},{6,18},{7,19},{8,28},{9,... | collective-permute-start | bytes 319496 | tf_op jit(solution)/shard_map/ppermute | solution.py:409
  86.1 0.7 collective-permute-start.24
  86.8 1.0 collective-permute-start.23
  87.8 3.2 %collective-permute-done.25.refs_4_ = bf16[416,128]{1,0:T(8,128)(2,1)S(1)} collective-permute-done((bf16[416,128]{1,0:T(8,128)(2,1)S(1)}, bf16[416,128]{1,0:T(8,128)(2,1)S(1)}, u32[]{:S(2)}, u32[]{:S(2)}) %collective-permute-start.25) | collective-permute-done | bytes 106528 | tf_op jit(solution)/shard_map/ppermute | solution.py:409
  90.9 1.9 %collective-permute-done.24.refs_3_ = bf16[416,128]{1,0:T(8,128)(2,1)S(1)} collective-permute-done((bf16[416,128]{1,0:T(8,128)(2,1)S(1)}, bf16[416,128]{1,0:T(8,128)(2,1)S(1)}, u32[]{:S(2)}, u32[]{:S(2)}) %collective-permute-start.24) | collective-permute-done | bytes 106528 | tf_op jit(solution)/shard_map/ppermute | solution.py:409
  92.8 0.2 collective-permute-done.23.refs_2_
  93.0 0.1 collective-permute-start.26
  93.1 1.9 %shard_map.209 = (f32[1536,384]{1,0:T(8,128)}, f32[384,1536]{1,0:T(8,128)}) custom-call(s32[1]{0:T(128)} %bitcast.refs_0_.core, bf16[3072,128]{1,0:T(8,128)(2,1)S(1)} %shard_map.206.own, bf16[3072,128]{1,0:T(8,128)(2,1)S(1)} %collective-permute-done.22.other), custom_call_target="tpu_custom_call" | custom-call | tf_op jit(solution)/shard_map/pallas_call | solution.py:548
  95.0 1.4 %shard_map.210 = (f32[1536,384]{1,0:T(8,128)}, f32[384,1536]{1,0:T(8,128)}, f32[7,7,384]{2,1,0:T(8,128)}, f32[384]{0:T(512)}, f32[384]{0:T(512)}, /*index=5*/f32...) custom-call(s32[1]{0:T(128)} %bitcast.refs_0_.core, ...), custom_call_target="tpu_custom_call", output_to_operand_aliasing={{0}: (3, {}), {1}: (4, {})} | custom-call | tf_op jit(solution)/shard_map/pallas_call | solution.py:548
  (42 shorter events, 0.3 us)
Async XLA Ops:
  0.6 9.1 %copy-start = (bf16[1,32,32,384]{3,2,1,0:T(8,128)(2,1)S(1)}, bf16[1,32,32,384]{3,2,1,0:T(8,128)(2,1)}, u32[]{:S(2)}) copy-start(bf16[1,32,32,384]{3,2,1,0:T(8,128)(2,1)} %param.11) | copy-start | bytes 2359300
  0.7 9.1 %copy-start.8 = (f32[384]{0:T(512)S(1)}, f32[384]{0:T(512)}, u32[]{:S(2)}) copy-start(f32[384]{0:T(512)} %refs_8_.3) | copy-start | bytes 4612
  0.7 9.1 %copy-start.4 = (f32[7,7,384]{2,1,0:T(8,128)S(1)}, f32[7,7,384]{2,1,0:T(8,128)}, u32[]{:S(2)}) copy-start(f32[7,7,384]{2,1,0:T(8,128)} %refs_5_.7) | copy-start | bytes 225796
  0.7 9.1 %copy-start.7 = (f32[384]{0:T(512)S(1)}, f32[384]{0:T(512)}, u32[]{:S(2)}) copy-start(f32[384]{0:T(512)} %refs_8_.2) | copy-start | bytes 4612
  0.7 9.1 %copy-start.6 = (f32[384]{0:T(512)S(1)}, f32[384]{0:T(512)}, u32[]{:S(2)}) copy-start(f32[384]{0:T(512)} %refs_6_.3) | copy-start | bytes 4612
  1.8 2.3 %collective-permute-start.1 = (bf16[3,32,384]{2,1,0:T(8,128)(2,1)S(1)}, bf16[3,32,384]{2,1,0:T(8,128)(2,1)S(1)}, u32[]{:S(2)}, u32[]{:S(2)}) collective-permute-start(bf16[3,32,384]{2,1,0:T(8,128)(2,1)S(1)} %get-tuple-element.159), channel_id=1, source_target_pairs={{0,8},{16,24},{8,0},{24,16},{1,9},{17,25},{9,1},{25,17},{2,10},{18... | collective-permute-start | bytes 221192 | tf_op jit(solution)/shard_map/ppermute | solution.py:45
  2.3 1.8 %collective-permute-start = (bf16[3,32,384]{2,1,0:T(8,128)(2,1)S(1)}, bf16[3,32,384]{2,1,0:T(8,128)(2,1)S(1)}, u32[]{:S(2)}, u32[]{:S(2)}) collective-permute-start(bf16[3,32,384]{2,1,0:T(8,128)(2,1)S(1)} %get-tuple-element.160), channel_id=1, source_target_pairs={{8,16},{16,8},{9,17},{17,9},{10,18},{18,10},{11,19},{19,11},{12,20... | collective-permute-start | bytes 221192 | tf_op jit(solution)/shard_map/ppermute | solution.py:45
  4.3 5.4 %collective-permute-start.2 = (bf16[38,3,384]{2,1,0:T(4,128)(2,1)S(1)}, bf16[38,3,384]{2,1,0:T(4,128)(2,1)S(1)}, u32[]{:S(2)}, u32[]{:S(2)}) collective-permute-start(bf16[38,3,384]{2,1,0:T(4,128)(2,1)S(1)} %maximum_select_fusion), channel_id=1, source_target_pairs={{0,4},{4,0},{1,5},{5,1},{2,6},{6,2},{3,7},{7,3},{8,12},{12,8},{9,1... | collective-permute-start | bytes 262664 | tf_op jit(solution)/shard_map/ppermute | solution.py:45
  9.8 7.4 %copy-start.1 = (bf16[1536,384]{1,0:T(8,128)(2,1)S(1)}, bf16[1536,384]{1,0:T(8,128)(2,1)}, u32[]{:S(2)}) copy-start(bf16[1536,384]{1,0:T(8,128)(2,1)} %refs_3_.3) | copy-start | bytes 3538948
  9.8 7.4 %copy-start.2 = (bf16[384,1536]{1,0:T(8,128)(2,1)S(1)}, bf16[384,1536]{1,0:T(8,128)(2,1)}, u32[]{:S(2)}) copy-start(bf16[384,1536]{1,0:T(8,128)(2,1)} %refs_4_.3) | copy-start | bytes 3538948
  9.8 7.4 %copy-start.3 = (bf16[1,32,32,384]{3,2,1,0:T(8,128)(2,1)S(1)}, bf16[1,32,32,384]{3,2,1,0:T(8,128)(2,1)}, u32[]{:S(2)}) copy-start(bf16[1,32,32,384]{3,2,1,0:T(8,128)(2,1)} %param.12) | copy-start | bytes 2359300
  9.9 7.4 %copy-start.5 = (f32[1536]{0:T(1024)S(1)}, f32[1536]{0:T(1024)}, u32[]{:S(2)}) copy-start(f32[1536]{0:T(1024)} %refs_5_.6) | copy-start | bytes 18436
  9.9 7.4 %copy-start.9 = (f32[384]{0:T(512)S(1)}, f32[384]{0:T(512)}, u32[]{:S(2)}) copy-start(f32[384]{0:T(512)} %refs_6_.5) | copy-start | bytes 4612
  17.3 11.9 %copy-start.10 = (f32[384]{0:T(512)S(1)}, f32[384]{0:T(512)}, u32[]{:S(2)}) copy-start(f32[384]{0:T(512)} %refs_7_.3) | copy-start | bytes 4612
  25.3 10.2 %collective-permute-start.3 = (bf16[3072,128]{1,0:T(8,128)(2,1)S(1)}, bf16[3072,128]{1,0:T(8,128)(2,1)S(1)}, u32[]{:S(2)}, u32[]{:S(2)}) collective-permute-start(bf16[3072,128]{1,0:T(8,128)(2,1)S(1)} %get-tuple-element.95), channel_id=1, source_target_pairs={{0,8},{1,9},{2,10},{3,11},{4,12},{5,13},{6,14},{7,15},{8,0},{9,1},... | collective-permute-start | bytes 2359304 | tf_op jit(solution)/shard_map/ppermute | solution.py:409
  35.6 6.5 %collective-permute-start.16 = (bf16[3,32,384]{2,1,0:T(8,128)(2,1)S(1)}, bf16[3,32,384]{2,1,0:T(8,128)(2,1)S(1)}, u32[]{:S(2)}, u32[]{:S(2)}) collective-permute-start(bf16[3,32,384]{2,1,0:T(8,128)(2,1)S(1)} %get-tuple-element.155), channel_id=1, source_target_pairs={{0,8},{16,24},{8,0},{24,16},{1,9},{17,25},{9,1},{25,17},{2,10},{18... | collective-permute-start | bytes 221192 | tf_op jit(solution)/shard_map/ppermute | solution.py:45
  35.7 7.7 %collective-permute-start.15 = (bf16[3,32,384]{2,1,0:T(8,128)(2,1)S(1)}, bf16[3,32,384]{2,1,0:T(8,128)(2,1)S(1)}, u32[]{:S(2)}, u32[]{:S(2)}) collective-permute-start(bf16[3,32,384]{2,1,0:T(8,128)(2,1)S(1)} %get-tuple-element.156), channel_id=1, source_target_pairs={{8,16},{16,8},{9,17},{17,9},{10,18},{18,10},{11,19},{19,11},{12,20... | collective-permute-start | bytes 221192 | tf_op jit(solution)/shard_map/ppermute | solution.py:45
  36.7 15.5 %collective-permute-start.5 = (bf16[768,128]{1,0:T(8,128)(2,1)S(1)}, bf16[768,128]{1,0:T(8,128)(2,1)S(1)}, u32[]{:S(2)}, u32[]{:S(2)}) collective-permute-start(bf16[768,128]{1,0:T(8,128)(2,1)S(1)} %get-tuple-element.102), channel_id=1, source_target_pairs={{0,4},{1,5},{2,6},{3,7},{4,0},{5,1},{6,2},{7,3},{8,12},{9,13},{10,... | collective-permute-start | bytes 589832 | tf_op jit(solution)/shard_map/ppermute | solution.py:409
  38.5 13.7 %collective-permute-start.6 = (bf16[768,128]{1,0:T(8,128)(2,1)S(1)}, bf16[768,128]{1,0:T(8,128)(2,1)S(1)}, u32[]{:S(2)}, u32[]{:S(2)}) collective-permute-start(bf16[768,128]{1,0:T(8,128)(2,1)S(1)} %get-tuple-element.103), channel_id=1, source_target_pairs={{0,20},{1,21},{2,22},{3,23},{4,16},{5,17},{6,18},{7,19},{8,28},{9,... | collective-permute-start | bytes 589832 | tf_op jit(solution)/shard_map/ppermute | solution.py:409
  42.1 10.2 %collective-permute-start.4 = (bf16[768,128]{1,0:T(8,128)(2,1)S(1)}, bf16[768,128]{1,0:T(8,128)(2,1)S(1)}, u32[]{:S(2)}, u32[]{:S(2)}) collective-permute-start(bf16[768,128]{1,0:T(8,128)(2,1)S(1)} %get-tuple-element.101.refs_10_), channel_id=1, source_target_pairs={{0,16},{1,17},{2,18},{3,19},{4,20},{5,21},{6,22},{7,23},{8,24},{9,... | collective-permute-start | bytes 589832 | tf_op jit(solution)/shard_map/ppermute | solution.py:409
  42.1 10.2 %collective-permute-start.7 = (bf16[1536,128]{1,0:T(8,128)(2,1)S(1)}, bf16[1536,128]{1,0:T(8,128)(2,1)S(1)}, u32[]{:S(2)}, u32[]{:S(2)}) collective-permute-start(bf16[1536,128]{1,0:T(8,128)(2,1)S(1)} %get-tuple-element.110), channel_id=1, source_target_pairs={{0,8},{1,9},{2,10},{3,11},{4,12},{5,13},{6,14},{7,15},{8,0},{9,1},... | collective-permute-start | bytes 1179656 | tf_op jit(solution)/shard_map/ppermute | solution.py:409
  43.6 14.2 %collective-permute-start.17 = (bf16[38,3,384]{2,1,0:T(4,128)(2,1)S(1)}, bf16[38,3,384]{2,1,0:T(4,128)(2,1)S(1)}, u32[]{:S(2)}, u32[]{:S(2)}) collective-permute-start(bf16[38,3,384]{2,1,0:T(4,128)(2,1)S(1)} %maximum_select_fusion.1), channel_id=1, source_target_pairs={{0,4},{4,0},{1,5},{5,1},{2,6},{6,2},{3,7},{7,3},{8,12},{12,8},{9,1... | collective-permute-start | bytes 262664 | tf_op jit(solution)/shard_map/ppermute | solution.py:45
  52.3 1.9 %collective-permute-start.9 = (bf16[128,128]{1,0:T(8,128)(2,1)S(1)}, bf16[128,128]{1,0:T(8,128)(2,1)S(1)}, u32[]{:S(2)}, u32[]{:S(2)}) collective-permute-start(bf16[128,128]{1,0:T(8,128)(2,1)S(1)} %get-tuple-element.118), channel_id=1, source_target_pairs={{0,8},{1,9},{2,10},{3,11},{4,12},{5,13},{6,14},{7,15},{8,0},{9,1},... | collective-permute-start | bytes 98312 | tf_op jit(solution)/shard_map/ppermute | solution.py:409
  52.5 9.9 %collective-permute-start.8 = (bf16[768,128]{1,0:T(8,128)(2,1)S(1)}, bf16[768,128]{1,0:T(8,128)(2,1)S(1)}, u32[]{:S(2)}, u32[]{:S(2)}) collective-permute-start(bf16[768,128]{1,0:T(8,128)(2,1)S(1)} %shard_map.199.refs_0_), channel_id=1, source_target_pairs={{0,1},{1,0},{2,3},{3,2},{4,5},{5,4},{6,7},{7,6},{8,9},{9,8},{10,11... | collective-permute-start | bytes 589832 | tf_op jit(solution)/shard_map/ppermute | solution.py:409
  54.2 5.6 %collective-permute-start.10 = (bf16[416,128]{1,0:T(8,128)(2,1)S(1)}, bf16[416,128]{1,0:T(8,128)(2,1)S(1)}, u32[]{:S(2)}, u32[]{:S(2)}) collective-permute-start(bf16[416,128]{1,0:T(8,128)(2,1)S(1)} %get-tuple-element.120), channel_id=1, source_target_pairs={{0,16},{1,17},{2,18},{3,19},{4,20},{5,21},{6,22},{7,23},{8,24},{9,... | collective-permute-start | bytes 319496 | tf_op jit(solution)/shard_map/ppermute | solution.py:409
  55.3 7.1 %collective-permute-start.11 = (bf16[416,128]{1,0:T(8,128)(2,1)S(1)}, bf16[416,128]{1,0:T(8,128)(2,1)S(1)}, u32[]{:S(2)}, u32[]{:S(2)}) collective-permute-start(bf16[416,128]{1,0:T(8,128)(2,1)S(1)} %get-tuple-element.121), channel_id=1, source_target_pairs={{0,4},{1,5},{2,6},{3,7},{4,0},{5,1},{6,2},{7,3},{8,12},{9,13},{10,... | collective-permute-start | bytes 319496 | tf_op jit(solution)/shard_map/ppermute | solution.py:409
  55.8 6.5 %collective-permute-start.12 = (bf16[416,128]{1,0:T(8,128)(2,1)S(1)}, bf16[416,128]{1,0:T(8,128)(2,1)S(1)}, u32[]{:S(2)}, u32[]{:S(2)}) collective-permute-start(bf16[416,128]{1,0:T(8,128)(2,1)S(1)} %get-tuple-element.122), channel_id=1, source_target_pairs={{0,20},{1,21},{2,22},{3,23},{4,16},{5,17},{6,18},{7,19},{8,28},{9,... | collective-permute-start | bytes 319496 | tf_op jit(solution)/shard_map/ppermute | solution.py:409
  62.5 10.3 %collective-permute-start.14 = (bf16[416,128]{1,0:T(8,128)(2,1)S(1)}, bf16[416,128]{1,0:T(8,128)(2,1)S(1)}, u32[]{:S(2)}, u32[]{:S(2)}) collective-permute-start(bf16[416,128]{1,0:T(8,128)(2,1)S(1)} %shard_map.202.refs_8_.refs_0_), channel_id=1, source_target_pairs={{0,1},{1,0},{2,3},{3,2},{4,5},{5,4},{6,7},{7,6},{8,9},{9,8},{10,11... | collective-permute-start | bytes 319496 | tf_op jit(solution)/shard_map/ppermute | solution.py:409
  63.5 10.0 %collective-permute-start.13 = (bf16[768,128]{1,0:T(8,128)(2,1)S(1)}, bf16[768,128]{1,0:T(8,128)(2,1)S(1)}, u32[]{:S(2)}, u32[]{:S(2)}) collective-permute-start(bf16[768,128]{1,0:T(8,128)(2,1)S(1)} %shard_map.201.refs_7_.refs_0_), channel_id=1, source_target_pairs={{0,2},{1,3},{2,0},{3,1},{4,6},{5,7},{6,4},{7,5},{8,10},{9,11},{10,... | collective-permute-start | bytes 589832 | tf_op jit(solution)/shard_map/ppermute | solution.py:409
  73.6 10.4 %collective-permute-start.20 = (bf16[768,128]{1,0:T(8,128)(2,1)S(1)}, bf16[768,128]{1,0:T(8,128)(2,1)S(1)}, u32[]{:S(2)}, u32[]{:S(2)}) collective-permute-start(bf16[768,128]{1,0:T(8,128)(2,1)S(1)} %shard_map.204.refs_1_), channel_id=1, source_target_pairs={{0,20},{1,21},{2,22},{3,23},{4,16},{5,17},{6,18},{7,19},{8,28},{9,... | collective-permute-start | bytes 589832 | tf_op jit(solution)/shard_map/ppermute | solution.py:409
  75.5 8.5 %collective-permute-start.19 = (bf16[768,128]{1,0:T(8,128)(2,1)S(1)}, bf16[768,128]{1,0:T(8,128)(2,1)S(1)}, u32[]{:S(2)}, u32[]{:S(2)}) collective-permute-start(bf16[768,128]{1,0:T(8,128)(2,1)S(1)} %shard_map.204.refs_1_), channel_id=1, source_target_pairs={{0,4},{1,5},{2,6},{3,7},{4,0},{5,1},{6,2},{7,3},{8,12},{9,13},{10,... | collective-permute-start | bytes 589832 | tf_op jit(solution)/shard_map/ppermute | solution.py:409
  76.2 7.8 %collective-permute-start.18 = (bf16[768,128]{1,0:T(8,128)(2,1)S(1)}, bf16[768,128]{1,0:T(8,128)(2,1)S(1)}, u32[]{:S(2)}, u32[]{:S(2)}) collective-permute-start(bf16[768,128]{1,0:T(8,128)(2,1)S(1)} %shard_map.204.refs_1_), channel_id=1, source_target_pairs={{0,16},{1,17},{2,18},{3,19},{4,20},{5,21},{6,22},{7,23},{8,24},{9,... | collective-permute-start | bytes 589832 | tf_op jit(solution)/shard_map/ppermute | solution.py:409
  77.2 6.8 %collective-permute-start.21 = (bf16[416,128]{1,0:T(8,128)(2,1)S(1)}, bf16[416,128]{1,0:T(8,128)(2,1)S(1)}, u32[]{:S(2)}, u32[]{:S(2)}) collective-permute-start(bf16[416,128]{1,0:T(8,128)(2,1)S(1)} %shard_map.205.refs_0_), channel_id=1, source_target_pairs={{0,2},{1,3},{2,0},{3,1},{4,6},{5,7},{6,4},{7,5},{8,10},{9,11},{10,... | collective-permute-start | bytes 319496 | tf_op jit(solution)/shard_map/ppermute | solution.py:409
  84.1 8.9 %collective-permute-start.22 = (bf16[3072,128]{1,0:T(8,128)(2,1)S(1)}, bf16[3072,128]{1,0:T(8,128)(2,1)S(1)}, u32[]{:S(2)}, u32[]{:S(2)}) collective-permute-start(bf16[3072,128]{1,0:T(8,128)(2,1)S(1)} %shard_map.206.own), channel_id=1, source_target_pairs={{0,8},{1,9},{2,10},{3,11},{4,12},{5,13},{6,14},{7,15},{8,0},{9,1},... | collective-permute-start | bytes 2359304 | tf_op jit(solution)/shard_map/ppermute | solution.py:409
  84.2 6.7 %collective-permute-start.25 = (bf16[416,128]{1,0:T(8,128)(2,1)S(1)}, bf16[416,128]{1,0:T(8,128)(2,1)S(1)}, u32[]{:S(2)}, u32[]{:S(2)}) collective-permute-start(bf16[416,128]{1,0:T(8,128)(2,1)S(1)} %shard_map.207.refs_1_), channel_id=1, source_target_pairs={{0,20},{1,21},{2,22},{3,23},{4,16},{5,17},{6,18},{7,19},{8,28},{9,... | collective-permute-start | bytes 319496 | tf_op jit(solution)/shard_map/ppermute | solution.py:409
  86.1 6.7 %collective-permute-start.24 = (bf16[416,128]{1,0:T(8,128)(2,1)S(1)}, bf16[416,128]{1,0:T(8,128)(2,1)S(1)}, u32[]{:S(2)}, u32[]{:S(2)}) collective-permute-start(bf16[416,128]{1,0:T(8,128)(2,1)S(1)} %shard_map.207.refs_1_), channel_id=1, source_target_pairs={{0,4},{1,5},{2,6},{3,7},{4,0},{5,1},{6,2},{7,3},{8,12},{9,13},{10,... | collective-permute-start | bytes 319496 | tf_op jit(solution)/shard_map/ppermute | solution.py:409
  86.8 6.2 %collective-permute-start.23 = (bf16[416,128]{1,0:T(8,128)(2,1)S(1)}, bf16[416,128]{1,0:T(8,128)(2,1)S(1)}, u32[]{:S(2)}, u32[]{:S(2)}) collective-permute-start(bf16[416,128]{1,0:T(8,128)(2,1)S(1)} %shard_map.207.refs_1_), channel_id=1, source_target_pairs={{0,16},{1,17},{2,18},{3,19},{4,20},{5,21},{6,22},{7,23},{8,24},{9,... | collective-permute-start | bytes 319496 | tf_op jit(solution)/shard_map/ppermute | solution.py:409
  93.0 1.9 %collective-permute-start.26 = (bf16[1664,128]{1,0:T(8,128)(2,1)S(1)}, bf16[1664,128]{1,0:T(8,128)(2,1)S(1)}, u32[]{:S(2)}, u32[]{:S(2)}) collective-permute-start(bf16[1664,128]{1,0:T(8,128)(2,1)S(1)} %shard_map.208.own), channel_id=1, source_target_pairs={{0,8},{1,9},{2,10},{3,11},{4,12},{5,13},{6,14},{7,15},{8,0},{9,1},... | collective-permute-start | bytes 1277960 | tf_op jit(solution)/shard_map/ppermute | solution.py:409

commit v11 on v10

--- a/solution.py
+++ b/solution.py
@@ -229,7 +229,7 @@
     gbin_ref[...] = jnp.sum(gbin[...], axis=0, keepdims=True)
 
 
-MLP_BLOCK = 256
+MLP_BLOCK = 512
 
 
 def mlp_first_kernel(

time: 96.5 us -> 96.3 us (level)
  transfers between devices with their start and end apart: 27 -> 27, of which waited for: 8 -> 8; matrix products, arithmetic and copies ran while one was open for 2% -> 2% of each run, Pallas kernels for 23% -> 24%
where the time goes in v11:
time: 96.3 us; the launch traced here: 96.2 us
  Pallas kernels  39.5 us (41%)
  starting transfers between devices  32.8 us (34%)
  waiting for transfers between devices  19.9 us (21%)
  other arithmetic  1.55 us (2%)
  local copies, waits for them, and re-layouts  1.29 us (1%)
  between operations  1.15 us (1%)
    pallas_call x15, Pallas kernels, call(): pl.pallas_call(kernel, out_shape=[jax.ShapeDtypeStruct(shape, dtype) for...  36.3 us
    ppermute x21, starting transfers between devices, exchange(): return lax.ppermute(x, AXES, perm)  26.7 us
    ppermute x21, waiting for transfers between devices, exchange(): return lax.ppermute(x, AXES, perm)  17.1 us
    ppermute x6, starting transfers between devices, swap_edges(): got.append(lax.ppermute(jnp.where(is_high, high, low), axis, pairs))  6.1 us
    pallas_call x2, Pallas kernels, finish(): pl.pallas_call(kernel, grid=(width // unit,), out_shape=[jax.ShapeDtypeSt...  3.22 us
    ppermute x6, waiting for transfers between devices, swap_edges(): got.append(lax.ppermute(jnp.where(is_high, high, low), axis, pairs))  2.81 us
  transfers between devices with their start and end apart: 27, of which 8 were waited for; matrix products, arithmetic and copies ran while one was open for 2% of the time, Pallas kernels for 24%

profile of v11, /device:TPU:0, one launch (start us, length us, event | category | flops | bytes accessed | tf_op | source)
XLA Modules:
  0.0 96.2 jit_solution(3181708159772685343)
XLA Ops:
  0.6 0.0 copy-start
  0.7 1.0 %broadcast_select_fusion.11 = (bf16[3,32,384]{2,1,0:T(8,128)(2,1)S(1)}, bf16[3,32,384]{2,1,0:T(8,128)(2,1)S(1)}) fusion(pred[]{:T(512)S(6)} %eq.12, bf16[32,32,384]{2,1,0:T(8,128)(2,1)} %bitcast.9, pred[]{:T(512)S(6)} %not.4), kind=kLoop, calls=%fused_computation.13 | loop fusion | flops 73728 | bytes 294914 | tf_op jit(solution)/shard_map/jit(_where)/select_n | solution.py:45
  1.8 0.5 collective-permute-start.1
  2.3 0.7 collective-permute-start
  2.9 1.1 %fusion.1 = (bf16[32,3,384]{2,1,0:T(4,128)(2,1)S(1)}, bf16[32,3,384]{2,1,0:T(4,128)(2,1)S(1)}) fusion(bf16[32,32,384]{2,1,0:T(8,128)(2,1)} %bitcast.10), kind=kLoop, calls=%fused_computation.15 | loop fusion | bytes 294912 | tf_op jit(solution)/shard_map/slice | solution.py:52
  4.1 0.2 maximum_select_fusion
  4.3 2.6 %collective-permute-start.2 = (bf16[38,3,384]{2,1,0:T(4,128)(2,1)S(1)}, bf16[38,3,384]{2,1,0:T(4,128)(2,1)S(1)}, u32[]{:S(2)}, u32[]{:S(2)}) collective-permute-start(bf16[38,3,384]{2,1,0:T(4,128)(2,1)S(1)} %maximum_select_fusion), channel_id=1, source_target_pairs={{0,4},{4,0},{1,5},{5,1},{2,6},{6,2},{3,7},{7,3},{8,12},{12,8},{9,1... | collective-permute-start | bytes 262664 | tf_op jit(solution)/shard_map/ppermute | solution.py:45
  6.9 2.8 %collective-permute-done.2 = bf16[38,3,384]{2,1,0:T(4,128)(2,1)S(1)} collective-permute-done((bf16[38,3,384]{2,1,0:T(4,128)(2,1)S(1)}, bf16[38,3,384]{2,1,0:T(4,128)(2,1)S(1)}, u32[]{:S(2)}, u32[]{:S(2)}) %collective-permute-start.2) | collective-permute-done | bytes 87584 | tf_op jit(solution)/shard_map/ppermute | solution.py:45
  9.7 0.1 broadcast_select_fusion.2
  9.8 0.0 copy-start.1
  9.8 0.0 copy-start.2
  9.8 0.0 copy-start.3
  9.9 0.0 copy-start.5
  9.9 0.0 copy-start.9
  9.9 7.3 %shard_map.194 = (f32[1024,384]{1,0:T(8,128)S(1)}, f32[1024,128]{1,0:T(8,128)S(1)}, bf16[1024,384]{1,0:T(8,128)(2,1)S(1)}) custom-call(bf16[32,32,384]{2,1,0:T(8,128)(2,1)S(1)} %bitcast.11, bf16[3,32,384]{2,1,0:T(8,128)(2,1)S(1)} %get-tuple-element.164.refs_1_.refs_2_, bf16[3,32,384]{2,1,0:T(8,128)(2,1)S(1)} %get-tuple-element.163.refs_2_.refs_3_, ...), custom_call_target="tpu_custom_call" | custom-call | flops 2312110080 | bytes 2257920 | tf_op jit(solution)/shard_map/pallas_call | solution.py:376
  17.3 0.0 copy-start.10
  17.3 7.9 %shard_map.195 = (f32[1024,384]{1,0:T(8,128)S(1)}, f32[1024,384]{1,0:T(8,128)S(1)}, bf16[1024,384]{1,0:T(8,128)(2,1)S(1)}, bf16[3072,128]{1,0:T(8,128)(2,1)S(1)}...) custom-call(s32[1]{0:T(128)} %bitcast.refs_0_.core, bf16[1024,384]{1,0:T(8,128)(2,1)S(1)} %get-tuple-element.86.refs_1_, ...), custom_call_target="tpu_custom_call" | custom-call | flops 7247757312 | bytes 7077888 | tf_op jit(solution)/shard_map/pallas_call | solution.py:376
  25.2 3.8 %collective-permute-start.3 = (bf16[3072,128]{1,0:T(8,128)(2,1)S(1)}, bf16[3072,128]{1,0:T(8,128)(2,1)S(1)}, u32[]{:S(2)}, u32[]{:S(2)}) collective-permute-start(bf16[3072,128]{1,0:T(8,128)(2,1)S(1)} %get-tuple-element.95), channel_id=1, source_target_pairs={{0,8},{1,9},{2,10},{3,11},{4,12},{5,13},{6,14},{7,15},{8,0},{9,1},... | collective-permute-start | bytes 2359304 | tf_op jit(solution)/shard_map/ppermute | solution.py:409
  29.0 6.4 %shard_map.196 = (bf16[1024,384]{1,0:T(8,128)(2,1)}, bf16[1024,384]{1,0:T(8,128)(2,1)S(1)}, bf16[1536,128]{1,0:T(8,128)(2,1)S(1)}, bf16[1536,128]{1,0:T(8,128)(2...) custom-call(s32[1]{0:T(128)} %bitcast.refs_0_.core, bf16[1024,384]{1,0:T(8,128)(2,1)S(1)} %get-tuple-element.86.refs_1_, ...), custom_call_target="tpu_custom_call" | custom-call | flops 7247757312 | bytes 7077888 | tf_op jit(solution)/shard_map/pallas_call | solution.py:376
  35.4 0.1 collective-permute-start.16
  35.5 0.7 collective-permute-start.15
  36.2 0.1 fusion
  36.3 0.3 shard_map.197
  36.5 1.8 %collective-permute-start.5 = (bf16[768,128]{1,0:T(8,128)(2,1)S(1)}, bf16[768,128]{1,0:T(8,128)(2,1)S(1)}, u32[]{:S(2)}, u32[]{:S(2)}) collective-permute-start(bf16[768,128]{1,0:T(8,128)(2,1)S(1)} %get-tuple-element.102), channel_id=1, source_target_pairs={{0,4},{1,5},{2,6},{3,7},{4,0},{5,1},{6,2},{7,3},{8,12},{9,13},{10,... | collective-permute-start | bytes 589832 | tf_op jit(solution)/shard_map/ppermute | solution.py:409
  38.4 3.5 %collective-permute-start.6 = (bf16[768,128]{1,0:T(8,128)(2,1)S(1)}, bf16[768,128]{1,0:T(8,128)(2,1)S(1)}, u32[]{:S(2)}, u32[]{:S(2)}) collective-permute-start(bf16[768,128]{1,0:T(8,128)(2,1)S(1)} %get-tuple-element.103), channel_id=1, source_target_pairs={{0,20},{1,21},{2,22},{3,23},{4,16},{5,17},{6,18},{7,19},{8,28},{9,... | collective-permute-start | bytes 589832 | tf_op jit(solution)/shard_map/ppermute | solution.py:409
  41.9 0.1 collective-permute-start.4
  42.0 1.2 %collective-permute-start.7 = (bf16[1536,128]{1,0:T(8,128)(2,1)S(1)}, bf16[1536,128]{1,0:T(8,128)(2,1)S(1)}, u32[]{:S(2)}, u32[]{:S(2)}) collective-permute-start(bf16[1536,128]{1,0:T(8,128)(2,1)S(1)} %get-tuple-element.110), channel_id=1, source_target_pairs={{0,8},{1,9},{2,10},{3,11},{4,12},{5,13},{6,14},{7,15},{8,0},{9,1},... | collective-permute-start | bytes 1179656 | tf_op jit(solution)/shard_map/ppermute | solution.py:409
  43.3 0.2 maximum_select_fusion.1
  43.4 1.6 %collective-permute-start.17 = (bf16[38,3,384]{2,1,0:T(4,128)(2,1)S(1)}, bf16[38,3,384]{2,1,0:T(4,128)(2,1)S(1)}, u32[]{:S(2)}, u32[]{:S(2)}) collective-permute-start(bf16[38,3,384]{2,1,0:T(4,128)(2,1)S(1)} %maximum_select_fusion.1), channel_id=1, source_target_pairs={{0,4},{4,0},{1,5},{5,1},{2,6},{6,2},{3,7},{7,3},{8,12},{12,8},{9,1... | collective-permute-start | bytes 262664 | tf_op jit(solution)/shard_map/ppermute | solution.py:45
  45.0 7.1 %shard_map.198 = (bf16[128,128]{1,0:T(8,128)(2,1)S(1)}, bf16[128,128]{1,0:T(8,128)(2,1)S(1)}) custom-call(s32[1]{0:T(128)} %bitcast.refs_0_.core, bf16[32,32,384]{2,1,0:T(8,128)(2,1)S(1)} %bitcast.13, bf16[3,32,384]{2,1,0:T(8,128)(2,1)S(1)} %get-tuple-element.164.refs_1_.refs_2_, bf16[3,32,384]{2,1,0:T(8,128)(2,1)S(1)} %get-tuple-element.163.refs_2_.refs_3_, ...), custom_call_target="tpu_custom_call" | custom-call | flops 2312110080 | bytes 2257920 | tf_op jit(solution)/shard_map/pallas_call | solution.py:376
  52.1 0.1 collective-permute-start.9
  52.2 0.1 shard_map.199.refs_0_
  52.3 1.6 %collective-permute-start.8 = (bf16[768,128]{1,0:T(8,128)(2,1)S(1)}, bf16[768,128]{1,0:T(8,128)(2,1)S(1)}, u32[]{:S(2)}, u32[]{:S(2)}) collective-permute-start(bf16[768,128]{1,0:T(8,128)(2,1)S(1)} %shard_map.199.refs_0_), channel_id=1, source_target_pairs={{0,1},{1,0},{2,3},{3,2},{4,5},{5,4},{6,7},{7,6},{8,9},{9,8},{10,11... | collective-permute-start | bytes 589832 | tf_op jit(solution)/shard_map/ppermute | solution.py:409
  54.0 0.1 shard_map.200
  54.1 1.0 %collective-permute-start.10 = (bf16[416,128]{1,0:T(8,128)(2,1)S(1)}, bf16[416,128]{1,0:T(8,128)(2,1)S(1)}, u32[]{:S(2)}, u32[]{:S(2)}) collective-permute-start(bf16[416,128]{1,0:T(8,128)(2,1)S(1)} %get-tuple-element.120), channel_id=1, source_target_pairs={{0,16},{1,17},{2,18},{3,19},{4,20},{5,21},{6,22},{7,23},{8,24},{9,... | collective-permute-start | bytes 319496 | tf_op jit(solution)/shard_map/ppermute | solution.py:409
  55.1 0.6 collective-permute-start.11
  55.7 2.0 %collective-permute-start.12 = (bf16[416,128]{1,0:T(8,128)(2,1)S(1)}, bf16[416,128]{1,0:T(8,128)(2,1)S(1)}, u32[]{:S(2)}, u32[]{:S(2)}) collective-permute-start(bf16[416,128]{1,0:T(8,128)(2,1)S(1)} %get-tuple-element.122), channel_id=1, source_target_pairs={{0,20},{1,21},{2,22},{3,23},{4,16},{5,17},{6,18},{7,19},{8,28},{9,... | collective-permute-start | bytes 319496 | tf_op jit(solution)/shard_map/ppermute | solution.py:409
  57.6 0.1 broadcast_select_fusion
  57.7 1.9 %collective-permute-done.10.refs_1_ = bf16[416,128]{1,0:T(8,128)(2,1)S(1)} collective-permute-done((bf16[416,128]{1,0:T(8,128)(2,1)S(1)}, bf16[416,128]{1,0:T(8,128)(2,1)S(1)}, u32[]{:S(2)}, u32[]{:S(2)}) %collective-permute-start.10) | collective-permute-done | bytes 106528 | tf_op jit(solution)/shard_map/ppermute | solution.py:409
  59.6 2.5 %collective-permute-done.11.refs_2_ = bf16[416,128]{1,0:T(8,128)(2,1)S(1)} collective-permute-done((bf16[416,128]{1,0:T(8,128)(2,1)S(1)}, bf16[416,128]{1,0:T(8,128)(2,1)S(1)}, u32[]{:S(2)}, u32[]{:S(2)}) %collective-permute-start.11) | collective-permute-done | bytes 106528 | tf_op jit(solution)/shard_map/ppermute | solution.py:409
  62.2 0.1 shard_map.201.refs_7_.refs_0_
  62.2 0.1 shard_map.202.refs_8_.refs_0_
  62.3 1.0 %collective-permute-start.14 = (bf16[416,128]{1,0:T(8,128)(2,1)S(1)}, bf16[416,128]{1,0:T(8,128)(2,1)S(1)}, u32[]{:S(2)}, u32[]{:S(2)}) collective-permute-start(bf16[416,128]{1,0:T(8,128)(2,1)S(1)} %shard_map.202.refs_8_.refs_0_), channel_id=1, source_target_pairs={{0,1},{1,0},{2,3},{3,2},{4,5},{5,4},{6,7},{7,6},{8,9},{9,8},{10,11... | collective-permute-start | bytes 319496 | tf_op jit(solution)/shard_map/ppermute | solution.py:409
  63.4 2.6 %collective-permute-start.13 = (bf16[768,128]{1,0:T(8,128)(2,1)S(1)}, bf16[768,128]{1,0:T(8,128)(2,1)S(1)}, u32[]{:S(2)}, u32[]{:S(2)}) collective-permute-start(bf16[768,128]{1,0:T(8,128)(2,1)S(1)} %shard_map.201.refs_7_.refs_0_), channel_id=1, source_target_pairs={{0,2},{1,3},{2,0},{3,1},{4,6},{5,7},{6,4},{7,5},{8,10},{9,11},{10,... | collective-permute-start | bytes 589832 | tf_op jit(solution)/shard_map/ppermute | solution.py:409
  66.0 6.7 %shard_map.203 = bf16[1024,384]{1,0:T(8,128)(2,1)} custom-call(bf16[32,32,384]{2,1,0:T(8,128)(2,1)S(1)} %bitcast.16, bf16[3,32,384]{2,1,0:T(8,128)(2,1)S(1)} %get-tuple-element.162.refs_1_, bf16[3,32,384]{2,1,0:T(8,128)(2,1)S(1)} %get-tuple-element.161.refs_2_, bf16[38,3,384]{2,1,0:T(4,128)(2,1)S(1)} %get-tuple-element.166.refs_3_, ...), custom_call_target="tpu_custom_call" | custom-call | flops 2312110080 | bytes 2257920 | tf_op jit(solution)/shard_map/pallas_call | solution.py:376
  72.7 0.6 collective-permute-done.13.refs_1_
  73.3 0.1 shard_map.204.refs_1_
  73.4 1.9 %collective-permute-start.20 = (bf16[768,128]{1,0:T(8,128)(2,1)S(1)}, bf16[768,128]{1,0:T(8,128)(2,1)S(1)}, u32[]{:S(2)}, u32[]{:S(2)}) collective-permute-start(bf16[768,128]{1,0:T(8,128)(2,1)S(1)} %shard_map.204.refs_1_), channel_id=1, source_target_pairs={{0,20},{1,21},{2,22},{3,23},{4,16},{5,17},{6,18},{7,19},{8,28},{9,... | collective-permute-start | bytes 589832 | tf_op jit(solution)/shard_map/ppermute | solution.py:409
  75.3 0.7 collective-permute-start.19
  76.0 0.9 collective-permute-start.18
  77.0 0.1 collective-permute-start.21
  77.1 6.7 %collective-permute-done.21.refs_1_ = bf16[416,128]{1,0:T(8,128)(2,1)S(1)} collective-permute-done((bf16[416,128]{1,0:T(8,128)(2,1)S(1)}, bf16[416,128]{1,0:T(8,128)(2,1)S(1)}, u32[]{:S(2)}, u32[]{:S(2)}) %collective-permute-start.21) | collective-permute-done | bytes 106528 | tf_op jit(solution)/shard_map/ppermute | solution.py:409
  83.8 0.1 shard_map.206.own
  83.9 0.1 collective-permute-start.22
  83.9 0.1 shard_map.207.refs_1_
  84.0 1.9 %collective-permute-start.25 = (bf16[416,128]{1,0:T(8,128)(2,1)S(1)}, bf16[416,128]{1,0:T(8,128)(2,1)S(1)}, u32[]{:S(2)}, u32[]{:S(2)}) collective-permute-start(bf16[416,128]{1,0:T(8,128)(2,1)S(1)} %shard_map.207.refs_1_), channel_id=1, source_target_pairs={{0,20},{1,21},{2,22},{3,23},{4,16},{5,17},{6,18},{7,19},{8,28},{9,... | collective-permute-start | bytes 319496 | tf_op jit(solution)/shard_map/ppermute | solution.py:409
  85.9 0.7 collective-permute-start.24
  86.6 0.9 collective-permute-start.23
  87.6 3.2 %collective-permute-done.25.refs_4_ = bf16[416,128]{1,0:T(8,128)(2,1)S(1)} collective-permute-done((bf16[416,128]{1,0:T(8,128)(2,1)S(1)}, bf16[416,128]{1,0:T(8,128)(2,1)S(1)}, u32[]{:S(2)}, u32[]{:S(2)}) %collective-permute-start.25) | collective-permute-done | bytes 106528 | tf_op jit(solution)/shard_map/ppermute | solution.py:409
  90.7 1.9 %collective-permute-done.24.refs_3_ = bf16[416,128]{1,0:T(8,128)(2,1)S(1)} collective-permute-done((bf16[416,128]{1,0:T(8,128)(2,1)S(1)}, bf16[416,128]{1,0:T(8,128)(2,1)S(1)}, u32[]{:S(2)}, u32[]{:S(2)}) %collective-permute-start.24) | collective-permute-done | bytes 106528 | tf_op jit(solution)/shard_map/ppermute | solution.py:409
  92.6 0.2 collective-permute-done.23.refs_2_
  92.9 0.1 collective-permute-start.26
  92.9 1.9 %shard_map.209 = (f32[1536,384]{1,0:T(8,128)}, f32[384,1536]{1,0:T(8,128)}) custom-call(s32[1]{0:T(128)} %bitcast.refs_0_.core, bf16[3072,128]{1,0:T(8,128)(2,1)S(1)} %shard_map.206.own, bf16[3072,128]{1,0:T(8,128)(2,1)S(1)} %collective-permute-done.22.other), custom_call_target="tpu_custom_call" | custom-call | tf_op jit(solution)/shard_map/pallas_call | solution.py:548
  94.8 1.4 %shard_map.210 = (f32[1536,384]{1,0:T(8,128)}, f32[384,1536]{1,0:T(8,128)}, f32[7,7,384]{2,1,0:T(8,128)}, f32[384]{0:T(512)}, f32[384]{0:T(512)}, /*index=5*/f32...) custom-call(s32[1]{0:T(128)} %bitcast.refs_0_.core, ...), custom_call_target="tpu_custom_call", output_to_operand_aliasing={{0}: (3, {}), {1}: (4, {})} | custom-call | tf_op jit(solution)/shard_map/pallas_call | solution.py:548
  (42 shorter events, 0.3 us)
Async XLA Ops:
  0.6 9.1 %copy-start = (bf16[1,32,32,384]{3,2,1,0:T(8,128)(2,1)S(1)}, bf16[1,32,32,384]{3,2,1,0:T(8,128)(2,1)}, u32[]{:S(2)}) copy-start(bf16[1,32,32,384]{3,2,1,0:T(8,128)(2,1)} %param.11) | copy-start | bytes 2359300
  0.7 9.1 %copy-start.8 = (f32[384]{0:T(512)S(1)}, f32[384]{0:T(512)}, u32[]{:S(2)}) copy-start(f32[384]{0:T(512)} %refs_8_.3) | copy-start | bytes 4612
  0.7 9.1 %copy-start.4 = (f32[7,7,384]{2,1,0:T(8,128)S(1)}, f32[7,7,384]{2,1,0:T(8,128)}, u32[]{:S(2)}) copy-start(f32[7,7,384]{2,1,0:T(8,128)} %refs_5_.7) | copy-start | bytes 225796
  0.7 9.1 %copy-start.7 = (f32[384]{0:T(512)S(1)}, f32[384]{0:T(512)}, u32[]{:S(2)}) copy-start(f32[384]{0:T(512)} %refs_8_.2) | copy-start | bytes 4612
  0.7 9.1 %copy-start.6 = (f32[384]{0:T(512)S(1)}, f32[384]{0:T(512)}, u32[]{:S(2)}) copy-start(f32[384]{0:T(512)} %refs_6_.3) | copy-start | bytes 4612
  1.8 2.3 %collective-permute-start.1 = (bf16[3,32,384]{2,1,0:T(8,128)(2,1)S(1)}, bf16[3,32,384]{2,1,0:T(8,128)(2,1)S(1)}, u32[]{:S(2)}, u32[]{:S(2)}) collective-permute-start(bf16[3,32,384]{2,1,0:T(8,128)(2,1)S(1)} %get-tuple-element.159), channel_id=1, source_target_pairs={{0,8},{16,24},{8,0},{24,16},{1,9},{17,25},{9,1},{25,17},{2,10},{18... | collective-permute-start | bytes 221192 | tf_op jit(solution)/shard_map/ppermute | solution.py:45
  2.3 1.8 %collective-permute-start = (bf16[3,32,384]{2,1,0:T(8,128)(2,1)S(1)}, bf16[3,32,384]{2,1,0:T(8,128)(2,1)S(1)}, u32[]{:S(2)}, u32[]{:S(2)}) collective-permute-start(bf16[3,32,384]{2,1,0:T(8,128)(2,1)S(1)} %get-tuple-element.160), channel_id=1, source_target_pairs={{8,16},{16,8},{9,17},{17,9},{10,18},{18,10},{11,19},{19,11},{12,20... | collective-permute-start | bytes 221192 | tf_op jit(solution)/shard_map/ppermute | solution.py:45
  4.3 5.4 %collective-permute-start.2 = (bf16[38,3,384]{2,1,0:T(4,128)(2,1)S(1)}, bf16[38,3,384]{2,1,0:T(4,128)(2,1)S(1)}, u32[]{:S(2)}, u32[]{:S(2)}) collective-permute-start(bf16[38,3,384]{2,1,0:T(4,128)(2,1)S(1)} %maximum_select_fusion), channel_id=1, source_target_pairs={{0,4},{4,0},{1,5},{5,1},{2,6},{6,2},{3,7},{7,3},{8,12},{12,8},{9,1... | collective-permute-start | bytes 262664 | tf_op jit(solution)/shard_map/ppermute | solution.py:45
  9.8 7.4 %copy-start.1 = (bf16[1536,384]{1,0:T(8,128)(2,1)S(1)}, bf16[1536,384]{1,0:T(8,128)(2,1)}, u32[]{:S(2)}) copy-start(bf16[1536,384]{1,0:T(8,128)(2,1)} %refs_3_.3) | copy-start | bytes 3538948
  9.8 7.4 %copy-start.2 = (bf16[384,1536]{1,0:T(8,128)(2,1)S(1)}, bf16[384,1536]{1,0:T(8,128)(2,1)}, u32[]{:S(2)}) copy-start(bf16[384,1536]{1,0:T(8,128)(2,1)} %refs_4_.3) | copy-start | bytes 3538948
  9.8 7.4 %copy-start.3 = (bf16[1,32,32,384]{3,2,1,0:T(8,128)(2,1)S(1)}, bf16[1,32,32,384]{3,2,1,0:T(8,128)(2,1)}, u32[]{:S(2)}) copy-start(bf16[1,32,32,384]{3,2,1,0:T(8,128)(2,1)} %param.12) | copy-start | bytes 2359300
  9.9 7.4 %copy-start.5 = (f32[1536]{0:T(1024)S(1)}, f32[1536]{0:T(1024)}, u32[]{:S(2)}) copy-start(f32[1536]{0:T(1024)} %refs_5_.6) | copy-start | bytes 18436
  9.9 7.4 %copy-start.9 = (f32[384]{0:T(512)S(1)}, f32[384]{0:T(512)}, u32[]{:S(2)}) copy-start(f32[384]{0:T(512)} %refs_6_.5) | copy-start | bytes 4612
  17.3 11.7 %copy-start.10 = (f32[384]{0:T(512)S(1)}, f32[384]{0:T(512)}, u32[]{:S(2)}) copy-start(f32[384]{0:T(512)} %refs_7_.3) | copy-start | bytes 4612
  25.2 10.2 %collective-permute-start.3 = (bf16[3072,128]{1,0:T(8,128)(2,1)S(1)}, bf16[3072,128]{1,0:T(8,128)(2,1)S(1)}, u32[]{:S(2)}, u32[]{:S(2)}) collective-permute-start(bf16[3072,128]{1,0:T(8,128)(2,1)S(1)} %get-tuple-element.95), channel_id=1, source_target_pairs={{0,8},{1,9},{2,10},{3,11},{4,12},{5,13},{6,14},{7,15},{8,0},{9,1},... | collective-permute-start | bytes 2359304 | tf_op jit(solution)/shard_map/ppermute | solution.py:409
  35.4 6.5 %collective-permute-start.16 = (bf16[3,32,384]{2,1,0:T(8,128)(2,1)S(1)}, bf16[3,32,384]{2,1,0:T(8,128)(2,1)S(1)}, u32[]{:S(2)}, u32[]{:S(2)}) collective-permute-start(bf16[3,32,384]{2,1,0:T(8,128)(2,1)S(1)} %get-tuple-element.155), channel_id=1, source_target_pairs={{0,8},{16,24},{8,0},{24,16},{1,9},{17,25},{9,1},{25,17},{2,10},{18... | collective-permute-start | bytes 221192 | tf_op jit(solution)/shard_map/ppermute | solution.py:45
  35.5 7.7 %collective-permute-start.15 = (bf16[3,32,384]{2,1,0:T(8,128)(2,1)S(1)}, bf16[3,32,384]{2,1,0:T(8,128)(2,1)S(1)}, u32[]{:S(2)}, u32[]{:S(2)}) collective-permute-start(bf16[3,32,384]{2,1,0:T(8,128)(2,1)S(1)} %get-tuple-element.156), channel_id=1, source_target_pairs={{8,16},{16,8},{9,17},{17,9},{10,18},{18,10},{11,19},{19,11},{12,20... | collective-permute-start | bytes 221192 | tf_op jit(solution)/shard_map/ppermute | solution.py:45
  36.5 15.5 %collective-permute-start.5 = (bf16[768,128]{1,0:T(8,128)(2,1)S(1)}, bf16[768,128]{1,0:T(8,128)(2,1)S(1)}, u32[]{:S(2)}, u32[]{:S(2)}) collective-permute-start(bf16[768,128]{1,0:T(8,128)(2,1)S(1)} %get-tuple-element.102), channel_id=1, source_target_pairs={{0,4},{1,5},{2,6},{3,7},{4,0},{5,1},{6,2},{7,3},{8,12},{9,13},{10,... | collective-permute-start | bytes 589832 | tf_op jit(solution)/shard_map/ppermute | solution.py:409
  38.4 13.7 %collective-permute-start.6 = (bf16[768,128]{1,0:T(8,128)(2,1)S(1)}, bf16[768,128]{1,0:T(8,128)(2,1)S(1)}, u32[]{:S(2)}, u32[]{:S(2)}) collective-permute-start(bf16[768,128]{1,0:T(8,128)(2,1)S(1)} %get-tuple-element.103), channel_id=1, source_target_pairs={{0,20},{1,21},{2,22},{3,23},{4,16},{5,17},{6,18},{7,19},{8,28},{9,... | collective-permute-start | bytes 589832 | tf_op jit(solution)/shard_map/ppermute | solution.py:409
  41.9 10.2 %collective-permute-start.4 = (bf16[768,128]{1,0:T(8,128)(2,1)S(1)}, bf16[768,128]{1,0:T(8,128)(2,1)S(1)}, u32[]{:S(2)}, u32[]{:S(2)}) collective-permute-start(bf16[768,128]{1,0:T(8,128)(2,1)S(1)} %get-tuple-element.101.refs_10_), channel_id=1, source_target_pairs={{0,16},{1,17},{2,18},{3,19},{4,20},{5,21},{6,22},{7,23},{8,24},{9,... | collective-permute-start | bytes 589832 | tf_op jit(solution)/shard_map/ppermute | solution.py:409
  42.0 10.2 %collective-permute-start.7 = (bf16[1536,128]{1,0:T(8,128)(2,1)S(1)}, bf16[1536,128]{1,0:T(8,128)(2,1)S(1)}, u32[]{:S(2)}, u32[]{:S(2)}) collective-permute-start(bf16[1536,128]{1,0:T(8,128)(2,1)S(1)} %get-tuple-element.110), channel_id=1, source_target_pairs={{0,8},{1,9},{2,10},{3,11},{4,12},{5,13},{6,14},{7,15},{8,0},{9,1},... | collective-permute-start | bytes 1179656 | tf_op jit(solution)/shard_map/ppermute | solution.py:409
  43.4 14.2 %collective-permute-start.17 = (bf16[38,3,384]{2,1,0:T(4,128)(2,1)S(1)}, bf16[38,3,384]{2,1,0:T(4,128)(2,1)S(1)}, u32[]{:S(2)}, u32[]{:S(2)}) collective-permute-start(bf16[38,3,384]{2,1,0:T(4,128)(2,1)S(1)} %maximum_select_fusion.1), channel_id=1, source_target_pairs={{0,4},{4,0},{1,5},{5,1},{2,6},{6,2},{3,7},{7,3},{8,12},{12,8},{9,1... | collective-permute-start | bytes 262664 | tf_op jit(solution)/shard_map/ppermute | solution.py:45
  52.1 1.9 %collective-permute-start.9 = (bf16[128,128]{1,0:T(8,128)(2,1)S(1)}, bf16[128,128]{1,0:T(8,128)(2,1)S(1)}, u32[]{:S(2)}, u32[]{:S(2)}) collective-permute-start(bf16[128,128]{1,0:T(8,128)(2,1)S(1)} %get-tuple-element.118), channel_id=1, source_target_pairs={{0,8},{1,9},{2,10},{3,11},{4,12},{5,13},{6,14},{7,15},{8,0},{9,1},... | collective-permute-start | bytes 98312 | tf_op jit(solution)/shard_map/ppermute | solution.py:409
  52.3 9.9 %collective-permute-start.8 = (bf16[768,128]{1,0:T(8,128)(2,1)S(1)}, bf16[768,128]{1,0:T(8,128)(2,1)S(1)}, u32[]{:S(2)}, u32[]{:S(2)}) collective-permute-start(bf16[768,128]{1,0:T(8,128)(2,1)S(1)} %shard_map.199.refs_0_), channel_id=1, source_target_pairs={{0,1},{1,0},{2,3},{3,2},{4,5},{5,4},{6,7},{7,6},{8,9},{9,8},{10,11... | collective-permute-start | bytes 589832 | tf_op jit(solution)/shard_map/ppermute | solution.py:409
  54.1 5.6 %collective-permute-start.10 = (bf16[416,128]{1,0:T(8,128)(2,1)S(1)}, bf16[416,128]{1,0:T(8,128)(2,1)S(1)}, u32[]{:S(2)}, u32[]{:S(2)}) collective-permute-start(bf16[416,128]{1,0:T(8,128)(2,1)S(1)} %get-tuple-element.120), channel_id=1, source_target_pairs={{0,16},{1,17},{2,18},{3,19},{4,20},{5,21},{6,22},{7,23},{8,24},{9,... | collective-permute-start | bytes 319496 | tf_op jit(solution)/shard_map/ppermute | solution.py:409
  55.1 7.1 %collective-permute-start.11 = (bf16[416,128]{1,0:T(8,128)(2,1)S(1)}, bf16[416,128]{1,0:T(8,128)(2,1)S(1)}, u32[]{:S(2)}, u32[]{:S(2)}) collective-permute-start(bf16[416,128]{1,0:T(8,128)(2,1)S(1)} %get-tuple-element.121), channel_id=1, source_target_pairs={{0,4},{1,5},{2,6},{3,7},{4,0},{5,1},{6,2},{7,3},{8,12},{9,13},{10,... | collective-permute-start | bytes 319496 | tf_op jit(solution)/shard_map/ppermute | solution.py:409
  55.7 6.5 %collective-permute-start.12 = (bf16[416,128]{1,0:T(8,128)(2,1)S(1)}, bf16[416,128]{1,0:T(8,128)(2,1)S(1)}, u32[]{:S(2)}, u32[]{:S(2)}) collective-permute-start(bf16[416,128]{1,0:T(8,128)(2,1)S(1)} %get-tuple-element.122), channel_id=1, source_target_pairs={{0,20},{1,21},{2,22},{3,23},{4,16},{5,17},{6,18},{7,19},{8,28},{9,... | collective-permute-start | bytes 319496 | tf_op jit(solution)/shard_map/ppermute | solution.py:409
  62.3 10.3 %collective-permute-start.14 = (bf16[416,128]{1,0:T(8,128)(2,1)S(1)}, bf16[416,128]{1,0:T(8,128)(2,1)S(1)}, u32[]{:S(2)}, u32[]{:S(2)}) collective-permute-start(bf16[416,128]{1,0:T(8,128)(2,1)S(1)} %shard_map.202.refs_8_.refs_0_), channel_id=1, source_target_pairs={{0,1},{1,0},{2,3},{3,2},{4,5},{5,4},{6,7},{7,6},{8,9},{9,8},{10,11... | collective-permute-start | bytes 319496 | tf_op jit(solution)/shard_map/ppermute | solution.py:409
  63.4 9.9 %collective-permute-start.13 = (bf16[768,128]{1,0:T(8,128)(2,1)S(1)}, bf16[768,128]{1,0:T(8,128)(2,1)S(1)}, u32[]{:S(2)}, u32[]{:S(2)}) collective-permute-start(bf16[768,128]{1,0:T(8,128)(2,1)S(1)} %shard_map.201.refs_7_.refs_0_), channel_id=1, source_target_pairs={{0,2},{1,3},{2,0},{3,1},{4,6},{5,7},{6,4},{7,5},{8,10},{9,11},{10,... | collective-permute-start | bytes 589832 | tf_op jit(solution)/shard_map/ppermute | solution.py:409
  73.4 10.4 %collective-permute-start.20 = (bf16[768,128]{1,0:T(8,128)(2,1)S(1)}, bf16[768,128]{1,0:T(8,128)(2,1)S(1)}, u32[]{:S(2)}, u32[]{:S(2)}) collective-permute-start(bf16[768,128]{1,0:T(8,128)(2,1)S(1)} %shard_map.204.refs_1_), channel_id=1, source_target_pairs={{0,20},{1,21},{2,22},{3,23},{4,16},{5,17},{6,18},{7,19},{8,28},{9,... | collective-permute-start | bytes 589832 | tf_op jit(solution)/shard_map/ppermute | solution.py:409
  75.3 8.5 %collective-permute-start.19 = (bf16[768,128]{1,0:T(8,128)(2,1)S(1)}, bf16[768,128]{1,0:T(8,128)(2,1)S(1)}, u32[]{:S(2)}, u32[]{:S(2)}) collective-permute-start(bf16[768,128]{1,0:T(8,128)(2,1)S(1)} %shard_map.204.refs_1_), channel_id=1, source_target_pairs={{0,4},{1,5},{2,6},{3,7},{4,0},{5,1},{6,2},{7,3},{8,12},{9,13},{10,... | collective-permute-start | bytes 589832 | tf_op jit(solution)/shard_map/ppermute | solution.py:409
  76.0 7.8 %collective-permute-start.18 = (bf16[768,128]{1,0:T(8,128)(2,1)S(1)}, bf16[768,128]{1,0:T(8,128)(2,1)S(1)}, u32[]{:S(2)}, u32[]{:S(2)}) collective-permute-start(bf16[768,128]{1,0:T(8,128)(2,1)S(1)} %shard_map.204.refs_1_), channel_id=1, source_target_pairs={{0,16},{1,17},{2,18},{3,19},{4,20},{5,21},{6,22},{7,23},{8,24},{9,... | collective-permute-start | bytes 589832 | tf_op jit(solution)/shard_map/ppermute | solution.py:409
  77.0 6.8 %collective-permute-start.21 = (bf16[416,128]{1,0:T(8,128)(2,1)S(1)}, bf16[416,128]{1,0:T(8,128)(2,1)S(1)}, u32[]{:S(2)}, u32[]{:S(2)}) collective-permute-start(bf16[416,128]{1,0:T(8,128)(2,1)S(1)} %shard_map.205.refs_0_), channel_id=1, source_target_pairs={{0,2},{1,3},{2,0},{3,1},{4,6},{5,7},{6,4},{7,5},{8,10},{9,11},{10,... | collective-permute-start | bytes 319496 | tf_op jit(solution)/shard_map/ppermute | solution.py:409
  83.9 9.0 %collective-permute-start.22 = (bf16[3072,128]{1,0:T(8,128)(2,1)S(1)}, bf16[3072,128]{1,0:T(8,128)(2,1)S(1)}, u32[]{:S(2)}, u32[]{:S(2)}) collective-permute-start(bf16[3072,128]{1,0:T(8,128)(2,1)S(1)} %shard_map.206.own), channel_id=1, source_target_pairs={{0,8},{1,9},{2,10},{3,11},{4,12},{5,13},{6,14},{7,15},{8,0},{9,1},... | collective-permute-start | bytes 2359304 | tf_op jit(solution)/shard_map/ppermute | solution.py:409
  84.0 6.7 %collective-permute-start.25 = (bf16[416,128]{1,0:T(8,128)(2,1)S(1)}, bf16[416,128]{1,0:T(8,128)(2,1)S(1)}, u32[]{:S(2)}, u32[]{:S(2)}) collective-permute-start(bf16[416,128]{1,0:T(8,128)(2,1)S(1)} %shard_map.207.refs_1_), channel_id=1, source_target_pairs={{0,20},{1,21},{2,22},{3,23},{4,16},{5,17},{6,18},{7,19},{8,28},{9,... | collective-permute-start | bytes 319496 | tf_op jit(solution)/shard_map/ppermute | solution.py:409
  85.9 6.7 %collective-permute-start.24 = (bf16[416,128]{1,0:T(8,128)(2,1)S(1)}, bf16[416,128]{1,0:T(8,128)(2,1)S(1)}, u32[]{:S(2)}, u32[]{:S(2)}) collective-permute-start(bf16[416,128]{1,0:T(8,128)(2,1)S(1)} %shard_map.207.refs_1_), channel_id=1, source_target_pairs={{0,4},{1,5},{2,6},{3,7},{4,0},{5,1},{6,2},{7,3},{8,12},{9,13},{10,... | collective-permute-start | bytes 319496 | tf_op jit(solution)/shard_map/ppermute | solution.py:409
  86.6 6.2 %collective-permute-start.23 = (bf16[416,128]{1,0:T(8,128)(2,1)S(1)}, bf16[416,128]{1,0:T(8,128)(2,1)S(1)}, u32[]{:S(2)}, u32[]{:S(2)}) collective-permute-start(bf16[416,128]{1,0:T(8,128)(2,1)S(1)} %shard_map.207.refs_1_), channel_id=1, source_target_pairs={{0,16},{1,17},{2,18},{3,19},{4,20},{5,21},{6,22},{7,23},{8,24},{9,... | collective-permute-start | bytes 319496 | tf_op jit(solution)/shard_map/ppermute | solution.py:409
  92.9 1.9 %collective-permute-start.26 = (bf16[1664,128]{1,0:T(8,128)(2,1)S(1)}, bf16[1664,128]{1,0:T(8,128)(2,1)S(1)}, u32[]{:S(2)}, u32[]{:S(2)}) collective-permute-start(bf16[1664,128]{1,0:T(8,128)(2,1)S(1)} %shard_map.208.own), channel_id=1, source_target_pairs={{0,8},{1,9},{2,10},{3,11},{4,12},{5,13},{6,14},{7,15},{8,0},{9,1},... | collective-permute-start | bytes 1277960 | tf_op jit(solution)/shard_map/ppermute | solution.py:409

commit v12 on v11

--- a/solution.py
+++ b/solution.py
@@ -185,7 +185,7 @@
     pl.when(core[0] != 0)(lambda: store(send, keep))
 
 
-PIXELS = 256
+PIXELS = 512
 
 
 def mlp_block(ln, d_branch, w_in, w_out, b_in, base, width, hid_ref, dpre_ref, gbin):

time: 96.3 us -> 95.7 us (level)
  transfers between devices with their start and end apart: 27 -> 27, of which waited for: 8 -> 7; matrix products, arithmetic and copies ran while one was open for 2% -> 2% of each run, Pallas kernels for 24% -> 23%
where the time goes in v12:
time: 95.7 us; the launch traced here: 95.6 us
  Pallas kernels  39.1 us (41%)
  starting transfers between devices  33.1 us (35%)
  waiting for transfers between devices  19.4 us (20%)
  other arithmetic  1.55 us (2%)
  local copies, waits for them, and re-layouts  1.29 us (1%)
  between operations  1.14 us (1%)
    pallas_call x15, Pallas kernels, call(): pl.pallas_call(kernel, out_shape=[jax.ShapeDtypeStruct(shape, dtype) for...  35.9 us
    ppermute x21, starting transfers between devices, exchange(): return lax.ppermute(x, AXES, perm)  26.8 us
    ppermute x21, waiting for transfers between devices, exchange(): return lax.ppermute(x, AXES, perm)  16.5 us
    ppermute x6, starting transfers between devices, swap_edges(): got.append(lax.ppermute(jnp.where(is_high, high, low), axis, pairs))  6.29 us
    pallas_call x2, Pallas kernels, finish(): pl.pallas_call(kernel, grid=(width // unit,), out_shape=[jax.ShapeDtypeSt...  3.19 us
    ppermute x6, waiting for transfers between devices, swap_edges(): got.append(lax.ppermute(jnp.where(is_high, high, low), axis, pairs))  2.81 us
  transfers between devices with their start and end apart: 27, of which 7 were waited for; matrix products, arithmetic and copies ran while one was open for 2% of the time, Pallas kernels for 23%

profile of v12, /device:TPU:0, one launch (start us, length us, event | category | flops | bytes accessed | tf_op | source)
XLA Modules:
  0.0 95.6 jit_solution(1040905303031546820)
XLA Ops:
  0.6 0.0 copy-start
  0.7 1.0 %broadcast_select_fusion.11 = (bf16[3,32,384]{2,1,0:T(8,128)(2,1)S(1)}, bf16[3,32,384]{2,1,0:T(8,128)(2,1)S(1)}) fusion(pred[]{:T(512)S(6)} %eq.12, bf16[32,32,384]{2,1,0:T(8,128)(2,1)} %bitcast.9, pred[]{:T(512)S(6)} %not.4), kind=kLoop, calls=%fused_computation.13 | loop fusion | flops 73728 | bytes 294914 | tf_op jit(solution)/shard_map/jit(_where)/select_n | solution.py:45
  1.8 0.5 collective-permute-start.1
  2.3 0.7 collective-permute-start
  2.9 1.1 %fusion.1 = (bf16[32,3,384]{2,1,0:T(4,128)(2,1)S(1)}, bf16[32,3,384]{2,1,0:T(4,128)(2,1)S(1)}) fusion(bf16[32,32,384]{2,1,0:T(8,128)(2,1)} %bitcast.10), kind=kLoop, calls=%fused_computation.15 | loop fusion | bytes 294912 | tf_op jit(solution)/shard_map/slice | solution.py:52
  4.0 0.0 collective-permute-done
  4.1 0.2 maximum_select_fusion
  4.3 2.6 %collective-permute-start.2 = (bf16[38,3,384]{2,1,0:T(4,128)(2,1)S(1)}, bf16[38,3,384]{2,1,0:T(4,128)(2,1)S(1)}, u32[]{:S(2)}, u32[]{:S(2)}) collective-permute-start(bf16[38,3,384]{2,1,0:T(4,128)(2,1)S(1)} %maximum_select_fusion), channel_id=1, source_target_pairs={{0,4},{4,0},{1,5},{5,1},{2,6},{6,2},{3,7},{7,3},{8,12},{12,8},{9,1... | collective-permute-start | bytes 262664 | tf_op jit(solution)/shard_map/ppermute | solution.py:45
  6.9 2.8 %collective-permute-done.2 = bf16[38,3,384]{2,1,0:T(4,128)(2,1)S(1)} collective-permute-done((bf16[38,3,384]{2,1,0:T(4,128)(2,1)S(1)}, bf16[38,3,384]{2,1,0:T(4,128)(2,1)S(1)}, u32[]{:S(2)}, u32[]{:S(2)}) %collective-permute-start.2) | collective-permute-done | bytes 87584 | tf_op jit(solution)/shard_map/ppermute | solution.py:45
  9.7 0.1 broadcast_select_fusion.2
  9.8 0.0 copy-start.1
  9.8 0.0 copy-start.2
  9.8 0.0 copy-start.3
  9.9 0.0 copy-start.5
  9.9 0.0 copy-start.9
  9.9 7.3 %shard_map.194 = (f32[1024,384]{1,0:T(8,128)S(1)}, f32[1024,128]{1,0:T(8,128)S(1)}, bf16[1024,384]{1,0:T(8,128)(2,1)S(1)}) custom-call(bf16[32,32,384]{2,1,0:T(8,128)(2,1)S(1)} %bitcast.11, bf16[3,32,384]{2,1,0:T(8,128)(2,1)S(1)} %get-tuple-element.164.refs_1_.refs_2_, bf16[3,32,384]{2,1,0:T(8,128)(2,1)S(1)} %get-tuple-element.163.refs_2_.refs_3_, ...), custom_call_target="tpu_custom_call" | custom-call | flops 2312110080 | bytes 2257920 | tf_op jit(solution)/shard_map/pallas_call | solution.py:376
  17.3 0.0 copy-start.10
  17.3 7.9 %shard_map.195 = (f32[1024,384]{1,0:T(8,128)S(1)}, f32[1024,384]{1,0:T(8,128)S(1)}, bf16[1024,384]{1,0:T(8,128)(2,1)S(1)}, bf16[3072,128]{1,0:T(8,128)(2,1)S(1)}...) custom-call(s32[1]{0:T(128)} %bitcast.refs_0_.core, bf16[1024,384]{1,0:T(8,128)(2,1)S(1)} %get-tuple-element.86.refs_1_, ...), custom_call_target="tpu_custom_call" | custom-call | flops 7247757312 | bytes 7077888 | tf_op jit(solution)/shard_map/pallas_call | solution.py:376
  25.2 3.8 %collective-permute-start.3 = (bf16[3072,128]{1,0:T(8,128)(2,1)S(1)}, bf16[3072,128]{1,0:T(8,128)(2,1)S(1)}, u32[]{:S(2)}, u32[]{:S(2)}) collective-permute-start(bf16[3072,128]{1,0:T(8,128)(2,1)S(1)} %get-tuple-element.95), channel_id=1, source_target_pairs={{0,8},{1,9},{2,10},{3,11},{4,12},{5,13},{6,14},{7,15},{8,0},{9,1},... | collective-permute-start | bytes 2359304 | tf_op jit(solution)/shard_map/ppermute | solution.py:409
  29.0 6.2 %shard_map.196 = (bf16[1024,384]{1,0:T(8,128)(2,1)}, bf16[1024,384]{1,0:T(8,128)(2,1)S(1)}, bf16[1536,128]{1,0:T(8,128)(2,1)S(1)}, bf16[1536,128]{1,0:T(8,128)(2...) custom-call(s32[1]{0:T(128)} %bitcast.refs_0_.core, bf16[1024,384]{1,0:T(8,128)(2,1)S(1)} %get-tuple-element.86.refs_1_, ...), custom_call_target="tpu_custom_call" | custom-call | flops 7247757312 | bytes 7077888 | tf_op jit(solution)/shard_map/pallas_call | solution.py:376
  35.3 0.1 collective-permute-start.16
  35.3 0.8 collective-permute-start.15
  36.2 0.1 fusion
  36.3 0.3 shard_map.197
  36.6 1.8 %collective-permute-start.5 = (bf16[768,128]{1,0:T(8,128)(2,1)S(1)}, bf16[768,128]{1,0:T(8,128)(2,1)S(1)}, u32[]{:S(2)}, u32[]{:S(2)}) collective-permute-start(bf16[768,128]{1,0:T(8,128)(2,1)S(1)} %get-tuple-element.102), channel_id=1, source_target_pairs={{0,4},{1,5},{2,6},{3,7},{4,0},{5,1},{6,2},{7,3},{8,12},{9,13},{10,... | collective-permute-start | bytes 589832 | tf_op jit(solution)/shard_map/ppermute | solution.py:409
  38.4 3.5 %collective-permute-start.6 = (bf16[768,128]{1,0:T(8,128)(2,1)S(1)}, bf16[768,128]{1,0:T(8,128)(2,1)S(1)}, u32[]{:S(2)}, u32[]{:S(2)}) collective-permute-start(bf16[768,128]{1,0:T(8,128)(2,1)S(1)} %get-tuple-element.103), channel_id=1, source_target_pairs={{0,20},{1,21},{2,22},{3,23},{4,16},{5,17},{6,18},{7,19},{8,28},{9,... | collective-permute-start | bytes 589832 | tf_op jit(solution)/shard_map/ppermute | solution.py:409
  41.9 0.1 collective-permute-start.4
  42.0 1.2 %collective-permute-start.7 = (bf16[1536,128]{1,0:T(8,128)(2,1)S(1)}, bf16[1536,128]{1,0:T(8,128)(2,1)S(1)}, u32[]{:S(2)}, u32[]{:S(2)}) collective-permute-start(bf16[1536,128]{1,0:T(8,128)(2,1)S(1)} %get-tuple-element.110), channel_id=1, source_target_pairs={{0,8},{1,9},{2,10},{3,11},{4,12},{5,13},{6,14},{7,15},{8,0},{9,1},... | collective-permute-start | bytes 1179656 | tf_op jit(solution)/shard_map/ppermute | solution.py:409
  43.3 0.2 maximum_select_fusion.1
  43.4 1.6 %collective-permute-start.17 = (bf16[38,3,384]{2,1,0:T(4,128)(2,1)S(1)}, bf16[38,3,384]{2,1,0:T(4,128)(2,1)S(1)}, u32[]{:S(2)}, u32[]{:S(2)}) collective-permute-start(bf16[38,3,384]{2,1,0:T(4,128)(2,1)S(1)} %maximum_select_fusion.1), channel_id=1, source_target_pairs={{0,4},{4,0},{1,5},{5,1},{2,6},{6,2},{3,7},{7,3},{8,12},{12,8},{9,1... | collective-permute-start | bytes 262664 | tf_op jit(solution)/shard_map/ppermute | solution.py:45
  45.0 6.9 %shard_map.198 = (bf16[128,128]{1,0:T(8,128)(2,1)S(1)}, bf16[128,128]{1,0:T(8,128)(2,1)S(1)}) custom-call(s32[1]{0:T(128)} %bitcast.refs_0_.core, bf16[32,32,384]{2,1,0:T(8,128)(2,1)S(1)} %bitcast.13, bf16[3,32,384]{2,1,0:T(8,128)(2,1)S(1)} %get-tuple-element.164.refs_1_.refs_2_, bf16[3,32,384]{2,1,0:T(8,128)(2,1)S(1)} %get-tuple-element.163.refs_2_.refs_3_, ...), custom_call_target="tpu_custom_call" | custom-call | flops 2312110080 | bytes 2257920 | tf_op jit(solution)/shard_map/pallas_call | solution.py:376
  52.0 0.1 collective-permute-start.9
  52.0 0.1 shard_map.199.refs_0_
  52.2 1.6 %collective-permute-start.8 = (bf16[768,128]{1,0:T(8,128)(2,1)S(1)}, bf16[768,128]{1,0:T(8,128)(2,1)S(1)}, u32[]{:S(2)}, u32[]{:S(2)}) collective-permute-start(bf16[768,128]{1,0:T(8,128)(2,1)S(1)} %shard_map.199.refs_0_), channel_id=1, source_target_pairs={{0,1},{1,0},{2,3},{3,2},{4,5},{5,4},{6,7},{7,6},{8,9},{9,8},{10,11... | collective-permute-start | bytes 589832 | tf_op jit(solution)/shard_map/ppermute | solution.py:409
  53.8 0.1 shard_map.200
  53.9 1.2 %collective-permute-start.10 = (bf16[416,128]{1,0:T(8,128)(2,1)S(1)}, bf16[416,128]{1,0:T(8,128)(2,1)S(1)}, u32[]{:S(2)}, u32[]{:S(2)}) collective-permute-start(bf16[416,128]{1,0:T(8,128)(2,1)S(1)} %get-tuple-element.120), channel_id=1, source_target_pairs={{0,16},{1,17},{2,18},{3,19},{4,20},{5,21},{6,22},{7,23},{8,24},{9,... | collective-permute-start | bytes 319496 | tf_op jit(solution)/shard_map/ppermute | solution.py:409
  55.1 0.5 collective-permute-start.11
  55.6 1.9 %collective-permute-start.12 = (bf16[416,128]{1,0:T(8,128)(2,1)S(1)}, bf16[416,128]{1,0:T(8,128)(2,1)S(1)}, u32[]{:S(2)}, u32[]{:S(2)}) collective-permute-start(bf16[416,128]{1,0:T(8,128)(2,1)S(1)} %get-tuple-element.122), channel_id=1, source_target_pairs={{0,20},{1,21},{2,22},{3,23},{4,16},{5,17},{6,18},{7,19},{8,28},{9,... | collective-permute-start | bytes 319496 | tf_op jit(solution)/shard_map/ppermute | solution.py:409
  57.5 0.1 broadcast_select_fusion
  57.6 1.7 %collective-permute-done.10.refs_1_ = bf16[416,128]{1,0:T(8,128)(2,1)S(1)} collective-permute-done((bf16[416,128]{1,0:T(8,128)(2,1)S(1)}, bf16[416,128]{1,0:T(8,128)(2,1)S(1)}, u32[]{:S(2)}, u32[]{:S(2)}) %collective-permute-start.10) | collective-permute-done | bytes 106528 | tf_op jit(solution)/shard_map/ppermute | solution.py:409
  59.3 2.9 %collective-permute-done.11.refs_2_ = bf16[416,128]{1,0:T(8,128)(2,1)S(1)} collective-permute-done((bf16[416,128]{1,0:T(8,128)(2,1)S(1)}, bf16[416,128]{1,0:T(8,128)(2,1)S(1)}, u32[]{:S(2)}, u32[]{:S(2)}) %collective-permute-start.11) | collective-permute-done | bytes 106528 | tf_op jit(solution)/shard_map/ppermute | solution.py:409
  62.2 0.1 shard_map.201.refs_7_.refs_0_
  62.3 0.1 shard_map.202.refs_8_.refs_0_
  62.4 1.0 %collective-permute-start.14 = (bf16[416,128]{1,0:T(8,128)(2,1)S(1)}, bf16[416,128]{1,0:T(8,128)(2,1)S(1)}, u32[]{:S(2)}, u32[]{:S(2)}) collective-permute-start(bf16[416,128]{1,0:T(8,128)(2,1)S(1)} %shard_map.202.refs_8_.refs_0_), channel_id=1, source_target_pairs={{0,1},{1,0},{2,3},{3,2},{4,5},{5,4},{6,7},{7,6},{8,9},{9,8},{10,11... | collective-permute-start | bytes 319496 | tf_op jit(solution)/shard_map/ppermute | solution.py:409
  63.4 2.6 %collective-permute-start.13 = (bf16[768,128]{1,0:T(8,128)(2,1)S(1)}, bf16[768,128]{1,0:T(8,128)(2,1)S(1)}, u32[]{:S(2)}, u32[]{:S(2)}) collective-permute-start(bf16[768,128]{1,0:T(8,128)(2,1)S(1)} %shard_map.201.refs_7_.refs_0_), channel_id=1, source_target_pairs={{0,2},{1,3},{2,0},{3,1},{4,6},{5,7},{6,4},{7,5},{8,10},{9,11},{10,... | collective-permute-start | bytes 589832 | tf_op jit(solution)/shard_map/ppermute | solution.py:409
  66.0 6.7 %shard_map.203 = bf16[1024,384]{1,0:T(8,128)(2,1)} custom-call(bf16[32,32,384]{2,1,0:T(8,128)(2,1)S(1)} %bitcast.16, bf16[3,32,384]{2,1,0:T(8,128)(2,1)S(1)} %get-tuple-element.162.refs_1_, bf16[3,32,384]{2,1,0:T(8,128)(2,1)S(1)} %get-tuple-element.161.refs_2_, bf16[38,3,384]{2,1,0:T(4,128)(2,1)S(1)} %get-tuple-element.166.refs_3_, ...), custom_call_target="tpu_custom_call" | custom-call | flops 2312110080 | bytes 2257920 | tf_op jit(solution)/shard_map/pallas_call | solution.py:376
  72.7 0.2 collective-permute-done.13.refs_1_
  72.9 0.1 shard_map.204.refs_1_
  73.0 2.5 %collective-permute-start.20 = (bf16[768,128]{1,0:T(8,128)(2,1)S(1)}, bf16[768,128]{1,0:T(8,128)(2,1)S(1)}, u32[]{:S(2)}, u32[]{:S(2)}) collective-permute-start(bf16[768,128]{1,0:T(8,128)(2,1)S(1)} %shard_map.204.refs_1_), channel_id=1, source_target_pairs={{0,20},{1,21},{2,22},{3,23},{4,16},{5,17},{6,18},{7,19},{8,28},{9,... | collective-permute-start | bytes 589832 | tf_op jit(solution)/shard_map/ppermute | solution.py:409
  75.5 0.5 collective-permute-start.19
  76.0 0.5 collective-permute-start.18
  76.6 0.2 collective-permute-start.21
  76.8 6.6 %collective-permute-done.21.refs_1_ = bf16[416,128]{1,0:T(8,128)(2,1)S(1)} collective-permute-done((bf16[416,128]{1,0:T(8,128)(2,1)S(1)}, bf16[416,128]{1,0:T(8,128)(2,1)S(1)}, u32[]{:S(2)}, u32[]{:S(2)}) %collective-permute-start.21) | collective-permute-done | bytes 106528 | tf_op jit(solution)/shard_map/ppermute | solution.py:409
  83.4 0.1 shard_map.206.own
  83.5 0.1 collective-permute-start.22
  83.5 0.1 shard_map.207.refs_1_
  83.6 2.5 %collective-permute-start.25 = (bf16[416,128]{1,0:T(8,128)(2,1)S(1)}, bf16[416,128]{1,0:T(8,128)(2,1)S(1)}, u32[]{:S(2)}, u32[]{:S(2)}) collective-permute-start(bf16[416,128]{1,0:T(8,128)(2,1)S(1)} %shard_map.207.refs_1_), channel_id=1, source_target_pairs={{0,20},{1,21},{2,22},{3,23},{4,16},{5,17},{6,18},{7,19},{8,28},{9,... | collective-permute-start | bytes 319496 | tf_op jit(solution)/shard_map/ppermute | solution.py:409
  86.1 0.5 collective-permute-start.24
  86.6 0.5 collective-permute-start.23
  87.2 2.9 %collective-permute-done.25.refs_4_ = bf16[416,128]{1,0:T(8,128)(2,1)S(1)} collective-permute-done((bf16[416,128]{1,0:T(8,128)(2,1)S(1)}, bf16[416,128]{1,0:T(8,128)(2,1)S(1)}, u32[]{:S(2)}, u32[]{:S(2)}) %collective-permute-start.25) | collective-permute-done | bytes 106528 | tf_op jit(solution)/shard_map/ppermute | solution.py:409
  90.0 2.2 %collective-permute-done.24.refs_3_ = bf16[416,128]{1,0:T(8,128)(2,1)S(1)} collective-permute-done((bf16[416,128]{1,0:T(8,128)(2,1)S(1)}, bf16[416,128]{1,0:T(8,128)(2,1)S(1)}, u32[]{:S(2)}, u32[]{:S(2)}) %collective-permute-start.24) | collective-permute-done | bytes 106528 | tf_op jit(solution)/shard_map/ppermute | solution.py:409
  92.2 0.1 collective-permute-start.26
  92.4 1.8 %shard_map.209 = (f32[1536,384]{1,0:T(8,128)}, f32[384,1536]{1,0:T(8,128)}) custom-call(s32[1]{0:T(128)} %bitcast.refs_0_.core, bf16[3072,128]{1,0:T(8,128)(2,1)S(1)} %shard_map.206.own, bf16[3072,128]{1,0:T(8,128)(2,1)S(1)} %collective-permute-done.22.other), custom_call_target="tpu_custom_call" | custom-call | tf_op jit(solution)/shard_map/pallas_call | solution.py:548
  94.2 1.4 %shard_map.210 = (f32[1536,384]{1,0:T(8,128)}, f32[384,1536]{1,0:T(8,128)}, f32[7,7,384]{2,1,0:T(8,128)}, f32[384]{0:T(512)}, f32[384]{0:T(512)}, /*index=5*/f32...) custom-call(s32[1]{0:T(128)} %bitcast.refs_0_.core, ...), custom_call_target="tpu_custom_call", output_to_operand_aliasing={{0}: (3, {}), {1}: (4, {})} | custom-call | tf_op jit(solution)/shard_map/pallas_call | solution.py:548
  (42 shorter events, 0.3 us)
Async XLA Ops:
  0.6 9.1 %copy-start = (bf16[1,32,32,384]{3,2,1,0:T(8,128)(2,1)S(1)}, bf16[1,32,32,384]{3,2,1,0:T(8,128)(2,1)}, u32[]{:S(2)}) copy-start(bf16[1,32,32,384]{3,2,1,0:T(8,128)(2,1)} %param.11) | copy-start | bytes 2359300
  0.7 9.1 %copy-start.8 = (f32[384]{0:T(512)S(1)}, f32[384]{0:T(512)}, u32[]{:S(2)}) copy-start(f32[384]{0:T(512)} %refs_8_.3) | copy-start | bytes 4612
  0.7 9.1 %copy-start.4 = (f32[7,7,384]{2,1,0:T(8,128)S(1)}, f32[7,7,384]{2,1,0:T(8,128)}, u32[]{:S(2)}) copy-start(f32[7,7,384]{2,1,0:T(8,128)} %refs_5_.7) | copy-start | bytes 225796
  0.7 9.1 %copy-start.7 = (f32[384]{0:T(512)S(1)}, f32[384]{0:T(512)}, u32[]{:S(2)}) copy-start(f32[384]{0:T(512)} %refs_8_.2) | copy-start | bytes 4612
  0.7 9.1 %copy-start.6 = (f32[384]{0:T(512)S(1)}, f32[384]{0:T(512)}, u32[]{:S(2)}) copy-start(f32[384]{0:T(512)} %refs_6_.3) | copy-start | bytes 4612
  1.8 2.3 %collective-permute-start.1 = (bf16[3,32,384]{2,1,0:T(8,128)(2,1)S(1)}, bf16[3,32,384]{2,1,0:T(8,128)(2,1)S(1)}, u32[]{:S(2)}, u32[]{:S(2)}) collective-permute-start(bf16[3,32,384]{2,1,0:T(8,128)(2,1)S(1)} %get-tuple-element.159), channel_id=1, source_target_pairs={{0,8},{16,24},{8,0},{24,16},{1,9},{17,25},{9,1},{25,17},{2,10},{18... | collective-permute-start | bytes 221192 | tf_op jit(solution)/shard_map/ppermute | solution.py:45
  2.3 1.8 %collective-permute-start = (bf16[3,32,384]{2,1,0:T(8,128)(2,1)S(1)}, bf16[3,32,384]{2,1,0:T(8,128)(2,1)S(1)}, u32[]{:S(2)}, u32[]{:S(2)}) collective-permute-start(bf16[3,32,384]{2,1,0:T(8,128)(2,1)S(1)} %get-tuple-element.160), channel_id=1, source_target_pairs={{8,16},{16,8},{9,17},{17,9},{10,18},{18,10},{11,19},{19,11},{12,20... | collective-permute-start | bytes 221192 | tf_op jit(solution)/shard_map/ppermute | solution.py:45
  4.3 5.4 %collective-permute-start.2 = (bf16[38,3,384]{2,1,0:T(4,128)(2,1)S(1)}, bf16[38,3,384]{2,1,0:T(4,128)(2,1)S(1)}, u32[]{:S(2)}, u32[]{:S(2)}) collective-permute-start(bf16[38,3,384]{2,1,0:T(4,128)(2,1)S(1)} %maximum_select_fusion), channel_id=1, source_target_pairs={{0,4},{4,0},{1,5},{5,1},{2,6},{6,2},{3,7},{7,3},{8,12},{12,8},{9,1... | collective-permute-start | bytes 262664 | tf_op jit(solution)/shard_map/ppermute | solution.py:45
  9.8 7.4 %copy-start.1 = (bf16[1536,384]{1,0:T(8,128)(2,1)S(1)}, bf16[1536,384]{1,0:T(8,128)(2,1)}, u32[]{:S(2)}) copy-start(bf16[1536,384]{1,0:T(8,128)(2,1)} %refs_3_.3) | copy-start | bytes 3538948
  9.8 7.4 %copy-start.2 = (bf16[384,1536]{1,0:T(8,128)(2,1)S(1)}, bf16[384,1536]{1,0:T(8,128)(2,1)}, u32[]{:S(2)}) copy-start(bf16[384,1536]{1,0:T(8,128)(2,1)} %refs_4_.3) | copy-start | bytes 3538948
  9.8 7.4 %copy-start.3 = (bf16[1,32,32,384]{3,2,1,0:T(8,128)(2,1)S(1)}, bf16[1,32,32,384]{3,2,1,0:T(8,128)(2,1)}, u32[]{:S(2)}) copy-start(bf16[1,32,32,384]{3,2,1,0:T(8,128)(2,1)} %param.12) | copy-start | bytes 2359300
  9.9 7.4 %copy-start.5 = (f32[1536]{0:T(1024)S(1)}, f32[1536]{0:T(1024)}, u32[]{:S(2)}) copy-start(f32[1536]{0:T(1024)} %refs_5_.6) | copy-start | bytes 18436
  9.9 7.4 %copy-start.9 = (f32[384]{0:T(512)S(1)}, f32[384]{0:T(512)}, u32[]{:S(2)}) copy-start(f32[384]{0:T(512)} %refs_6_.5) | copy-start | bytes 4612
  17.3 11.7 %copy-start.10 = (f32[384]{0:T(512)S(1)}, f32[384]{0:T(512)}, u32[]{:S(2)}) copy-start(f32[384]{0:T(512)} %refs_7_.3) | copy-start | bytes 4612
  25.2 10.1 %collective-permute-start.3 = (bf16[3072,128]{1,0:T(8,128)(2,1)S(1)}, bf16[3072,128]{1,0:T(8,128)(2,1)S(1)}, u32[]{:S(2)}, u32[]{:S(2)}) collective-permute-start(bf16[3072,128]{1,0:T(8,128)(2,1)S(1)} %get-tuple-element.95), channel_id=1, source_target_pairs={{0,8},{1,9},{2,10},{3,11},{4,12},{5,13},{6,14},{7,15},{8,0},{9,1},... | collective-permute-start | bytes 2359304 | tf_op jit(solution)/shard_map/ppermute | solution.py:409
  35.3 6.7 %collective-permute-start.16 = (bf16[3,32,384]{2,1,0:T(8,128)(2,1)S(1)}, bf16[3,32,384]{2,1,0:T(8,128)(2,1)S(1)}, u32[]{:S(2)}, u32[]{:S(2)}) collective-permute-start(bf16[3,32,384]{2,1,0:T(8,128)(2,1)S(1)} %get-tuple-element.155), channel_id=1, source_target_pairs={{0,8},{16,24},{8,0},{24,16},{1,9},{17,25},{9,1},{25,17},{2,10},{18... | collective-permute-start | bytes 221192 | tf_op jit(solution)/shard_map/ppermute | solution.py:45
  35.3 7.9 %collective-permute-start.15 = (bf16[3,32,384]{2,1,0:T(8,128)(2,1)S(1)}, bf16[3,32,384]{2,1,0:T(8,128)(2,1)S(1)}, u32[]{:S(2)}, u32[]{:S(2)}) collective-permute-start(bf16[3,32,384]{2,1,0:T(8,128)(2,1)S(1)} %get-tuple-element.156), channel_id=1, source_target_pairs={{8,16},{16,8},{9,17},{17,9},{10,18},{18,10},{11,19},{19,11},{12,20... | collective-permute-start | bytes 221192 | tf_op jit(solution)/shard_map/ppermute | solution.py:45
  36.6 15.4 %collective-permute-start.5 = (bf16[768,128]{1,0:T(8,128)(2,1)S(1)}, bf16[768,128]{1,0:T(8,128)(2,1)S(1)}, u32[]{:S(2)}, u32[]{:S(2)}) collective-permute-start(bf16[768,128]{1,0:T(8,128)(2,1)S(1)} %get-tuple-element.102), channel_id=1, source_target_pairs={{0,4},{1,5},{2,6},{3,7},{4,0},{5,1},{6,2},{7,3},{8,12},{9,13},{10,... | collective-permute-start | bytes 589832 | tf_op jit(solution)/shard_map/ppermute | solution.py:409
  38.4 13.6 %collective-permute-start.6 = (bf16[768,128]{1,0:T(8,128)(2,1)S(1)}, bf16[768,128]{1,0:T(8,128)(2,1)S(1)}, u32[]{:S(2)}, u32[]{:S(2)}) collective-permute-start(bf16[768,128]{1,0:T(8,128)(2,1)S(1)} %get-tuple-element.103), channel_id=1, source_target_pairs={{0,20},{1,21},{2,22},{3,23},{4,16},{5,17},{6,18},{7,19},{8,28},{9,... | collective-permute-start | bytes 589832 | tf_op jit(solution)/shard_map/ppermute | solution.py:409
  41.9 10.0 %collective-permute-start.4 = (bf16[768,128]{1,0:T(8,128)(2,1)S(1)}, bf16[768,128]{1,0:T(8,128)(2,1)S(1)}, u32[]{:S(2)}, u32[]{:S(2)}) collective-permute-start(bf16[768,128]{1,0:T(8,128)(2,1)S(1)} %get-tuple-element.101.refs_10_), channel_id=1, source_target_pairs={{0,16},{1,17},{2,18},{3,19},{4,20},{5,21},{6,22},{7,23},{8,24},{9,... | collective-permute-start | bytes 589832 | tf_op jit(solution)/shard_map/ppermute | solution.py:409
  42.0 10.0 %collective-permute-start.7 = (bf16[1536,128]{1,0:T(8,128)(2,1)S(1)}, bf16[1536,128]{1,0:T(8,128)(2,1)S(1)}, u32[]{:S(2)}, u32[]{:S(2)}) collective-permute-start(bf16[1536,128]{1,0:T(8,128)(2,1)S(1)} %get-tuple-element.110), channel_id=1, source_target_pairs={{0,8},{1,9},{2,10},{3,11},{4,12},{5,13},{6,14},{7,15},{8,0},{9,1},... | collective-permute-start | bytes 1179656 | tf_op jit(solution)/shard_map/ppermute | solution.py:409
  43.4 14.0 %collective-permute-start.17 = (bf16[38,3,384]{2,1,0:T(4,128)(2,1)S(1)}, bf16[38,3,384]{2,1,0:T(4,128)(2,1)S(1)}, u32[]{:S(2)}, u32[]{:S(2)}) collective-permute-start(bf16[38,3,384]{2,1,0:T(4,128)(2,1)S(1)} %maximum_select_fusion.1), channel_id=1, source_target_pairs={{0,4},{4,0},{1,5},{5,1},{2,6},{6,2},{3,7},{7,3},{8,12},{12,8},{9,1... | collective-permute-start | bytes 262664 | tf_op jit(solution)/shard_map/ppermute | solution.py:45
  52.0 1.9 %collective-permute-start.9 = (bf16[128,128]{1,0:T(8,128)(2,1)S(1)}, bf16[128,128]{1,0:T(8,128)(2,1)S(1)}, u32[]{:S(2)}, u32[]{:S(2)}) collective-permute-start(bf16[128,128]{1,0:T(8,128)(2,1)S(1)} %get-tuple-element.118), channel_id=1, source_target_pairs={{0,8},{1,9},{2,10},{3,11},{4,12},{5,13},{6,14},{7,15},{8,0},{9,1},... | collective-permute-start | bytes 98312 | tf_op jit(solution)/shard_map/ppermute | solution.py:409
  52.2 10.0 %collective-permute-start.8 = (bf16[768,128]{1,0:T(8,128)(2,1)S(1)}, bf16[768,128]{1,0:T(8,128)(2,1)S(1)}, u32[]{:S(2)}, u32[]{:S(2)}) collective-permute-start(bf16[768,128]{1,0:T(8,128)(2,1)S(1)} %shard_map.199.refs_0_), channel_id=1, source_target_pairs={{0,1},{1,0},{2,3},{3,2},{4,5},{5,4},{6,7},{7,6},{8,9},{9,8},{10,11... | collective-permute-start | bytes 589832 | tf_op jit(solution)/shard_map/ppermute | solution.py:409
  53.9 5.4 %collective-permute-start.10 = (bf16[416,128]{1,0:T(8,128)(2,1)S(1)}, bf16[416,128]{1,0:T(8,128)(2,1)S(1)}, u32[]{:S(2)}, u32[]{:S(2)}) collective-permute-start(bf16[416,128]{1,0:T(8,128)(2,1)S(1)} %get-tuple-element.120), channel_id=1, source_target_pairs={{0,16},{1,17},{2,18},{3,19},{4,20},{5,21},{6,22},{7,23},{8,24},{9,... | collective-permute-start | bytes 319496 | tf_op jit(solution)/shard_map/ppermute | solution.py:409
  55.1 7.1 %collective-permute-start.11 = (bf16[416,128]{1,0:T(8,128)(2,1)S(1)}, bf16[416,128]{1,0:T(8,128)(2,1)S(1)}, u32[]{:S(2)}, u32[]{:S(2)}) collective-permute-start(bf16[416,128]{1,0:T(8,128)(2,1)S(1)} %get-tuple-element.121), channel_id=1, source_target_pairs={{0,4},{1,5},{2,6},{3,7},{4,0},{5,1},{6,2},{7,3},{8,12},{9,13},{10,... | collective-permute-start | bytes 319496 | tf_op jit(solution)/shard_map/ppermute | solution.py:409
  55.6 6.6 %collective-permute-start.12 = (bf16[416,128]{1,0:T(8,128)(2,1)S(1)}, bf16[416,128]{1,0:T(8,128)(2,1)S(1)}, u32[]{:S(2)}, u32[]{:S(2)}) collective-permute-start(bf16[416,128]{1,0:T(8,128)(2,1)S(1)} %get-tuple-element.122), channel_id=1, source_target_pairs={{0,20},{1,21},{2,22},{3,23},{4,16},{5,17},{6,18},{7,19},{8,28},{9,... | collective-permute-start | bytes 319496 | tf_op jit(solution)/shard_map/ppermute | solution.py:409
  62.4 10.3 %collective-permute-start.14 = (bf16[416,128]{1,0:T(8,128)(2,1)S(1)}, bf16[416,128]{1,0:T(8,128)(2,1)S(1)}, u32[]{:S(2)}, u32[]{:S(2)}) collective-permute-start(bf16[416,128]{1,0:T(8,128)(2,1)S(1)} %shard_map.202.refs_8_.refs_0_), channel_id=1, source_target_pairs={{0,1},{1,0},{2,3},{3,2},{4,5},{5,4},{6,7},{7,6},{8,9},{9,8},{10,11... | collective-permute-start | bytes 319496 | tf_op jit(solution)/shard_map/ppermute | solution.py:409
  63.4 9.5 %collective-permute-start.13 = (bf16[768,128]{1,0:T(8,128)(2,1)S(1)}, bf16[768,128]{1,0:T(8,128)(2,1)S(1)}, u32[]{:S(2)}, u32[]{:S(2)}) collective-permute-start(bf16[768,128]{1,0:T(8,128)(2,1)S(1)} %shard_map.201.refs_7_.refs_0_), channel_id=1, source_target_pairs={{0,2},{1,3},{2,0},{3,1},{4,6},{5,7},{6,4},{7,5},{8,10},{9,11},{10,... | collective-permute-start | bytes 589832 | tf_op jit(solution)/shard_map/ppermute | solution.py:409
  73.0 10.4 %collective-permute-start.20 = (bf16[768,128]{1,0:T(8,128)(2,1)S(1)}, bf16[768,128]{1,0:T(8,128)(2,1)S(1)}, u32[]{:S(2)}, u32[]{:S(2)}) collective-permute-start(bf16[768,128]{1,0:T(8,128)(2,1)S(1)} %shard_map.204.refs_1_), channel_id=1, source_target_pairs={{0,20},{1,21},{2,22},{3,23},{4,16},{5,17},{6,18},{7,19},{8,28},{9,... | collective-permute-start | bytes 589832 | tf_op jit(solution)/shard_map/ppermute | solution.py:409
  75.5 7.9 %collective-permute-start.19 = (bf16[768,128]{1,0:T(8,128)(2,1)S(1)}, bf16[768,128]{1,0:T(8,128)(2,1)S(1)}, u32[]{:S(2)}, u32[]{:S(2)}) collective-permute-start(bf16[768,128]{1,0:T(8,128)(2,1)S(1)} %shard_map.204.refs_1_), channel_id=1, source_target_pairs={{0,4},{1,5},{2,6},{3,7},{4,0},{5,1},{6,2},{7,3},{8,12},{9,13},{10,... | collective-permute-start | bytes 589832 | tf_op jit(solution)/shard_map/ppermute | solution.py:409
  76.0 7.4 %collective-permute-start.18 = (bf16[768,128]{1,0:T(8,128)(2,1)S(1)}, bf16[768,128]{1,0:T(8,128)(2,1)S(1)}, u32[]{:S(2)}, u32[]{:S(2)}) collective-permute-start(bf16[768,128]{1,0:T(8,128)(2,1)S(1)} %shard_map.204.refs_1_), channel_id=1, source_target_pairs={{0,16},{1,17},{2,18},{3,19},{4,20},{5,21},{6,22},{7,23},{8,24},{9,... | collective-permute-start | bytes 589832 | tf_op jit(solution)/shard_map/ppermute | solution.py:409
  76.6 6.8 %collective-permute-start.21 = (bf16[416,128]{1,0:T(8,128)(2,1)S(1)}, bf16[416,128]{1,0:T(8,128)(2,1)S(1)}, u32[]{:S(2)}, u32[]{:S(2)}) collective-permute-start(bf16[416,128]{1,0:T(8,128)(2,1)S(1)} %shard_map.205.refs_0_), channel_id=1, source_target_pairs={{0,2},{1,3},{2,0},{3,1},{4,6},{5,7},{6,4},{7,5},{8,10},{9,11},{10,... | collective-permute-start | bytes 319496 | tf_op jit(solution)/shard_map/ppermute | solution.py:409
  83.5 8.8 %collective-permute-start.22 = (bf16[3072,128]{1,0:T(8,128)(2,1)S(1)}, bf16[3072,128]{1,0:T(8,128)(2,1)S(1)}, u32[]{:S(2)}, u32[]{:S(2)}) collective-permute-start(bf16[3072,128]{1,0:T(8,128)(2,1)S(1)} %shard_map.206.own), channel_id=1, source_target_pairs={{0,8},{1,9},{2,10},{3,11},{4,12},{5,13},{6,14},{7,15},{8,0},{9,1},... | collective-permute-start | bytes 2359304 | tf_op jit(solution)/shard_map/ppermute | solution.py:409
  83.6 6.4 %collective-permute-start.25 = (bf16[416,128]{1,0:T(8,128)(2,1)S(1)}, bf16[416,128]{1,0:T(8,128)(2,1)S(1)}, u32[]{:S(2)}, u32[]{:S(2)}) collective-permute-start(bf16[416,128]{1,0:T(8,128)(2,1)S(1)} %shard_map.207.refs_1_), channel_id=1, source_target_pairs={{0,20},{1,21},{2,22},{3,23},{4,16},{5,17},{6,18},{7,19},{8,28},{9,... | collective-permute-start | bytes 319496 | tf_op jit(solution)/shard_map/ppermute | solution.py:409
  86.1 6.1 %collective-permute-start.24 = (bf16[416,128]{1,0:T(8,128)(2,1)S(1)}, bf16[416,128]{1,0:T(8,128)(2,1)S(1)}, u32[]{:S(2)}, u32[]{:S(2)}) collective-permute-start(bf16[416,128]{1,0:T(8,128)(2,1)S(1)} %shard_map.207.refs_1_), channel_id=1, source_target_pairs={{0,4},{1,5},{2,6},{3,7},{4,0},{5,1},{6,2},{7,3},{8,12},{9,13},{10,... | collective-permute-start | bytes 319496 | tf_op jit(solution)/shard_map/ppermute | solution.py:409
  86.6 5.6 %collective-permute-start.23 = (bf16[416,128]{1,0:T(8,128)(2,1)S(1)}, bf16[416,128]{1,0:T(8,128)(2,1)S(1)}, u32[]{:S(2)}, u32[]{:S(2)}) collective-permute-start(bf16[416,128]{1,0:T(8,128)(2,1)S(1)} %shard_map.207.refs_1_), channel_id=1, source_target_pairs={{0,16},{1,17},{2,18},{3,19},{4,20},{5,21},{6,22},{7,23},{8,24},{9,... | collective-permute-start | bytes 319496 | tf_op jit(solution)/shard_map/ppermute | solution.py:409
  92.2 1.9 %collective-permute-start.26 = (bf16[1664,128]{1,0:T(8,128)(2,1)S(1)}, bf16[1664,128]{1,0:T(8,128)(2,1)S(1)}, u32[]{:S(2)}, u32[]{:S(2)}) collective-permute-start(bf16[1664,128]{1,0:T(8,128)(2,1)S(1)} %shard_map.208.own), channel_id=1, source_target_pairs={{0,8},{1,9},{2,10},{3,11},{4,12},{5,13},{6,14},{7,15},{8,0},{9,1},... | collective-permute-start | bytes 1277960 | tf_op jit(solution)/shard_map/ppermute | solution.py:409
